TPU v7x, 32 devices: a whole 2x2x4 slice. The times are simulated.
32 devices in a mesh: section: 2 (over core), dp: 16 (over z, y, x).
Axes of the slice: x: 2, y: 2, z: 4, core: 2. Of those that a mesh axis runs over, the one named last changes fastest.
Arguments:
- block_input: bfloat16 [6, 4096, 1280], P(None, 'dp'), may hold values from -6 to 6
- output_cotangent: bfloat16 [6, 4096, 1280], P(None, 'dp'), may hold values from -6 to 6
- residues_before: int32 [6, 4096], P(None, 'dp'), may hold values from 0 to 1023, as said below
- residues_after: int32 [6, 4096], P(None, 'dp'), may hold values from 0 to 1023, as said below
- residue_types: int32 [6, 4096], P(None, 'dp'), may hold values from 0 to 24
- loss_mask: int32 [6, 4096], P(None, 'dp'), may hold values from 0 to 1, as said below
- first_gain: float32 [2, 1280], P('section'), may hold values from 0.5 to 1.5
- first_shift: float32 [2, 1280], P('section'), may hold values from -3 to 3
- narrow_weight: bfloat16 [2, 1280, 640], P('section'), may hold values from -0.15625 to 0.15625
- narrow_bias: float32 [2, 640], P('section'), may hold values from -3 to 3
- middle_gain: float32 [2, 640], P('section'), may hold values from 0.5 to 1.5
- middle_shift: float32 [2, 640], P('section'), may hold values from -3 to 3
- conv_weight: bfloat16 [2, 5, 640, 640], P('section'), may hold values from -0.109375 to 0.109375
- conv_bias: float32 [2, 640], P('section'), may hold values from -3 to 3
- last_gain: float32 [2, 640], P('section'), may hold values from 0.5 to 1.5
- last_shift: float32 [2, 640], P('section'), may hold values from -3 to 3
- widen_weight: bfloat16 [2, 640, 1280], P('section'), may hold values from -0.3125 to 0.3125
- widen_bias: float32 [2, 1280], P('section'), may hold values from -3 to 3
- head_weight: bfloat16 [1280, 30], replicated, may hold values from -0.3125 to 0.3125
Outputs:
- block_outputs: bfloat16 [2, 6, 4096, 1280], P('section', None, 'dp')
- input_grads: bfloat16 [2, 6, 4096, 1280], P('section', None, 'dp')
- first_gain_grad: float32 [2, 1280], P('section')
- first_shift_grad: float32 [2, 1280], P('section')
- narrow_weight_grad: float32 [2, 1280, 640], P('section')
- narrow_bias_grad: float32 [2, 640], P('section')
- middle_gain_grad: float32 [2, 640], P('section')
- middle_shift_grad: float32 [2, 640], P('section')
- conv_weight_grad: float32 [2, 5, 640, 640], P('section')
- conv_bias_grad: float32 [2, 640], P('section')
- last_gain_grad: float32 [2, 640], P('section')
- last_shift_grad: float32 [2, 640], P('section')
- widen_weight_grad: float32 [2, 640, 1280], P('section')
- widen_bias_grad: float32 [2, 1280], P('section')
- type_counts: int32 [30], replicated
- type_loss: float32 [30], replicated
Inputs may be any that keep to these rules, and one draw needn't show every extreme that they name: Each micro-batch's stream is packed with whole proteins laid end to end; residues_before and residues_after count the residues of the same protein before and after each position, so they fall to 0 at the first and last residue of every protein. No protein has more than 1024 residues, and each micro-batch holds one of exactly 1024. `residues_after`: consistent with residues_before: the two add up to the protein's length minus one. `residue_types`: types 30 - 5 to 29 never occur. `loss_mask`: each residue is scored with a chance that rises from 1/20 at the start of the stream to 3/10 at its end.
All inputs are finite; a program needn't handle non-finite values.
Results may differ from a plain program's by a relative error of at most 0.0095.
Values may be sent and summed in bfloat16 or wider, within the bound.
No kernel may reach another device: no remote copies, remote signals or barrier semaphores. Data moves between devices by JAX's collectives and lax.ppermute only.
A program may use at most 320 MiB of HBM per device.

v0:
```python
import jax
import jax.numpy as jnp
from jax import lax
from jax.sharding import PartitionSpec as P

KERNEL_TAPS = 5
DILATION_BLOCK1 = 2
DILATION_BLOCK2 = 64


epsilon = 1e-05


def extended_2(cells, sides, width):
    for axis, dim in sides:
        count = lax.axis_size(axis)
        ends = count - 1
        head = lax.slice_in_dim(cells, 0, width, axis=dim)
        tail = lax.slice_in_dim(cells, cells.shape[dim] - width, cells.shape[dim], axis=dim)
        cells = jnp.concatenate(
            [
                lax.ppermute(tail, axis, [(i, (i + 1) % count) for i in range(ends)]),
                cells,
                lax.ppermute(head, axis, [((i + 1) % count, i) for i in range(ends)]),
            ],
            axis=dim,
        )
    return cells


def passed_along(block, axis, distance):
    devices = range(lax.axis_size(axis))
    route = [(i - distance, i) for i in devices if i - distance in devices]
    return lax.ppermute(block, axis, route)


def norm_act(values, gain_row, shift_row):
    center = values - jnp.mean(values, axis=-1, keepdims=True)
    spread = jnp.mean(center * center, axis=-1, keepdims=True)
    return jax.nn.gelu(
        center * lax.rsqrt(spread + epsilon) * gain_row + shift_row, approximate=False
    )


def tap_valid_mask(leading_rows, following_rows, dilation_size):
    offsets = (jnp.arange(KERNEL_TAPS, dtype=jnp.int32) - KERNEL_TAPS // 2) * dilation_size
    return (
        (offsets[None, :] >= -leading_rows[:, None]) & (offsets[None, :] <= following_rows[:, None])
    ).astype(jnp.float32)


def contract_rows(left_side, right_side):
    return lax.dot_general(
        left_side, right_side, (((0,), (0,)), ((), ())), preferred_element_type=jnp.float32
    )


def contract_cols(left_side, right_side):
    return lax.dot_general(
        left_side, right_side, (((1,), (1,)), ((), ())), preferred_element_type=jnp.float32
    )


def type_terms(logits, type_ids, mask_rows):
    row_max = jnp.max(logits, axis=1, keepdims=True)
    log_total = row_max[:, 0] + jnp.log(jnp.sum(jnp.exp(logits - row_max), axis=1))
    onehot = (type_ids[:, None] == jnp.arange(logits.shape[1], dtype=jnp.int32)[None, :]).astype(
        jnp.float32
    )
    picked = jnp.sum(logits * onehot, axis=1)
    weighting = mask_rows.astype(jnp.float32)
    row_loss = (log_total - picked) * weighting
    return (
        jnp.sum(onehot * weighting[:, None], axis=0),
        jnp.sum(onehot * row_loss[:, None], axis=0),
    )


def forward_pass(stream, live_taps, dilation_size, params):
    border_extent = KERNEL_TAPS // 2 * DILATION_BLOCK2
    length = stream.shape[0]
    source_input = stream.astype(jnp.float32)
    activated = norm_act(source_input, params[0], params[1]).astype(jnp.bfloat16)
    narrow = jnp.dot(activated, params[2], preferred_element_type=jnp.float32) + params[3]
    middle = norm_act(narrow, params[4], params[5]).astype(jnp.bfloat16)
    padded = extended_2(middle, (("dp", 0),), border_extent)
    pieces = []
    for column in range(KERNEL_TAPS):
        begin_at = border_extent + (column - KERNEL_TAPS // 2) * dilation_size
        sliced = lax.dynamic_slice_in_dim(padded, begin_at, length, 0)
        pieces.append(sliced * live_taps[:, column : column + 1].astype(jnp.bfloat16))
    stacked = jnp.concatenate(pieces, axis=1)
    conv_matrix = params[6].reshape(-1, params[6].shape[-1])
    convolved = jnp.dot(stacked, conv_matrix, preferred_element_type=jnp.float32) + params[7]
    outer_act = norm_act(convolved, params[8], params[9]).astype(jnp.bfloat16)
    result = (
        source_input
        + jnp.dot(outer_act, params[10], preferred_element_type=jnp.float32)
        + params[11]
    )
    return (result, (stream, activated, narrow, stacked, convolved, outer_act))


def backward_pass(result_grad, saved_state, live_taps, dilation_size, params):
    stream, activated, narrow, stacked, convolved, outer_act = saved_state
    border_extent = KERNEL_TAPS // 2 * DILATION_BLOCK2
    length = stream.shape[0]
    inner = narrow.shape[1]
    source_input = stream.astype(jnp.float32)
    branch_grad = result_grad.astype(jnp.bfloat16)
    widen_grad = contract_rows(outer_act, branch_grad)
    widen_bias_grad = jnp.sum(branch_grad.astype(jnp.float32), axis=0)
    outer_grad = contract_cols(branch_grad, params[10])
    _, pullback = jax.vjp(norm_act, convolved, params[8], params[9])
    conv_in_grad, last_gain_grad, last_shift_grad = pullback(outer_grad)
    conv_grad = conv_in_grad.astype(jnp.bfloat16)
    conv_matrix = params[6].reshape(-1, params[6].shape[-1])
    conv_weight_grad = contract_rows(stacked, conv_grad)
    conv_bias_grad = jnp.sum(conv_grad.astype(jnp.float32), axis=0)
    stacked_grad = contract_cols(conv_grad, conv_matrix)
    extended = jnp.zeros((length + 2 * border_extent, inner), jnp.float32)
    for column in range(KERNEL_TAPS):
        begin_at = border_extent + (column - KERNEL_TAPS // 2) * dilation_size
        contribution = (
            stacked_grad[:, column * inner : (column + 1) * inner]
            * live_taps[:, column : column + 1]
        )
        current = lax.dynamic_slice_in_dim(extended, begin_at, length, 0)
        extended = lax.dynamic_update_slice_in_dim(extended, current + contribution, begin_at, 0)
    rim_terms = jnp.concatenate(
        [extended[:border_extent], extended[length + border_extent :]], axis=0
    )
    arrived = extended_2(rim_terms.astype(jnp.bfloat16), (("dp", 0),), border_extent).astype(
        rim_terms.dtype
    )
    middle_grad = extended[border_extent : border_extent + length]
    middle_grad = middle_grad.at[:border_extent].add(arrived[:border_extent])
    middle_grad = middle_grad.at[length - border_extent :].add(arrived[3 * border_extent :])
    _, pullback = jax.vjp(norm_act, narrow, params[4], params[5])
    narrow_in_grad, middle_gain_grad, middle_shift_grad = pullback(middle_grad)
    narrow_grad = narrow_in_grad.astype(jnp.bfloat16)
    narrow_weight_grad = contract_rows(activated, narrow_grad)
    narrow_bias_grad = jnp.sum(narrow_grad.astype(jnp.float32), axis=0)
    activated_grad = contract_cols(narrow_grad, params[2])
    _, pullback = jax.vjp(norm_act, source_input, params[0], params[1])
    source_part, first_gain_grad, first_shift_grad = pullback(activated_grad)
    stream_grad = result_grad + source_part
    grads = (
        first_gain_grad,
        first_shift_grad,
        narrow_weight_grad,
        narrow_bias_grad,
        middle_gain_grad,
        middle_shift_grad,
        conv_weight_grad.reshape(params[6].shape),
        conv_bias_grad,
        last_gain_grad,
        last_shift_grad,
        widen_grad,
        widen_bias_grad,
    )
    return (stream_grad, grads)


def body(
    block_input,
    output_cotangent,
    residues_before,
    residues_after,
    residue_types,
    loss_mask,
    first_gain,
    first_shift,
    narrow_weight,
    narrow_bias,
    middle_gain,
    middle_shift,
    conv_weight,
    conv_bias,
    last_gain,
    last_shift,
    widen_weight,
    widen_bias,
    head_weight,
):
    params = tuple(
        (
            tensor[0]
            for tensor in (
                first_gain,
                first_shift,
                narrow_weight,
                narrow_bias,
                middle_gain,
                middle_shift,
                conv_weight,
                conv_bias,
                last_gain,
                last_shift,
                widen_weight,
                widen_bias,
            )
        )
    )
    segment_position = lax.axis_index("section")
    is_upper = segment_position == 1
    upper_share = is_upper.astype(jnp.float32)
    dilation_size = DILATION_BLOCK1 + (DILATION_BLOCK2 - DILATION_BLOCK1) * segment_position
    micro_count = block_input.shape[0]
    vocab_count = head_weight.shape[1]

    def per_section(array, lower_at, upper_at):
        lower_row = array[min(max(lower_at, 0), micro_count - 1)]
        upper_row = array[min(max(upper_at, 0), micro_count - 1)]
        return jnp.where(is_upper, upper_row, lower_row)

    arrived_acts = jnp.zeros(block_input.shape[1:], jnp.bfloat16)
    arrived_grads = jnp.zeros(block_input.shape[1:], jnp.bfloat16)
    totals = tuple((jnp.zeros(tensor.shape, jnp.float32) for tensor in params))
    counts = jnp.zeros((vocab_count,), jnp.float32)
    losses = jnp.zeros((vocab_count,), jnp.float32)
    history = []
    results_by_tick = []
    grads_by_tick = []
    for tick_index in range(micro_count + 2):
        forward_in = jnp.where(
            is_upper, arrived_acts, block_input[min(tick_index, micro_count - 1)]
        )
        leading_rows = per_section(residues_before, tick_index, tick_index - 1)
        following_rows = per_section(residues_after, tick_index, tick_index - 1)
        live_taps = tap_valid_mask(leading_rows, following_rows, dilation_size)
        result, saved_state = forward_pass(forward_in, live_taps, dilation_size, params)
        result_low = result.astype(jnp.bfloat16)
        forward_live = jnp.where(
            is_upper, float(1 <= tick_index <= micro_count), float(tick_index < micro_count)
        )
        logits = jnp.dot(result_low, head_weight, preferred_element_type=jnp.float32)
        part_counts, part_losses = type_terms(
            logits,
            per_section(residue_types, tick_index, tick_index - 1),
            per_section(loss_mask, tick_index, tick_index - 1),
        )
        counts = counts + upper_share * forward_live * part_counts
        losses = losses + upper_share * forward_live * part_losses
        history.append((saved_state, live_taps))
        results_by_tick.append(result_low)
        earlier = history[tick_index - 2] if tick_index >= 2 else history[tick_index]
        chosen_state, chosen_live = jax.tree.map(
            lambda current_item, earlier_item: jnp.where(is_upper, current_item, earlier_item),
            history[tick_index],
            earlier,
        )
        backward_live = jnp.where(
            is_upper,
            float(1 <= tick_index <= micro_count),
            float(2 <= tick_index <= micro_count + 1),
        )
        cotangent = output_cotangent[min(max(tick_index - 1, 0), micro_count - 1)].astype(
            jnp.float32
        )
        result_grad = (
            jnp.where(is_upper, cotangent, arrived_grads.astype(jnp.float32)) * backward_live
        )
        stream_grad, grads = backward_pass(
            result_grad, chosen_state, chosen_live, dilation_size, params
        )
        totals = tuple((running + term for running, term in zip(totals, grads)))
        stream_low = stream_grad.astype(jnp.bfloat16)
        grads_by_tick.append(stream_low)
        if tick_index <= micro_count:
            arrived_acts = passed_along(result_low, "section", 1)
            arrived_grads = passed_along(stream_low, "section", -1)
    summed = lax.psum(
        (
            totals[0],
            totals[1],
            totals[2],
            totals[3],
            totals[4],
            totals[5],
            totals[6],
            totals[7],
            totals[8],
            totals[9],
            totals[10],
            totals[11],
        ),
        "dp",
    )
    type_total, loss_total = lax.psum((counts, losses), ("section", "dp"))
    block_outputs = jnp.stack(
        [
            jnp.where(is_upper, results_by_tick[batch + 1], results_by_tick[batch])
            for batch in range(micro_count)
        ]
    )[None]
    input_grads = jnp.stack(
        [
            jnp.where(is_upper, grads_by_tick[batch + 1], grads_by_tick[batch + 2])
            for batch in range(micro_count)
        ]
    )[None]
    return (
        block_outputs,
        input_grads,
        summed[0][None],
        summed[1][None],
        summed[2][None],
        summed[3][None],
        summed[4][None],
        summed[5][None],
        summed[6][None],
        summed[7][None],
        summed[8][None],
        summed[9][None],
        summed[10][None],
        summed[11][None],
        type_total.astype(jnp.int32),
        loss_total / jnp.maximum(type_total, 1.0),
    )


def solution(mesh):
    placed = (
        P(None, "dp", None),
        P(None, "dp", None),
        P(None, "dp"),
        P(None, "dp"),
        P(None, "dp"),
        P(None, "dp"),
        P("section", None),
        P("section", None),
        P("section", None, None),
        P("section", None),
        P("section", None),
        P("section", None),
        P("section", None, None, None),
        P("section", None),
        P("section", None),
        P("section", None),
        P("section", None, None),
        P("section", None),
        P(),
    )
    return jax.shard_map(
        body,
        mesh=mesh,
        in_specs=placed,
        out_specs=(
            P("section", None, "dp", None),
            P("section", None, "dp", None),
            P("section", None),
            P("section", None),
            P("section", None, None),
            P("section", None),
            P("section", None),
            P("section", None),
            P("section", None, None, None),
            P("section", None),
            P("section", None),
            P("section", None),
            P("section", None, None),
            P("section", None),
            P(),
            P(),
        ),
        check_vma=False,
    )
```

profile of v0, /device:TPU:0, one launch (start us, length us, event | category | flops | bytes accessed | tf_op | source)
XLA Modules:
  0.0 1219.6 jit_solution(8281712489835554694)
XLA Ops:
  10.3 5.4 fusion.1076
  18.4 4.9 collective-permute-start
  25.4 5.3 multiply_convert_fusion
  68.8 4.8 collective-permute-start.20
  77.3 5.2 collective-permute-done.21
  88.1 4.2 multiply_convert_fusion.1
  102.2 4.4 collective-permute-done.4
  128.2 4.7 collective-permute-start.6
  137.2 6.0 collective-permute-done.7
  154.7 4.7 fusion.1114
  173.2 4.3 collective-permute-done.10
  195.7 4.9 collective-permute-start.12
  203.4 4.4 collective-permute-done.13
  224.7 4.4 collective-permute-start.15
  233.1 4.4 collective-permute-done.16
  257.2 5.5 collective-permute-start.18
  266.7 4.3 collective-permute-done.19
  292.2 4.1 collective-permute-start.42
  300.3 4.3 collective-permute-done.43
  341.8 4.9 collective-permute-start.23
  349.5 4.4 collective-permute-done.24
  363.8 4.7 fusion.1115
  400.4 4.2 collective-permute-start.26
  408.9 4.4 collective-permute-done.27
  417.6 4.4 fusion.991
  427.8 4.7 fusion.96
  466.9 5.8 collective-permute-start.29
  474.4 6.2 fusion.94
  485.9 4.4 fusion.992
  533.1 4.7 collective-permute-start.32
  539.4 3.9 fusion.902
  543.4 3.7 collective-permute-done.33
  551.4 4.4 fusion.993
  561.6 4.7 fusion.92
  605.9 4.8 fusion.90
  618.2 4.4 fusion.994
  665.4 5.6 collective-permute-start.38
  672.5 4.9 fusion.88
  684.0 4.4 fusion.995
  734.5 4.4 collective-permute-start.44
  740.8 22.7 %add_add_fusion = f32[3200,640]{1,0:T(8,128)} fusion(f32[3200,640]{1,0:T(8,128)} %fusion.88, f32[3200,640]{1,0:T(8,128)} %fusion.90, f32[3200,640]{1,0:T(8,128)} %fusion.92, f32[3200,640]{1,0:T(8,128)} %fusion.94, f32[3200,640]{1,0:T(8,128)} %fusion.96, f32[3200,640]{1,0:T(8,128)} %fusion.1114, f32[3200,640]{1,0:T(8,128)} %fusion.1115, ...), kind=kOutput, calls=%fused_computation | convolution fusion | flops 1063731200 | bytes 69140480 | tf_op jit(solution)/shard_map/dot_general | solution.py:53
  763.6 11.3 fusion.5
  801.9 47.9 %all-reduce = (f32[30]{0:T(128)S(1)}, f32[30]{0:T(128)S(1)}) all-reduce(f32[30]{0:T(128)S(1)} %multiply_add_fusion.60, f32[30]{0:T(128)S(1)} %multiply_add_fusion.59), channel_id=1, replica_groups=mesh['section'=2,'dp'=16] {'section','dp'}, use_global_device_ids=true, to_apply=%region_223.224 | all-reduce | flops 60 | bytes 480 | tf_op jit(solution)/shard_map/psum | solution.py:290
  855.0 5.4 fusion.996
  862.2 79.0 %all-reduce.1 = (f32[1,1280]{1,0:T(1,128)}, f32[1,1280]{1,0:T(1,128)}, f32[1,640]{1,0:T(1,128)}, f32[1,640]{1,0:T(1,128)}, f32[1,640]{1,0:T(1,128)}, /*index=5*/...) all-reduce(f32[1,1280]{1,0:T(1,128)S(1)} %broadcast_in_dim.174, ...), channel_id=1, replica_groups=mesh['section'=2,'dp'=16] {'dp'}, use_global_device_ids=true, to_apply=%region_138.139 | all-reduce | flops 7680 | bytes 61440 | tf_op jit(solution)/shard_map/psum | solution.py:273
  944.4 255.3 %all-reduce.5.cloned.1.call-done = (f32[1,1280,640]{2,1,0:T(8,128)}, f32[1,5,640,640]{3,2,1,0:T(8,128)}, f32[1,640,1280]{2,1,0:T(8,128)}) async-done(((f32[1,1280,640]{2,1,0:T(8,128)}, f32[1,5,640,640]{3,2,1,0:T(8,128)}, f32[1,640,1280]{2,1,0:T(8,128)}), (f32[1,1280,640]{2,1,0:T(8,128)}, f32[1,5,640,640]{3,2,1,0:T(8,128)}, f32[1,640,1280]{2,1,0:T(8,128)})) %all-reduce.5.cloned.1.call-update) | async-done | bytes 14745616 | tf_op jit(solution)/shard_map/psum | solution.py:273
  1199.7 3.8 copy.140
  1203.6 7.3 copy.141
  (1396 shorter events, 578.3 us)
Async XLA Ops:
  7.2 1192.5 %all-reduce.5.cloned.1.call-start = ((), (), s32[]{:S(2)}) async-start(), calls=%async_computation | async-start | bytes 29491200 | tf_op jit(solution)/shard_map/psum | solution.py:273
  18.4 14.3 %collective-permute-start = (bf16[128,640]{1,0:T(8,128)(2,1)S(1)}, bf16[128,640]{1,0:T(8,128)(2,1)S(1)}, u32[]{:S(2)}, u32[]{:S(2)}) collective-permute-start(bf16[128,640]{1,0:T(8,128)(2,1)S(1)} %get-tuple-element.581), channel_id=1, source_target_pairs={{0,1},{1,2},{2,3},{3,4},{4,5},{5,6},{6,7},{7,8},{8,9},{9,10},{10,1... | collective-permute-start | bytes 491528 | tf_op jit(solution)/shard_map/ppermute | solution.py:22
  23.3 9.5 collective-permute-start.1
  68.8 8.5 collective-permute-start.20
  73.6 8.9 collective-permute-start.21
  75.6 9.2 collective-permute-start.2
  95.9 6.3 collective-permute-start.3
  99.4 7.2 collective-permute-start.4
  114.8 3.0 collective-permute-start.5
  128.2 9.0 collective-permute-start.6
  132.9 10.3 collective-permute-start.7
  149.0 124.9 %copy-start.110 = (f32[256,640]{1,0:T(8,128)}, f32[256,640]{1,0:T(8,128)S(1)}, u32[]{:S(2)}) copy-start(f32[256,640]{1,0:T(8,128)S(1)} %get-tuple-element.689) | copy-start | bytes 1966084
  152.8 6.6 collective-permute-start.8
  166.6 6.7 collective-permute-start.9
  170.3 7.2 collective-permute-start.10
  184.2 4.3 collective-permute-start.11
  195.7 7.7 collective-permute-start.12
  200.6 7.2 collective-permute-start.13
  214.6 3.0 collective-permute-start.14
  224.7 8.4 collective-permute-start.15
  229.1 8.4 collective-permute-start.16
  244.3 3.1 collective-permute-start.17
  257.2 9.5 collective-permute-start.18
  262.8 8.2 collective-permute-start.19
  277.4 3.4 collective-permute-start.41
  292.2 8.0 collective-permute-start.42
  296.3 8.2 collective-permute-start.43
  297.6 9.6 collective-permute-start.22
  341.8 7.7 collective-permute-start.23
  346.7 7.2 collective-permute-start.24
  361.8 6.8 collective-permute-start.25
  400.4 8.5 collective-permute-start.26
  404.6 8.7 collective-permute-start.27
  426.1 8.9 collective-permute-start.28
  466.9 13.9 %collective-permute-start.29 = (bf16[128,640]{1,0:T(8,128)(2,1)S(1)}, bf16[128,640]{1,0:T(8,128)(2,1)S(1)}, u32[]{:S(2)}, u32[]{:S(2)}) collective-permute-start(bf16[128,640]{1,0:T(8,128)(2,1)S(1)} %get-tuple-element.559), channel_id=1, source_target_pairs={{0,1},{1,2},{2,3},{3,4},{4,5},{5,6},{6,7},{7,8},{8,9},{9,10},{10,1... | collective-permute-start | bytes 491528 | tf_op jit(solution)/shard_map/ppermute | solution.py:22
  472.6 8.6 collective-permute-start.30
  494.4 6.7 collective-permute-start.31
  533.1 10.2 collective-permute-start.32
  537.8 9.3 collective-permute-start.33
  559.9 8.9 collective-permute-start.34
  600.8 10.0 collective-permute-start.35
  604.1 9.8 collective-permute-start.36
  626.7 6.6 collective-permute-start.37
  665.4 12.1 collective-permute-start.38
  671.0 8.7 collective-permute-start.39
  692.5 6.7 collective-permute-start.40
  734.5 40.5 %collective-permute-start.44 = (bf16[128,640]{1,0:T(8,128)(2,1)S(1)}, bf16[128,640]{1,0:T(8,128)(2,1)S(1)}, u32[]{:S(2)}, u32[]{:S(2)}) collective-permute-start(bf16[128,640]{1,0:T(8,128)(2,1)S(1)} %get-tuple-element.536), channel_id=1, source_target_pairs={{0,1},{1,2},{2,3},{3,4},{4,5},{5,6},{6,7},{7,8},{8,9},{9,10},{10,1... | collective-permute-start | bytes 491528 | tf_op jit(solution)/shard_map/ppermute | solution.py:22
  738.9 36.0 %collective-permute-start.45 = (bf16[128,640]{1,0:T(8,128)(2,1)S(1)}, bf16[128,640]{1,0:T(8,128)(2,1)S(1)}, u32[]{:S(2)}, u32[]{:S(2)}) collective-permute-start(bf16[128,640]{1,0:T(8,128)(2,1)S(1)} %get-tuple-element.537), channel_id=1, source_target_pairs={{1,0},{2,1},{3,2},{4,3},{5,4},{6,5},{7,6},{8,7},{9,8},{10,9},{11,1... | collective-permute-start | bytes 491528 | tf_op jit(solution)/shard_map/ppermute | solution.py:24
  (372 other events, 3528.7 us)
Sparse Core Ops, SparseCore 0:
  782.5 417.1 all-reduce.4
where the time goes:
time: 1230 us; the launch traced here: 1220 us
  waiting for transfers between devices  323 us (26%)
  other arithmetic  261 us (21%)
  matrix products  206 us (17%)
  local copies, waits for them, and re-layouts  161 us (13%)
  blocking collectives  127 us (10%)
  starting transfers between devices  121 us (10%)
  between operations  20.3 us (2%)
    psum x1, waiting for transfers between devices, body(): lax.psum((totals[0], totals[1], totals[2], totals[3], totals[4], totals[5...  255 us
    dynamic_update_slice x32, local copies, waits for them, and re-layouts, backward_pass(): lax.dynamic_update_slice_in_dim(extended, current + contribution, begin_a...  117 us
    dot_general x24, matrix products, contract_rows(): lax.dot_general(left_side, right_side, (((0,), (0,)), ((), ())), preferre...  105 us
    psum x1, blocking collectives, body(): lax.psum((totals[0], totals[1], totals[2], totals[3], totals[4], totals[5...  79 us
    ppermute x16, starting transfers between devices, extended_2(): lax.ppermute(tail, axis, [(i, (i + 1) % count) for i in range(ends)])  73.3 us
    dot_general x24, matrix products, contract_cols(): lax.dot_general(left_side, right_side, (((1,), (1,)), ((), ())), preferre...  64.5 us
    ppermute x16, waiting for transfers between devices, extended_2(): lax.ppermute(head, axis, [((i + 1) % count, i) for i in range(ends)])  55.5 us
    add x24, other arithmetic, backward_pass(): current + contribution  49.8 us
  transfers between devices with their start and end apart: 47, of which 26 were waited for; matrix products, arithmetic and copies ran while one was open for 12% of the time, Pallas kernels for 0%

commit v1 on v0

v1 whole, which is shorter than its diff:
```python
import functools

import jax
import jax.numpy as jnp
from jax import lax
from jax.experimental import pallas as pl
from jax.experimental.pallas import tpu as pltpu
from jax.sharding import PartitionSpec as P

TAPS = 5
DIL0 = 2
DIL1 = 64
EPS = 1e-05
RIM0 = 8
RIM1 = TAPS // 2 * DIL1
F32 = jnp.float32
BF16 = jnp.bfloat16
FG, FS, NB, MG, MS, CB, LG, LS, WB = range(9)
VROWS = 16
LANES = 128
TYPE_COL, MASK_COL = 16, 17
VMEM_LIMIT = 56 * 1024 * 1024
ANY = pl.BlockSpec(memory_space=pl.ANY)


def dot_nn(a, b):
    return lax.dot_general(a, b, (((1,), (0,)), ((), ())), preferred_element_type=F32)


def dot_nt(a, b):
    return lax.dot_general(a, b, (((1,), (1,)), ((), ())), preferred_element_type=F32)


def dot_tn(a, b):
    return lax.dot_general(a, b, (((0,), (0,)), ((), ())), preferred_element_type=F32)


def gelu_parts(y):
    d = jnp.abs(y) * (0.3275911 * 0.7071067811865476) + 1.0
    t = pl.reciprocal(d, approx=True)
    t = t * (2.0 - d * t)
    e = jnp.exp(y * y * -0.5)
    tail = 0.5 * 1.061405429
    tail = tail * t + 0.5 * -1.453152027
    tail = tail * t + 0.5 * 1.421413741
    tail = tail * t + 0.5 * -0.284496736
    tail = tail * t + 0.5 * 0.254829592
    tail = tail * t * e
    phi_big = jnp.where(y >= 0, 1.0 - tail, tail)
    return y * phi_big, phi_big + y * e * 0.3989422804014327


def normed_of(u):
    mean = jnp.mean(u, axis=-1, keepdims=True)
    center = u - mean
    scale = lax.rsqrt(jnp.mean(center * center, axis=-1, keepdims=True) + EPS)
    return center * scale, mean, scale


def norm_back(err, slope, normed, scale, gain):
    q = err * slope
    p = q * gain
    m1 = jnp.mean(p, axis=-1, keepdims=True)
    m2 = jnp.mean(p * normed, axis=-1, keepdims=True)
    return (p - m1 - normed * m2) * scale, q * normed, q


def fold8(v):
    return sum(v[k : k + 8] for k in range(0, v.shape[0], 8))


def chunks(rows, size, body):
    lax.fori_loop(0, rows // size, lambda i, c: (body(pl.multiple_of(i * size, size)), c)[1], 0)


def pick_copy(cond, one, other, dst, sem):
    @pl.when(cond)
    def _():
        pltpu.make_async_copy(one, dst, sem).start()

    @pl.when(jnp.logical_not(cond))
    def _():
        pltpu.make_async_copy(other, dst, sem).start()

    return pltpu.make_async_copy(one, dst, sem)


def conv_copy(cond, one, other, dst, sem):
    inner = one.shape[1]
    waits = []
    for j in range(TAPS):
        part = dst.at[:, (TAPS - 1 - j) * inner : (TAPS - j) * inner]
        waits.append(pick_copy(cond, one.at[j], other.at[j], part, sem.at[j]))
    return waits


def f0_kernel(c_ref, x_ref, xh_ref, mk_ref, v0_ref, v1_ref, nwo, nwx, cwo, cwx, wwo, wwx,
              act0, slx0, mux0, rsx0, nn0, sln0, rsn0, st0, nc0, slc0, rsc0, oa0, out0,
              act1, slx1, mux1, rsx1, nn1, sln1, rsn1, mid1,
              nw0, cw0, ww0, nw1, act_s, n32, mid32, c32, r32, sems):
    low = c_ref[0] == 0
    first = pl.program_id(0) == 0
    rows = x_ref.shape[1]
    inner = n32.shape[1]

    def copies(start):
        pairs = ((nwo, nwx, nw0, 0), (cwo, cwx, cw0, 1), (wwo, wwx, ww0, 2), (nwx, nwo, nw1, 3))
        for one, other, dst, k in pairs:
            if start:
                pick_copy(low, one, other, dst, sems.at[k])
            else:
                pltpu.make_async_copy(one, dst, sems.at[k]).wait()

    @pl.when(first)
    def _():
        copies(True)

    def first_norm(u, k):
        normed, mean, scale = normed_of(u)
        act, slope = gelu_parts(normed * v0_ref[FG : FG + 1] + v0_ref[FS : FS + 1])
        return act.astype(BF16), slope, mean, scale

    def stage1(r):
        s = pl.ds(r, 16)
        act, slope, mean, scale = first_norm(x_ref[0, s, :].astype(F32), 0)
        act_s[s, :] = act
        act0[0, s, :] = act
        slx0[0, s, :] = slope.astype(BF16)
        mux0[0, s, :] = mean
        rsx0[0, s, :] = scale

    chunks(rows, 16, stage1)
    act, _, _, _ = first_norm(xh_ref[0].astype(F32), 0)
    act_s[rows : rows + 2 * RIM0, :] = act

    @pl.when(first)
    def _():
        copies(False)

    n32[...] = dot_nn(act_s[...], nw0[...])

    def mid_norm(u, v_ref):
        normed, _, scale = normed_of(u + v_ref[NB : NB + 1, :inner])
        act, slope = gelu_parts(normed * v_ref[MG : MG + 1, :inner] + v_ref[MS : MS + 1, :inner])
        return act.astype(BF16), slope, normed, scale

    def stage2(r):
        s = pl.ds(r, 16)
        mid, slope, normed, scale = mid_norm(n32[s, :], v0_ref)
        mid32[pl.ds(r + RIM0, 16), :] = mid.astype(F32)
        nn0[0, s, :] = normed.astype(BF16)
        sln0[0, s, :] = slope.astype(BF16)
        rsn0[0, s, :] = scale

    chunks(rows, 16, stage2)
    rim, _, _, _ = mid_norm(n32[rows : rows + 2 * RIM0, :], v0_ref)
    rim = rim.astype(F32)
    mid32[0:RIM0, :] = rim[:RIM0]
    mid32[rows + RIM0 : rows + 2 * RIM0, :] = rim[RIM0:]

    def stage3(r):
        s = pl.ds(r, 16)
        window = mid32[pl.ds(r, 32), :]
        for j in range(TAPS):
            at = RIM0 + (j - TAPS // 2) * DIL0
            live = mk_ref[0, s, j : j + 1]
            st0[0, s, j * inner : (j + 1) * inner] = (window[at : at + 16] * live).astype(BF16)

    chunks(rows, 16, stage3)
    c32[...] = dot_nn(st0[0], cw0[...].reshape(TAPS * inner, inner))

    def stage4(r):
        s = pl.ds(r, 16)
        normed, _, scale = normed_of(c32[s, :] + v0_ref[CB : CB + 1, :inner])
        act, slope = gelu_parts(normed * v0_ref[LG : LG + 1, :inner] + v0_ref[LS : LS + 1, :inner])
        oa0[0, s, :] = act.astype(BF16)
        nc0[0, s, :] = normed.astype(BF16)
        slc0[0, s, :] = slope.astype(BF16)
        rsc0[0, s, :] = scale

    chunks(rows, 16, stage4)
    r32[...] = dot_nn(oa0[0], ww0[...])

    def stage5(r):
        s = pl.ds(r, 16)
        res = (x_ref[0, s, :].astype(F32) + (r32[s, :] + v0_ref[WB : WB + 1])).astype(BF16)
        out0[0, s, :] = res
        normed, mean, scale = normed_of(res.astype(F32))
        act, slope = gelu_parts(normed * v1_ref[FG : FG + 1] + v1_ref[FS : FS + 1])
        act1[0, s, :] = act.astype(BF16)
        slx1[0, s, :] = slope.astype(BF16)
        mux1[0, s, :] = mean
        rsx1[0, s, :] = scale

    chunks(rows, 16, stage5)
    n32[0:rows, :] = dot_nn(act1[0], nw1[...])

    def stage6(r):
        s = pl.ds(r, 16)
        mid, slope, normed, scale = mid_norm(n32[s, :], v1_ref)
        mid1[0, s, :] = mid
        nn1[0, s, :] = normed.astype(BF16)
        sln1[0, s, :] = slope.astype(BF16)
        rsn1[0, s, :] = scale

    chunks(rows, 16, stage6)


def f1_kernel(c_ref, mid_ref, up_ref, dn_ref, mk_ref, v1_ref, cot_ref, cwo, cwx, wwo, wwx,
              st1, oa1, cg1, vec,
              cw1, ww1, ext, c32, e32, acc, sems):
    low = c_ref[0] == 0
    step = pl.program_id(0)
    rows = mid_ref.shape[1]
    inner = c32.shape[1]

    @pl.when(step == 0)
    def _():
        pick_copy(low, cwx, cwo, cw1, sems.at[0])
        pick_copy(low, wwx, wwo, ww1, sems.at[1])
        acc[...] = jnp.zeros_like(acc)

    ext[0:RIM1, :] = up_ref[0]
    ext[RIM1 : RIM1 + rows, :] = mid_ref[0]
    ext[RIM1 + rows : 2 * RIM1 + rows, :] = dn_ref[0]

    def stack(r):
        s = pl.ds(r, 32)
        for j in range(TAPS):
            at = RIM1 + (j - TAPS // 2) * DIL1
            live = mk_ref[0, s, 8 + j : 9 + j]
            part = ext[pl.ds(r + at, 32), :].astype(F32) * live
            st1[0, s, j * inner : (j + 1) * inner] = part.astype(BF16)

    chunks(rows, 32, stack)

    def cot_sum(r):
        acc[3, :, :] += fold8(cot_ref[0, pl.ds(r, 16), :].astype(F32))

    chunks(rows, 16, cot_sum)

    @pl.when(step == 0)
    def _():
        pltpu.make_async_copy(cwx, cw1, sems.at[0]).wait()
        pltpu.make_async_copy(wwx, ww1, sems.at[1]).wait()

    e32[...] = dot_nt(cot_ref[0], ww1[...])
    c32[...] = dot_nn(st1[0], cw1[...].reshape(TAPS * inner, inner))

    def stage(r):
        s = pl.ds(r, 16)
        gain = v1_ref[LG : LG + 1, :inner]
        normed, _, scale = normed_of(c32[s, :] + v1_ref[CB : CB + 1, :inner])
        act, slope = gelu_parts(normed * gain + v1_ref[LS : LS + 1, :inner])
        oa1[0, s, :] = act.astype(BF16)
        du, dgain, dshift = norm_back(e32[s, :], slope, normed, scale, gain)
        du = du.astype(BF16)
        cg1[0, s, :] = du
        acc[0, :, :inner] += fold8(dgain)
        acc[1, :, :inner] += fold8(dshift)
        acc[2, :, :inner] += fold8(du.astype(F32))

    chunks(rows, 16, stage)

    @pl.when(step == pl.num_programs(0) - 1)
    def _():
        vec[...] = jnp.sum(acc[...], axis=1)


def o1_kernel(c_ref, out0_ref, oa_ref, mk_ref, v1_ref, head_ref, wwo, wwx, out1, tot, ww1, r32, lg, acc, sems, *, vocab):
    low = c_ref[0] == 0
    step = pl.program_id(0)
    rows = oa_ref.shape[1]

    @pl.when(step == 0)
    def _():
        pick_copy(low, wwx, wwo, ww1, sems.at[0])
        acc[...] = jnp.zeros_like(acc)
        pltpu.make_async_copy(wwx, ww1, sems.at[0]).wait()

    r32[...] = dot_nn(oa_ref[0], ww1[...])

    def stage(r):
        s = pl.ds(r, 16)
        out1[0, s, :] = (out0_ref[0, s, :].astype(F32) + (r32[s, :] + v1_ref[WB : WB + 1])).astype(BF16)

    chunks(rows, 16, stage)
    lg[...] = dot_nn(out1[0], head_ref[...])

    def loss(r):
        s = pl.ds(r, 32)
        lane = lax.broadcasted_iota(jnp.int32, (32, LANES), 1)
        logits = jnp.where(lane < vocab, lg[s, :], -1e30)
        top = jnp.max(logits, axis=-1, keepdims=True)
        log_total = top + jnp.log(jnp.sum(jnp.exp(logits - top), axis=-1, keepdims=True))
        kind = mk_ref[0, s, TYPE_COL : TYPE_COL + 1].astype(jnp.int32)
        weight = mk_ref[0, s, MASK_COL : MASK_COL + 1]
        onehot = jnp.where(lane == kind, weight, 0.0)
        acc[0] += fold8(onehot)
        acc[1] += fold8(onehot * (log_total - logits))

    chunks(rows, 32, loss)

    @pl.when(step == pl.num_programs(0) - 1)
    def _():
        tot[...] = jnp.sum(acc[...], axis=1)


def back_conv(dst32, stg, cw2):
    dst32[...] = dot_nt(stg[...], cw2[...])


def back_mid(rows, inner, m32, sln, nn, rsn, v_ref, ng, acc, at):
    def stage(r):
        s = pl.ds(r, 16)
        du, dgain, dshift = norm_back(
            m32[s, :], sln[0, s, :].astype(F32), nn[0, s, :].astype(F32), rsn[0, s, :], v_ref[MG : MG + 1, :inner]
        )
        du = du.astype(BF16)
        ng[0, s, :] = du
        acc[at, :, :inner] += fold8(dgain)
        acc[at + 1, :, :inner] += fold8(dshift)
        acc[at + 2, :, :inner] += fold8(du.astype(F32))

    chunks(rows, 16, stage)


def back_first(rows, a32, slx, src, mux, rsx, v_ref, grad, ig, acc, at):
    def stage(r):
        s = pl.ds(r, 16)
        scale = rsx[0, s, :]
        normed = (src[0, s, :].astype(F32) - mux[0, s, :]) * scale
        du, dgain, dshift = norm_back(a32[s, :], slx[0, s, :].astype(F32), normed, scale, v_ref[FG : FG + 1])
        ig[0, s, :] = (grad[0, s, :].astype(F32) + du).astype(BF16)
        acc[at, :, :] += fold8(dgain)
        acc[at + 1, :, :] += fold8(dshift)

    chunks(rows, 16, stage)


def b10_kernel(c_ref, cg_ref, up_ref, dn_ref, mk_ref, v0_ref, v1_ref, cot_ref, sln1, nn1, rsn1, slx1, out0, mux1, rsx1,
               slc0, nc0, rsc0, cwo, cwx, nwo, nwx, wwo, wwx,
               ng1, ig1, cg0, vec,
               cw2, nw1, ww0, ext, stg, m32, a32, acc, sems):
    low = c_ref[0] == 0
    step = pl.program_id(0)
    rows = cg_ref.shape[1]
    inner = m32.shape[1]

    @pl.when(step == 0)
    def _():
        waits = conv_copy(low, cwx, cwo, cw2, sems)
        waits.append(pick_copy(low, nwx, nwo, nw1, sems.at[TAPS]))
        waits.append(pick_copy(low, wwo, wwx, ww0, sems.at[TAPS + 1]))
        acc[...] = jnp.zeros_like(acc)
        for w in waits:
            w.wait()

    ext[0:RIM1, :] = up_ref[0]
    ext[RIM1 : RIM1 + rows, :] = cg_ref[0]
    ext[RIM1 + rows : 2 * RIM1 + rows, :] = dn_ref[0]

    def stack(r):
        s = pl.ds(r, 32)
        for j in range(TAPS):
            at = RIM1 + (j - TAPS // 2) * DIL1
            live = mk_ref[0, s, 8 + j : 9 + j]
            part = ext[pl.ds(r + at, 32), :].astype(F32) * live
            stg[s, j * inner : (j + 1) * inner] = part.astype(BF16)

    chunks(rows, 32, stack)
    back_conv(m32, stg, cw2)
    back_mid(rows, inner, m32, sln1, nn1, rsn1, v1_ref, ng1, acc, 0)
    a32[...] = dot_nt(ng1[0], nw1[...])
    back_first(rows, a32, slx1, out0, mux1, rsx1, v1_ref, cot_ref, ig1, acc, 3)
    m32[...] = dot_nt(ig1[0], ww0[...])

    def stage(r):
        s = pl.ds(r, 16)
        du, dgain, dshift = norm_back(
            m32[s, :], slc0[0, s, :].astype(F32), nc0[0, s, :].astype(F32), rsc0[0, s, :], v0_ref[LG : LG + 1, :inner]
        )
        du = du.astype(BF16)
        cg0[0, s, :] = du
        acc[5, :, :inner] += fold8(dgain)
        acc[6, :, :inner] += fold8(dshift)
        acc[7, :, :inner] += fold8(du.astype(F32))
        acc[8, :, :] += fold8(ig1[0, s, :].astype(F32))

    chunks(rows, 16, stage)

    @pl.when(step == pl.num_programs(0) - 1)
    def _():
        vec[...] = jnp.sum(acc[...], axis=1)


def b0_kernel(c_ref, cg_ref, rim_ref, mk_ref, v0_ref, ig1_ref, sln0, nn0, rsn0, slx0, x_ref, mux0, rsx0,
              cwo, cwx, nwo, nwx,
              ng0, ig0, vec,
              cw2, nw0, ext, stg, m32, a32, acc, sems):
    low = c_ref[0] == 0
    step = pl.program_id(0)
    rows = cg_ref.shape[1]
    inner = m32.shape[1]

    @pl.when(step == 0)
    def _():
        waits = conv_copy(low, cwo, cwx, cw2, sems)
        waits.append(pick_copy(low, nwo, nwx, nw0, sems.at[TAPS]))
        acc[...] = jnp.zeros_like(acc)
        for w in waits:
            w.wait()

    rim = rim_ref[0].astype(F32)
    ext[0:RIM0, :] = rim[:RIM0]
    ext[rows + RIM0 : rows + 2 * RIM0, :] = rim[RIM0:]

    def widen(r):
        ext[pl.ds(r + RIM0, 16), :] = cg_ref[0, pl.ds(r, 16), :].astype(F32)

    chunks(rows, 16, widen)

    def stack(r):
        s = pl.ds(r, 16)
        window = ext[pl.ds(r, 32), :]
        for j in range(TAPS):
            at = RIM0 + (j - TAPS // 2) * DIL0
            live = mk_ref[0, s, j : j + 1]
            stg[s, j * inner : (j + 1) * inner] = (window[at : at + 16] * live).astype(BF16)

    chunks(rows, 16, stack)
    back_conv(m32, stg, cw2)
    back_mid(rows, inner, m32, sln0, nn0, rsn0, v0_ref, ng0, acc, 0)
    a32[...] = dot_nt(ng0[0], nw0[...])
    back_first(rows, a32, slx0, x_ref, mux0, rsx0, v0_ref, ig1_ref, ig0, acc, 3)

    @pl.when(step == pl.num_programs(0) - 1)
    def _():
        vec[...] = jnp.sum(acc[...], axis=1)


def weight_terms(pairs, tile, out_rows):
    specs, args, spans = [], [], []
    at = 0
    for a, g in pairs:
        rows = a.shape[0]
        na, ng = a.shape[1] // tile, g.shape[1] // tile

        def a_map(s, at=at, na=na, ng=ng):
            return (0, jnp.clip(s - at, 0, na * ng - 1) % na)

        def g_map(s, at=at, na=na, ng=ng):
            return (0, jnp.clip(s - at, 0, na * ng - 1) // na)

        specs += [pl.BlockSpec((rows, tile), a_map), pl.BlockSpec((rows, tile), g_map)]
        args += [a, g]
        spans.append((at, at + na * ng))
        at += na * ng

    def kernel(*refs):
        out = refs[-1]
        s = pl.program_id(0)
        for k, (lo, hi) in enumerate(spans):

            @pl.when((s >= lo) & (s < hi))
            def _(k=k):
                out[...] = dot_tn(refs[2 * k][...], refs[2 * k + 1][...]).astype(BF16)

    flops = at * 2 * tile * tile * args[0].shape[0]
    return pl.pallas_call(
        kernel,
        grid=(at,),
        in_specs=specs,
        out_specs=pl.BlockSpec((tile, tile), lambda s: (s, 0)),
        out_shape=jax.ShapeDtypeStruct((out_rows, tile), BF16),
        compiler_params=pltpu.CompilerParams(vmem_limit_bytes=VMEM_LIMIT),
        cost_estimate=pl.CostEstimate(flops=flops, bytes_accessed=4 * out_rows * tile, transcendentals=0),
    )(*args)


def add_low(one, other):
    return (one.astype(F32) + other.astype(F32)).astype(BF16)


def halves(buf, bit):
    rows = buf.shape[0] // 2
    keep = lax.dynamic_slice_in_dim(buf, bit * rows, rows, 0)
    send = lax.dynamic_slice_in_dim(buf, (1 - bit) * rows, rows, 0)
    return keep, send


def dp_steps(count, sec, at):
    bits = count.bit_length() - 1
    orders = [list(range(bits)), [1, 0] + list(range(2, bits))]
    out = []
    for k in range(bits):
        pairs = [
            (s * count + d, s * count + (d ^ (1 << orders[s][k])))
            for s in range(2)
            for d in range(count)
        ]
        place = jnp.where(sec == 0, orders[0][k], orders[1][k])
        out.append((pairs, (at >> place) & 1))
    return out


def body(block_input, output_cotangent, residues_before, residues_after, residue_types, loss_mask,
         first_gain, first_shift, narrow_weight, narrow_bias, middle_gain, middle_shift,
         conv_weight, conv_bias, last_gain, last_shift, widen_weight, widen_bias, head_weight):
    sec = lax.axis_index("section")
    at = lax.axis_index("dp")
    count = lax.axis_size("dp")
    low = sec == 0
    micro, rows, width = block_input.shape
    own = micro // 2
    inner = narrow_weight.shape[2]
    vocab = head_weight.shape[1]
    swap = [(0, 1), (1, 0)]
    ahead = [(i, (i + 1) % count) for i in range(count)]
    behind = [((i + 1) % count, i) for i in range(count)]
    c_arr = sec.astype(jnp.int32).reshape(1)

    def other(v):
        return lax.ppermute(v, "section", swap)

    nwo, cwo, wwo = narrow_weight[0], conv_weight[0], widen_weight[0]
    nwx, cwx, wwx = other(nwo), other(cwo), other(wwo)
    vectors = (first_gain, first_shift, narrow_bias, middle_gain, middle_shift, conv_bias, last_gain, last_shift, widen_bias)
    packed = jnp.concatenate(
        [jnp.pad(v, ((0, 0), (0, width - v.shape[1]))) for v in vectors] + [jnp.zeros((VROWS - len(vectors), width), F32)]
    )
    packed_x = other(packed)
    v0 = jnp.where(low, packed, packed_x)
    v1 = jnp.where(low, packed_x, packed)

    x_own = lax.dynamic_slice_in_dim(block_input, sec * own, own, 0)
    xh = jnp.concatenate(
        [lax.ppermute(x_own[:, -RIM0:], "dp", ahead), lax.ppermute(x_own[:, :RIM0], "dp", behind)], axis=1
    )

    lane = jnp.arange(LANES, dtype=jnp.int32)[None, None, :]
    offset = jnp.where(lane < 8, (lane - TAPS // 2) * DIL0, (lane - 8 - TAPS // 2) * DIL1)
    masks = ((offset >= -residues_before[..., None]) & (offset <= residues_after[..., None])).astype(F32)
    masks = jnp.where(lane == TYPE_COL, residue_types[..., None].astype(F32), masks)
    masks = jnp.where(lane == MASK_COL, loss_mask[..., None].astype(F32), masks)

    def mine(shape):
        return pl.BlockSpec((1, *shape), lambda i, c: (c[0] * own + i, 0, 0))

    def each(n, w):
        return pl.BlockSpec((1, n, w), lambda i, c: (i, 0, 0))

    def whole(*shape):
        return pl.BlockSpec(shape, lambda i, c: (0,) * len(shape))

    def call(kernel, ins, in_specs, outs, scratch, flops, nbytes, trans=0):
        return pl.pallas_call(
            kernel,
            grid_spec=pltpu.PrefetchScalarGridSpec(
                num_scalar_prefetch=1,
                grid=(own,),
                in_specs=in_specs,
                out_specs=[o[1] for o in outs],
                scratch_shapes=scratch,
            ),
            out_shape=[o[0] for o in outs],
            compiler_params=pltpu.CompilerParams(vmem_limit_bytes=VMEM_LIMIT),
            cost_estimate=pl.CostEstimate(flops=flops, bytes_accessed=nbytes, transcendentals=trans),
        )(c_arr, *ins)

    def o_each(w, dtype=BF16):
        return (jax.ShapeDtypeStruct((own, rows, w), dtype), each(rows, w))

    def o_vec(n, w):
        return (jax.ShapeDtypeStruct((n, w), F32), whole(n, w))

    dma = pltpu.SemaphoreType.DMA
    vspec = whole(VROWS, width)
    mm = 2 * own * rows * width * inner
    wide, thin, one = o_each(width), o_each(inner), o_each(1, F32)
    (act0, slx0, mux0, rsx0, nn0, sln0, rsn0, st0, nc0, slc0, rsc0, oa0, out0,
     act1, slx1, mux1, rsx1, nn1, sln1, rsn1, mid1) = call(
        f0_kernel,
        (block_input, xh, masks, v0, v1, nwo, nwx, cwo, cwx, wwo, wwx),
        [mine((rows, width)), each(2 * RIM0, width), mine((rows, LANES)), vspec, vspec] + [ANY] * 6,
        [wide, wide, one, one, thin, thin, one, o_each(TAPS * inner), thin, thin, one, thin, wide,
         wide, wide, one, one, thin, thin, one, thin],
        [
            pltpu.VMEM((width, inner), BF16),
            pltpu.VMEM((TAPS, inner, inner), BF16),
            pltpu.VMEM((inner, width), BF16),
            pltpu.VMEM((width, inner), BF16),
            pltpu.VMEM((rows + 2 * RIM0, width), BF16),
            pltpu.VMEM((rows + 2 * RIM0, inner), F32),
            pltpu.VMEM((rows + 2 * RIM0, inner), F32),
            pltpu.VMEM((rows, inner), F32),
            pltpu.VMEM((rows, width), F32),
            dma((4,)),
        ],
        int(5.5 * mm), 40_000_000, own * rows * 8 * width,
    )

    up1 = lax.ppermute(mid1[:, -RIM1:], "dp", ahead)
    dn1 = lax.ppermute(mid1[:, :RIM1], "dp", behind)
    st1, oa1, cg1, vec1 = call(
        f1_kernel,
        (mid1, up1, dn1, masks, v1, output_cotangent, cwo, cwx, wwo, wwx),
        [each(rows, inner), each(RIM1, inner), each(RIM1, inner), mine((rows, LANES)), vspec, mine((rows, width))] + [ANY] * 4,
        [o_each(TAPS * inner), thin, thin, o_vec(4, width)],
        [
            pltpu.VMEM((TAPS, inner, inner), BF16),
            pltpu.VMEM((inner, width), BF16),
            pltpu.VMEM((rows + 2 * RIM1, inner), BF16),
            pltpu.VMEM((rows, inner), F32),
            pltpu.VMEM((rows, inner), F32),
            pltpu.VMEM((4, 8, width), F32),
            dma((2,)),
        ],
        int(3.5 * mm), 20_000_000, own * rows * 2 * inner,
    )

    upg = lax.ppermute(cg1[:, -RIM1:], "dp", ahead)
    dng = lax.ppermute(cg1[:, :RIM1], "dp", behind)

    def flat(v):
        return v.reshape(own * rows, v.shape[2])

    cot_own = flat(lax.dynamic_slice_in_dim(output_cotangent, sec * own, own, 0))
    unit = 2 * count * 8

    def padded(n):
        return -(-n // unit) * unit

    rows_a = padded((TAPS + width // inner) * inner)
    rows_b = padded(width)
    pay_a1 = weight_terms([(flat(oa1), cot_own), (flat(st1), flat(cg1))], inner, rows_a)

    ng1, ig1, cg0, vec10 = call(
        b10_kernel,
        (cg1, upg, dng, masks, v0, v1, output_cotangent, sln1, nn1, rsn1, slx1, out0, mux1, rsx1, slc0, nc0, rsc0,
         cwo, cwx, nwo, nwx, wwo, wwx),
        [each(rows, inner), each(RIM1, inner), each(RIM1, inner), mine((rows, LANES)), vspec, vspec, mine((rows, width)),
         each(rows, inner), each(rows, inner), each(rows, 1), each(rows, width), each(rows, width), each(rows, 1), each(rows, 1),
         each(rows, inner), each(rows, inner), each(rows, 1)] + [ANY] * 6,
        [thin, wide, thin, o_vec(9, width)],
        [
            pltpu.VMEM((inner, TAPS * inner), BF16),
            pltpu.VMEM((width, inner), BF16),
            pltpu.VMEM((inner, width), BF16),
            pltpu.VMEM((rows + 2 * RIM1, inner), BF16),
            pltpu.VMEM((rows, TAPS * inner), BF16),
            pltpu.VMEM((rows, inner), F32),
            pltpu.VMEM((rows, width), F32),
            pltpu.VMEM((9, 8, width), F32),
            dma((TAPS + 2,)),
        ],
        int(4.5 * mm), 30_000_000,
    )

    upz = lax.ppermute(cg0[:, -RIM0:], "dp", ahead)
    dnz = lax.ppermute(cg0[:, :RIM0], "dp", behind)
    rim0 = jnp.concatenate([upz, dnz], axis=1)
    pay_b1 = weight_terms([(flat(act1), flat(ng1))], inner, rows_b)
    pay_a0 = weight_terms([(flat(oa0), flat(ig1)), (flat(st0), flat(cg0))], inner, rows_a)

    ng0, ig0, vec0 = call(
        b0_kernel,
        (cg0, rim0, masks, v0, ig1, sln0, nn0, rsn0, slx0, block_input, mux0, rsx0, cwo, cwx, nwo, nwx),
        [each(rows, inner), each(2 * RIM0, inner), mine((rows, LANES)), vspec, each(rows, width),
         each(rows, inner), each(rows, inner), each(rows, 1), each(rows, width), mine((rows, width)), each(rows, 1), each(rows, 1)]
        + [ANY] * 4,
        [thin, wide, o_vec(5, width)],
        [
            pltpu.VMEM((inner, TAPS * inner), BF16),
            pltpu.VMEM((width, inner), BF16),
            pltpu.VMEM((rows + 2 * RIM0, inner), F32),
            pltpu.VMEM((rows, TAPS * inner), BF16),
            pltpu.VMEM((rows, inner), F32),
            pltpu.VMEM((rows, width), F32),
            pltpu.VMEM((5, 8, width), F32),
            dma((TAPS + 1,)),
        ],
        int(3.5 * mm), 25_000_000,
    )
    pay_b0 = weight_terms([(flat(act0), flat(ng0))], inner, rows_b)

    head = jnp.pad(head_weight, ((0, 0), (0, LANES - vocab)))
    out1, tot = call(
        functools.partial(o1_kernel, vocab=vocab),
        (out0, oa1, masks, v1, head, wwo, wwx),
        [each(rows, width), each(rows, inner), mine((rows, LANES)), vspec, whole(width, LANES), ANY, ANY],
        [wide, o_vec(2, LANES)],
        [
            pltpu.VMEM((inner, width), BF16),
            pltpu.VMEM((rows, width), F32),
            pltpu.VMEM((rows, LANES), F32),
            pltpu.VMEM((2, 8, LANES), F32),
            dma((1,)),
        ],
        int(1.2 * mm), 8_000_000,
    )

    steps = dp_steps(count, sec, at)

    def hop(v, pairs):
        return lax.ppermute(v, ("section", "dp"), pairs)

    def summed(pay):
        keep, send = halves(pay, sec)
        buf = add_low(keep, other(send))
        for pairs, bit in steps:
            keep, send = halves(buf, bit)
            buf = add_low(keep, hop(send, pairs))
        for pairs, bit in reversed(steps):
            come = hop(buf, pairs)
            one, two = jnp.where(bit == 0, buf, come), jnp.where(bit == 0, come, buf)
            buf = jnp.concatenate([one, two], axis=0)
        return buf

    half_a1, half_b1, half_a0, half_b0 = summed(pay_a1), summed(pay_b1), summed(pay_a0), summed(pay_b0)

    def joined(half0, half1):
        keep = jnp.where(low, half0, half1)
        come = other(jnp.where(low, half1, half0))
        return jnp.concatenate([jnp.where(low, keep, come), jnp.where(low, come, keep)], axis=0)

    full_a, full_b = joined(half_a0, half_a1), joined(half_b0, half_b1)
    cols = width // inner
    widen_grad = jnp.concatenate([full_a[k * inner : (k + 1) * inner] for k in range(cols)], axis=1).astype(F32)
    conv_grad = full_a[cols * inner : (cols + TAPS) * inner].astype(F32).reshape(TAPS, inner, inner)
    narrow_grad = full_b[:width].astype(F32)

    small = jnp.concatenate([vec1, vec10, vec0, jnp.pad(tot, ((0, 0), (0, width - LANES)))], axis=0)
    small = jnp.pad(small, ((0, -small.shape[0] % 8), (0, 0)))
    for pairs, _ in steps:
        small = small + hop(small, pairs)
    small = small + other(small)
    n1, n10 = vec1.shape[0], vec10.shape[0]
    s1, s10, s0 = small[:n1], small[n1 : n1 + n10], small[n1 + n10 : n1 + n10 + vec0.shape[0]]
    type_total, loss_total = small[n1 + n10 + vec0.shape[0]], small[n1 + n10 + vec0.shape[0] + 1]
    type_total, loss_total = type_total[:vocab], loss_total[:vocab]

    def sel(in0, in1):
        return jnp.where(low, in0, in1)[None]

    first_gain_grad = sel(s0[3], s10[3])
    first_shift_grad = sel(s0[4], s10[4])
    middle_gain_grad = sel(s0[0], s10[0])[:, :inner]
    middle_shift_grad = sel(s0[1], s10[1])[:, :inner]
    narrow_bias_grad = sel(s0[2], s10[2])[:, :inner]
    last_gain_grad = sel(s10[5], s1[0])[:, :inner]
    last_shift_grad = sel(s10[6], s1[1])[:, :inner]
    conv_bias_grad = sel(s10[7], s1[2])[:, :inner]
    widen_bias_grad = sel(s10[8], s1[3])

    def gathered(in0, in1):
        keep = jnp.where(low, in0, in1)
        come = other(jnp.where(low, in1, in0))
        return jnp.concatenate([jnp.where(low, keep, come), jnp.where(low, come, keep)], axis=0)[None]

    return (
        gathered(out0, out1),
        gathered(ig0, ig1),
        first_gain_grad,
        first_shift_grad,
        narrow_grad[None],
        narrow_bias_grad,
        middle_gain_grad,
        middle_shift_grad,
        conv_grad[None],
        conv_bias_grad,
        last_gain_grad,
        last_shift_grad,
        widen_grad[None],
        widen_bias_grad,
        type_total.astype(jnp.int32),
        loss_total / jnp.maximum(type_total, 1.0),
    )


def solution(mesh):
    rows = P(None, "dp", None)
    ids = P(None, "dp")
    vec = P("section", None)
    mat = P("section", None, None)
    conv = P("section", None, None, None)
    weights = (vec, vec, mat, vec, vec, vec, conv, vec, vec, vec, mat, vec)
    grads = P("section", None, "dp", None)
    return jax.shard_map(
        body,
        mesh=mesh,
        in_specs=(rows, rows, ids, ids, ids, ids, *weights, P()),
        out_specs=(grads, grads, *weights, P(), P()),
        check_vma=False,
    )
```

time: 1230 us -> 559 us (0.45)
  Pallas kernels: 0 us -> 233 us
  matrix products: 206 us -> 0 us
  other arithmetic: 261 us -> 57.1 us
  waiting for transfers between devices: 323 us -> 163 us
  local copies, waits for them, and re-layouts: 161 us -> 32.8 us
  blocking collectives: 127 us -> 0 us
  starting transfers between devices: 121 us -> 64.5 us
  between operations: 20.3 us -> 1.95 us
    psum x1 -> x0, waiting for transfers between devices: 255 us -> none  [body(): lax.psum((totals[0], totals[1], totals[2], totals[3], totals[4], totals[5...]
    pallas_call x0 -> x9, Pallas kernels: none -> 233 us  [the longest x5 201 us: call(): pl.pallas_call(kernel, grid_spec=pltpu.PrefetchScalarGridSpec(num_scalar_...]
    dot_general x79 -> x0, matrix products: 206 us -> none  [the longest x24 105 us: contract_rows(): lax.dot_general(left_side, right_side, (((0,), (0,)), ((), ())), preferre...]
    psum x2 -> x0, blocking collectives: 127 us -> none  [the longest x1 79 us: body(): lax.psum((totals[0], totals[1], totals[2], totals[3], totals[4], totals[5...]
    dynamic_update_slice x32 -> x0, local copies, waits for them, and re-layouts: 117 us -> none  [backward_pass(): lax.dynamic_update_slice_in_dim(extended, current + contribution, begin_a...]
    ppermute x46 -> x57, waiting for transfers between devices: 67.4 us -> 163 us  [the longest x36 150 us: hop(): return lax.ppermute(v, ('section', 'dp'), pairs)]
    reduce_sum x127 -> x0, other arithmetic: 94.1 us -> none  [the longest x16 26.3 us: norm_act(): center * lax.rsqrt(spread + epsilon) * gain_row + shift_row]
    ppermute x46 -> x57, starting transfers between devices: 121 us -> 64.5 us  [the longest x36 40 us: hop(): return lax.ppermute(v, ('section', 'dp'), pairs)]
  transfers between devices with their start and end apart: 47 -> 57, of which waited for: 26 -> 23; matrix products, arithmetic and copies ran while one was open for 12% -> 12% of each run, Pallas kernels for 0% -> 22%
where the time goes in v1:
time: 559 us; the launch traced here: 552 us
  Pallas kernels  233 us (42%)
  waiting for transfers between devices  163 us (29%)
  starting transfers between devices  64.5 us (12%)
  other arithmetic  57.1 us (10%)
  local copies, waits for them, and re-layouts  32.8 us (6%)
    pallas_call x5, Pallas kernels, call(): pl.pallas_call(kernel, grid_spec=pltpu.PrefetchScalarGridSpec(num_scalar_...  201 us
    ppermute x36, waiting for transfers between devices, hop(): return lax.ppermute(v, ('section', 'dp'), pairs)  150 us
    ppermute x36, starting transfers between devices, hop(): return lax.ppermute(v, ('section', 'dp'), pairs)  40 us
    pallas_call x4, Pallas kernels, weight_terms(): pl.pallas_call(kernel, grid=(at,), in_specs=specs, out_specs=pl.BlockSpec...  31.7 us
    ppermute x1, waiting for transfers between devices, body(): up1 = lax.ppermute(mid1[:, -RIM1:], 'dp', ahead)  12.2 us
    dynamic_slice x20, local copies, waits for them, and re-layouts, halves(): send = lax.dynamic_slice_in_dim(buf, (1 - bit) * rows, rows, 0)  11.6 us
  transfers between devices with their start and end apart: 57, of which 23 were waited for; matrix products, arithmetic and copies ran while one was open for 12% of the time, Pallas kernels for 22%

profile of v1, /device:TPU:0, one launch (start us, length us, event | category | flops | bytes accessed | tf_op | source)
XLA Modules:
  0.0 551.9 jit_solution(1009678607559682601)
XLA Ops:
  3.2 2.6 collective-permute-start
  5.7 4.0 collective-permute-start.1
  11.8 3.3 select_select_fusion.mk_ref
  26.2 82.2 %shard_map.306 = (bf16[3,256,1280]{2,1,0:T(8,128)(2,1)}, bf16[3,256,1280]{2,1,0:T(8,128)(2,1)}, f32[3,256,1]{2,1,0:T(8,128)}, f32[3,256,1]{2,1,0:T(8,128)}, bf16...) custom-call(s32[1]{0:T(128)} %bitcast.c_ref, ...), custom_call_target="tpu_custom_call" | custom-call | flops 6920601600 | bytes 40000000 | tf_op jit(solution)/shard_map/pallas_call | solution.py:557
  109.8 5.6 %collective-permute-start.7 = (bf16[3,128,640]{2,1,0:T(8,128)(2,1)S(1)}, bf16[3,128,640]{2,1,0:T(8,128)(2,1)S(1)}, u32[]{:S(2)}, u32[]{:S(2)}) collective-permute-start(bf16[3,128,640]{2,1,0:T(8,128)(2,1)S(1)} %get-tuple-element.108), channel_id=1, source_target_pairs={{1,0},{2,1},{3,2},{4,3},{5,4},{6,5},{7,6},{8,7},{9,8},{10,9},{11,1... | collective-permute-start | bytes 1474568 | tf_op jit(solution)/shard_map/ppermute | solution.py:604
  116.5 2.9 constant_dynamic-slice_fusion.6
  119.4 12.2 %collective-permute-done.6.up_ref = bf16[3,128,640]{2,1,0:T(8,128)(2,1)S(1)} collective-permute-done((bf16[3,128,640]{2,1,0:T(8,128)(2,1)S(1)}, bf16[3,128,640]{2,1,0:T(8,128)(2,1)S(1)}, u32[]{:S(2)}, u32[]{:S(2)}) %collective-permute-start.6) | collective-permute-done | bytes 491552 | tf_op jit(solution)/shard_map/ppermute | solution.py:603
  133.2 29.4 %shard_map.307 = (bf16[3,256,3200]{2,1,0:T(8,128)(2,1)}, bf16[3,256,640]{2,1,0:T(8,128)(2,1)}, bf16[3,256,640]{2,1,0:T(8,128)(2,1)}, f32[4,1280]{1,0:T(4,128)}) custom-call(s32[1]{0:T(128)} %bitcast.c_ref, bf16[3,256,640]{2,1,0:T(8,128)(2,1)} %get-tuple-element.51.mid_ref, bf16[3,128,640]{2,1,0:T(8,128)(2,1)} %copy-done.12, bf16[3,128,640]{2,1,0:T(8,128)(2,1)} %copy-done.13, ...), custom_call_target="tpu_custom_call" | custom-call | flops 4404019200 | bytes 20000000 | tf_op jit(solution)/shard_map/pallas_call | solution.py:557
  163.9 4.2 collective-permute-start.10
  168.2 11.3 %shard_map.314 = bf16[4608,640]{1,0:T(8,128)(2,1)} custom-call(bf16[768,640]{1,0:T(8,128)(2,1)} %bitcast.57, bf16[768,1280]{1,0:T(8,128)(2,1)} %bitcast.55, bf16[768,3200]{1,0:T(8,128)(2,1)} %bitcast.58, bf16[768,640]{1,0:T(8,128)(2,1)} %bitcast.54), custom_call_target="tpu_custom_call" | custom-call | flops 4404019200 | bytes 11796480 | tf_op jit(solution)/shard_map/pallas_call | solution.py:470
  179.5 3.7 constant_dynamic-slice_fusion.5
  183.2 13.9 %shard_map.308 = (bf16[3,256,1280]{2,1,0:T(8,128)(2,1)}, f32[2,128]{1,0:T(2,128)}) custom-call(s32[1]{0:T(128)} %bitcast.c_ref, bf16[3,256,1280]{2,1,0:T(8,128)(2,1)} %get-tuple-element.50.out0_ref.out0, bf16[3,256,640]{2,1,0:T(8,128)(2,1)} %get-tuple-element.52.oa_ref, f32[6,256,128]{2,1,0:T(8,128)} %select_select_fusion.mk_ref, ...), custom_call_target="tpu_custom_call" | custom-call | flops 1509949440 | bytes 8000000 | tf_op jit(solution)/shard_map/pallas_call | solution.py:557
  198.0 41.3 %shard_map.309 = (bf16[3,256,640]{2,1,0:T(8,128)(2,1)}, bf16[3,256,1280]{2,1,0:T(8,128)(2,1)}, bf16[3,256,640]{2,1,0:T(8,128)(2,1)}, f32[9,1280]{1,0:T(8,128)}) custom-call(s32[1]{0:T(128)} %bitcast.c_ref, bf16[3,256,640]{2,1,0:T(8,128)(2,1)} %get-tuple-element.54.cg_ref, bf16[3,128,640]{2,1,0:T(8,128)(2,1)} %copy-done.11, bf16[3,128,640]{2,1,0:T(8,128)(2,1)} %copy-done.10, ...), custom_call_target="tpu_custom_call" | custom-call | flops 5662310400 | bytes 30000000 | tf_op jit(solution)/shard_map/pallas_call | solution.py:557
  241.3 4.4 collective-permute-start.12
  248.3 34.1 %shard_map.310 = (bf16[3,256,640]{2,1,0:T(8,128)(2,1)}, bf16[3,256,1280]{2,1,0:T(8,128)(2,1)}, f32[5,1280]{1,0:T(8,128)}) custom-call(s32[1]{0:T(128)} %bitcast.c_ref, bf16[3,256,640]{2,1,0:T(8,128)(2,1)} %get-tuple-element.64.cg_ref, bf16[3,16,640]{2,1,0:T(8,128)(2,1)} %pad_maximum_fusion.18.rim_ref, f32[6,256,128]{2,1,0:T(8,128)} %select_select_fusion.mk_ref, ...), custom_call_target="tpu_custom_call" | custom-call | flops 4404019200 | bytes 25000000 | tf_op jit(solution)/shard_map/pallas_call | solution.py:557
  283.4 11.3 %shard_map.313 = bf16[4608,640]{1,0:T(8,128)(2,1)} custom-call(bf16[768,640]{1,0:T(8,128)(2,1)} %bitcast.64, bf16[768,1280]{1,0:T(8,128)(2,1)} %bitcast.39, bf16[768,3200]{1,0:T(8,128)(2,1)} %bitcast.61, bf16[768,640]{1,0:T(8,128)(2,1)} %bitcast.56), custom_call_target="tpu_custom_call" | custom-call | flops 4404019200 | bytes 11796480 | tf_op jit(solution)/shard_map/pallas_call | solution.py:470
  295.0 3.7 constant_dynamic-slice_fusion.11
  298.7 4.5 shard_map.312
  309.0 5.3 collective-permute-start.17
  315.8 4.6 shard_map.311
  331.2 5.1 collective-permute-done.29
  336.4 4.2 collective-permute-done.20
  340.8 5.6 %collective-permute-done.30 = bf16[160,640]{1,0:T(8,128)(2,1)S(1)} collective-permute-done((bf16[160,640]{1,0:T(8,128)(2,1)S(1)}, bf16[160,640]{1,0:T(8,128)(2,1)S(1)}, u32[]{:S(2)}, u32[]{:S(2)}) %collective-permute-start.30) | collective-permute-done | bytes 204832 | tf_op jit(solution)/shard_map/ppermute | solution.py:706
  346.5 5.7 %collective-permute-done.21 = bf16[160,640]{1,0:T(8,128)(2,1)S(1)} collective-permute-done((bf16[160,640]{1,0:T(8,128)(2,1)S(1)}, bf16[160,640]{1,0:T(8,128)(2,1)S(1)}, u32[]{:S(2)}, u32[]{:S(2)}) %collective-permute-start.21) | collective-permute-done | bytes 204832 | tf_op jit(solution)/shard_map/ppermute | solution.py:706
  354.4 2.9 add_convert_fusion
  357.6 2.6 add_convert_fusion.1
  364.8 13.0 %collective-permute-done.48 = bf16[1152,640]{1,0:T(8,128)(2,1)S(1)} collective-permute-done((bf16[1152,640]{1,0:T(8,128)(2,1)S(1)}, bf16[1152,640]{1,0:T(8,128)(2,1)S(1)}, u32[]{:S(2)}, u32[]{:S(2)}) %collective-permute-start.48) | collective-permute-done | bytes 1474592 | tf_op jit(solution)/shard_map/ppermute | solution.py:706
  380.2 22.9 %collective-permute-done.39 = bf16[1152,640]{1,0:T(8,128)(2,1)S(1)} collective-permute-done((bf16[1152,640]{1,0:T(8,128)(2,1)S(1)}, bf16[1152,640]{1,0:T(8,128)(2,1)S(1)}, u32[]{:S(2)}, u32[]{:S(2)}) %collective-permute-start.39) | collective-permute-done | bytes 1474592 | tf_op jit(solution)/shard_map/ppermute | solution.py:706
  405.0 2.6 collective-permute-start.33
  408.1 10.3 %collective-permute-done.50 = bf16[288,640]{1,0:T(8,128)(2,1)S(1)} collective-permute-done((bf16[288,640]{1,0:T(8,128)(2,1)S(1)}, bf16[288,640]{1,0:T(8,128)(2,1)S(1)}, u32[]{:S(2)}, u32[]{:S(2)}) %collective-permute-start.50) | collective-permute-done | bytes 368672 | tf_op jit(solution)/shard_map/ppermute | solution.py:706
  420.2 2.7 collective-permute-start.41
  423.0 7.7 %collective-permute-done.51 = bf16[144,640]{1,0:T(8,128)(2,1)S(1)} collective-permute-done((bf16[144,640]{1,0:T(8,128)(2,1)S(1)}, bf16[144,640]{1,0:T(8,128)(2,1)S(1)}, u32[]{:S(2)}, u32[]{:S(2)}) %collective-permute-start.51) | collective-permute-done | bytes 184352 | tf_op jit(solution)/shard_map/ppermute | solution.py:706
  430.8 6.6 %collective-permute-done.41 = bf16[288,640]{1,0:T(8,128)(2,1)S(1)} collective-permute-done((bf16[288,640]{1,0:T(8,128)(2,1)S(1)}, bf16[288,640]{1,0:T(8,128)(2,1)S(1)}, u32[]{:S(2)}, u32[]{:S(2)}) %collective-permute-start.41) | collective-permute-done | bytes 368672 | tf_op jit(solution)/shard_map/ppermute | solution.py:706
  437.7 6.8 %collective-permute-done.52 = bf16[144,640]{1,0:T(8,128)(2,1)S(1)} collective-permute-done((bf16[144,640]{1,0:T(8,128)(2,1)S(1)}, bf16[144,640]{1,0:T(8,128)(2,1)S(1)}, u32[]{:S(2)}, u32[]{:S(2)}) %collective-permute-start.52) | collective-permute-done | bytes 184352 | tf_op jit(solution)/shard_map/ppermute | solution.py:706
  447.7 7.8 %collective-permute-done.43 = bf16[144,640]{1,0:T(8,128)(2,1)S(1)} collective-permute-done((bf16[144,640]{1,0:T(8,128)(2,1)S(1)}, bf16[144,640]{1,0:T(8,128)(2,1)S(1)}, u32[]{:S(2)}, u32[]{:S(2)}) %collective-permute-start.43) | collective-permute-done | bytes 184352 | tf_op jit(solution)/shard_map/ppermute | solution.py:706
  455.6 3.1 collective-permute-start.44
  459.0 3.3 collective-permute-start.54
  464.5 3.3 collective-permute-start.45
  468.0 11.7 %collective-permute-done.54 = bf16[576,640]{1,0:T(8,128)(2,1)S(1)} collective-permute-done((bf16[576,640]{1,0:T(8,128)(2,1)S(1)}, bf16[576,640]{1,0:T(8,128)(2,1)S(1)}, u32[]{:S(2)}, u32[]{:S(2)}) %collective-permute-start.54) | collective-permute-done | bytes 737312 | tf_op jit(solution)/shard_map/ppermute | solution.py:706
  480.2 15.3 %collective-permute-done.45 = bf16[576,640]{1,0:T(8,128)(2,1)S(1)} collective-permute-done((bf16[576,640]{1,0:T(8,128)(2,1)S(1)}, bf16[576,640]{1,0:T(8,128)(2,1)S(1)}, u32[]{:S(2)}, u32[]{:S(2)}) %collective-permute-start.45) | collective-permute-done | bytes 737312 | tf_op jit(solution)/shard_map/ppermute | solution.py:706
  500.4 3.9 collective-permute-done.26
  504.9 10.4 %collective-permute-done.46 = bf16[1152,640]{1,0:T(8,128)(2,1)S(1)} collective-permute-done((bf16[1152,640]{1,0:T(8,128)(2,1)S(1)}, bf16[1152,640]{1,0:T(8,128)(2,1)S(1)}, u32[]{:S(2)}, u32[]{:S(2)}) %collective-permute-start.46) | collective-permute-done | bytes 1474592 | tf_op jit(solution)/shard_map/ppermute | solution.py:706
  515.9 5.6 %broadcast_select_fusion.2 = bf16[2304,640]{1,0:T(8,128)(2,1)S(1)} fusion(pred[]{:T(512)S(6)} %eq.28, bf16[1152,640]{1,0:T(8,128)(2,1)S(1)} %get-tuple-element.97, bf16[1152,640]{1,0:T(8,128)(2,1)S(1)} %get-tuple-element.96, bf16[1152,640]{1,0:T(8,128)(2,1)S(1)} %get-tuple-element.95, bf16[1152,640]{1,0:T(8,128)(2,1)S(1)} %get-tuple-element.94), kind=kLoop, calls=%fused_computation.11 | loop fusion | flops 13271040 | bytes 8847361 | tf_op jit(solution)/shard_map/jit(_where)/select_n | solution.py:724
  521.7 2.3 maximum_bitcast_fusion
  524.2 5.5 collective-permute-done.27
  532.0 2.3 maximum_bitcast_fusion.1
  536.6 6.8 %broadcast_select_fusion.1 = (bf16[2304,640]{1,0:T(8,128)(2,1)S(1)}, bf16[2304,640]{1,0:T(8,128)(2,1)}) fusion(bf16[2304,640]{1,0:T(8,128)(2,1)S(1)} %collective-permute-done.56, pred[]{:T(512)S(6)} %eq.28, bf16[1152,640]{1,0:T(8,128)(2,1)S(1)} %get-tuple-element.97, bf16[1152,640]{1,0:T(8,128)(2,1)S(1)} %get-tuple-element.96, ...), kind=kLoop, calls=%fused_computation.10 | loop fusion | flops 16220160 | bytes 14745601 | tf_op jit(solution)/shard_map/jit(_where)/select_n | solution.py:725
  545.7 3.9 convert.1
  (243 shorter events, 81.4 us)
Async XLA Ops:
  0.6 23.8 %collective-permute-start.4 = (bf16[5,640,640]{2,1,0:T(8,128)(2,1)}, bf16[5,640,640]{2,1,0:T(8,128)(2,1)}, u32[]{:S(2)}, u32[]{:S(2)}) collective-permute-start(bf16[5,640,640]{2,1,0:T(8,128)(2,1)} %bitcast.34), channel_id=1, source_target_pairs={{0,16},{16,0},{1,17},{17,1},{2,18},{18,2},{3,19},{19,3},{4,20},{20... | collective-permute-start | bytes 12288008 | tf_op jit(solution)/shard_map/ppermute | solution.py:524
  1.2 23.3 %collective-permute-start.5 = (bf16[640,1280]{1,0:T(8,128)(2,1)}, bf16[640,1280]{1,0:T(8,128)(2,1)S(1)}, u32[]{:S(2)}, u32[]{:S(2)}) collective-permute-start(bf16[640,1280]{1,0:T(8,128)(2,1)} %bitcast.41), channel_id=1, source_target_pairs={{0,16},{16,0},{1,17},{17,1},{2,18},{18,2},{3,19},{19,3},{4,20},{20... | collective-permute-start | bytes 4915208 | tf_op jit(solution)/shard_map/ppermute | solution.py:524
  1.2 23.2 %collective-permute-start.3 = (bf16[1280,640]{1,0:T(8,128)(2,1)}, bf16[1280,640]{1,0:T(8,128)(2,1)S(1)}, u32[]{:S(2)}, u32[]{:S(2)}) collective-permute-start(bf16[1280,640]{1,0:T(8,128)(2,1)} %bitcast.46), channel_id=1, source_target_pairs={{0,16},{16,0},{1,17},{17,1},{2,18},{18,2},{3,19},{19,3},{4,20},{20... | collective-permute-start | bytes 4915208 | tf_op jit(solution)/shard_map/ppermute | solution.py:524
  3.2 18.8 %collective-permute-start = (bf16[3,8,1280]{2,1,0:T(8,128)(2,1)}, bf16[3,8,1280]{2,1,0:T(8,128)(2,1)S(1)}, u32[]{:S(2)}, u32[]{:S(2)}) collective-permute-start(bf16[3,8,1280]{2,1,0:T(8,128)(2,1)} %get-tuple-element.90), channel_id=1, source_target_pairs={{0,1},{1,2},{2,3},{3,4},{4,5},{5,6},{6,7},{7,8},{8,9},{9,10},{10,1... | collective-permute-start | bytes 184328 | tf_op jit(solution)/shard_map/ppermute | solution.py:538
  5.7 16.5 %collective-permute-start.1 = (bf16[3,8,1280]{2,1,0:T(8,128)(2,1)S(1)}, bf16[3,8,1280]{2,1,0:T(8,128)(2,1)}, u32[]{:S(2)}, u32[]{:S(2)}) collective-permute-start(bf16[3,8,1280]{2,1,0:T(8,128)(2,1)S(1)} %get-tuple-element.91), channel_id=1, source_target_pairs={{1,0},{2,1},{3,2},{4,3},{5,4},{6,5},{7,6},{8,7},{9,8},{10,9},{11,1... | collective-permute-start | bytes 184328 | tf_op jit(solution)/shard_map/ppermute | solution.py:538
  109.8 21.9 %collective-permute-start.6 = (bf16[3,128,640]{2,1,0:T(8,128)(2,1)S(1)}, bf16[3,128,640]{2,1,0:T(8,128)(2,1)S(1)}, u32[]{:S(2)}, u32[]{:S(2)}) collective-permute-start(bf16[3,128,640]{2,1,0:T(8,128)(2,1)S(1)} %get-tuple-element.109), channel_id=1, source_target_pairs={{0,1},{1,2},{2,3},{3,4},{4,5},{5,6},{6,7},{7,8},{8,9},{9,10},{10,1... | collective-permute-start | bytes 1474568 | tf_op jit(solution)/shard_map/ppermute | solution.py:603
  109.8 22.4 %collective-permute-start.7 = (bf16[3,128,640]{2,1,0:T(8,128)(2,1)S(1)}, bf16[3,128,640]{2,1,0:T(8,128)(2,1)S(1)}, u32[]{:S(2)}, u32[]{:S(2)}) collective-permute-start(bf16[3,128,640]{2,1,0:T(8,128)(2,1)S(1)} %get-tuple-element.108), channel_id=1, source_target_pairs={{1,0},{2,1},{3,2},{4,3},{5,4},{6,5},{7,6},{8,7},{9,8},{10,9},{11,1... | collective-permute-start | bytes 1474568 | tf_op jit(solution)/shard_map/ppermute | solution.py:604
  163.9 33.2 %collective-permute-start.10 = (bf16[3,128,640]{2,1,0:T(8,128)(2,1)S(1)}, bf16[3,128,640]{2,1,0:T(8,128)(2,1)S(1)}, u32[]{:S(2)}, u32[]{:S(2)}) collective-permute-start(bf16[3,128,640]{2,1,0:T(8,128)(2,1)S(1)} %get-tuple-element.106), channel_id=1, source_target_pairs={{1,0},{2,1},{3,2},{4,3},{5,4},{6,5},{7,6},{8,7},{9,8},{10,9},{11,1... | collective-permute-start | bytes 1474568 | tf_op jit(solution)/shard_map/ppermute | solution.py:623
  168.1 29.0 %collective-permute-start.9 = (bf16[3,128,640]{2,1,0:T(8,128)(2,1)S(1)}, bf16[3,128,640]{2,1,0:T(8,128)(2,1)S(1)}, u32[]{:S(2)}, u32[]{:S(2)}) collective-permute-start(bf16[3,128,640]{2,1,0:T(8,128)(2,1)S(1)} %get-tuple-element.107), channel_id=1, source_target_pairs={{0,1},{1,2},{2,3},{3,4},{4,5},{5,6},{6,7},{7,8},{8,9},{9,10},{10,1... | collective-permute-start | bytes 1474568 | tf_op jit(solution)/shard_map/ppermute | solution.py:622
  183.2 170.8 %collective-permute-start.47 = (bf16[2304,640]{1,0:T(8,128)(2,1)}, bf16[2304,640]{1,0:T(8,128)(2,1)}, u32[]{:S(2)}, u32[]{:S(2)}) collective-permute-start(bf16[2304,640]{1,0:T(8,128)(2,1)} %constant_dynamic-slice_fusion.5), channel_id=1, source_target_pairs={{0,16},{16,0},{1,17},{17,1},{2,18},{18,2},{3,19},{19,3},{4,20},{20... | collective-permute-start | bytes 8847368 | tf_op jit(solution)/shard_map/ppermute | solution.py:524
  247.2 113.1 %collective-permute-start.8 = (bf16[3,256,1280]{2,1,0:T(8,128)(2,1)}, bf16[3,256,1280]{2,1,0:T(8,128)(2,1)S(1)}, u32[]{:S(2)}, u32[]{:S(2)}) collective-permute-start(bf16[3,256,1280]{2,1,0:T(8,128)(2,1)} %broadcast_select_fusion.10), channel_id=1, source_target_pairs={{0,16},{16,0},{1,17},{17,1},{2,18},{18,2},{3,19},{19,3},{4,20},{20... | collective-permute-start | bytes 5898248 | tf_op jit(solution)/shard_map/ppermute | solution.py:524
  283.3 11.4 %collective-permute-start.14 = (f32[24,1280]{1,0:T(8,128)S(1)}, f32[24,1280]{1,0:T(8,128)S(1)}, u32[]{:S(2)}, u32[]{:S(2)}) collective-permute-start(f32[24,1280]{1,0:T(8,128)S(1)} %pad.39), channel_id=1, source_target_pairs={{0,1},{1,0},{2,3},{3,2},{4,5},{5,4},{6,7},{7,6},{8,9},{9,8},{10,11... | collective-permute-start | bytes 368648 | tf_op jit(solution)/shard_map/ppermute | solution.py:706
  294.7 8.5 %collective-permute-start.15 = (f32[24,1280]{1,0:T(8,128)S(1)}, f32[24,1280]{1,0:T(8,128)S(1)}, u32[]{:S(2)}, u32[]{:S(2)}) collective-permute-start(f32[24,1280]{1,0:T(8,128)S(1)} %pad_add_fusion), channel_id=1, source_target_pairs={{0,2},{1,3},{2,0},{3,1},{4,6},{5,7},{6,4},{7,5},{8,10},{9,11},{10,... | collective-permute-start | bytes 368648 | tf_op jit(solution)/shard_map/ppermute | solution.py:706
  298.6 58.8 %collective-permute-start.38 = (bf16[2304,640]{1,0:T(8,128)(2,1)}, bf16[2304,640]{1,0:T(8,128)(2,1)}, u32[]{:S(2)}, u32[]{:S(2)}) collective-permute-start(bf16[2304,640]{1,0:T(8,128)(2,1)} %constant_dynamic-slice_fusion.11), channel_id=1, source_target_pairs={{0,16},{16,0},{1,17},{17,1},{2,18},{18,2},{3,19},{19,3},{4,20},{20... | collective-permute-start | bytes 8847368 | tf_op jit(solution)/shard_map/ppermute | solution.py:524
  307.0 19.5 %collective-permute-start.28 = (bf16[640,640]{1,0:T(8,128)(2,1)}, bf16[640,640]{1,0:T(8,128)(2,1)}, u32[]{:S(2)}, u32[]{:S(2)}) collective-permute-start(bf16[640,640]{1,0:T(8,128)(2,1)} %constant_dynamic-slice_fusion.16), channel_id=1, source_target_pairs={{0,16},{16,0},{1,17},{17,1},{2,18},{18,2},{3,19},{19,3},{4,20},{20... | collective-permute-start | bytes 2457608 | tf_op jit(solution)/shard_map/ppermute | solution.py:524
  309.0 11.4 %collective-permute-start.17 = (f32[24,1280]{1,0:T(8,128)S(1)}, f32[24,1280]{1,0:T(8,128)S(1)}, u32[]{:S(2)}, u32[]{:S(2)}) collective-permute-start(f32[24,1280]{1,0:T(8,128)S(1)} %add.197), channel_id=1, source_target_pairs={{0,8},{1,9},{2,10},{3,11},{4,12},{5,13},{6,14},{7,15},{8,0},{9,1},... | collective-permute-start | bytes 368648 | tf_op jit(solution)/shard_map/ppermute | solution.py:706
  328.3 8.0 %collective-permute-start.29 = (bf16[320,640]{1,0:T(8,128)(2,1)S(1)}, bf16[320,640]{1,0:T(8,128)(2,1)S(1)}, u32[]{:S(2)}, u32[]{:S(2)}) collective-permute-start(bf16[320,640]{1,0:T(8,128)(2,1)S(1)} %constant_dynamic-slice_fusion.15), channel_id=1, source_target_pairs={{0,1},{1,0},{2,3},{3,2},{4,5},{5,4},{6,7},{7,6},{8,9},{9,8},{10,11... | collective-permute-start | bytes 1228808 | tf_op jit(solution)/shard_map/ppermute | solution.py:706
  328.7 12.0 %collective-permute-start.20 = (bf16[320,640]{1,0:T(8,128)(2,1)S(1)}, bf16[320,640]{1,0:T(8,128)(2,1)S(1)}, u32[]{:S(2)}, u32[]{:S(2)}) collective-permute-start(bf16[320,640]{1,0:T(8,128)(2,1)S(1)} %constant_dynamic-slice_fusion.20), channel_id=1, source_target_pairs={{0,1},{1,0},{2,3},{3,2},{4,5},{5,4},{6,7},{7,6},{8,9},{9,8},{10,11... | collective-permute-start | bytes 1228808 | tf_op jit(solution)/shard_map/ppermute | solution.py:706
  336.3 193.8 %collective-permute-start.13 = (bf16[3,256,1280]{2,1,0:T(8,128)(2,1)}, bf16[3,256,1280]{2,1,0:T(8,128)(2,1)}, u32[]{:S(2)}, u32[]{:S(2)}) collective-permute-start(bf16[3,256,1280]{2,1,0:T(8,128)(2,1)} %broadcast_select_fusion.6), channel_id=1, source_target_pairs={{0,16},{16,0},{1,17},{17,1},{2,18},{18,2},{3,19},{19,3},{4,20},{20... | collective-permute-start | bytes 5898248 | tf_op jit(solution)/shard_map/ppermute | solution.py:524
  352.2 10.5 %collective-permute-start.31 = (bf16[80,640]{1,0:T(8,128)(2,1)S(1)}, bf16[80,640]{1,0:T(8,128)(2,1)S(1)}, u32[]{:S(2)}, u32[]{:S(2)}) collective-permute-start(bf16[80,640]{1,0:T(8,128)(2,1)S(1)} %constant_dynamic-slice_fusion.13), channel_id=1, source_target_pairs={{0,4},{1,5},{2,6},{3,7},{4,0},{5,1},{6,2},{7,3},{8,12},{9,13},{10,... | collective-permute-start | bytes 307208 | tf_op jit(solution)/shard_map/ppermute | solution.py:706
  354.0 10.8 %collective-permute-start.22 = (bf16[80,640]{1,0:T(8,128)(2,1)S(1)}, bf16[80,640]{1,0:T(8,128)(2,1)S(1)}, u32[]{:S(2)}, u32[]{:S(2)}) collective-permute-start(bf16[80,640]{1,0:T(8,128)(2,1)S(1)} %constant_dynamic-slice_fusion.18), channel_id=1, source_target_pairs={{0,4},{1,5},{2,6},{3,7},{4,0},{5,1},{6,2},{7,3},{8,12},{9,13},{10,... | collective-permute-start | bytes 307208 | tf_op jit(solution)/shard_map/ppermute | solution.py:706
  357.4 20.4 %collective-permute-start.48 = (bf16[1152,640]{1,0:T(8,128)(2,1)S(1)}, bf16[1152,640]{1,0:T(8,128)(2,1)S(1)}, u32[]{:S(2)}, u32[]{:S(2)}) collective-permute-start(bf16[1152,640]{1,0:T(8,128)(2,1)S(1)} %constant_dynamic-slice_fusion.4), channel_id=1, source_target_pairs={{0,1},{1,0},{2,3},{3,2},{4,5},{5,4},{6,7},{7,6},{8,9},{9,8},{10,11... | collective-permute-start | bytes 4423688 | tf_op jit(solution)/shard_map/ppermute | solution.py:706
  360.3 42.8 %collective-permute-start.39 = (bf16[1152,640]{1,0:T(8,128)(2,1)S(1)}, bf16[1152,640]{1,0:T(8,128)(2,1)S(1)}, u32[]{:S(2)}, u32[]{:S(2)}) collective-permute-start(bf16[1152,640]{1,0:T(8,128)(2,1)S(1)} %constant_dynamic-slice_fusion.10), channel_id=1, source_target_pairs={{0,1},{1,0},{2,3},{3,2},{4,5},{5,4},{6,7},{7,6},{8,9},{9,8},{10,11... | collective-permute-start | bytes 4423688 | tf_op jit(solution)/shard_map/ppermute | solution.py:706
  362.8 42.3 %collective-permute-start.32 = (bf16[40,640]{1,0:T(8,128)(2,1)S(1)}, bf16[40,640]{1,0:T(8,128)(2,1)S(1)}, u32[]{:S(2)}, u32[]{:S(2)}) collective-permute-start(bf16[40,640]{1,0:T(8,128)(2,1)S(1)} %constant_dynamic-slice_fusion.12), channel_id=1, source_target_pairs={{0,8},{1,9},{2,10},{3,11},{4,12},{5,13},{6,14},{7,15},{8,0},{9,1},... | collective-permute-start | bytes 153608 | tf_op jit(solution)/shard_map/ppermute | solution.py:706
  378.3 25.4 %collective-permute-start.49 = (bf16[576,640]{1,0:T(8,128)(2,1)S(1)}, bf16[576,640]{1,0:T(8,128)(2,1)S(1)}, u32[]{:S(2)}, u32[]{:S(2)}) collective-permute-start(bf16[576,640]{1,0:T(8,128)(2,1)S(1)} %constant_dynamic-slice_fusion.3), channel_id=1, source_target_pairs={{0,2},{1,3},{2,0},{3,1},{4,6},{5,7},{6,4},{7,5},{8,10},{9,11},{10,... | collective-permute-start | bytes 2211848 | tf_op jit(solution)/shard_map/ppermute | solution.py:706
  378.4 29.3 %collective-permute-start.23 = (bf16[40,640]{1,0:T(8,128)(2,1)S(1)}, bf16[40,640]{1,0:T(8,128)(2,1)S(1)}, u32[]{:S(2)}, u32[]{:S(2)}) collective-permute-start(bf16[40,640]{1,0:T(8,128)(2,1)S(1)} %constant_dynamic-slice_fusion.17), channel_id=1, source_target_pairs={{0,8},{1,9},{2,10},{3,11},{4,12},{5,13},{6,14},{7,15},{8,0},{9,1},... | collective-permute-start | bytes 153608 | tf_op jit(solution)/shard_map/ppermute | solution.py:706
  403.6 16.4 %collective-permute-start.40 = (bf16[576,640]{1,0:T(8,128)(2,1)S(1)}, bf16[576,640]{1,0:T(8,128)(2,1)S(1)}, u32[]{:S(2)}, u32[]{:S(2)}) collective-permute-start(bf16[576,640]{1,0:T(8,128)(2,1)S(1)} %constant_dynamic-slice_fusion.9), channel_id=1, source_target_pairs={{0,2},{1,3},{2,0},{3,1},{4,6},{5,7},{6,4},{7,5},{8,10},{9,11},{10,... | collective-permute-start | bytes 2211848 | tf_op jit(solution)/shard_map/ppermute | solution.py:706
  403.9 14.6 %collective-permute-start.50 = (bf16[288,640]{1,0:T(8,128)(2,1)S(1)}, bf16[288,640]{1,0:T(8,128)(2,1)S(1)}, u32[]{:S(2)}, u32[]{:S(2)}) collective-permute-start(bf16[288,640]{1,0:T(8,128)(2,1)S(1)} %constant_dynamic-slice_fusion.2), channel_id=1, source_target_pairs={{0,4},{1,5},{2,6},{3,7},{4,0},{5,1},{6,2},{7,3},{8,12},{9,13},{10,... | collective-permute-start | bytes 1105928 | tf_op jit(solution)/shard_map/ppermute | solution.py:706
  405.0 17.8 %collective-permute-start.33 = (bf16[40,640]{1,0:T(8,128)(2,1)S(1)}, bf16[40,640]{1,0:T(8,128)(2,1)S(1)}, u32[]{:S(2)}, u32[]{:S(2)}) collective-permute-start(bf16[40,640]{1,0:T(8,128)(2,1)S(1)} %add_convert_fusion.18), channel_id=1, source_target_pairs={{0,8},{1,9},{2,10},{3,11},{4,12},{5,13},{6,14},{7,15},{8,0},{9,1},... | collective-permute-start | bytes 153608 | tf_op jit(solution)/shard_map/ppermute | solution.py:706
  407.7 40.0 %collective-permute-start.24 = (bf16[40,640]{1,0:T(8,128)(2,1)S(1)}, bf16[40,640]{1,0:T(8,128)(2,1)S(1)}, u32[]{:S(2)}, u32[]{:S(2)}) collective-permute-start(bf16[40,640]{1,0:T(8,128)(2,1)S(1)} %add_convert_fusion.19), channel_id=1, source_target_pairs={{0,8},{1,9},{2,10},{3,11},{4,12},{5,13},{6,14},{7,15},{8,0},{9,1},... | collective-permute-start | bytes 153608 | tf_op jit(solution)/shard_map/ppermute | solution.py:706
  418.6 12.1 %collective-permute-start.51 = (bf16[144,640]{1,0:T(8,128)(2,1)S(1)}, bf16[144,640]{1,0:T(8,128)(2,1)S(1)}, u32[]{:S(2)}, u32[]{:S(2)}) collective-permute-start(bf16[144,640]{1,0:T(8,128)(2,1)S(1)} %constant_dynamic-slice_fusion.1), channel_id=1, source_target_pairs={{0,8},{1,9},{2,10},{3,11},{4,12},{5,13},{6,14},{7,15},{8,0},{9,1},... | collective-permute-start | bytes 552968 | tf_op jit(solution)/shard_map/ppermute | solution.py:706
  420.2 17.2 %collective-permute-start.41 = (bf16[288,640]{1,0:T(8,128)(2,1)S(1)}, bf16[288,640]{1,0:T(8,128)(2,1)S(1)}, u32[]{:S(2)}, u32[]{:S(2)}) collective-permute-start(bf16[288,640]{1,0:T(8,128)(2,1)S(1)} %constant_dynamic-slice_fusion.8), channel_id=1, source_target_pairs={{0,4},{1,5},{2,6},{3,7},{4,0},{5,1},{6,2},{7,3},{8,12},{9,13},{10,... | collective-permute-start | bytes 1105928 | tf_op jit(solution)/shard_map/ppermute | solution.py:706
  422.9 44.9 %collective-permute-start.34 = (bf16[80,640]{1,0:T(8,128)(2,1)S(1)}, bf16[80,640]{1,0:T(8,128)(2,1)S(1)}, u32[]{:S(2)}, u32[]{:S(2)}) collective-permute-start(bf16[80,640]{1,0:T(8,128)(2,1)S(1)} %pad_maximum_fusion.17), channel_id=1, source_target_pairs={{0,4},{1,5},{2,6},{3,7},{4,0},{5,1},{6,2},{7,3},{8,12},{9,13},{10,... | collective-permute-start | bytes 307208 | tf_op jit(solution)/shard_map/ppermute | solution.py:706
  430.7 13.8 %collective-permute-start.52 = (bf16[144,640]{1,0:T(8,128)(2,1)S(1)}, bf16[144,640]{1,0:T(8,128)(2,1)S(1)}, u32[]{:S(2)}, u32[]{:S(2)}) collective-permute-start(bf16[144,640]{1,0:T(8,128)(2,1)S(1)} %add_convert_fusion.14), channel_id=1, source_target_pairs={{0,8},{1,9},{2,10},{3,11},{4,12},{5,13},{6,14},{7,15},{8,0},{9,1},... | collective-permute-start | bytes 552968 | tf_op jit(solution)/shard_map/ppermute | solution.py:706
  437.6 8.9 %collective-permute-start.42 = (bf16[144,640]{1,0:T(8,128)(2,1)S(1)}, bf16[144,640]{1,0:T(8,128)(2,1)S(1)}, u32[]{:S(2)}, u32[]{:S(2)}) collective-permute-start(bf16[144,640]{1,0:T(8,128)(2,1)S(1)} %constant_dynamic-slice_fusion.7), channel_id=1, source_target_pairs={{0,8},{1,9},{2,10},{3,11},{4,12},{5,13},{6,14},{7,15},{8,0},{9,1},... | collective-permute-start | bytes 552968 | tf_op jit(solution)/shard_map/ppermute | solution.py:706
  444.6 14.2 %collective-permute-start.53 = (bf16[288,640]{1,0:T(8,128)(2,1)S(1)}, bf16[288,640]{1,0:T(8,128)(2,1)S(1)}, u32[]{:S(2)}, u32[]{:S(2)}) collective-permute-start(bf16[288,640]{1,0:T(8,128)(2,1)S(1)} %pad_maximum_fusion.12), channel_id=1, source_target_pairs={{0,4},{1,5},{2,6},{3,7},{4,0},{5,1},{6,2},{7,3},{8,12},{9,13},{10,... | collective-permute-start | bytes 1105928 | tf_op jit(solution)/shard_map/ppermute | solution.py:706
  446.5 9.0 %collective-permute-start.43 = (bf16[144,640]{1,0:T(8,128)(2,1)S(1)}, bf16[144,640]{1,0:T(8,128)(2,1)S(1)}, u32[]{:S(2)}, u32[]{:S(2)}) collective-permute-start(bf16[144,640]{1,0:T(8,128)(2,1)S(1)} %add_convert_fusion.15), channel_id=1, source_target_pairs={{0,8},{1,9},{2,10},{3,11},{4,12},{5,13},{6,14},{7,15},{8,0},{9,1},... | collective-permute-start | bytes 552968 | tf_op jit(solution)/shard_map/ppermute | solution.py:706
  455.6 8.6 %collective-permute-start.44 = (bf16[288,640]{1,0:T(8,128)(2,1)S(1)}, bf16[288,640]{1,0:T(8,128)(2,1)S(1)}, u32[]{:S(2)}, u32[]{:S(2)}) collective-permute-start(bf16[288,640]{1,0:T(8,128)(2,1)S(1)} %pad_maximum_fusion.11), channel_id=1, source_target_pairs={{0,4},{1,5},{2,6},{3,7},{4,0},{5,1},{6,2},{7,3},{8,12},{9,13},{10,... | collective-permute-start | bytes 1105928 | tf_op jit(solution)/shard_map/ppermute | solution.py:706
  459.0 20.7 %collective-permute-start.54 = (bf16[576,640]{1,0:T(8,128)(2,1)S(1)}, bf16[576,640]{1,0:T(8,128)(2,1)S(1)}, u32[]{:S(2)}, u32[]{:S(2)}) collective-permute-start(bf16[576,640]{1,0:T(8,128)(2,1)S(1)} %pad_maximum_fusion.8), channel_id=1, source_target_pairs={{0,2},{1,3},{2,0},{3,1},{4,6},{5,7},{6,4},{7,5},{8,10},{9,11},{10,... | collective-permute-start | bytes 2211848 | tf_op jit(solution)/shard_map/ppermute | solution.py:706
  462.3 33.7 %collective-permute-start.25 = (bf16[80,640]{1,0:T(8,128)(2,1)S(1)}, bf16[80,640]{1,0:T(8,128)(2,1)S(1)}, u32[]{:S(2)}, u32[]{:S(2)}) collective-permute-start(bf16[80,640]{1,0:T(8,128)(2,1)S(1)} %pad_maximum_fusion.16), channel_id=1, source_target_pairs={{0,4},{1,5},{2,6},{3,7},{4,0},{5,1},{6,2},{7,3},{8,12},{9,13},{10,... | collective-permute-start | bytes 307208 | tf_op jit(solution)/shard_map/ppermute | solution.py:706
  464.5 31.1 %collective-permute-start.45 = (bf16[576,640]{1,0:T(8,128)(2,1)S(1)}, bf16[576,640]{1,0:T(8,128)(2,1)S(1)}, u32[]{:S(2)}, u32[]{:S(2)}) collective-permute-start(bf16[576,640]{1,0:T(8,128)(2,1)S(1)} %pad_maximum_fusion.7), channel_id=1, source_target_pairs={{0,2},{1,3},{2,0},{3,1},{4,6},{5,7},{6,4},{7,5},{8,10},{9,11},{10,... | collective-permute-start | bytes 2211848 | tf_op jit(solution)/shard_map/ppermute | solution.py:706
  467.9 32.0 %collective-permute-start.35 = (bf16[160,640]{1,0:T(8,128)(2,1)S(1)}, bf16[160,640]{1,0:T(8,128)(2,1)S(1)}, u32[]{:S(2)}, u32[]{:S(2)}) collective-permute-start(bf16[160,640]{1,0:T(8,128)(2,1)S(1)} %pad_maximum_fusion.14), channel_id=1, source_target_pairs={{0,2},{1,3},{2,0},{3,1},{4,6},{5,7},{6,4},{7,5},{8,10},{9,11},{10,... | collective-permute-start | bytes 614408 | tf_op jit(solution)/shard_map/ppermute | solution.py:706
  480.1 24.2 %collective-permute-start.55 = (bf16[1152,640]{1,0:T(8,128)(2,1)S(1)}, bf16[1152,640]{1,0:T(8,128)(2,1)S(1)}, u32[]{:S(2)}, u32[]{:S(2)}) collective-permute-start(bf16[1152,640]{1,0:T(8,128)(2,1)S(1)} %pad_maximum_fusion.4), channel_id=1, source_target_pairs={{0,1},{1,0},{2,3},{3,2},{4,5},{5,4},{6,7},{7,6},{8,9},{9,8},{10,11... | collective-permute-start | bytes 4423688 | tf_op jit(solution)/shard_map/ppermute | solution.py:706
  495.9 19.4 %collective-permute-start.46 = (bf16[1152,640]{1,0:T(8,128)(2,1)S(1)}, bf16[1152,640]{1,0:T(8,128)(2,1)S(1)}, u32[]{:S(2)}, u32[]{:S(2)}) collective-permute-start(bf16[1152,640]{1,0:T(8,128)(2,1)S(1)} %pad_maximum_fusion.3), channel_id=1, source_target_pairs={{0,1},{1,0},{2,3},{3,2},{4,5},{5,4},{6,7},{7,6},{8,9},{9,8},{10,11... | collective-permute-start | bytes 4423688 | tf_op jit(solution)/shard_map/ppermute | solution.py:706
  496.1 8.2 %collective-permute-start.26 = (bf16[160,640]{1,0:T(8,128)(2,1)S(1)}, bf16[160,640]{1,0:T(8,128)(2,1)S(1)}, u32[]{:S(2)}, u32[]{:S(2)}) collective-permute-start(bf16[160,640]{1,0:T(8,128)(2,1)S(1)} %pad_maximum_fusion.13), channel_id=1, source_target_pairs={{0,2},{1,3},{2,0},{3,1},{4,6},{5,7},{6,4},{7,5},{8,10},{9,11},{10,... | collective-permute-start | bytes 614408 | tf_op jit(solution)/shard_map/ppermute | solution.py:706
  500.0 24.0 %collective-permute-start.36 = (bf16[320,640]{1,0:T(8,128)(2,1)S(1)}, bf16[320,640]{1,0:T(8,128)(2,1)S(1)}, u32[]{:S(2)}, u32[]{:S(2)}) collective-permute-start(bf16[320,640]{1,0:T(8,128)(2,1)S(1)} %pad_maximum_fusion.10), channel_id=1, source_target_pairs={{0,1},{1,0},{2,3},{3,2},{4,5},{5,4},{6,7},{7,6},{8,9},{9,8},{10,11... | collective-permute-start | bytes 1228808 | tf_op jit(solution)/shard_map/ppermute | solution.py:706
  521.5 15.1 %collective-permute-start.56 = (bf16[2304,640]{1,0:T(8,128)(2,1)S(1)}, bf16[2304,640]{1,0:T(8,128)(2,1)S(1)}, u32[]{:S(2)}, u32[]{:S(2)}) collective-permute-start(bf16[2304,640]{1,0:T(8,128)(2,1)S(1)} %broadcast_select_fusion.2), channel_id=1, source_target_pairs={{0,16},{16,0},{1,17},{17,1},{2,18},{18,2},{3,19},{19,3},{4,20},{20... | collective-permute-start | bytes 8847368 | tf_op jit(solution)/shard_map/ppermute | solution.py:524
  521.7 8.0 %collective-permute-start.27 = (bf16[320,640]{1,0:T(8,128)(2,1)S(1)}, bf16[320,640]{1,0:T(8,128)(2,1)S(1)}, u32[]{:S(2)}, u32[]{:S(2)}) collective-permute-start(bf16[320,640]{1,0:T(8,128)(2,1)S(1)} %pad_maximum_fusion.9), channel_id=1, source_target_pairs={{0,1},{1,0},{2,3},{3,2},{4,5},{5,4},{6,7},{7,6},{8,9},{9,8},{10,11... | collective-permute-start | bytes 1228808 | tf_op jit(solution)/shard_map/ppermute | solution.py:706
  (31 other events, 361.4 us)

commit v2 on v1

v2 whole, which is shorter than its diff:
```python
import functools

import jax
import jax.numpy as jnp
from jax import lax
from jax.experimental import pallas as pl
from jax.experimental.pallas import tpu as pltpu
from jax.sharding import PartitionSpec as P

TAPS = 5
MID = TAPS // 2
DIL0 = 2
DIL1 = 64
EPS = 1e-05
SCALE = 2
RIM0 = 8
RIM1 = MID * DIL1
F32 = jnp.float32
BF16 = jnp.bfloat16
LANES = 128
LIVE1 = 8
VMEM_LIMIT = 56 * 1024 * 1024
ANY = pl.BlockSpec(memory_space=pl.ANY)


def dot_nn(a, b):
    return lax.dot_general(a, b, (((1,), (0,)), ((), ())), preferred_element_type=F32)


def dot_nt(a, b):
    return lax.dot_general(a, b, (((1,), (1,)), ((), ())), preferred_element_type=F32)


def dot_tn(a, b):
    return lax.dot_general(a, b, (((0,), (0,)), ((), ())), preferred_element_type=F32)


def gelu_parts(y):
    phi_big = lax.erf(y * 0.7071067811865476) * 0.5 + 0.5
    e = jnp.exp(y * y * -0.5)
    return y * phi_big, phi_big + y * e * 0.3989422804014327


def normed_of(u):
    mean = jnp.mean(u, axis=-1, keepdims=True)
    center = u - mean
    scale = lax.rsqrt(jnp.mean(center * center, axis=-1, keepdims=True) + EPS)
    return center * scale, mean, scale


def norm_back(err, slope, normed, scale, gain):
    q = err * slope
    p = q * gain
    m1 = jnp.mean(p, axis=-1, keepdims=True)
    m2 = jnp.mean(p * normed, axis=-1, keepdims=True)
    return (p - m1 - normed * m2) * scale, q * normed, q


def fold8(v):
    return sum(v[k : k + 8] for k in range(0, v.shape[0], 8))


def chunks(rows, size, body):
    steps = rows // size
    lax.fori_loop(0, steps, lambda i, c: (body(pl.multiple_of(i * size, size)), c)[1], 0, unroll=min(8, steps))


def summed_chunks(rows, size, width, terms, body):
    steps = rows // size

    def one(i, held):
        return tuple(h + fold8(v) for h, v in zip(held, body(pl.multiple_of(i * size, size))))

    return lax.fori_loop(0, steps, one, (jnp.zeros((8, width), F32),) * terms, unroll=min(8, steps))


def pick_copy(cond, one, other, dst, sem):
    @pl.when(cond)
    def _():
        pltpu.make_async_copy(one, dst, sem).start()

    @pl.when(jnp.logical_not(cond))
    def _():
        pltpu.make_async_copy(other, dst, sem).start()


def pick_wait(one, dst, sem):
    pltpu.make_async_copy(one, dst, sem).wait()


def conv_parts(one, dst):
    inner = one.shape[1]
    return [(j, dst.at[:, (TAPS - 1 - j) * inner : (TAPS - j) * inner]) for j in range(TAPS)]


def columns(row):
    return jnp.broadcast_to(row, (LANES, row.shape[1])).T


class Vectors:
    def __init__(self, ref, width, inner):
        at = 0
        for name in ("fg", "fs", "wb"):
            setattr(self, name, ref[:, at : at + width])
            at += width
        for name in ("nb", "mg", "ms", "cb", "lg", "ls"):
            setattr(self, name, ref[:, at : at + inner])
            at += inner


def f0_kernel(c_ref, x_ref, xh_ref, rb_ref, ra_ref, v0_ref, v1_ref, nwo, nwx, cwo, cwx, wwo, wwx,
              mk, act0, slx0, mux0, rsx0, nn0, sln0, rsn0, st0, nc0, slc0, rsc0, oa0, out0,
              act1, slx1, mux1, rsx1, nn1, sln1, rsn1, mid1,
              nw0, cw0, ww0, nw1, act_s, n32, mid32, c32, r32, sems):
    low = c_ref[0] == 0
    first = pl.program_id(0) == 0
    rows, width = x_ref.shape[1:]
    inner = n32.shape[1]
    v0, v1 = Vectors(v0_ref, width, inner), Vectors(v1_ref, width, inner)

    @pl.when(first)
    def _():
        pick_copy(low, nwo, nwx, nw0, sems.at[0])
        pick_copy(low, cwo, cwx, cw0, sems.at[1])
        pick_copy(low, wwo, wwx, ww0, sems.at[2])
        pick_copy(low, nwx, nwo, nw1, sems.at[3])

    lane = lax.broadcasted_iota(jnp.int32, (rows, LANES), 1)
    offset = jnp.where(lane < LIVE1, (lane - MID) * DIL0, (lane - LIVE1 - MID) * DIL1).astype(F32)
    before, after = columns(rb_ref[0].astype(F32)), columns(ra_ref[0].astype(F32))
    mk[0] = jnp.where((offset >= -before) & (offset <= after), 1.0, 0.0)

    def first_norm(u, v):
        normed, mean, scale = normed_of(u)
        act, slope = gelu_parts(normed * v.fg + v.fs)
        return act.astype(BF16), slope.astype(BF16), mean, scale

    def stage1(r):
        s = pl.ds(r, 16)
        act, slope, mean, scale = first_norm(x_ref[0, s, :].astype(F32), v0)
        act_s[s, :] = act
        act0[0, s, :] = act
        slx0[0, s, :] = slope
        mux0[0, s, :] = mean
        rsx0[0, s, :] = scale

    chunks(rows, 16, stage1)
    act, _, _, _ = first_norm(xh_ref[0].astype(F32), v0)
    act_s[rows : rows + 2 * RIM0, :] = act

    @pl.when(first)
    def _():
        pick_wait(nwo, nw0, sems.at[0])

    n32[...] = dot_nn(act_s[...], nw0[...])

    def mid_norm(u, v):
        normed, _, scale = normed_of(u + v.nb)
        act, slope = gelu_parts(normed * v.mg + v.ms)
        return act.astype(BF16), slope.astype(BF16), normed.astype(BF16), scale

    def stage2(r):
        s = pl.ds(r, 32)
        mid, slope, normed, scale = mid_norm(n32[s, :], v0)
        mid32[pl.ds(r + RIM0, 32), :] = mid.astype(F32)
        nn0[0, s, :] = normed
        sln0[0, s, :] = slope
        rsn0[0, s, :] = scale

    chunks(rows, 32, stage2)
    rim = mid_norm(n32[rows : rows + 2 * RIM0, :], v0)[0].astype(F32)
    mid32[0:RIM0, :] = rim[:RIM0]
    mid32[rows + RIM0 : rows + 2 * RIM0, :] = rim[RIM0:]
    near_taps(rows, inner, mid32, mk, st0.at[0])

    @pl.when(first)
    def _():
        pick_wait(cwo, cw0, sems.at[1])

    c32[...] = dot_nn(st0[0], cw0[...].reshape(TAPS * inner, inner))

    def stage4(r):
        s = pl.ds(r, 32)
        normed, _, scale = normed_of(c32[s, :] + v0.cb)
        act, slope = gelu_parts(normed * v0.lg + v0.ls)
        oa0[0, s, :] = act.astype(BF16)
        nc0[0, s, :] = normed.astype(BF16)
        slc0[0, s, :] = slope.astype(BF16)
        rsc0[0, s, :] = scale

    chunks(rows, 32, stage4)

    @pl.when(first)
    def _():
        pick_wait(wwo, ww0, sems.at[2])
        pick_wait(nwx, nw1, sems.at[3])

    r32[...] = dot_nn(oa0[0], ww0[...])

    def stage5(r):
        s = pl.ds(r, 16)
        res = (x_ref[0, s, :].astype(F32) + (r32[s, :] + v0.wb)).astype(BF16)
        out0[0, s, :] = res
        act, slope, mean, scale = first_norm(res.astype(F32), v1)
        act1[0, s, :] = act
        slx1[0, s, :] = slope
        mux1[0, s, :] = mean
        rsx1[0, s, :] = scale

    chunks(rows, 16, stage5)
    n32[0:rows, :] = dot_nn(act1[0], nw1[...])

    def stage6(r):
        s = pl.ds(r, 32)
        mid, slope, normed, scale = mid_norm(n32[s, :], v1)
        mid1[0, s, :] = mid
        nn1[0, s, :] = normed
        sln1[0, s, :] = slope
        rsn1[0, s, :] = scale

    chunks(rows, 32, stage6)


def near_taps(rows, inner, ext32, mk, dst):
    def stack(r):
        s = pl.ds(r, 16)
        window = ext32[pl.ds(r, 32), :]
        for j in range(TAPS):
            at = RIM0 + (j - MID) * DIL0
            live = mk[0, s, j : j + 1]
            dst[s, j * inner : (j + 1) * inner] = (window[at : at + 16] * live).astype(BF16)

    chunks(rows, 16, stack)


def far_taps(rows, inner, own_ref, up_ref, dn_ref, mk, dst):
    pieces = rows // DIL1
    for k in range(pieces):
        for j in range(TAPS):
            at = k + j - MID
            live = mk[0, k * DIL1 : (k + 1) * DIL1, LIVE1 + j : LIVE1 + j + 1]
            if at < 0:
                part = up_ref[0, (at + MID) * DIL1 : (at + MID + 1) * DIL1, :]
            elif at >= pieces:
                part = dn_ref[0, (at - pieces) * DIL1 : (at - pieces + 1) * DIL1, :]
            else:
                part = own_ref[0, at * DIL1 : (at + 1) * DIL1, :]
            dst[k * DIL1 : (k + 1) * DIL1, j * inner : (j + 1) * inner] = (part.astype(F32) * live).astype(BF16)


def f1_kernel(c_ref, mid_ref, up_ref, dn_ref, mk, v1_ref, cot_ref, cwo, cwx, wwo, wwx,
              st1, oa1, cg1, vec, cw1, ww1, c32, e32, acc, sems):
    low = c_ref[0] == 0
    step = pl.program_id(0)
    rows, width = cot_ref.shape[1:]
    inner = c32.shape[1]
    v1 = Vectors(v1_ref, width, inner)

    @pl.when(step == 0)
    def _():
        pick_copy(low, wwx, wwo, ww1, sems.at[1])
        pick_copy(low, cwx, cwo, cw1, sems.at[0])
        acc[...] = jnp.zeros_like(acc)

    far_taps(rows, inner, mid_ref, up_ref, dn_ref, mk, st1.at[0])
    (cot_sum,) = summed_chunks(rows, 16, width, 1, lambda r: (cot_ref[0, pl.ds(r, 16), :].astype(F32),))
    acc[3] += cot_sum

    @pl.when(step == 0)
    def _():
        pick_wait(wwx, ww1, sems.at[1])

    e32[...] = dot_nt(cot_ref[0], ww1[...])

    @pl.when(step == 0)
    def _():
        pick_wait(cwx, cw1, sems.at[0])

    c32[...] = dot_nn(st1[0], cw1[...].reshape(TAPS * inner, inner))

    def stage(r):
        s = pl.ds(r, 16)
        normed, _, scale = normed_of(c32[s, :] + v1.cb)
        act, slope = gelu_parts(normed * v1.lg + v1.ls)
        oa1[0, s, :] = act.astype(BF16)
        du, dgain, dshift = norm_back(e32[s, :], slope, normed, scale, v1.lg)
        du = du.astype(BF16)
        cg1[0, s, :] = du
        return dgain, dshift, du.astype(F32)

    sums = summed_chunks(rows, 16, inner, 3, stage)
    for k in range(3):
        acc[k, :, :inner] += sums[k]

    @pl.when(step == pl.num_programs(0) - 1)
    def _():
        vec[...] = jnp.sum(acc[...], axis=1)


def o1_kernel(c_ref, out0_ref, oa_ref, rt_ref, lm_ref, v1_ref, head_ref, wwo, wwx,
              out1, tot, ww1, r32, lg, acc, sems, *, vocab):
    low = c_ref[0] == 0
    step = pl.program_id(0)
    rows, width = out0_ref.shape[1:]
    v1 = Vectors(v1_ref, width, oa_ref.shape[2])

    @pl.when(step == 0)
    def _():
        pick_copy(low, wwx, wwo, ww1, sems.at[0])
        acc[...] = jnp.zeros_like(acc)
        pick_wait(wwx, ww1, sems.at[0])

    r32[...] = dot_nn(oa_ref[0], ww1[...])

    def stage(r):
        s = pl.ds(r, 16)
        out1[0, s, :] = (out0_ref[0, s, :].astype(F32) + (r32[s, :] + v1.wb)).astype(BF16)

    chunks(rows, 16, stage)
    lg[...] = dot_nn(out1[0], head_ref[...])
    lane = lax.broadcasted_iota(jnp.int32, (rows, LANES), 1)
    logits = jnp.where(lane < vocab, lg[...], -1e30)
    top = jnp.max(logits, axis=-1, keepdims=True)
    log_total = top + jnp.log(jnp.sum(jnp.exp(logits - top), axis=-1, keepdims=True))
    kind, weight = columns(rt_ref[0].astype(F32)), columns(lm_ref[0].astype(F32))
    onehot = jnp.where(lane == kind.astype(jnp.int32), weight, 0.0)
    acc[0] += fold8(onehot)
    acc[1] += fold8(onehot * (log_total - logits))

    @pl.when(step == pl.num_programs(0) - 1)
    def _():
        tot[...] = jnp.sum(acc[...], axis=1)


def middle_back(rows, inner, m32, sln, nn, rsn, gain, ng, acc):
    def stage(r):
        s = pl.ds(r, 16)
        du, dgain, dshift = norm_back(m32[s, :], sln[0, s, :].astype(F32), nn[0, s, :].astype(F32), rsn[0, s, :], gain)
        du = du.astype(BF16)
        ng[0, s, :] = du
        return dgain, dshift, du.astype(F32)

    sums = summed_chunks(rows, 16, inner, 3, stage)
    for k in range(3):
        acc[k] += sums[k]


def mid_kernel(c_ref, cg_ref, *refs, far, block):
    if far:
        up_ref, dn_ref, mk, v_ref, sln, nn, rsn, cwo, cwx, ng, vec, cw2, stg, m32, acc, sems = refs
    else:
        rim_ref, mk, v_ref, sln, nn, rsn, cwo, cwx, ng, vec, cw2, ext, stg, m32, acc, sems = refs
    low = c_ref[0] == block
    step = pl.program_id(0)
    rows, inner = cg_ref.shape[1:]
    parts = conv_parts(cwo, cw2)

    @pl.when(step == 0)
    def _():
        for j, dst in parts:
            pick_copy(low, cwo.at[j], cwx.at[j], dst, sems.at[j])
        acc[...] = jnp.zeros_like(acc)

    if far:
        far_taps(rows, inner, cg_ref, up_ref, dn_ref, mk, stg)
    else:
        rim = rim_ref[0].astype(F32)
        ext[0:RIM0, :] = rim[:RIM0]
        ext[rows + RIM0 : rows + 2 * RIM0, :] = rim[RIM0:]

        def widen(r):
            ext[pl.ds(r + RIM0, 16), :] = cg_ref[0, pl.ds(r, 16), :].astype(F32)

        chunks(rows, 16, widen)
        near_taps(rows, inner, ext, mk, stg)

    @pl.when(step == 0)
    def _():
        for j, dst in parts:
            pick_wait(cwo.at[j], dst, sems.at[j])

    m32[...] = dot_nt(stg[...], cw2[...])
    at = v_ref.shape[1] - 5 * inner
    middle_back(rows, inner, m32, sln, nn, rsn, v_ref[:, at : at + inner], ng, acc)

    @pl.when(step == pl.num_programs(0) - 1)
    def _():
        vec[...] = jnp.sum(acc[...], axis=1)


def first_kernel(c_ref, ng_ref, v_ref, grad, slx, src, mux, rsx, nwo, nwx, ig, vec, nw, a32, acc, sems, *, block):
    low = c_ref[0] == block
    step = pl.program_id(0)
    rows, width = grad.shape[1:]
    gain = v_ref[:, :width]

    @pl.when(step == 0)
    def _():
        pick_copy(low, nwo, nwx, nw, sems.at[0])
        acc[...] = jnp.zeros_like(acc)
        pick_wait(nwo, nw, sems.at[0])

    a32[...] = dot_nt(ng_ref[0], nw[...])

    def stage(r):
        s = pl.ds(r, 16)
        scale = rsx[0, s, :]
        normed = (src[0, s, :].astype(F32) - mux[0, s, :]) * scale
        du, dgain, dshift = norm_back(a32[s, :], slx[0, s, :].astype(F32), normed, scale, gain)
        ig[0, s, :] = (grad[0, s, :].astype(F32) + du).astype(BF16)
        return dgain, dshift

    sums = summed_chunks(rows, 16, width, 2, stage)
    for k in range(2):
        acc[k] += sums[k]

    @pl.when(step == pl.num_programs(0) - 1)
    def _():
        vec[...] = jnp.sum(acc[...], axis=1)


def last_kernel(c_ref, ig_ref, v_ref, slc, nc, rsc, wwo, wwx, cg, vec, ww, e32, acc, sems):
    low = c_ref[0] == 0
    step = pl.program_id(0)
    rows, width = ig_ref.shape[1:]
    inner = e32.shape[1]
    gain = Vectors(v_ref, width, inner).lg

    @pl.when(step == 0)
    def _():
        pick_copy(low, wwo, wwx, ww, sems.at[0])
        acc[...] = jnp.zeros_like(acc)

    (ig_sum,) = summed_chunks(rows, 16, width, 1, lambda r: (ig_ref[0, pl.ds(r, 16), :].astype(F32),))
    acc[3] += ig_sum

    @pl.when(step == 0)
    def _():
        pick_wait(wwo, ww, sems.at[0])

    e32[...] = dot_nt(ig_ref[0], ww[...])

    def stage(r):
        s = pl.ds(r, 16)
        du, dgain, dshift = norm_back(e32[s, :], slc[0, s, :].astype(F32), nc[0, s, :].astype(F32), rsc[0, s, :], gain)
        du = du.astype(BF16)
        cg[0, s, :] = du
        return dgain, dshift, du.astype(F32)

    sums = summed_chunks(rows, 16, inner, 3, stage)
    for k in range(3):
        acc[k, :, :inner] += sums[k]

    @pl.when(step == pl.num_programs(0) - 1)
    def _():
        vec[...] = jnp.sum(acc[...], axis=1)


def weight_terms(c_arr, pairs, own, tile, unit):
    specs, args, spans = [], [], []
    at = 0

    def index(v, pick):
        if v.shape[0] == own:
            return lambda s, c: (0, 0, pick(s))
        return lambda s, c: (c[0], 0, pick(s))

    for a, g in pairs:
        na, ng = a.shape[2] // tile, g.shape[2] // tile
        local = functools.partial(lambda s, lo, n: jnp.clip(s - lo, 0, n - 1), lo=at, n=na * ng)
        block = (own, a.shape[1], tile)
        specs.append(pl.BlockSpec(block, index(a, lambda s, local=local, na=na: local(s) % na)))
        specs.append(pl.BlockSpec(block, index(g, lambda s, local=local, na=na: local(s) // na)))
        args += [a, g]
        spans.append((at, at + na * ng))
        at += na * ng
    half = tile // 2
    depth = own * args[0].shape[1]
    out_rows = -(-at * half // unit) * unit

    def kernel(c_ref, *refs):
        keep, send, whole = refs[-3:]
        s = pl.program_id(0)
        for k, (lo, hi) in enumerate(spans):

            @pl.when((s >= lo) & (s < hi))
            def _(k=k):
                a, g = (refs[2 * k + i][...].reshape(depth, tile) for i in range(2))
                whole[...] = dot_tn(a, g).astype(BF16)

        stay = pl.multiple_of(c_ref[0] * half, half)
        keep[...] = whole[pl.ds(stay, half), :]
        send[...] = whole[pl.ds(half - stay, half), :]

    return pl.pallas_call(
        kernel,
        grid_spec=pltpu.PrefetchScalarGridSpec(
            num_scalar_prefetch=1,
            grid=(at,),
            in_specs=specs,
            out_specs=[pl.BlockSpec((half, tile), lambda s, c: (s, 0))] * 2,
            scratch_shapes=[pltpu.VMEM((tile, tile), BF16)],
        ),
        out_shape=[jax.ShapeDtypeStruct((out_rows, tile), BF16)] * 2,
        compiler_params=pltpu.CompilerParams(vmem_limit_bytes=VMEM_LIMIT),
        cost_estimate=pl.CostEstimate(
            flops=at * 2 * tile * tile * depth // SCALE, bytes_accessed=4 * out_rows * tile // SCALE, transcendentals=0
        ),
    )(c_arr, *args)


def unpack_kernel(c_ref, row_ref, sig_ref, *refs, groups, count, cols):
    n = sum(len(g[2]) for g in groups)
    ins, (conv, widen, narrow), (held, sems) = refs[:n], refs[n : n + 3], refs[n + 3 :]
    s = pl.program_id(0)
    half = conv.shape[1] // 2

    def fetch(k):
        _, base, numbers = groups[k]
        arrays = [ins[i] for i in numbers]
        rows = sum(a.shape[0] for a in arrays) // 2
        shard = rows // count
        first = 0
        for a in arrays:
            mine = 0 if first < count else 1
            for p in range(a.shape[0] // shard):
                h = c_ref[0] if mine == 0 else 1 - c_ref[0]
                to = pl.multiple_of(((first + p) % count ^ sig_ref[mine]) * shard + base, 16)
                pltpu.make_async_copy(a.at[pl.ds(p * shard, shard)], held.at[h, pl.ds(to, shard)], sems.at[k]).start()
            first += a.shape[0] // shard

    def landed(k):
        _, base, numbers = groups[k]
        rows = sum(ins[i].shape[0] for i in numbers) // 2
        part = held.at[:, base : base + rows]
        pltpu.make_async_copy(part, part, sems.at[k]).wait()

    @pl.when(s == 0)
    def _():
        for step in (fetch, landed):
            for k, (core, _, _) in enumerate(groups):
                if core is None:
                    step(k)
                else:
                    pl.when(c_ref[0] == core)(functools.partial(step, k))

    def rows_of(step):
        at = pl.multiple_of(row_ref[step], half)
        return held[0, pl.ds(at, half), :].astype(F32), held[1, pl.ds(at, half), :].astype(F32)

    @pl.when(s < TAPS)
    def _():
        conv[0, :half, :], conv[0, half:, :] = rows_of(s)

    @pl.when((s >= TAPS) & (s < TAPS + cols))
    def _():
        widen[:half, :], widen[half:, :] = rows_of(s)

    @pl.when(s >= TAPS + cols)
    def _():
        narrow[:half, :], narrow[half:, :] = rows_of(s)


def add_low(one, other):
    return (one.astype(F32) + other.astype(F32)).astype(BF16)


def part(v, at, rows):
    return lax.dynamic_slice_in_dim(v, at * rows, rows, 0)


def tie(value, *after):
    return lax.optimization_barrier((value, *after))[0]


def dim_orders(count):
    rest = list(range(2, count.bit_length() - 1))
    return [[0, *rest[:1], 1, *rest[1:]], [1, 0, *rest]]


class Chain:
    def __init__(self, keep, send, steps):
        self.keep, self.send, self.steps = keep, send, steps
        self.at = -1
        self.pieces = None

    def ready(self, *after):
        bits = len(self.steps)
        if after:
            self.come = tie(self.come, *after)
            if self.pieces is not None:
                self.pieces = (self.pieces[0], self.come)
        if 0 <= self.at < bits:
            bit = self.steps[self.at][1]
            rows = self.keep.shape[0] // 2
            self.send = add_low(part(self.keep, 1 - bit, rows), part(self.come, 1 - bit, rows))
            self.keep = add_low(part(self.keep, bit, rows), part(self.come, bit, rows))
        elif self.at == bits:
            self.send = add_low(self.keep, self.come)
        elif self.at > bits:
            self.send = jnp.concatenate(self.pieces, axis=0)
        return self.send

    def go(self, *after):
        send = tie(self.send, *after) if after else self.send
        bits = len(self.steps)
        if self.at < 0:
            self.come = swapped(send)
        elif self.at < bits:
            self.come = hop(send, self.steps[self.at][0])
        else:
            self.come = hop(send, self.steps[2 * bits - 1 - self.at][0])
            self.pieces = (send, self.come)
        self.at += 1
        return self.come

    def step(self, *after):
        self.ready()
        return self.go(*after)

    def done(self):
        return self.at == 2 * len(self.steps)

    def finish(self):
        while not self.done():
            self.step()
        return [*self.pieces, *(swapped(p) for p in self.pieces)]


def swapped(v):
    return lax.ppermute(v, "section", [(0, 1), (1, 0)])


def hop(v, pairs):
    return lax.ppermute(v, ("section", "dp"), pairs)


def body(block_input, output_cotangent, residues_before, residues_after, residue_types, loss_mask,
         first_gain, first_shift, narrow_weight, narrow_bias, middle_gain, middle_shift,
         conv_weight, conv_bias, last_gain, last_shift, widen_weight, widen_bias, head_weight):
    sec = lax.axis_index("section")
    at = lax.axis_index("dp")
    count = lax.axis_size("dp")
    low = sec == 0
    micro, rows, width = block_input.shape
    own = micro // 2
    inner = narrow_weight.shape[2]
    vocab = head_weight.shape[1]
    ahead = [(i, (i + 1) % count) for i in range(count)]
    behind = [((i + 1) % count, i) for i in range(count)]
    c_arr = sec.astype(jnp.int32).reshape(1)

    nwo, cwo, wwo = narrow_weight[0], conv_weight[0], widen_weight[0]
    nwx, cwx, wwx = swapped(nwo), swapped(cwo), swapped(wwo)
    packed = jnp.concatenate(
        (first_gain, first_shift, widen_bias, narrow_bias, middle_gain, middle_shift, conv_bias, last_gain, last_shift), axis=1
    )
    packed_x = swapped(packed)
    v0 = jnp.where(low, packed, packed_x)
    v1 = jnp.where(low, packed_x, packed)

    x_own = lax.dynamic_slice_in_dim(block_input, sec * own, own, 0)
    xh = jnp.concatenate(
        [lax.ppermute(x_own[:, -RIM0:], "dp", ahead), lax.ppermute(x_own[:, :RIM0], "dp", behind)], axis=1
    )
    before, after, kinds, scored = (v[:, None, :] for v in (residues_before, residues_after, residue_types, loss_mask))

    def mine(n, w):
        return pl.BlockSpec((1, n, w), lambda i, c: (c[0] * own + i, 0, 0))

    def each(n, w):
        return pl.BlockSpec((1, n, w), lambda i, c: (i, 0, 0))

    def whole(*shape):
        return pl.BlockSpec(shape, lambda i, c: (0,) * len(shape))

    def call(kernel, c, ins, in_specs, outs, scratch, flops, nbytes, trans=0):
        return pl.pallas_call(
            kernel,
            grid_spec=pltpu.PrefetchScalarGridSpec(
                num_scalar_prefetch=1,
                grid=(own,),
                in_specs=in_specs,
                out_specs=[o[1] for o in outs],
                scratch_shapes=scratch,
            ),
            out_shape=[o[0] for o in outs],
            compiler_params=pltpu.CompilerParams(vmem_limit_bytes=VMEM_LIMIT),
            cost_estimate=pl.CostEstimate(flops=int(flops / SCALE), bytes_accessed=int(nbytes / SCALE), transcendentals=0),
        )(c, *ins)

    def o_each(w, dtype=BF16):
        return (jax.ShapeDtypeStruct((own, rows, w), dtype), each(rows, w))

    def o_vec(n, w):
        return (jax.ShapeDtypeStruct((n, w), F32), whole(n, w))

    dma = pltpu.SemaphoreType.DMA
    vspec = whole(1, packed.shape[1])
    mm = 2 * own * rows * width * inner
    wide, thin, one, masks, taps = o_each(width), o_each(inner), o_each(1, F32), o_each(LANES, F32), o_each(TAPS * inner)
    e_wide, e_thin, e_one, e_masks = wide[1], thin[1], one[1], masks[1]
    id_spec = mine(1, rows)
    (mk, act0, slx0, mux0, rsx0, nn0, sln0, rsn0, st0, nc0, slc0, rsc0, oa0, out0,
     act1, slx1, mux1, rsx1, nn1, sln1, rsn1, mid1) = call(
        f0_kernel,
        c_arr,
        (block_input, xh, before, after, v0, v1, nwo, nwx, cwo, cwx, wwo, wwx),
        [mine(rows, width), each(2 * RIM0, width), id_spec, id_spec, vspec, vspec] + [ANY] * 6,
        [masks, wide, wide, one, one, thin, thin, one, taps, thin, thin, one, thin, wide, wide, wide, one, one, thin, thin, one, thin],
        [
            pltpu.VMEM((width, inner), BF16),
            pltpu.VMEM((TAPS, inner, inner), BF16),
            pltpu.VMEM((inner, width), BF16),
            pltpu.VMEM((width, inner), BF16),
            pltpu.VMEM((rows + 2 * RIM0, width), BF16),
            pltpu.VMEM((rows + 2 * RIM0, inner), F32),
            pltpu.VMEM((rows + 2 * RIM0, inner), F32),
            pltpu.VMEM((rows, inner), F32),
            pltpu.VMEM((rows, width), F32),
            dma((4,)),
        ],
        5.5 * mm, 40_000_000, own * rows * 8 * width,
    )

    up1 = lax.ppermute(mid1[:, -RIM1:], "dp", ahead)
    dn1 = lax.ppermute(mid1[:, :RIM1], "dp", behind)
    st1, oa1, cg1, vec1 = call(
        f1_kernel,
        c_arr,
        (mid1, up1, dn1, mk, v1, output_cotangent, cwo, cwx, wwo, wwx),
        [e_thin, each(RIM1, inner), each(RIM1, inner), e_masks, vspec, mine(rows, width)] + [ANY] * 4,
        [taps, thin, thin, o_vec(4, width)],
        [
            pltpu.VMEM((TAPS, inner, inner), BF16),
            pltpu.VMEM((inner, width), BF16),
            pltpu.VMEM((rows, inner), F32),
            pltpu.VMEM((rows, inner), F32),
            pltpu.VMEM((4, 8, width), F32),
            dma((2,)),
        ],
        3.5 * mm, 20_000_000, own * rows * 2 * inner,
    )

    rim_up, rim_dn = cg1[:, -RIM1:], cg1[:, :RIM1]
    upg = lax.ppermute(rim_up, "dp", ahead)
    dng = lax.ppermute(rim_dn, "dp", behind)

    orders = dim_orders(count)
    steps, signs = [], [0, 0]
    bits = len(orders[0])
    for k in range(bits):
        pairs = [(s * count + d, s * count + (d ^ (1 << orders[s][k]))) for s in range(2) for d in range(count)]
        place = [(at >> orders[s][k]) & 1 for s in range(2)]
        steps.append((pairs, jnp.where(low, place[0], place[1])))
        signs = [g + (p << (bits - 1 - k)) for g, p in zip(signs, place)]
    unit = 16 * count
    terms = functools.partial(weight_terms, own=own, tile=inner, unit=unit)

    g1 = Chain(*terms(tie(c_arr, rim_up, rim_dn), [(oa1, output_cotangent), (st1, cg1)]), steps)
    g1_come = g1.step()
    head = jnp.pad(head_weight, ((0, 0), (0, LANES - vocab)))
    out1, tot = call(
        functools.partial(o1_kernel, vocab=vocab),
        tie(c_arr, g1.keep),
        (out0, oa1, kinds, scored, v1, head, wwo, wwx),
        [e_wide, e_thin, id_spec, id_spec, vspec, whole(width, LANES), ANY, ANY],
        [wide, o_vec(2, LANES)],
        [
            pltpu.VMEM((inner, width), BF16),
            pltpu.VMEM((rows, width), F32),
            pltpu.VMEM((rows, LANES), F32),
            pltpu.VMEM((2, 8, LANES), F32),
            dma((1,)),
        ],
        1.2 * mm, 8_000_000,
    )

    def mid_scratch(ext):
        return [
            pltpu.VMEM((inner, TAPS * inner), BF16),
            *ext,
            pltpu.VMEM((rows, TAPS * inner), BF16),
            pltpu.VMEM((rows, inner), F32),
            pltpu.VMEM((3, 8, inner), F32),
            dma((TAPS,)),
        ]

    def first(c, block, ng, v, grad, grad_spec, slx, src, src_spec, mux, rsx):
        return call(
            functools.partial(first_kernel, block=block),
            c,
            (ng, v, grad, slx, src, mux, rsx, nwo, nwx),
            [e_thin, vspec, grad_spec, e_wide, src_spec, e_one, e_one, ANY, ANY],
            [wide, o_vec(2, width)],
            [pltpu.VMEM((width, inner), BF16), pltpu.VMEM((rows, width), F32), pltpu.VMEM((2, 8, width), F32), dma((1,))],
            1.3 * mm, 10_000_000,
        )

    ng1, vecm1 = call(
        functools.partial(mid_kernel, far=True, block=1),
        tie(c_arr, tot, g1.ready()),
        (cg1, upg, dng, mk, v1, sln1, nn1, rsn1, cwo, cwx),
        [e_thin, each(RIM1, inner), each(RIM1, inner), e_masks, vspec, e_thin, e_thin, e_one, ANY, ANY],
        [thin, o_vec(3, inner)],
        mid_scratch([]),
        2.6 * mm, 10_000_000,
    )
    r1 = g1.go(upg, dng, tot)
    ig1, vecf1 = first(c_arr, 1, ng1, v1, output_cotangent, mine(rows, width), slx1, out0, e_wide, mux1, rsx1)
    cg0, vecl0 = call(
        last_kernel,
        tie(c_arr, g1.ready(ig1)),
        (ig1, v0, slc0, nc0, rsc0, wwo, wwx),
        [e_wide, vspec, e_thin, e_thin, e_one, ANY, ANY],
        [thin, o_vec(4, width)],
        [pltpu.VMEM((inner, width), BF16), pltpu.VMEM((rows, inner), F32), pltpu.VMEM((4, 8, width), F32), dma((1,))],
        1.3 * mm, 8_000_000,
    )
    g1.go()
    rim_up0, rim_dn0 = cg0[:, -RIM0:], cg0[:, :RIM0]
    rim0 = jnp.concatenate([lax.ppermute(rim_up0, "dp", ahead), lax.ppermute(rim_dn0, "dp", behind)], axis=1)
    g3 = Chain(*terms(tie(c_arr, g1.ready(rim_up0), rim_up0, rim_dn0), [(st0, cg0)]), steps)
    g1.go()
    g3.step()
    g2 = Chain(*terms(tie(c_arr, g1.ready(g3.keep), g3.keep), [(act1, ng1), (oa0, ig1)]), steps)
    g1.go()
    g3.ready(g2.keep)
    g2.step()
    ng0, vecm0 = call(
        functools.partial(mid_kernel, far=False, block=0),
        tie(c_arr, g1.ready(g2.keep), g3.send, g2.keep),
        (cg0, rim0, mk, v0, sln0, nn0, rsn0, cwo, cwx),
        [e_thin, each(2 * RIM0, inner), e_masks, vspec, e_thin, e_thin, e_one, ANY, ANY],
        [thin, o_vec(3, inner)],
        mid_scratch([pltpu.VMEM((rows + 2 * RIM0, inner), F32)]),
        2.6 * mm, 10_000_000,
    )
    g1.go()
    g3.go()
    g4 = Chain(*terms(tie(c_arr, g1.ready(ng0), g3.ready(ng0), g2.ready(ng0)), [(act0, ng0)]), steps)
    g1.go()
    g3.go()
    g2.go()
    g4.step()
    ig0, vecf0 = first(
        tie(c_arr, g4.keep, g1.ready(g4.keep), g3.ready(g4.keep), g2.ready(g4.keep)),
        0, ng0, v0, ig1, e_wide, slx0, block_input, mine(rows, width), mux0, rsx0,
    )
    g1.go()
    g3.go()
    g2.go()
    while not all(g.done() for g in (g1, g3, g2, g4)):
        for g in (g1, g3, g2, g4):
            if not g.done():
                g.step()

    parts, groups, base = [], [], 0
    for core, chain in ((1, g1), (0, g3), (None, g2), (0, g4)):
        pieces = chain.finish()
        height = sum(p.shape[0] for p in pieces) // 2
        if chain is g3:
            base = 0
        groups.append((core, base, list(range(len(parts), len(parts) + len(pieces)))))
        base += height
        if chain is g3:
            base = max(base, groups[0][1] + sum(p.shape[0] for p in parts[:4]) // 2)
        parts += pieces
    half = inner // 2
    cols = width // inner
    at2, at4 = groups[2][1], groups[3][1]
    conv_rows = [k * half for k in range(TAPS)]
    row0 = conv_rows + [at2 + (cols + k) * half for k in range(cols)] + [at4 + k * half for k in range(cols)]
    row1 = [r + cols * half for r in conv_rows] + [k * half for k in range(cols)] + [at2 + k * half for k in range(cols)]
    row_arr = jnp.where(low, jnp.array(row0, jnp.int32), jnp.array(row1, jnp.int32))
    sig_arr = jnp.where(low, jnp.stack(signs), jnp.stack(signs[::-1])).astype(jnp.int32)
    conv_grad, widen_grad, narrow_grad = pl.pallas_call(
        functools.partial(unpack_kernel, groups=groups, count=count, cols=cols),
        grid_spec=pltpu.PrefetchScalarGridSpec(
            num_scalar_prefetch=3,
            grid=(TAPS + 2 * cols,),
            in_specs=[ANY] * len(parts),
            out_specs=[
                pl.BlockSpec((1, inner, inner), lambda s, *_: (jnp.minimum(s, TAPS - 1), 0, 0)),
                pl.BlockSpec((inner, inner), lambda s, *_: (0, jnp.clip(s - TAPS, 0, cols - 1))),
                pl.BlockSpec((inner, inner), lambda s, *_: (jnp.clip(s - TAPS - cols, 0, cols - 1), 0)),
            ],
            scratch_shapes=[pltpu.VMEM((2, base, inner), BF16), dma((len(groups),))],
        ),
        out_shape=[
            jax.ShapeDtypeStruct((TAPS, inner, inner), F32),
            jax.ShapeDtypeStruct((inner, width), F32),
            jax.ShapeDtypeStruct((width, inner), F32),
        ],
        compiler_params=pltpu.CompilerParams(vmem_limit_bytes=VMEM_LIMIT),
        cost_estimate=pl.CostEstimate(flops=0, bytes_accessed=25_000_000, transcendentals=0),
    )(c_arr, row_arr, sig_arr, *parts)

    def padded(v):
        return jnp.pad(v, ((0, 0), (0, width - v.shape[1])))

    terms_small = [vec1, padded(vecm1), vecf1, vecl0, padded(vecm0), vecf0, padded(tot)]
    small = jnp.concatenate(terms_small, axis=0)
    small = jnp.pad(small, ((0, -small.shape[0] % 8), (0, 0)))
    small = small + swapped(small)
    for pairs, _ in steps:
        small = small + hop(small, pairs)
    s1, sm1, sf1, sl0, sm0, sf0, st = jnp.split(small, [4, 7, 9, 13, 16, 18], axis=0)
    type_total, loss_total = st[0, :vocab], st[1, :vocab]

    def sel(in0, in1, n=width):
        return jnp.where(low, in0, in1)[None, :n]

    def gathered(in0, in1):
        keep = jnp.where(low, in0, in1)
        come = swapped(jnp.where(low, in1, in0))
        return jnp.concatenate([jnp.where(low, keep, come), jnp.where(low, come, keep)], axis=0)[None]

    return (
        gathered(out0, out1),
        gathered(ig0, ig1),
        sel(sf0[0], sf1[0]),
        sel(sf0[1], sf1[1]),
        narrow_grad[None],
        sel(sm0[2], sm1[2], inner),
        sel(sm0[0], sm1[0], inner),
        sel(sm0[1], sm1[1], inner),
        conv_grad[None],
        sel(sl0[2], s1[2], inner),
        sel(sl0[0], s1[0], inner),
        sel(sl0[1], s1[1], inner),
        widen_grad[None],
        sel(sl0[3], s1[3]),
        type_total.astype(jnp.int32),
        loss_total / jnp.maximum(type_total, 1.0),
    )


def solution(mesh):
    rows = P(None, "dp", None)
    ids = P(None, "dp")
    vec = P("section", None)
    mat = P("section", None, None)
    conv = P("section", None, None, None)
    weights = (vec, vec, mat, vec, vec, vec, conv, vec, vec, vec, mat, vec)
    grads = P("section", None, "dp", None)
    return jax.shard_map(
        body,
        mesh=mesh,
        in_specs=(rows, rows, ids, ids, ids, ids, *weights, P()),
        out_specs=(grads, grads, *weights, P(), P()),
        check_vma=False,
    )
```

time: 559 us -> 403 us (0.72)
  Pallas kernels: 233 us -> 152 us
  waiting for transfers between devices: 163 us -> 106 us
  other arithmetic: 57.1 us -> 41.5 us
  local copies, waits for them, and re-layouts: 32.8 us -> 23.1 us
  starting transfers between devices: 64.5 us -> 72.7 us
    pallas_call x5 -> x8, Pallas kernels: 201 us -> 107 us  [call(): pl.pallas_call(kernel, grid_spec=pltpu.PrefetchScalarGridSpec(num_scalar_...]
    ppermute x36, waiting for transfers between devices: 150 us -> 70 us  [hop(): return lax.ppermute(v, ('section', 'dp'), pairs)]
    select_n x30 -> x8, other arithmetic: 25.7 us -> 5.36 us  [the longest x4 2.46 us: sel(): return jnp.where(low, in0, in1)[None, :n]]
    ppermute x17 -> x23, waiting for transfers between devices: 0.29 us -> 19.4 us  [the longest x1 6.13 us: body(): lax.ppermute(rim_up0, 'dp', ahead)]
    dynamic_slice x21 -> x0, local copies, waits for them, and re-layouts: 14.5 us -> none  [the longest x20 11.6 us: halves(): send = lax.dynamic_slice_in_dim(buf, (1 - bit) * rows, rows, 0)]
    pallas_call x4 -> x5, Pallas kernels: 31.7 us -> 44.8 us  [the longest x4 32.9 us: weight_terms(): pl.pallas_call(kernel, grid_spec=pltpu.PrefetchScalarGridSpec(num_scalar_...]
    convert_element_type x20, other arithmetic: 9.22 us -> 21.5 us  [add_low(): return (one.astype(F32) + other.astype(F32)).astype(BF16)]
    ppermute x36, starting transfers between devices: 40 us -> 46.6 us  [hop(): return lax.ppermute(v, ('section', 'dp'), pairs)]
  transfers between devices with their start and end apart: 57 -> 63, of which waited for: 23 -> 23; matrix products, arithmetic and copies ran while one was open for 12% -> 13% of each run, Pallas kernels for 22% -> 18%
where the time goes in v2:
time: 403 us; the launch traced here: 396 us
  Pallas kernels  152 us (38%)
  waiting for transfers between devices  106 us (26%)
  starting transfers between devices  72.7 us (18%)
  other arithmetic  41.5 us (10%)
  local copies, waits for them, and re-layouts  23.1 us (6%)
    pallas_call x8, Pallas kernels, call(): pl.pallas_call(kernel, grid_spec=pltpu.PrefetchScalarGridSpec(num_scalar_...  107 us
    ppermute x36, waiting for transfers between devices, hop(): return lax.ppermute(v, ('section', 'dp'), pairs)  70 us
    ppermute x36, starting transfers between devices, hop(): return lax.ppermute(v, ('section', 'dp'), pairs)  46.6 us
    pallas_call x4, Pallas kernels, weight_terms(): pl.pallas_call(kernel, grid_spec=pltpu.PrefetchScalarGridSpec(num_scalar_...  32.9 us
    convert_element_type x20, other arithmetic, add_low(): return (one.astype(F32) + other.astype(F32)).astype(BF16)  21.5 us
    ppermute x1, waiting for transfers between devices, body(): up1 = lax.ppermute(mid1[:, -RIM1:], 'dp', ahead)  15.7 us
    pallas_call x1, Pallas kernels, body(): pl.pallas_call(functools.partial(unpack_kernel, groups=groups, count=coun...  11.9 us
    unnamed x105, local copies, waits for them, and re-layouts  11.5 us
  transfers between devices with their start and end apart: 63, of which 23 were waited for; matrix products, arithmetic and copies ran while one was open for 13% of the time, Pallas kernels for 18%

profile of v2, /device:TPU:0, one launch (start us, length us, event | category | flops | bytes accessed | tf_op | source)
XLA Modules:
  0.0 396.5 jit_solution(15214431164881165163)
XLA Ops:
  8.3 3.0 collective-permute-start
  11.3 4.1 %collective-permute-start.1 = (bf16[3,8,1280]{2,1,0:T(8,128)(2,1)S(1)}, bf16[3,8,1280]{2,1,0:T(8,128)(2,1)S(1)}, u32[]{:S(2)}, u32[]{:S(2)}) collective-permute-start(bf16[3,8,1280]{2,1,0:T(8,128)(2,1)S(1)} %get-tuple-element.165), channel_id=1, source_target_pairs={{1,0},{2,1},{3,2},{4,3},{5,4},{6,5},{7,6},{8,7},{9,8},{10,9},{11,1... | collective-permute-start | bytes 184328 | tf_op jit(solution)/shard_map/ppermute | solution.py:664
  23.0 29.5 %shard_map.324 = (f32[3,256,128]{2,1,0:T(8,128)}, bf16[3,256,1280]{2,1,0:T(8,128)(2,1)}, bf16[3,256,1280]{2,1,0:T(8,128)(2,1)}, f32[3,256,1]{2,1,0:T(8,128)}, f3...) custom-call(s32[1]{0:T(128)} %bitcast.c_ref, ...), custom_call_target="tpu_custom_call" | custom-call | flops 3460300800 | bytes 20000000 | tf_op jit(solution)/shard_map/pallas_call | solution.py:678
  53.8 6.1 %collective-permute-start.7 = (bf16[3,128,640]{2,1,0:T(8,128)(2,1)S(1)}, bf16[3,128,640]{2,1,0:T(8,128)(2,1)S(1)}, u32[]{:S(2)}, u32[]{:S(2)}) collective-permute-start(bf16[3,128,640]{2,1,0:T(8,128)(2,1)S(1)} %get-tuple-element.186), channel_id=1, source_target_pairs={{1,0},{2,1},{3,2},{4,3},{5,4},{6,5},{7,6},{8,7},{9,8},{10,9},{11,1... | collective-permute-start | bytes 1474568 | tf_op jit(solution)/shard_map/ppermute | solution.py:727
  59.9 15.7 %collective-permute-done.6.up_ref = bf16[3,128,640]{2,1,0:T(8,128)(2,1)S(1)} collective-permute-done((bf16[3,128,640]{2,1,0:T(8,128)(2,1)S(1)}, bf16[3,128,640]{2,1,0:T(8,128)(2,1)S(1)}, u32[]{:S(2)}, u32[]{:S(2)}) %collective-permute-start.6) | collective-permute-done | bytes 491552 | tf_op jit(solution)/shard_map/ppermute | solution.py:726
  76.9 16.8 %shard_map.325 = (bf16[3,256,3200]{2,1,0:T(8,128)(2,1)}, bf16[3,256,640]{2,1,0:T(8,128)(2,1)}, bf16[3,256,640]{2,1,0:T(8,128)(2,1)}, f32[4,1280]{1,0:T(4,128)}) custom-call(s32[1]{0:T(128)} %bitcast.c_ref, bf16[3,256,640]{2,1,0:T(8,128)(2,1)} %get-tuple-element.87.mid_ref, bf16[3,128,640]{2,1,0:T(8,128)(2,1)} %copy-done.32, bf16[3,128,640]{2,1,0:T(8,128)(2,1)} %copy-done.33, ...), custom_call_target="tpu_custom_call" | custom-call | flops 2202009600 | bytes 10000000 | tf_op jit(solution)/shard_map/pallas_call | solution.py:678
  93.7 2.2 fusion.2
  96.0 11.7 %shard_map.326 = (bf16[2304,640]{1,0:T(8,128)(2,1)}, bf16[2304,640]{1,0:T(8,128)(2,1)}) custom-call(s32[1]{0:T(128)} %bitcast.c_ref, bf16[3,256,640]{2,1,0:T(8,128)(2,1)} %get-tuple-element.91.refs_0_.oa_ref, bf16[6,256,1280]{2,1,0:T(8,128)(2,1)} %grad.1, bf16[3,256,3200]{2,1,0:T(8,128)(2,1)} %get-tuple-element.92.refs_2_, ...), custom_call_target="tpu_custom_call" | custom-call | flops 2202009600 | bytes 2949120 | tf_op jit(solution)/shard_map/pallas_call | solution.py:495
  109.7 3.7 collective-permute-start.11
  115.6 8.9 %shard_map.327 = (bf16[3,256,1280]{2,1,0:T(8,128)(2,1)}, f32[2,128]{1,0:T(2,128)}) custom-call(s32[1]{0:T(128)} %bitcast.c_ref, bf16[3,256,1280]{2,1,0:T(8,128)(2,1)} %get-tuple-element.86.out0_ref.src, bf16[3,256,640]{2,1,0:T(8,128)(2,1)} %get-tuple-element.91.refs_0_.oa_ref, s32[6,1,256]{2,1,0:T(1,128)} %broadcast_in_dim.38.rt_ref, ...), custom_call_target="tpu_custom_call" | custom-call | flops 754974720 | bytes 4000000 | tf_op jit(solution)/shard_map/pallas_call | solution.py:678
  124.5 2.5 add_convert_fusion.1
  127.1 4.6 %collective-permute-done.10.refs_0_ = bf16[3,128,640]{2,1,0:T(8,128)(2,1)S(1)} collective-permute-done((bf16[3,128,640]{2,1,0:T(8,128)(2,1)}, bf16[3,128,640]{2,1,0:T(8,128)(2,1)S(1)}, u32[]{:S(2)}, u32[]{:S(2)}) %collective-permute-start.10) | collective-permute-done | bytes 491552 | tf_op jit(solution)/shard_map/ppermute | solution.py:746
  131.7 2.7 collective-permute-done.11.refs_1_
  134.8 11.5 %shard_map.328 = (bf16[3,256,640]{2,1,0:T(8,128)(2,1)}, f32[3,640]{1,0:T(4,128)}) custom-call(s32[1]{0:T(128)} %bitcast.c_ref, bf16[3,256,640]{2,1,0:T(8,128)(2,1)} %get-tuple-element.89.refs_3_.cg_ref, bf16[3,128,640]{2,1,0:T(8,128)(2,1)} %copy-done.30, bf16[3,128,640]{2,1,0:T(8,128)(2,1)} %collective-permute-done.11.refs_1_, ...), custom_call_target="tpu_custom_call" | custom-call | flops 1635778560 | bytes 5000000 | tf_op jit(solution)/shard_map/pallas_call | solution.py:678
  146.3 10.1 %shard_map.329 = (bf16[3,256,1280]{2,1,0:T(8,128)(2,1)}, f32[2,1280]{1,0:T(2,128)}) custom-call(s32[1]{0:T(128)} %bitcast.c_ref, bf16[3,256,640]{2,1,0:T(8,128)(2,1)} %get-tuple-element.103.ng_ref.refs_1_, f32[1,7680]{1,0:T(1,128)} %get-tuple-element.209.v1_ref.refs_3_.v_ref, bf16[6,256,1280]{2,1,0:T(8,128)(2,1)} %grad.1, ...), custom_call_target="tpu_custom_call" | custom-call | flops 817889280 | bytes 5000000 | tf_op jit(solution)/shard_map/pallas_call | solution.py:678
  159.1 7.9 %shard_map.330 = (bf16[3,256,640]{2,1,0:T(8,128)(2,1)}, f32[4,1280]{1,0:T(4,128)}) custom-call(s32[1]{0:T(128)} %bitcast.c_ref, bf16[3,256,1280]{2,1,0:T(8,128)(2,1)} %get-tuple-element.107.ig_ref.refs_3_.grad, f32[1,7680]{1,0:T(1,128)} %get-tuple-element.210.v0_ref.v_ref.refs_2_, bf16[3,256,640]{2,1,0:T(8,128)(2,1)} %get-tuple-element.110.slc, ...), custom_call_target="tpu_custom_call" | custom-call | flops 817889280 | bytes 4000000 | tf_op jit(solution)/shard_map/pallas_call | solution.py:678
  169.8 8.7 %shard_map.331 = (bf16[1792,640]{1,0:T(8,128)(2,1)}, bf16[1792,640]{1,0:T(8,128)(2,1)}) custom-call(s32[1]{0:T(128)} %bitcast.c_ref, bf16[3,256,3200]{2,1,0:T(8,128)(2,1)} %get-tuple-element.116.refs_0_, bf16[3,256,640]{2,1,0:T(8,128)(2,1)} %get-tuple-element.113.refs_1_.cg_ref), custom_call_target="tpu_custom_call" | custom-call | flops 1572864000 | bytes 2293760 | tf_op jit(solution)/shard_map/pallas_call | solution.py:495
  178.9 7.1 %collective-permute-done.14 = bf16[288,640]{1,0:T(8,128)(2,1)S(1)} collective-permute-done((bf16[288,640]{1,0:T(8,128)(2,1)S(1)}, bf16[288,640]{1,0:T(8,128)(2,1)S(1)}, u32[]{:S(2)}, u32[]{:S(2)}) %collective-permute-start.14) | collective-permute-done | bytes 368672 | tf_op jit(solution)/shard_map/ppermute | solution.py:635
  186.8 7.9 %shard_map.332 = (bf16[1280,640]{1,0:T(8,128)(2,1)}, bf16[1280,640]{1,0:T(8,128)(2,1)}) custom-call(s32[1]{0:T(128)} %bitcast.c_ref, bf16[3,256,1280]{2,1,0:T(8,128)(2,1)} %get-tuple-element.120.refs_0_, bf16[3,256,640]{2,1,0:T(8,128)(2,1)} %get-tuple-element.103.ng_ref.refs_1_, bf16[3,256,640]{2,1,0:T(8,128)(2,1)} %get-tuple-element.121.refs_2_, ...), custom_call_target="tpu_custom_call" | custom-call | flops 1258291200 | bytes 1638400 | tf_op jit(solution)/shard_map/pallas_call | solution.py:495
  200.4 6.1 %collective-permute-done.18 = bf16[3,8,640]{2,1,0:T(8,128)(2,1)S(1)} collective-permute-done((bf16[3,8,640]{2,1,0:T(8,128)(2,1)S(1)}, bf16[3,8,640]{2,1,0:T(8,128)(2,1)S(1)}, u32[]{:S(2)}, u32[]{:S(2)}) %collective-permute-start.18) | collective-permute-done | bytes 30752 | tf_op jit(solution)/shard_map/ppermute | solution.py:822
  206.7 3.9 collective-permute-done.19
  211.3 3.9 add_convert_fusion.2
  215.3 12.2 %shard_map.333 = (bf16[3,256,640]{2,1,0:T(8,128)(2,1)}, f32[3,640]{1,0:T(4,128)}) custom-call(s32[1]{0:T(128)} %bitcast.c_ref, bf16[3,256,640]{2,1,0:T(8,128)(2,1)} %get-tuple-element.113.refs_1_.cg_ref, bf16[3,16,640]{2,1,0:T(8,128)(2,1)} %pad_maximum_fusion.13.refs_0_, f32[3,256,128]{2,1,0:T(8,128)} %get-tuple-element.88.mk.refs_2_.refs_1_, ...), custom_call_target="tpu_custom_call" | custom-call | flops 1635778560 | bytes 5000000 | tf_op jit(solution)/shard_map/pallas_call | solution.py:678
  227.6 3.0 add_convert_fusion.4
  233.2 5.4 %collective-permute-start.16 = (bf16[144,640]{1,0:T(8,128)(2,1)S(1)}, bf16[144,640]{1,0:T(8,128)(2,1)S(1)}, u32[]{:S(2)}, u32[]{:S(2)}) collective-permute-start(bf16[144,640]{1,0:T(8,128)(2,1)S(1)} %add_convert_fusion.22), channel_id=1, source_target_pairs={{0,8},{1,9},{2,10},{3,11},{4,12},{5,13},{6,14},{7,15},{8,0},{9,1},... | collective-permute-start | bytes 552968 | tf_op jit(solution)/shard_map/ppermute | solution.py:635
  239.2 4.5 %collective-permute-done.16 = bf16[144,640]{1,0:T(8,128)(2,1)S(1)} collective-permute-done((bf16[144,640]{1,0:T(8,128)(2,1)S(1)}, bf16[144,640]{1,0:T(8,128)(2,1)S(1)}, u32[]{:S(2)}, u32[]{:S(2)}) %collective-permute-start.16) | collective-permute-done | bytes 184352 | tf_op jit(solution)/shard_map/ppermute | solution.py:635
  245.6 2.3 add_convert_fusion.8
  247.9 4.7 %shard_map.334 = (bf16[768,640]{1,0:T(8,128)(2,1)}, bf16[768,640]{1,0:T(8,128)(2,1)}) custom-call(s32[1]{0:T(128)} %bitcast.c_ref, bf16[3,256,1280]{2,1,0:T(8,128)(2,1)} %get-tuple-element.136.refs_0_, bf16[3,256,640]{2,1,0:T(8,128)(2,1)} %get-tuple-element.130.refs_1_.ng_ref), custom_call_target="tpu_custom_call" | custom-call | flops 629145600 | bytes 983040 | tf_op jit(solution)/shard_map/pallas_call | solution.py:495
  256.1 3.9 broadcast_select_fusion.5
  265.9 10.2 %shard_map.335 = (bf16[3,256,1280]{2,1,0:T(8,128)(2,1)}, f32[2,1280]{1,0:T(2,128)}) custom-call(s32[1]{0:T(128)} %bitcast.c_ref, bf16[3,256,640]{2,1,0:T(8,128)(2,1)} %get-tuple-element.130.refs_1_.ng_ref, f32[1,7680]{1,0:T(1,128)} %get-tuple-element.210.v0_ref.v_ref.refs_2_, bf16[3,256,1280]{2,1,0:T(8,128)(2,1)} %get-tuple-element.107.ig_ref.refs_3_.grad, ...), custom_call_target="tpu_custom_call" | custom-call | flops 817889280 | bytes 5000000 | tf_op jit(solution)/shard_map/pallas_call | solution.py:678
  277.7 2.2 collective-permute-start.25
  282.5 2.5 collective-permute-start.53
  285.0 2.8 collective-permute-done.45
  291.8 2.5 collective-permute-start.36
  297.8 5.8 %collective-permute-done.54 = bf16[192,640]{1,0:T(8,128)(2,1)S(1)} collective-permute-done((bf16[192,640]{1,0:T(8,128)(2,1)S(1)}, bf16[192,640]{1,0:T(8,128)(2,1)S(1)}, u32[]{:S(2)}, u32[]{:S(2)}) %collective-permute-start.54) | collective-permute-done | bytes 245792 | tf_op jit(solution)/shard_map/ppermute | solution.py:635
  310.4 3.2 collective-permute-start.47
  313.7 2.2 collective-permute-start.56
  315.9 3.1 collective-permute-done.56
  319.0 2.9 collective-permute-start.38
  323.3 4.4 %collective-permute-done.57 = bf16[48,640]{1,0:T(8,128)(2,1)S(1)} collective-permute-done((bf16[48,640]{1,0:T(8,128)(2,1)S(1)}, bf16[48,640]{1,0:T(8,128)(2,1)S(1)}, u32[]{:S(2)}, u32[]{:S(2)}) %collective-permute-start.57) | collective-permute-done | bytes 61472 | tf_op jit(solution)/shard_map/ppermute | solution.py:635
  329.1 4.9 %collective-permute-done.30 = f32[24,1280]{1,0:T(8,128)S(1)} collective-permute-done((f32[24,1280]{1,0:T(8,128)S(1)}, f32[24,1280]{1,0:T(8,128)S(1)}, u32[]{:S(2)}, u32[]{:S(2)}) %collective-permute-start.30) | collective-permute-done | bytes 122912 | tf_op jit(solution)/shard_map/ppermute | solution.py:635
  336.1 2.3 maximum_bitcast_fusion
  338.4 3.6 collective-permute-done.48
  342.1 6.0 %collective-permute-done.39 = bf16[448,640]{1,0:T(8,128)(2,1)S(1)} collective-permute-done((bf16[448,640]{1,0:T(8,128)(2,1)S(1)}, bf16[448,640]{1,0:T(8,128)(2,1)S(1)}, u32[]{:S(2)}, u32[]{:S(2)}) %collective-permute-start.39) | collective-permute-done | bytes 573472 | tf_op jit(solution)/shard_map/ppermute | solution.py:635
  354.2 6.3 %collective-permute-done.49.refs_9_ = bf16[640,640]{1,0:T(8,128)(2,1)S(1)} collective-permute-done((bf16[640,640]{1,0:T(8,128)(2,1)S(1)}, bf16[640,640]{1,0:T(8,128)(2,1)S(1)}, u32[]{:S(2)}, u32[]{:S(2)}) %collective-permute-start.49) | collective-permute-done | bytes 819232 | tf_op jit(solution)/shard_map/ppermute | solution.py:635
  362.7 15.3 %collective-permute-done.60.refs_13_ = bf16[384,640]{1,0:T(8,128)(2,1)S(1)} collective-permute-done((bf16[384,640]{1,0:T(8,128)(2,1)S(1)}, bf16[384,640]{1,0:T(8,128)(2,1)S(1)}, u32[]{:S(2)}, u32[]{:S(2)}) %collective-permute-start.60) | collective-permute-done | bytes 491552 | tf_op jit(solution)/shard_map/ppermute | solution.py:635
  379.5 2.3 maximum_bitcast_fusion.1
  384.3 11.9 %shard_map.336 = (f32[5,640,640]{2,1,0:T(8,128)}, f32[640,1280]{1,0:T(8,128)}, f32[1280,640]{1,0:T(8,128)}) custom-call(s32[1]{0:T(128)} %bitcast.c_ref, s32[9]{0:T(128)} %broadcast_select_fusion.20.row_ref, s32[2]{0:T(128)} %broadcast_select_fusion.19.sig_ref, bf16[1152,640]{1,0:T(8,128)(2,1)} %copy-done.9, bf16[1152,640]{1,0:T(8,128)(2,1)} %copy-done.16, ...), custom_call_target="tpu_custom_call" | custom-call | bytes 25000000 | tf_op jit(solution)/shard_map/pallas_call | solution.py:877
  (264 shorter events, 86.0 us)
Async XLA Ops:
  0.6 21.2 %collective-permute-start.4 = (bf16[5,640,640]{2,1,0:T(8,128)(2,1)}, bf16[5,640,640]{2,1,0:T(8,128)(2,1)}, u32[]{:S(2)}, u32[]{:S(2)}) collective-permute-start(bf16[5,640,640]{2,1,0:T(8,128)(2,1)} %bitcast.17), channel_id=1, source_target_pairs={{0,16},{16,0},{1,17},{17,1},{2,18},{18,2},{3,19},{19,3},{4,20},{20... | collective-permute-start | bytes 12288008 | tf_op jit(solution)/shard_map/ppermute | solution.py:631
  7.4 10.6 %collective-permute-start.2 = (f32[1,7680]{1,0:T(1,128)S(1)}, f32[1,7680]{1,0:T(1,128)S(1)}, u32[]{:S(2)}, u32[]{:S(2)}) collective-permute-start(f32[1,7680]{1,0:T(1,128)S(1)} %constant_dynamic-update-slice_fusion), channel_id=1, source_target_pairs={{0,16},{16,0},{1,17},{17,1},{2,18},{18,2},{3,19},{19,3},{4,20},{20... | collective-permute-start | bytes 92168 | tf_op jit(solution)/shard_map/ppermute | solution.py:631
  8.3 10.8 %collective-permute-start = (bf16[3,8,1280]{2,1,0:T(8,128)(2,1)S(1)}, bf16[3,8,1280]{2,1,0:T(8,128)(2,1)S(1)}, u32[]{:S(2)}, u32[]{:S(2)}) collective-permute-start(bf16[3,8,1280]{2,1,0:T(8,128)(2,1)S(1)} %get-tuple-element.164), channel_id=1, source_target_pairs={{0,1},{1,2},{2,3},{3,4},{4,5},{5,6},{6,7},{7,8},{8,9},{9,10},{10,1... | collective-permute-start | bytes 184328 | tf_op jit(solution)/shard_map/ppermute | solution.py:664
  53.7 21.9 %collective-permute-start.6 = (bf16[3,128,640]{2,1,0:T(8,128)(2,1)S(1)}, bf16[3,128,640]{2,1,0:T(8,128)(2,1)S(1)}, u32[]{:S(2)}, u32[]{:S(2)}) collective-permute-start(bf16[3,128,640]{2,1,0:T(8,128)(2,1)S(1)} %get-tuple-element.187), channel_id=1, source_target_pairs={{0,1},{1,2},{2,3},{3,4},{4,5},{5,6},{6,7},{7,8},{8,9},{9,10},{10,1... | collective-permute-start | bytes 1474568 | tf_op jit(solution)/shard_map/ppermute | solution.py:726
  53.8 22.4 %collective-permute-start.7 = (bf16[3,128,640]{2,1,0:T(8,128)(2,1)S(1)}, bf16[3,128,640]{2,1,0:T(8,128)(2,1)S(1)}, u32[]{:S(2)}, u32[]{:S(2)}) collective-permute-start(bf16[3,128,640]{2,1,0:T(8,128)(2,1)S(1)} %get-tuple-element.186), channel_id=1, source_target_pairs={{1,0},{2,1},{3,2},{4,3},{5,4},{6,5},{7,6},{8,7},{9,8},{10,9},{11,1... | collective-permute-start | bytes 1474568 | tf_op jit(solution)/shard_map/ppermute | solution.py:727
  107.6 16.9 %collective-permute-start.9 = (bf16[2304,640]{1,0:T(8,128)(2,1)}, bf16[2304,640]{1,0:T(8,128)(2,1)}, u32[]{:S(2)}, u32[]{:S(2)}) collective-permute-start(bf16[2304,640]{1,0:T(8,128)(2,1)} %get-tuple-element.96), channel_id=1, source_target_pairs={{0,16},{16,0},{1,17},{17,1},{2,18},{18,2},{3,19},{19,3},{4,20},{20... | collective-permute-start | bytes 8847368 | tf_op jit(solution)/shard_map/ppermute | solution.py:631
  107.6 24.1 %collective-permute-start.10 = (bf16[3,128,640]{2,1,0:T(8,128)(2,1)}, bf16[3,128,640]{2,1,0:T(8,128)(2,1)S(1)}, u32[]{:S(2)}, u32[]{:S(2)}) collective-permute-start(bf16[3,128,640]{2,1,0:T(8,128)(2,1)} %get-tuple-element.185), channel_id=1, source_target_pairs={{0,1},{1,2},{2,3},{3,4},{4,5},{5,6},{6,7},{7,8},{8,9},{9,10},{10,1... | collective-permute-start | bytes 1474568 | tf_op jit(solution)/shard_map/ppermute | solution.py:746
  109.7 24.7 %collective-permute-start.11 = (bf16[3,128,640]{2,1,0:T(8,128)(2,1)}, bf16[3,128,640]{2,1,0:T(8,128)(2,1)}, u32[]{:S(2)}, u32[]{:S(2)}) collective-permute-start(bf16[3,128,640]{2,1,0:T(8,128)(2,1)} %get-tuple-element.184), channel_id=1, source_target_pairs={{1,0},{2,1},{3,2},{4,3},{5,4},{6,5},{7,6},{8,7},{9,8},{10,9},{11,1... | collective-permute-start | bytes 1474568 | tf_op jit(solution)/shard_map/ppermute | solution.py:747
  134.5 21.9 %collective-permute-start.12 = (bf16[1152,640]{1,0:T(8,128)(2,1)S(1)}, bf16[1152,640]{1,0:T(8,128)(2,1)}, u32[]{:S(2)}, u32[]{:S(2)}) collective-permute-start(bf16[1152,640]{1,0:T(8,128)(2,1)S(1)} %get-tuple-element.98), channel_id=1, source_target_pairs={{0,1},{1,0},{2,3},{3,2},{4,5},{5,4},{6,7},{7,6},{8,9},{9,8},{10,11... | collective-permute-start | bytes 4423688 | tf_op jit(solution)/shard_map/ppermute | solution.py:635
  158.0 11.5 %collective-permute-start.13 = (bf16[576,640]{1,0:T(8,128)(2,1)S(1)}, bf16[576,640]{1,0:T(8,128)(2,1)S(1)}, u32[]{:S(2)}, u32[]{:S(2)}) collective-permute-start(bf16[576,640]{1,0:T(8,128)(2,1)S(1)} %get-tuple-element.169), channel_id=1, source_target_pairs={{0,4},{1,5},{2,6},{3,7},{4,0},{5,1},{6,2},{7,3},{8,12},{9,13},{10,... | collective-permute-start | bytes 2211848 | tf_op jit(solution)/shard_map/ppermute | solution.py:635
  178.5 32.8 %collective-permute-start.17 = (bf16[1792,640]{1,0:T(8,128)(2,1)}, bf16[1792,640]{1,0:T(8,128)(2,1)}, u32[]{:S(2)}, u32[]{:S(2)}) collective-permute-start(bf16[1792,640]{1,0:T(8,128)(2,1)} %get-tuple-element.124), channel_id=1, source_target_pairs={{0,16},{16,0},{1,17},{17,1},{2,18},{18,2},{3,19},{19,3},{4,20},{20... | collective-permute-start | bytes 6881288 | tf_op jit(solution)/shard_map/ppermute | solution.py:631
  194.6 32.9 %collective-permute-start.21 = (bf16[1280,640]{1,0:T(8,128)(2,1)}, bf16[1280,640]{1,0:T(8,128)(2,1)}, u32[]{:S(2)}, u32[]{:S(2)}) collective-permute-start(bf16[1280,640]{1,0:T(8,128)(2,1)} %get-tuple-element.133), channel_id=1, source_target_pairs={{0,16},{16,0},{1,17},{17,1},{2,18},{18,2},{3,19},{19,3},{4,20},{20... | collective-permute-start | bytes 4915208 | tf_op jit(solution)/shard_map/ppermute | solution.py:631
  196.2 59.9 %collective-permute-start.8 = (bf16[3,256,1280]{2,1,0:T(8,128)(2,1)}, bf16[3,256,1280]{2,1,0:T(8,128)(2,1)}, u32[]{:S(2)}, u32[]{:S(2)}) collective-permute-start(bf16[3,256,1280]{2,1,0:T(8,128)(2,1)} %broadcast_select_fusion.6), channel_id=1, source_target_pairs={{0,16},{16,0},{1,17},{17,1},{2,18},{18,2},{3,19},{19,3},{4,20},{20... | collective-permute-start | bytes 5898248 | tf_op jit(solution)/shard_map/ppermute | solution.py:631
  196.7 14.6 %collective-permute-start.15 = (bf16[144,640]{1,0:T(8,128)(2,1)S(1)}, bf16[144,640]{1,0:T(8,128)(2,1)S(1)}, u32[]{:S(2)}, u32[]{:S(2)}) collective-permute-start(bf16[144,640]{1,0:T(8,128)(2,1)S(1)} %add_convert_fusion.23), channel_id=1, source_target_pairs={{0,8},{1,9},{2,10},{3,11},{4,12},{5,13},{6,14},{7,15},{8,0},{9,1},... | collective-permute-start | bytes 552968 | tf_op jit(solution)/shard_map/ppermute | solution.py:635
  198.7 7.9 %collective-permute-start.18 = (bf16[3,8,640]{2,1,0:T(8,128)(2,1)S(1)}, bf16[3,8,640]{2,1,0:T(8,128)(2,1)S(1)}, u32[]{:S(2)}, u32[]{:S(2)}) collective-permute-start(bf16[3,8,640]{2,1,0:T(8,128)(2,1)S(1)} %get-tuple-element.183), channel_id=1, source_target_pairs={{0,1},{1,2},{2,3},{3,4},{4,5},{5,6},{6,7},{7,8},{8,9},{9,10},{10,1... | collective-permute-start | bytes 92168 | tf_op jit(solution)/shard_map/ppermute | solution.py:822
  215.2 30.4 %collective-permute-start.20 = (bf16[896,640]{1,0:T(8,128)(2,1)}, bf16[896,640]{1,0:T(8,128)(2,1)}, u32[]{:S(2)}, u32[]{:S(2)}) collective-permute-start(bf16[896,640]{1,0:T(8,128)(2,1)} %get-tuple-element.163), channel_id=1, source_target_pairs={{0,1},{1,0},{2,3},{3,2},{4,5},{5,4},{6,7},{7,6},{8,9},{9,8},{10,11... | collective-permute-start | bytes 3440648 | tf_op jit(solution)/shard_map/ppermute | solution.py:635
  230.6 22.0 %collective-permute-start.24 = (bf16[640,640]{1,0:T(8,128)(2,1)}, bf16[640,640]{1,0:T(8,128)(2,1)}, u32[]{:S(2)}, u32[]{:S(2)}) collective-permute-start(bf16[640,640]{1,0:T(8,128)(2,1)} %get-tuple-element.167), channel_id=1, source_target_pairs={{0,1},{1,0},{2,3},{3,2},{4,5},{5,4},{6,7},{7,6},{8,9},{9,8},{10,11... | collective-permute-start | bytes 2457608 | tf_op jit(solution)/shard_map/ppermute | solution.py:635
  233.2 10.4 %collective-permute-start.16 = (bf16[144,640]{1,0:T(8,128)(2,1)S(1)}, bf16[144,640]{1,0:T(8,128)(2,1)S(1)}, u32[]{:S(2)}, u32[]{:S(2)}) collective-permute-start(bf16[144,640]{1,0:T(8,128)(2,1)S(1)} %add_convert_fusion.22), channel_id=1, source_target_pairs={{0,8},{1,9},{2,10},{3,11},{4,12},{5,13},{6,14},{7,15},{8,0},{9,1},... | collective-permute-start | bytes 552968 | tf_op jit(solution)/shard_map/ppermute | solution.py:635
  244.4 15.6 %collective-permute-start.22 = (bf16[288,640]{1,0:T(8,128)(2,1)}, bf16[288,640]{1,0:T(8,128)(2,1)S(1)}, u32[]{:S(2)}, u32[]{:S(2)}) collective-permute-start(bf16[288,640]{1,0:T(8,128)(2,1)} %pad_maximum_fusion.7), channel_id=1, source_target_pairs={{0,2},{1,3},{2,0},{3,1},{4,6},{5,7},{6,4},{7,5},{8,10},{9,11},{10,... | collective-permute-start | bytes 1105928 | tf_op jit(solution)/shard_map/ppermute | solution.py:635
  247.9 16.0 %collective-permute-start.23 = (bf16[448,640]{1,0:T(8,128)(2,1)}, bf16[448,640]{1,0:T(8,128)(2,1)S(1)}, u32[]{:S(2)}, u32[]{:S(2)}) collective-permute-start(bf16[448,640]{1,0:T(8,128)(2,1)} %get-tuple-element.171), channel_id=1, source_target_pairs={{0,4},{1,5},{2,6},{3,7},{4,0},{5,1},{6,2},{7,3},{8,12},{9,13},{10,... | collective-permute-start | bytes 1720328 | tf_op jit(solution)/shard_map/ppermute | solution.py:635
  254.1 8.1 %collective-permute-start.43 = (bf16[320,640]{1,0:T(8,128)(2,1)S(1)}, bf16[320,640]{1,0:T(8,128)(2,1)S(1)}, u32[]{:S(2)}, u32[]{:S(2)}) collective-permute-start(bf16[320,640]{1,0:T(8,128)(2,1)S(1)} %get-tuple-element.175), channel_id=1, source_target_pairs={{0,4},{1,5},{2,6},{3,7},{4,0},{5,1},{6,2},{7,3},{8,12},{9,13},{10,... | collective-permute-start | bytes 1228808 | tf_op jit(solution)/shard_map/ppermute | solution.py:635
  260.0 19.8 %collective-permute-start.52 = (bf16[768,640]{1,0:T(8,128)(2,1)}, bf16[768,640]{1,0:T(8,128)(2,1)}, u32[]{:S(2)}, u32[]{:S(2)}) collective-permute-start(bf16[768,640]{1,0:T(8,128)(2,1)} %get-tuple-element.152), channel_id=1, source_target_pairs={{0,16},{16,0},{1,17},{17,1},{2,18},{18,2},{3,19},{19,3},{4,20},{20... | collective-permute-start | bytes 2949128 | tf_op jit(solution)/shard_map/ppermute | solution.py:631
  261.1 33.4 %collective-permute-start.31 = (bf16[576,640]{1,0:T(8,128)(2,1)}, bf16[576,640]{1,0:T(8,128)(2,1)}, u32[]{:S(2)}, u32[]{:S(2)}) collective-permute-start(bf16[576,640]{1,0:T(8,128)(2,1)} %pad_maximum_fusion.3), channel_id=1, source_target_pairs={{0,4},{1,5},{2,6},{3,7},{4,0},{5,1},{6,2},{7,3},{8,12},{9,13},{10,... | collective-permute-start | bytes 2211848 | tf_op jit(solution)/shard_map/ppermute | solution.py:635
  263.0 14.6 %collective-permute-start.44 = (bf16[160,640]{1,0:T(8,128)(2,1)}, bf16[160,640]{1,0:T(8,128)(2,1)S(1)}, u32[]{:S(2)}, u32[]{:S(2)}) collective-permute-start(bf16[160,640]{1,0:T(8,128)(2,1)} %get-tuple-element.189), channel_id=1, source_target_pairs={{0,2},{1,3},{2,0},{3,1},{4,6},{5,7},{6,4},{7,5},{8,10},{9,11},{10,... | collective-permute-start | bytes 614408 | tf_op jit(solution)/shard_map/ppermute | solution.py:635
  264.8 25.6 %collective-permute-start.35 = (bf16[224,640]{1,0:T(8,128)(2,1)}, bf16[224,640]{1,0:T(8,128)(2,1)}, u32[]{:S(2)}, u32[]{:S(2)}) collective-permute-start(bf16[224,640]{1,0:T(8,128)(2,1)} %get-tuple-element.179), channel_id=1, source_target_pairs={{0,2},{1,3},{2,0},{3,1},{4,6},{5,7},{6,4},{7,5},{8,10},{9,11},{10,... | collective-permute-start | bytes 860168 | tf_op jit(solution)/shard_map/ppermute | solution.py:635
  277.7 85.0 %collective-permute-start.25 = (bf16[3,256,1280]{2,1,0:T(8,128)(2,1)S(1)}, bf16[3,256,1280]{2,1,0:T(8,128)(2,1)S(1)}, u32[]{:S(2)}, u32[]{:S(2)}) collective-permute-start(bf16[3,256,1280]{2,1,0:T(8,128)(2,1)S(1)} %broadcast_select_fusion.2), channel_id=1, source_target_pairs={{0,16},{16,0},{1,17},{17,1},{2,18},{18,2},{3,19},{19,3},{4,20},{20... | collective-permute-start | bytes 5898248 | tf_op jit(solution)/shard_map/ppermute | solution.py:631
  279.9 8.0 %collective-permute-start.45 = (bf16[80,640]{1,0:T(8,128)(2,1)S(1)}, bf16[80,640]{1,0:T(8,128)(2,1)S(1)}, u32[]{:S(2)}, u32[]{:S(2)}) collective-permute-start(bf16[80,640]{1,0:T(8,128)(2,1)S(1)} %add_convert_fusion.31), channel_id=1, source_target_pairs={{0,8},{1,9},{2,10},{3,11},{4,12},{5,13},{6,14},{7,15},{8,0},{9,1},... | collective-permute-start | bytes 307208 | tf_op jit(solution)/shard_map/ppermute | solution.py:635
  282.5 9.3 %collective-permute-start.53 = (bf16[384,640]{1,0:T(8,128)(2,1)S(1)}, bf16[384,640]{1,0:T(8,128)(2,1)S(1)}, u32[]{:S(2)}, u32[]{:S(2)}) collective-permute-start(bf16[384,640]{1,0:T(8,128)(2,1)S(1)} %get-tuple-element.173), channel_id=1, source_target_pairs={{0,1},{1,0},{2,3},{3,2},{4,5},{5,4},{6,7},{7,6},{8,9},{9,8},{10,11... | collective-permute-start | bytes 1474568 | tf_op jit(solution)/shard_map/ppermute | solution.py:635
  287.9 8.7 %collective-permute-start.27 = (f32[24,1280]{1,0:T(8,128)S(1)}, f32[24,1280]{1,0:T(8,128)S(1)}, u32[]{:S(2)}, u32[]{:S(2)}) collective-permute-start(f32[24,1280]{1,0:T(8,128)S(1)} %pad_add_fusion), channel_id=1, source_target_pairs={{0,1},{1,0},{2,3},{3,2},{4,5},{5,4},{6,7},{7,6},{8,9},{9,8},{10,11... | collective-permute-start | bytes 368648 | tf_op jit(solution)/shard_map/ppermute | solution.py:635
  290.4 16.2 %collective-permute-start.46 = (bf16[80,640]{1,0:T(8,128)(2,1)S(1)}, bf16[80,640]{1,0:T(8,128)(2,1)S(1)}, u32[]{:S(2)}, u32[]{:S(2)}) collective-permute-start(bf16[80,640]{1,0:T(8,128)(2,1)S(1)} %add_convert_fusion.30), channel_id=1, source_target_pairs={{0,8},{1,9},{2,10},{3,11},{4,12},{5,13},{6,14},{7,15},{8,0},{9,1},... | collective-permute-start | bytes 307208 | tf_op jit(solution)/shard_map/ppermute | solution.py:635
  291.8 11.9 %collective-permute-start.36 = (bf16[112,640]{1,0:T(8,128)(2,1)S(1)}, bf16[112,640]{1,0:T(8,128)(2,1)S(1)}, u32[]{:S(2)}, u32[]{:S(2)}) collective-permute-start(bf16[112,640]{1,0:T(8,128)(2,1)S(1)} %add_convert_fusion.26), channel_id=1, source_target_pairs={{0,8},{1,9},{2,10},{3,11},{4,12},{5,13},{6,14},{7,15},{8,0},{9,1},... | collective-permute-start | bytes 430088 | tf_op jit(solution)/shard_map/ppermute | solution.py:635
  294.5 9.1 %collective-permute-start.54 = (bf16[192,640]{1,0:T(8,128)(2,1)S(1)}, bf16[192,640]{1,0:T(8,128)(2,1)S(1)}, u32[]{:S(2)}, u32[]{:S(2)}) collective-permute-start(bf16[192,640]{1,0:T(8,128)(2,1)S(1)} %get-tuple-element.181), channel_id=1, source_target_pairs={{0,4},{1,5},{2,6},{3,7},{4,0},{5,1},{6,2},{7,3},{8,12},{9,13},{10,... | collective-permute-start | bytes 737288 | tf_op jit(solution)/shard_map/ppermute | solution.py:635
  296.5 53.2 %collective-permute-start.32 = (bf16[1152,640]{1,0:T(8,128)(2,1)S(1)}, bf16[1152,640]{1,0:T(8,128)(2,1)S(1)}, u32[]{:S(2)}, u32[]{:S(2)}) collective-permute-start(bf16[1152,640]{1,0:T(8,128)(2,1)S(1)} %pad_maximum_fusion.refs_0_), channel_id=1, source_target_pairs={{0,1},{1,0},{2,3},{3,2},{4,5},{5,4},{6,7},{7,6},{8,9},{9,8},{10,11... | collective-permute-start | bytes 4423688 | tf_op jit(solution)/shard_map/ppermute | solution.py:635
  303.7 9.9 %collective-permute-start.55 = (bf16[96,640]{1,0:T(8,128)(2,1)S(1)}, bf16[96,640]{1,0:T(8,128)(2,1)S(1)}, u32[]{:S(2)}, u32[]{:S(2)}) collective-permute-start(bf16[96,640]{1,0:T(8,128)(2,1)S(1)} %get-tuple-element.191), channel_id=1, source_target_pairs={{0,2},{1,3},{2,0},{3,1},{4,6},{5,7},{6,4},{7,5},{8,10},{9,11},{10,... | collective-permute-start | bytes 368648 | tf_op jit(solution)/shard_map/ppermute | solution.py:635
  310.4 11.5 %collective-permute-start.47 = (bf16[160,640]{1,0:T(8,128)(2,1)S(1)}, bf16[160,640]{1,0:T(8,128)(2,1)S(1)}, u32[]{:S(2)}, u32[]{:S(2)}) collective-permute-start(bf16[160,640]{1,0:T(8,128)(2,1)S(1)} %pad_maximum_fusion.10), channel_id=1, source_target_pairs={{0,2},{1,3},{2,0},{3,1},{4,6},{5,7},{6,4},{7,5},{8,10},{9,11},{10,... | collective-permute-start | bytes 614408 | tf_op jit(solution)/shard_map/ppermute | solution.py:635
  313.6 9.6 %collective-permute-start.29 = (f32[24,1280]{1,0:T(8,128)S(1)}, f32[24,1280]{1,0:T(8,128)S(1)}, u32[]{:S(2)}, u32[]{:S(2)}) collective-permute-start(f32[24,1280]{1,0:T(8,128)S(1)} %add.318), channel_id=1, source_target_pairs={{0,2},{1,3},{2,0},{3,1},{4,6},{5,7},{6,4},{7,5},{8,10},{9,11},{10,... | collective-permute-start | bytes 368648 | tf_op jit(solution)/shard_map/ppermute | solution.py:635
  319.0 9.4 %collective-permute-start.38 = (bf16[224,640]{1,0:T(8,128)(2,1)S(1)}, bf16[224,640]{1,0:T(8,128)(2,1)S(1)}, u32[]{:S(2)}, u32[]{:S(2)}) collective-permute-start(bf16[224,640]{1,0:T(8,128)(2,1)S(1)} %pad_maximum_fusion.8), channel_id=1, source_target_pairs={{0,2},{1,3},{2,0},{3,1},{4,6},{5,7},{6,4},{7,5},{8,10},{9,11},{10,... | collective-permute-start | bytes 860168 | tf_op jit(solution)/shard_map/ppermute | solution.py:635
  323.2 30.3 %collective-permute-start.33 = (bf16[1152,640]{1,0:T(8,128)(2,1)S(1)}, bf16[1152,640]{1,0:T(8,128)(2,1)S(1)}, u32[]{:S(2)}, u32[]{:S(2)}) collective-permute-start(bf16[1152,640]{1,0:T(8,128)(2,1)S(1)} %pad_maximum_fusion.refs_0_), channel_id=1, source_target_pairs={{0,16},{16,0},{1,17},{17,1},{2,18},{18,2},{3,19},{19,3},{4,20},{20... | collective-permute-start | bytes 4423688 | tf_op jit(solution)/shard_map/ppermute | solution.py:631
  334.0 8.0 %collective-permute-start.48 = (bf16[320,640]{1,0:T(8,128)(2,1)S(1)}, bf16[320,640]{1,0:T(8,128)(2,1)S(1)}, u32[]{:S(2)}, u32[]{:S(2)}) collective-permute-start(bf16[320,640]{1,0:T(8,128)(2,1)S(1)} %pad_maximum_fusion.6), channel_id=1, source_target_pairs={{0,4},{1,5},{2,6},{3,7},{4,0},{5,1},{6,2},{7,3},{8,12},{9,13},{10,... | collective-permute-start | bytes 1228808 | tf_op jit(solution)/shard_map/ppermute | solution.py:635
  334.0 14.1 %collective-permute-start.39 = (bf16[448,640]{1,0:T(8,128)(2,1)S(1)}, bf16[448,640]{1,0:T(8,128)(2,1)S(1)}, u32[]{:S(2)}, u32[]{:S(2)}) collective-permute-start(bf16[448,640]{1,0:T(8,128)(2,1)S(1)} %pad_maximum_fusion.4), channel_id=1, source_target_pairs={{0,4},{1,5},{2,6},{3,7},{4,0},{5,1},{6,2},{7,3},{8,12},{9,13},{10,... | collective-permute-start | bytes 1720328 | tf_op jit(solution)/shard_map/ppermute | solution.py:635
  342.0 8.8 %collective-permute-start.59 = (bf16[192,640]{1,0:T(8,128)(2,1)S(1)}, bf16[192,640]{1,0:T(8,128)(2,1)S(1)}, u32[]{:S(2)}, u32[]{:S(2)}) collective-permute-start(bf16[192,640]{1,0:T(8,128)(2,1)S(1)} %pad_maximum_fusion.9), channel_id=1, source_target_pairs={{0,4},{1,5},{2,6},{3,7},{4,0},{5,1},{6,2},{7,3},{8,12},{9,13},{10,... | collective-permute-start | bytes 737288 | tf_op jit(solution)/shard_map/ppermute | solution.py:635
  348.1 12.3 %collective-permute-start.49 = (bf16[640,640]{1,0:T(8,128)(2,1)S(1)}, bf16[640,640]{1,0:T(8,128)(2,1)S(1)}, u32[]{:S(2)}, u32[]{:S(2)}) collective-permute-start(bf16[640,640]{1,0:T(8,128)(2,1)S(1)} %pad_maximum_fusion.2.refs_8_), channel_id=1, source_target_pairs={{0,1},{1,0},{2,3},{3,2},{4,5},{5,4},{6,7},{7,6},{8,9},{9,8},{10,11... | collective-permute-start | bytes 2457608 | tf_op jit(solution)/shard_map/ppermute | solution.py:635
  349.8 11.3 %collective-permute-start.50 = (bf16[640,640]{1,0:T(8,128)(2,1)S(1)}, bf16[640,640]{1,0:T(8,128)(2,1)}, u32[]{:S(2)}, u32[]{:S(2)}) collective-permute-start(bf16[640,640]{1,0:T(8,128)(2,1)S(1)} %pad_maximum_fusion.2.refs_8_), channel_id=1, source_target_pairs={{0,16},{16,0},{1,17},{17,1},{2,18},{18,2},{3,19},{19,3},{4,20},{20... | collective-permute-start | bytes 2457608 | tf_op jit(solution)/shard_map/ppermute | solution.py:631
  350.8 27.8 %collective-permute-start.40 = (bf16[896,640]{1,0:T(8,128)(2,1)S(1)}, bf16[896,640]{1,0:T(8,128)(2,1)S(1)}, u32[]{:S(2)}, u32[]{:S(2)}) collective-permute-start(bf16[896,640]{1,0:T(8,128)(2,1)S(1)} %pad_maximum_fusion.1.refs_4_), channel_id=1, source_target_pairs={{0,1},{1,0},{2,3},{3,2},{4,5},{5,4},{6,7},{7,6},{8,9},{9,8},{10,11... | collective-permute-start | bytes 3440648 | tf_op jit(solution)/shard_map/ppermute | solution.py:635
  353.6 24.4 %collective-permute-start.60 = (bf16[384,640]{1,0:T(8,128)(2,1)S(1)}, bf16[384,640]{1,0:T(8,128)(2,1)S(1)}, u32[]{:S(2)}, u32[]{:S(2)}) collective-permute-start(bf16[384,640]{1,0:T(8,128)(2,1)S(1)} %pad_maximum_fusion.5.refs_12_), channel_id=1, source_target_pairs={{0,1},{1,0},{2,3},{3,2},{4,5},{5,4},{6,7},{7,6},{8,9},{9,8},{10,11... | collective-permute-start | bytes 1474568 | tf_op jit(solution)/shard_map/ppermute | solution.py:635
  360.5 17.6 %collective-permute-start.61 = (bf16[384,640]{1,0:T(8,128)(2,1)S(1)}, bf16[384,640]{1,0:T(8,128)(2,1)S(1)}, u32[]{:S(2)}, u32[]{:S(2)}) collective-permute-start(bf16[384,640]{1,0:T(8,128)(2,1)S(1)} %pad_maximum_fusion.5.refs_12_), channel_id=1, source_target_pairs={{0,16},{16,0},{1,17},{17,1},{2,18},{18,2},{3,19},{19,3},{4,20},{20... | collective-permute-start | bytes 1474568 | tf_op jit(solution)/shard_map/ppermute | solution.py:631
  361.1 20.7 %collective-permute-start.34 = (bf16[1152,640]{1,0:T(8,128)(2,1)S(1)}, bf16[1152,640]{1,0:T(8,128)(2,1)S(1)}, u32[]{:S(2)}, u32[]{:S(2)}) collective-permute-start(bf16[1152,640]{1,0:T(8,128)(2,1)S(1)} %collective-permute-done.32.refs_1_), channel_id=1, source_target_pairs={{0,16},{16,0},{1,17},{17,1},{2,18},{18,2},{3,19},{19,3},{4,20},{20... | collective-permute-start | bytes 4423688 | tf_op jit(solution)/shard_map/ppermute | solution.py:631
  362.7 19.1 %collective-permute-start.41 = (bf16[896,640]{1,0:T(8,128)(2,1)S(1)}, bf16[896,640]{1,0:T(8,128)(2,1)S(1)}, u32[]{:S(2)}, u32[]{:S(2)}) collective-permute-start(bf16[896,640]{1,0:T(8,128)(2,1)S(1)} %pad_maximum_fusion.1.refs_4_), channel_id=1, source_target_pairs={{0,16},{16,0},{1,17},{17,1},{2,18},{18,2},{3,19},{19,3},{4,20},{20... | collective-permute-start | bytes 3440648 | tf_op jit(solution)/shard_map/ppermute | solution.py:631
  (63 other events, 616.8 us)

commit v3 on v2

--- a/solution.py
+++ b/solution.py
@@ -12,7 +12,8 @@
 DIL0 = 2
 DIL1 = 64
 EPS = 1e-05
-SCALE = 2
+SCALE = 100
+
 RIM0 = 8
 RIM1 = MID * DIL1
 F32 = jnp.float32
@@ -108,9 +109,32 @@
             at += inner
 
 
+def pack_kernel(*refs):
+    at = 0
+    for ref in refs[:-1]:
+        refs[-1][:, at : at + ref.shape[1]] = ref[...]
+        at += ref.shape[1]
+
+
+def first_norm(u, v):
+    normed, mean, scale = normed_of(u)
+    act, slope = gelu_parts(normed * v.fg + v.fs)
+    return act.astype(BF16), slope.astype(BF16), mean, scale
+
+
+def mid_norm(u, v):
+    normed, _, scale = normed_of(u + v.nb)
+    act, slope = gelu_parts(normed * v.mg + v.ms)
+    return act.astype(BF16), slope.astype(BF16), normed.astype(BF16), scale
+
+
+def my_row(c_ref, ref):
+    return ref[pl.ds(c_ref[0] * pl.num_programs(0) + pl.program_id(0), 1), :].astype(F32)
+
+
 def f0_kernel(c_ref, x_ref, xh_ref, rb_ref, ra_ref, v0_ref, v1_ref, nwo, nwx, cwo, cwx, wwo, wwx,
               mk, act0, slx0, mux0, rsx0, nn0, sln0, rsn0, st0, nc0, slc0, rsc0, oa0, out0,
-              act1, slx1, mux1, rsx1, nn1, sln1, rsn1, mid1,
+              act1, slx1, mux1, rsx1, nn1, sln1, rsn1, mid1, head1, tail1,
               nw0, cw0, ww0, nw1, act_s, n32, mid32, c32, r32, sems):
     low = c_ref[0] == 0
     first = pl.program_id(0) == 0
@@ -127,13 +151,8 @@
 
     lane = lax.broadcasted_iota(jnp.int32, (rows, LANES), 1)
     offset = jnp.where(lane < LIVE1, (lane - MID) * DIL0, (lane - LIVE1 - MID) * DIL1).astype(F32)
-    before, after = columns(rb_ref[0].astype(F32)), columns(ra_ref[0].astype(F32))
+    before, after = columns(my_row(c_ref, rb_ref)), columns(my_row(c_ref, ra_ref))
     mk[0] = jnp.where((offset >= -before) & (offset <= after), 1.0, 0.0)
-
-    def first_norm(u, v):
-        normed, mean, scale = normed_of(u)
-        act, slope = gelu_parts(normed * v.fg + v.fs)
-        return act.astype(BF16), slope.astype(BF16), mean, scale
 
     def stage1(r):
         s = pl.ds(r, 16)
@@ -153,11 +172,6 @@
         pick_wait(nwo, nw0, sems.at[0])
 
     n32[...] = dot_nn(act_s[...], nw0[...])
-
-    def mid_norm(u, v):
-        normed, _, scale = normed_of(u + v.nb)
-        act, slope = gelu_parts(normed * v.mg + v.ms)
-        return act.astype(BF16), slope.astype(BF16), normed.astype(BF16), scale
 
     def stage2(r):
         s = pl.ds(r, 32)
@@ -219,6 +233,8 @@
         rsn1[0, s, :] = scale
 
     chunks(rows, 32, stage6)
+    head1[...] = mid1[:, :RIM1]
+    tail1[...] = mid1[:, rows - RIM1 :]
 
 
 def near_taps(rows, inner, ext32, mk, dst):
@@ -249,7 +265,7 @@
 
 
 def f1_kernel(c_ref, mid_ref, up_ref, dn_ref, mk, v1_ref, cot_ref, cwo, cwx, wwo, wwx,
-              st1, oa1, cg1, vec, cw1, ww1, c32, e32, acc, sems):
+              st1, oa1, cg1, head, tail, vec, cw1, ww1, c32, e32, acc, sems):
     low = c_ref[0] == 0
     step = pl.program_id(0)
     rows, width = cot_ref.shape[1:]
@@ -291,6 +307,8 @@
     sums = summed_chunks(rows, 16, inner, 3, stage)
     for k in range(3):
         acc[k, :, :inner] += sums[k]
+    head[...] = cg1[:, :RIM1]
+    tail[...] = cg1[:, rows - RIM1 :]
 
     @pl.when(step == pl.num_programs(0) - 1)
     def _():
@@ -322,7 +340,7 @@
     logits = jnp.where(lane < vocab, lg[...], -1e30)
     top = jnp.max(logits, axis=-1, keepdims=True)
     log_total = top + jnp.log(jnp.sum(jnp.exp(logits - top), axis=-1, keepdims=True))
-    kind, weight = columns(rt_ref[0].astype(F32)), columns(lm_ref[0].astype(F32))
+    kind, weight = columns(my_row(c_ref, rt_ref)), columns(my_row(c_ref, lm_ref))
     onehot = jnp.where(lane == kind.astype(jnp.int32), weight, 0.0)
     acc[0] += fold8(onehot)
     acc[1] += fold8(onehot * (log_total - logits))
@@ -419,7 +437,7 @@
         vec[...] = jnp.sum(acc[...], axis=1)
 
 
-def last_kernel(c_ref, ig_ref, v_ref, slc, nc, rsc, wwo, wwx, cg, vec, ww, e32, acc, sems):
+def last_kernel(c_ref, ig_ref, v_ref, slc, nc, rsc, wwo, wwx, cg, head, tail, vec, ww, e32, acc, sems):
     low = c_ref[0] == 0
     step = pl.program_id(0)
     rows, width = ig_ref.shape[1:]
@@ -450,6 +468,8 @@
     sums = summed_chunks(rows, 16, inner, 3, stage)
     for k in range(3):
         acc[k, :, :inner] += sums[k]
+    head[0] = cg[0, : 2 * RIM0, :].astype(F32)[:RIM0].astype(BF16)
+    tail[0] = cg[0, rows - 2 * RIM0 :, :].astype(F32)[RIM0:].astype(BF16)
 
     @pl.when(step == pl.num_programs(0) - 1)
     def _():
@@ -509,56 +529,42 @@
     )(c_arr, *args)
 
 
-def unpack_kernel(c_ref, row_ref, sig_ref, *refs, groups, count, cols):
-    n = sum(len(g[2]) for g in groups)
-    ins, (conv, widen, narrow), (held, sems) = refs[:n], refs[n : n + 3], refs[n + 3 :]
+def unpack_kernel(c_ref, row_ref, sig_ref, *refs, sets, count, outs):
+    n = sum(len(g[1]) for g in sets)
+    ins, grads, (held, sem) = refs[:n], refs[n:-2], refs[-2:]
     s = pl.program_id(0)
-    half = conv.shape[1] // 2
-
-    def fetch(k):
-        _, base, numbers = groups[k]
+    half = held.shape[2] // 2
+
+    def fetch(numbers):
         arrays = [ins[i] for i in numbers]
-        rows = sum(a.shape[0] for a in arrays) // 2
-        shard = rows // count
+        shard = held.shape[1] // count
         first = 0
         for a in arrays:
             mine = 0 if first < count else 1
             for p in range(a.shape[0] // shard):
                 h = c_ref[0] if mine == 0 else 1 - c_ref[0]
-                to = pl.multiple_of(((first + p) % count ^ sig_ref[mine]) * shard + base, 16)
-                pltpu.make_async_copy(a.at[pl.ds(p * shard, shard)], held.at[h, pl.ds(to, shard)], sems.at[k]).start()
+                to = pl.multiple_of(((first + p) % count ^ sig_ref[mine]) * shard, 16)
+                pltpu.make_async_copy(a.at[pl.ds(p * shard, shard)], held.at[h, pl.ds(to, shard)], sem).start()
             first += a.shape[0] // shard
 
-    def landed(k):
-        _, base, numbers = groups[k]
-        rows = sum(ins[i].shape[0] for i in numbers) // 2
-        part = held.at[:, base : base + rows]
-        pltpu.make_async_copy(part, part, sems.at[k]).wait()
-
     @pl.when(s == 0)
     def _():
-        for step in (fetch, landed):
-            for k, (core, _, _) in enumerate(groups):
-                if core is None:
-                    step(k)
-                else:
-                    pl.when(c_ref[0] == core)(functools.partial(step, k))
-
-    def rows_of(step):
-        at = pl.multiple_of(row_ref[step], half)
-        return held[0, pl.ds(at, half), :].astype(F32), held[1, pl.ds(at, half), :].astype(F32)
-
-    @pl.when(s < TAPS)
-    def _():
-        conv[0, :half, :], conv[0, half:, :] = rows_of(s)
-
-    @pl.when((s >= TAPS) & (s < TAPS + cols))
-    def _():
-        widen[:half, :], widen[half:, :] = rows_of(s)
-
-    @pl.when(s >= TAPS + cols)
-    def _():
-        narrow[:half, :], narrow[half:, :] = rows_of(s)
+        for core, numbers in sets:
+            if core is None:
+                fetch(numbers)
+            else:
+                pl.when(c_ref[0] == core)(functools.partial(fetch, numbers))
+        pltpu.make_async_copy(held, held, sem).wait()
+
+    at = pl.multiple_of(row_ref[s], half)
+    for k, grad in enumerate(grads):
+        last = outs[k + 1] if k + 1 < len(outs) else None
+
+        @pl.when((s >= outs[k]) if last is None else (s >= outs[k]) & (s < last))
+        def _(grad=grad):
+            lead = (0,) if len(grad.shape) == 3 else ()
+            for h in range(2):
+                grad[(*lead, pl.ds(h * half, half), slice(None))] = held[h, pl.ds(at, half), :].astype(F32)
 
 
 def add_low(one, other):
@@ -573,58 +579,69 @@
     return lax.optimization_barrier((value, *after))[0]
 
 
-def dim_orders(count):
-    rest = list(range(2, count.bit_length() - 1))
-    return [[0, *rest[:1], 1, *rest[1:]], [1, 0, *rest]]
+class Route:
+    def __init__(self, orders, whole, sec, at, count):
+        self.split = len(orders[0]) - whole
+        self.steps, signs = [], [0, 0]
+        for k in range(len(orders[0])):
+            pairs = [(s * count + d, s * count + (d ^ (1 << orders[s][k]))) for s in range(2) for d in range(count)]
+            place = [(at >> orders[s][k]) & 1 for s in range(2)]
+            self.steps.append((pairs, jnp.where(sec == 0, place[0], place[1])))
+            if k < self.split:
+                signs = [g + (p << (self.split - 1 - k)) for g, p in zip(signs, place)]
+        signs = jnp.where(sec == 0, jnp.stack(signs), jnp.stack(signs[::-1]))
+        self.signs = signs.astype(jnp.int32)
+        self.shards = 1 << self.split
 
 
 class Chain:
-    def __init__(self, keep, send, steps):
-        self.keep, self.send, self.steps = keep, send, steps
+    def __init__(self, keep, send, route):
+        self.keep, self.send, self.route = keep, [send], route
         self.at = -1
-        self.pieces = None
-
-    def ready(self, *after):
-        bits = len(self.steps)
-        if after:
-            self.come = tie(self.come, *after)
-            if self.pieces is not None:
-                self.pieces = (self.pieces[0], self.come)
-        if 0 <= self.at < bits:
-            bit = self.steps[self.at][1]
+        self.fly, self.pieces = [], []
+        self.last = len(route.steps) + route.split
+
+    def ready(self):
+        bits, split = len(self.route.steps), self.route.split
+        if 0 <= self.at < split:
+            (come,) = self.fly
+            bit = self.route.steps[self.at][1]
             rows = self.keep.shape[0] // 2
-            self.send = add_low(part(self.keep, 1 - bit, rows), part(self.come, 1 - bit, rows))
-            self.keep = add_low(part(self.keep, bit, rows), part(self.come, bit, rows))
-        elif self.at == bits:
-            self.send = add_low(self.keep, self.come)
+            self.send = [add_low(part(self.keep, 1 - bit, rows), part(come, 1 - bit, rows))]
+            self.keep = add_low(part(self.keep, bit, rows), part(come, bit, rows))
+        elif split <= self.at <= bits:
+            self.keep = add_low(self.keep, self.fly[0])
+            self.pieces = self.send = [self.keep]
         elif self.at > bits:
-            self.send = jnp.concatenate(self.pieces, axis=0)
-        return self.send
-
-    def go(self, *after):
-        send = tie(self.send, *after) if after else self.send
-        bits = len(self.steps)
+            self.pieces = self.send = [jnp.concatenate(self.pieces + self.fly, axis=0)]
+        return tuple(self.send)
+
+    def go(self):
+        bits = len(self.route.steps)
         if self.at < 0:
-            self.come = swapped(send)
-        elif self.at < bits:
-            self.come = hop(send, self.steps[self.at][0])
+            self.fly = [swapped(v) for v in self.send]
         else:
-            self.come = hop(send, self.steps[2 * bits - 1 - self.at][0])
-            self.pieces = (send, self.come)
+            step = self.at if self.at < bits else self.route.split - 1 - (self.at - bits)
+            self.fly = [hop(v, self.route.steps[step][0]) for v in self.send]
         self.at += 1
-        return self.come
-
-    def step(self, *after):
-        self.ready()
-        return self.go(*after)
 
     def done(self):
-        return self.at == 2 * len(self.steps)
+        return self.at == self.last
 
     def finish(self):
         while not self.done():
-            self.step()
-        return [*self.pieces, *(swapped(p) for p in self.pieces)]
+            self.ready()
+            self.go()
+        pieces = self.pieces + self.fly
+        return pieces + [swapped(p) for p in pieces]
+
+
+def meet(chains, *values):
+    fly = [v for g in chains for v in g.fly]
+    out = list(lax.optimization_barrier((*fly, *values)))
+    for g in chains:
+        g.fly, out = out[: len(g.fly)], out[len(g.fly) :]
+    return out[0] if len(out) == 1 else out
 
 
 def swapped(v):
@@ -652,9 +669,10 @@
 
     nwo, cwo, wwo = narrow_weight[0], conv_weight[0], widen_weight[0]
     nwx, cwx, wwx = swapped(nwo), swapped(cwo), swapped(wwo)
-    packed = jnp.concatenate(
-        (first_gain, first_shift, widen_bias, narrow_bias, middle_gain, middle_shift, conv_bias, last_gain, last_shift), axis=1
-    )
+    vectors = (first_gain, first_shift, widen_bias, narrow_bias, middle_gain, middle_shift, conv_bias, last_gain, last_shift)
+    packed = pl.pallas_call(
+        pack_kernel, out_shape=jax.ShapeDtypeStruct((1, sum(v.shape[1] for v in vectors)), F32)
+    )(*vectors)
     packed_x = swapped(packed)
     v0 = jnp.where(low, packed, packed_x)
     v1 = jnp.where(low, packed_x, packed)
@@ -663,7 +681,6 @@
     xh = jnp.concatenate(
         [lax.ppermute(x_own[:, -RIM0:], "dp", ahead), lax.ppermute(x_own[:, :RIM0], "dp", behind)], axis=1
     )
-    before, after, kinds, scored = (v[:, None, :] for v in (residues_before, residues_after, residue_types, loss_mask))
 
     def mine(n, w):
         return pl.BlockSpec((1, n, w), lambda i, c: (c[0] * own + i, 0, 0))
@@ -700,14 +717,18 @@
     mm = 2 * own * rows * width * inner
     wide, thin, one, masks, taps = o_each(width), o_each(inner), o_each(1, F32), o_each(LANES, F32), o_each(TAPS * inner)
     e_wide, e_thin, e_one, e_masks = wide[1], thin[1], one[1], masks[1]
-    id_spec = mine(1, rows)
+    id_spec = whole(micro, rows)
+    def o_rim(n):
+        return (jax.ShapeDtypeStruct((own, n, inner), BF16), each(n, inner))
+
     (mk, act0, slx0, mux0, rsx0, nn0, sln0, rsn0, st0, nc0, slc0, rsc0, oa0, out0,
-     act1, slx1, mux1, rsx1, nn1, sln1, rsn1, mid1) = call(
+     act1, slx1, mux1, rsx1, nn1, sln1, rsn1, mid1, head1, tail1) = call(
         f0_kernel,
         c_arr,
-        (block_input, xh, before, after, v0, v1, nwo, nwx, cwo, cwx, wwo, wwx),
+        (block_input, xh, residues_before, residues_after, v0, v1, nwo, nwx, cwo, cwx, wwo, wwx),
         [mine(rows, width), each(2 * RIM0, width), id_spec, id_spec, vspec, vspec] + [ANY] * 6,
-        [masks, wide, wide, one, one, thin, thin, one, taps, thin, thin, one, thin, wide, wide, wide, one, one, thin, thin, one, thin],
+        [masks, wide, wide, one, one, thin, thin, one, taps, thin, thin, one, thin, wide,
+         wide, wide, one, one, thin, thin, one, thin, o_rim(RIM1), o_rim(RIM1)],
         [
             pltpu.VMEM((width, inner), BF16),
             pltpu.VMEM((TAPS, inner, inner), BF16),
@@ -720,17 +741,17 @@
             pltpu.VMEM((rows, width), F32),
             dma((4,)),
         ],
-        5.5 * mm, 40_000_000, own * rows * 8 * width,
-    )
-
-    up1 = lax.ppermute(mid1[:, -RIM1:], "dp", ahead)
-    dn1 = lax.ppermute(mid1[:, :RIM1], "dp", behind)
-    st1, oa1, cg1, vec1 = call(
+        5.5 * mm, 40_000_000,
+    )
+
+    up1 = lax.ppermute(tail1, "dp", ahead)
+    dn1 = lax.ppermute(head1, "dp", behind)
+    st1, oa1, cg1, rim_dn, rim_up, vec1 = call(
         f1_kernel,
         c_arr,
         (mid1, up1, dn1, mk, v1, output_cotangent, cwo, cwx, wwo, wwx),
         [e_thin, each(RIM1, inner), each(RIM1, inner), e_masks, vspec, mine(rows, width)] + [ANY] * 4,
-        [taps, thin, thin, o_vec(4, width)],
+        [taps, thin, thin, o_rim(RIM1), o_rim(RIM1), o_vec(4, width)],
         [
             pltpu.VMEM((TAPS, inner, inner), BF16),
             pltpu.VMEM((inner, width), BF16),
@@ -739,31 +760,80 @@
             pltpu.VMEM((4, 8, width), F32),
             dma((2,)),
         ],
-        3.5 * mm, 20_000_000, own * rows * 2 * inner,
-    )
-
-    rim_up, rim_dn = cg1[:, -RIM1:], cg1[:, :RIM1]
+        3.5 * mm, 20_000_000,
+    )
+
     upg = lax.ppermute(rim_up, "dp", ahead)
     dng = lax.ppermute(rim_dn, "dp", behind)
 
-    orders = dim_orders(count)
-    steps, signs = [], [0, 0]
-    bits = len(orders[0])
-    for k in range(bits):
-        pairs = [(s * count + d, s * count + (d ^ (1 << orders[s][k]))) for s in range(2) for d in range(count)]
-        place = [(at >> orders[s][k]) & 1 for s in range(2)]
-        steps.append((pairs, jnp.where(low, place[0], place[1])))
-        signs = [g + (p << (bits - 1 - k)) for g, p in zip(signs, place)]
+    rest = list(range(2, count.bit_length() - 1))
+    big = Route([[0, *rest[:1], 1, *rest[1:]], [1, 0, *rest]], 1, sec, at, count)
     unit = 16 * count
     terms = functools.partial(weight_terms, own=own, tile=inner, unit=unit)
 
-    g1 = Chain(*terms(tie(c_arr, rim_up, rim_dn), [(oa1, output_cotangent), (st1, cg1)]), steps)
-    g1_come = g1.step()
+    g1_terms = terms(tie(c_arr, rim_up, rim_dn), [(oa1, output_cotangent), (st1, cg1)])
+    upg, dng, *g1_terms = meet([], upg, dng, *g1_terms)
+    g1 = Chain(*g1_terms, big)
+    g1.go()
+    def mid_scratch(ext):
+        return [
+            pltpu.VMEM((inner, TAPS * inner), BF16),
+            *ext,
+            pltpu.VMEM((rows, TAPS * inner), BF16),
+            pltpu.VMEM((rows, inner), F32),
+            pltpu.VMEM((3, 8, inner), F32),
+            dma((TAPS,)),
+        ]
+
+    def first(c, block, ng, v, grad, grad_spec, slx, src, src_spec, mux, rsx):
+        return call(
+            functools.partial(first_kernel, block=block),
+            c,
+            (ng, v, grad, slx, src, mux, rsx, nwo, nwx),
+            [e_thin, vspec, grad_spec, e_wide, src_spec, e_one, e_one, ANY, ANY],
+            [wide, o_vec(2, width)],
+            [pltpu.VMEM((width, inner), BF16), pltpu.VMEM((rows, width), F32), pltpu.VMEM((2, 8, width), F32), dma((1,))],
+            1.3 * mm, 10_000_000,
+        )
+
+    ng1, vecm1 = call(
+        functools.partial(mid_kernel, far=True, block=1),
+        c_arr,
+        (cg1, upg, dng, mk, v1, sln1, nn1, rsn1, cwo, cwx),
+        [e_thin, each(RIM1, inner), each(RIM1, inner), e_masks, vspec, e_thin, e_thin, e_one, ANY, ANY],
+        [thin, o_vec(3, inner)],
+        mid_scratch([]),
+        2.6 * mm, 10_000_000,
+    )
+    ng1 = meet([g1], ng1)
+    c_n1 = tie(c_arr, *g1.ready())
+    g1.go()
+    ig1, vecf1 = first(c_n1, 1, ng1, v1, output_cotangent, mine(rows, width), slx1, out0, e_wide, mux1, rsx1)
+    cg0, rim_dn0, rim_up0, vecl0 = call(
+        last_kernel,
+        c_arr,
+        (ig1, v0, slc0, nc0, rsc0, wwo, wwx),
+        [e_wide, vspec, e_thin, e_thin, e_one, ANY, ANY],
+        [thin, o_rim(RIM0), o_rim(RIM0), o_vec(4, width)],
+        [pltpu.VMEM((inner, width), BF16), pltpu.VMEM((rows, inner), F32), pltpu.VMEM((4, 8, width), F32), dma((1,))],
+        1.3 * mm, 8_000_000,
+    )
+    cg0, rim_dn0, rim_up0 = meet([g1], cg0, rim_dn0, rim_up0)
+    up0, dn0 = lax.ppermute(rim_up0, "dp", ahead), lax.ppermute(rim_dn0, "dp", behind)
+    g3_terms = terms(tie(c_arr, *g1.ready(), rim_up0, rim_dn0), [(oa0, ig1), (st0, cg0)])
+    g1.go()
+    up0, dn0, *g3_terms = meet([g1], up0, dn0, *g3_terms)
+    rim0 = jnp.concatenate([up0, dn0], axis=1)
+    g3 = Chain(*g3_terms, big)
+    g3.go()
+    g1.ready()
+    g1.go()
+
     head = jnp.pad(head_weight, ((0, 0), (0, LANES - vocab)))
     out1, tot = call(
         functools.partial(o1_kernel, vocab=vocab),
-        tie(c_arr, g1.keep),
-        (out0, oa1, kinds, scored, v1, head, wwo, wwx),
+        tie(c_arr, g3.keep, *g1.send),
+        (out0, oa1, residue_types, loss_mask, v1, head, wwo, wwx),
         [e_wide, e_thin, id_spec, id_spec, vspec, whole(width, LANES), ANY, ANY],
         [wide, o_vec(2, LANES)],
         [
@@ -776,60 +846,18 @@
         1.2 * mm, 8_000_000,
     )
 
-    def mid_scratch(ext):
-        return [
-            pltpu.VMEM((inner, TAPS * inner), BF16),
-            *ext,
-            pltpu.VMEM((rows, TAPS * inner), BF16),
-            pltpu.VMEM((rows, inner), F32),
-            pltpu.VMEM((3, 8, inner), F32),
-            dma((TAPS,)),
-        ]
-
-    def first(c, block, ng, v, grad, grad_spec, slx, src, src_spec, mux, rsx):
-        return call(
-            functools.partial(first_kernel, block=block),
-            c,
-            (ng, v, grad, slx, src, mux, rsx, nwo, nwx),
-            [e_thin, vspec, grad_spec, e_wide, src_spec, e_one, e_one, ANY, ANY],
-            [wide, o_vec(2, width)],
-            [pltpu.VMEM((width, inner), BF16), pltpu.VMEM((rows, width), F32), pltpu.VMEM((2, 8, width), F32), dma((1,))],
-            1.3 * mm, 10_000_000,
-        )
-
-    ng1, vecm1 = call(
-        functools.partial(mid_kernel, far=True, block=1),
-        tie(c_arr, tot, g1.ready()),
-        (cg1, upg, dng, mk, v1, sln1, nn1, rsn1, cwo, cwx),
-        [e_thin, each(RIM1, inner), each(RIM1, inner), e_masks, vspec, e_thin, e_thin, e_one, ANY, ANY],
-        [thin, o_vec(3, inner)],
-        mid_scratch([]),
-        2.6 * mm, 10_000_000,
-    )
-    r1 = g1.go(upg, dng, tot)
-    ig1, vecf1 = first(c_arr, 1, ng1, v1, output_cotangent, mine(rows, width), slx1, out0, e_wide, mux1, rsx1)
-    cg0, vecl0 = call(
-        last_kernel,
-        tie(c_arr, g1.ready(ig1)),
-        (ig1, v0, slc0, nc0, rsc0, wwo, wwx),
-        [e_wide, vspec, e_thin, e_thin, e_one, ANY, ANY],
-        [thin, o_vec(4, width)],
-        [pltpu.VMEM((inner, width), BF16), pltpu.VMEM((rows, inner), F32), pltpu.VMEM((4, 8, width), F32), dma((1,))],
-        1.3 * mm, 8_000_000,
-    )
-    g1.go()
-    rim_up0, rim_dn0 = cg0[:, -RIM0:], cg0[:, :RIM0]
-    rim0 = jnp.concatenate([lax.ppermute(rim_up0, "dp", ahead), lax.ppermute(rim_dn0, "dp", behind)], axis=1)
-    g3 = Chain(*terms(tie(c_arr, g1.ready(rim_up0), rim_up0, rim_dn0), [(st0, cg0)]), steps)
-    g1.go()
-    g3.step()
-    g2 = Chain(*terms(tie(c_arr, g1.ready(g3.keep), g3.keep), [(act1, ng1), (oa0, ig1)]), steps)
-    g1.go()
-    g3.ready(g2.keep)
-    g2.step()
+    def handed(in0, in1):
+        return jnp.where(low, in0, in1), swapped(jnp.where(low, in1, in0))
+
+    def gathered(keep, come):
+        return jnp.concatenate([jnp.where(low, keep, come), jnp.where(low, come, keep)], axis=0)[None]
+
+    held_out = handed(out0, out1)
+    tot = meet([g1, g3], tot)
+    g1.ready()
     ng0, vecm0 = call(
         functools.partial(mid_kernel, far=False, block=0),
-        tie(c_arr, g1.ready(g2.keep), g3.send, g2.keep),
+        tie(c_arr, *g3.ready(), *g1.send),
         (cg0, rim0, mk, v0, sln0, nn0, rsn0, cwo, cwx),
         [e_thin, each(2 * RIM0, inner), e_masks, vspec, e_thin, e_thin, e_one, ANY, ANY],
         [thin, o_vec(3, inner)],
@@ -838,63 +866,18 @@
     )
     g1.go()
     g3.go()
-    g4 = Chain(*terms(tie(c_arr, g1.ready(ng0), g3.ready(ng0), g2.ready(ng0)), [(act0, ng0)]), steps)
+    ng0 = meet([g1], ng0)
+    g4_terms = terms(tie(c_arr, *g1.ready()), [(act1, ng1), (act0, ng0)])
+    g1.go()
+    g4_terms = meet([g1, g3], *g4_terms)
+    g4 = Chain(*g4_terms, big)
+    g4.go()
+    ig0, vecf0 = first(
+        tie(c_arr, *g1.ready(), *g3.ready()), 0, ng0, v0, ig1, e_wide, slx0, block_input, mine(rows, width), mux0, rsx0
+    )
     g1.go()
     g3.go()
-    g2.go()
-    g4.step()
-    ig0, vecf0 = first(
-        tie(c_arr, g4.keep, g1.ready(g4.keep), g3.ready(g4.keep), g2.ready(g4.keep)),
-        0, ng0, v0, ig1, e_wide, slx0, block_input, mine(rows, width), mux0, rsx0,
-    )
-    g1.go()
-    g3.go()
-    g2.go()
-    while not all(g.done() for g in (g1, g3, g2, g4)):
-        for g in (g1, g3, g2, g4):
-            if not g.done():
-                g.step()
-
-    parts, groups, base = [], [], 0
-    for core, chain in ((1, g1), (0, g3), (None, g2), (0, g4)):
-        pieces = chain.finish()
-        height = sum(p.shape[0] for p in pieces) // 2
-        if chain is g3:
-            base = 0
-        groups.append((core, base, list(range(len(parts), len(parts) + len(pieces)))))
-        base += height
-        if chain is g3:
-            base = max(base, groups[0][1] + sum(p.shape[0] for p in parts[:4]) // 2)
-        parts += pieces
-    half = inner // 2
-    cols = width // inner
-    at2, at4 = groups[2][1], groups[3][1]
-    conv_rows = [k * half for k in range(TAPS)]
-    row0 = conv_rows + [at2 + (cols + k) * half for k in range(cols)] + [at4 + k * half for k in range(cols)]
-    row1 = [r + cols * half for r in conv_rows] + [k * half for k in range(cols)] + [at2 + k * half for k in range(cols)]
-    row_arr = jnp.where(low, jnp.array(row0, jnp.int32), jnp.array(row1, jnp.int32))
-    sig_arr = jnp.where(low, jnp.stack(signs), jnp.stack(signs[::-1])).astype(jnp.int32)
-    conv_grad, widen_grad, narrow_grad = pl.pallas_call(
-        functools.partial(unpack_kernel, groups=groups, count=count, cols=cols),
-        grid_spec=pltpu.PrefetchScalarGridSpec(
-            num_scalar_prefetch=3,
-            grid=(TAPS + 2 * cols,),
-            in_specs=[ANY] * len(parts),
-            out_specs=[
-                pl.BlockSpec((1, inner, inner), lambda s, *_: (jnp.minimum(s, TAPS - 1), 0, 0)),
-                pl.BlockSpec((inner, inner), lambda s, *_: (0, jnp.clip(s - TAPS, 0, cols - 1))),
-                pl.BlockSpec((inner, inner), lambda s, *_: (jnp.clip(s - TAPS - cols, 0, cols - 1), 0)),
-            ],
-            scratch_shapes=[pltpu.VMEM((2, base, inner), BF16), dma((len(groups),))],
-        ),
-        out_shape=[
-            jax.ShapeDtypeStruct((TAPS, inner, inner), F32),
-            jax.ShapeDtypeStruct((inner, width), F32),
-            jax.ShapeDtypeStruct((width, inner), F32),
-        ],
-        compiler_params=pltpu.CompilerParams(vmem_limit_bytes=VMEM_LIMIT),
-        cost_estimate=pl.CostEstimate(flops=0, bytes_accessed=25_000_000, transcendentals=0),
-    )(c_arr, row_arr, sig_arr, *parts)
+    ig0, vecf0 = meet([g1, g3, g4], ig0, vecf0)
 
     def padded(v):
         return jnp.pad(v, ((0, 0), (0, width - v.shape[1])))
@@ -903,22 +886,62 @@
     small = jnp.concatenate(terms_small, axis=0)
     small = jnp.pad(small, ((0, -small.shape[0] % 8), (0, 0)))
     small = small + swapped(small)
-    for pairs, _ in steps:
+    for pairs, _ in big.steps:
         small = small + hop(small, pairs)
     s1, sm1, sf1, sl0, sm0, sf0, st = jnp.split(small, [4, 7, 9, 13, 16, 18], axis=0)
     type_total, loss_total = st[0, :vocab], st[1, :vocab]
 
+    half = inner // 2
+    cols = width // inner
+
+    block_outputs, input_grads = gathered(*held_out), gathered(*handed(ig0, ig1))
+
+    def unpacked(c, chains, row_arr, out_specs, out_shape, firsts):
+        parts, sets = [], []
+        for core, chain in chains:
+            pieces = chain.finish()
+            sets.append((core, list(range(len(parts), len(parts) + len(pieces)))))
+            parts += pieces
+        return pl.pallas_call(
+            functools.partial(unpack_kernel, sets=sets, count=chain.route.shards, outs=firsts),
+            grid_spec=pltpu.PrefetchScalarGridSpec(
+                num_scalar_prefetch=3,
+                grid=(row_arr.shape[0],),
+                in_specs=[ANY] * len(parts),
+                out_specs=out_specs,
+                scratch_shapes=[pltpu.VMEM((2, sum(p.shape[0] for p in pieces) // 2, inner), BF16), dma(())],
+            ),
+            out_shape=out_shape,
+            compiler_params=pltpu.CompilerParams(vmem_limit_bytes=VMEM_LIMIT),
+            cost_estimate=pl.CostEstimate(flops=0, bytes_accessed=5_000_000, transcendentals=0),
+        )(c, row_arr, chain.route.signs, *parts)
+
+    widen_grad, conv_grad = unpacked(
+        tie(c_arr, block_outputs, input_grads),
+        [(1, g1), (0, g3)],
+        jnp.arange(cols + TAPS, dtype=jnp.int32) * half,
+        [
+            pl.BlockSpec((inner, inner), lambda s, *_: (0, jnp.minimum(s, cols - 1))),
+            pl.BlockSpec((1, inner, inner), lambda s, *_: (jnp.maximum(s - cols, 0), 0, 0)),
+        ],
+        [jax.ShapeDtypeStruct((inner, width), F32), jax.ShapeDtypeStruct((TAPS, inner, inner), F32)],
+        [0, cols],
+    )
+    (narrow_grad,) = unpacked(
+        tie(c_arr, conv_grad),
+        [(None, g4)],
+        (jnp.arange(cols, dtype=jnp.int32) + jnp.where(low, cols, 0).astype(jnp.int32)) * half,
+        [pl.BlockSpec((inner, inner), lambda s, *_: (s, 0))],
+        [jax.ShapeDtypeStruct((width, inner), F32)],
+        [0],
+    )
+
     def sel(in0, in1, n=width):
         return jnp.where(low, in0, in1)[None, :n]
 
-    def gathered(in0, in1):
-        keep = jnp.where(low, in0, in1)
-        come = swapped(jnp.where(low, in1, in0))
-        return jnp.concatenate([jnp.where(low, keep, come), jnp.where(low, come, keep)], axis=0)[None]
-
     return (
-        gathered(out0, out1),
-        gathered(ig0, ig1),
+        block_outputs,
+        input_grads,
         sel(sf0[0], sf1[0]),
         sel(sf0[1], sf1[1]),
         narrow_grad[None],

time: 403 us -> 354 us (0.88); the launches traced: 396 us -> 353 us
  starting transfers between devices: 72.7 us -> 50.4 us
  local copies, waits for them, and re-layouts: 23.1 us -> 9.8 us
  other arithmetic: 41.5 us -> 33.8 us
    ppermute x36 -> x25, starting transfers between devices: 46.6 us -> 23.6 us  [hop(): return lax.ppermute(v, ('section', 'dp'), pairs)]
    ppermute x1, waiting for transfers between devices: 6.13 us -> 0.01 us  [body(): lax.ppermute(rim_up0, 'dp', ahead)]
    ppermute x36 -> x25, waiting for transfers between devices: 70 us -> 75.6 us  [hop(): return lax.ppermute(v, ('section', 'dp'), pairs)]
    convert_element_type x20 -> x15, other arithmetic: 21.5 us -> 16.3 us  [add_low(): return (one.astype(F32) + other.astype(F32)).astype(BF16)]
    ppermute x1, starting transfers between devices: 0.2 us -> 5.06 us  [body(): lax.ppermute(rim_dn0, 'dp', behind)]
    unnamed x105 -> x81, local copies, waits for them, and re-layouts: 11.5 us -> 6.94 us
    slice x3 -> x0, local copies, waits for them, and re-layouts: 4.27 us -> none  [the longest x1 2.23 us: body(): rim_up, rim_dn = (cg1[:, -RIM1:], cg1[:, :RIM1])]
    pallas_call x1 -> x3, Pallas kernels: 11.9 us -> 14.9 us  [the longest x2 13.4 us: unpacked(): pl.pallas_call(functools.partial(unpack_kernel, sets=sets, count=chain.ro...]
  transfers between devices with their start and end apart: 63 -> 49, of which waited for: 23 -> 21; matrix products, arithmetic and copies ran while one was open for 13% -> 8% of each run, Pallas kernels for 18% -> 29%
where the time goes in v3:
time: 354 us; the launch traced here: 353 us
  Pallas kernels  153 us (43%)
  waiting for transfers between devices  104 us (29%)
  starting transfers between devices  50.4 us (14%)
  other arithmetic  33.8 us (10%)
  local copies, waits for them, and re-layouts  9.8 us (3%)
    pallas_call x8, Pallas kernels, call(): pl.pallas_call(kernel, grid_spec=pltpu.PrefetchScalarGridSpec(num_scalar_...  107 us
    ppermute x25, waiting for transfers between devices, hop(): return lax.ppermute(v, ('section', 'dp'), pairs)  75.6 us
    pallas_call x3, Pallas kernels, weight_terms(): pl.pallas_call(kernel, grid_spec=pltpu.PrefetchScalarGridSpec(num_scalar_...  31.1 us
    ppermute x25, starting transfers between devices, hop(): return lax.ppermute(v, ('section', 'dp'), pairs)  23.6 us
    ppermute x1, waiting for transfers between devices, body(): up1 = lax.ppermute(tail1, 'dp', ahead)  16.3 us
    convert_element_type x15, other arithmetic, add_low(): return (one.astype(F32) + other.astype(F32)).astype(BF16)  16.3 us
    pallas_call x2, Pallas kernels, unpacked(): pl.pallas_call(functools.partial(unpack_kernel, sets=sets, count=chain.ro...  13.4 us
  transfers between devices with their start and end apart: 49, of which 21 were waited for; matrix products, arithmetic and copies ran while one was open for 8% of the time, Pallas kernels for 29%

profile of v3, /device:TPU:0, one launch (start us, length us, event | category | flops | bytes accessed | tf_op | source)
XLA Modules:
  0.0 352.6 jit_solution(16157453516669984275)
XLA Ops:
  3.5 3.0 collective-permute-start
  6.5 4.1 %collective-permute-start.1 = (bf16[3,8,1280]{2,1,0:T(8,128)(2,1)S(1)}, bf16[3,8,1280]{2,1,0:T(8,128)(2,1)S(1)}, u32[]{:S(2)}, u32[]{:S(2)}) collective-permute-start(bf16[3,8,1280]{2,1,0:T(8,128)(2,1)S(1)} %get-tuple-element.205), channel_id=1, source_target_pairs={{1,0},{2,1},{3,2},{4,3},{5,4},{6,5},{7,6},{8,7},{9,8},{10,9},{11,1... | collective-permute-start | bytes 184328 | tf_op jit(solution)/shard_map/ppermute | solution.py:682
  14.3 2.3 collective-permute-done.3.nwx
  17.8 29.6 %shard_map.307 = (f32[3,256,128]{2,1,0:T(8,128)}, bf16[3,256,1280]{2,1,0:T(8,128)(2,1)}, bf16[3,256,1280]{2,1,0:T(8,128)(2,1)}, f32[3,256,1]{2,1,0:T(8,128)}, f3...) custom-call(s32[1]{0:T(128)} %bitcast.c_ref, ...), custom_call_target="tpu_custom_call" | custom-call | flops 69206016 | bytes 400000 | tf_op jit(solution)/shard_map/pallas_call | solution.py:695
  47.5 5.6 %collective-permute-start.7 = (bf16[3,128,640]{2,1,0:T(8,128)(2,1)}, bf16[3,128,640]{2,1,0:T(8,128)(2,1)S(1)}, u32[]{:S(2)}, u32[]{:S(2)}) collective-permute-start(bf16[3,128,640]{2,1,0:T(8,128)(2,1)} %get-tuple-element.109), channel_id=1, source_target_pairs={{1,0},{2,1},{3,2},{4,3},{5,4},{6,5},{7,6},{8,7},{9,8},{10,9},{11,1... | collective-permute-start | bytes 1474568 | tf_op jit(solution)/shard_map/ppermute | solution.py:748
  53.1 16.3 %collective-permute-done.6.up_ref = bf16[3,128,640]{2,1,0:T(8,128)(2,1)S(1)} collective-permute-done((bf16[3,128,640]{2,1,0:T(8,128)(2,1)}, bf16[3,128,640]{2,1,0:T(8,128)(2,1)S(1)}, u32[]{:S(2)}, u32[]{:S(2)}) %collective-permute-start.6) | collective-permute-done | bytes 491552 | tf_op jit(solution)/shard_map/ppermute | solution.py:747
  70.8 17.0 %shard_map.308 = (bf16[3,256,3200]{2,1,0:T(8,128)(2,1)}, bf16[3,256,640]{2,1,0:T(8,128)(2,1)}, bf16[3,256,640]{2,1,0:T(8,128)(2,1)}, bf16[3,128,640]{2,1,0:T(8,1...) custom-call(s32[1]{0:T(128)} %bitcast.c_ref, bf16[3,256,640]{2,1,0:T(8,128)(2,1)} %get-tuple-element.107.mid_ref, ...), custom_call_target="tpu_custom_call" | custom-call | flops 44040192 | bytes 200000 | tf_op jit(solution)/shard_map/pallas_call | solution.py:695
  87.7 2.1 collective-permute-start.8
  89.8 3.6 %collective-permute-start.9 = (bf16[3,128,640]{2,1,0:T(8,128)(2,1)}, bf16[3,128,640]{2,1,0:T(8,128)(2,1)S(1)}, u32[]{:S(2)}, u32[]{:S(2)}) collective-permute-start(bf16[3,128,640]{2,1,0:T(8,128)(2,1)} %get-tuple-element.112), channel_id=1, source_target_pairs={{1,0},{2,1},{3,2},{4,3},{5,4},{6,5},{7,6},{8,7},{9,8},{10,9},{11,1... | collective-permute-start | bytes 1474568 | tf_op jit(solution)/shard_map/ppermute | solution.py:767
  93.4 11.6 %shard_map.309 = (bf16[2304,640]{1,0:T(8,128)(2,1)}, bf16[2304,640]{1,0:T(8,128)(2,1)}) custom-call(s32[1]{0:T(128)} %bitcast.c_ref, bf16[3,256,640]{2,1,0:T(8,128)(2,1)} %get-tuple-element.114.refs_0_.oa_ref, bf16[6,256,1280]{2,1,0:T(8,128)(2,1)} %grad.1, bf16[3,256,3200]{2,1,0:T(8,128)(2,1)} %get-tuple-element.115.refs_2_, ...), custom_call_target="tpu_custom_call" | custom-call | flops 44040192 | bytes 58982 | tf_op jit(solution)/shard_map/pallas_call | solution.py:515
  105.0 5.9 %collective-permute-done.8.refs_0_ = bf16[3,128,640]{2,1,0:T(8,128)(2,1)S(1)} collective-permute-done((bf16[3,128,640]{2,1,0:T(8,128)(2,1)}, bf16[3,128,640]{2,1,0:T(8,128)(2,1)S(1)}, u32[]{:S(2)}, u32[]{:S(2)}) %collective-permute-start.8) | collective-permute-done | bytes 491552 | tf_op jit(solution)/shard_map/ppermute | solution.py:766
  110.9 1.8 collective-permute-done.9.refs_1_
  113.5 11.8 %shard_map.310 = (bf16[3,256,640]{2,1,0:T(8,128)(2,1)}, f32[3,640]{1,0:T(4,128)}) custom-call(s32[1]{0:T(128)} %bitcast.c_ref, bf16[3,256,640]{2,1,0:T(8,128)(2,1)} %get-tuple-element.116.refs_3_.cg_ref, bf16[3,128,640]{2,1,0:T(8,128)(2,1)} %copy-done.27, bf16[3,128,640]{2,1,0:T(8,128)(2,1)} %copy-done.28, ...), custom_call_target="tpu_custom_call" | custom-call | flops 32715572 | bytes 100000 | tf_op jit(solution)/shard_map/pallas_call | solution.py:695
  127.0 2.5 add_convert_fusion.3
  130.3 10.0 %shard_map.311 = (bf16[3,256,1280]{2,1,0:T(8,128)(2,1)}, f32[2,1280]{1,0:T(2,128)}) custom-call(s32[1]{0:T(128)} %bitcast.c_ref, bf16[3,256,640]{2,1,0:T(8,128)(2,1)} %get-tuple-element.129.ng_ref.refs_1_, f32[1,7680]{1,0:T(1,128)} %get-tuple-element.231.v1_ref.refs_3_.v_ref, bf16[6,256,1280]{2,1,0:T(8,128)(2,1)} %grad.1, ...), custom_call_target="tpu_custom_call" | custom-call | flops 16357785 | bytes 100000 | tf_op jit(solution)/shard_map/pallas_call | solution.py:695
  140.3 7.9 %shard_map.312 = (bf16[3,256,640]{2,1,0:T(8,128)(2,1)}, bf16[3,8,640]{2,1,0:T(8,128)(2,1)}, bf16[3,8,640]{2,1,0:T(8,128)(2,1)}, f32[4,1280]{1,0:T(4,128)}) custom-call(s32[1]{0:T(128)} %bitcast.c_ref, bf16[3,256,1280]{2,1,0:T(8,128)(2,1)} %get-tuple-element.133.ig_ref.refs_1_.grad, f32[1,7680]{1,0:T(1,128)} %get-tuple-element.232.v0_ref.v_ref.refs_2_, ...), custom_call_target="tpu_custom_call" | custom-call | flops 16357785 | bytes 80000 | tf_op jit(solution)/shard_map/pallas_call | solution.py:695
  149.0 1.7 add_convert_fusion.8
  150.7 2.2 collective-permute-start.12
  153.5 5.1 %collective-permute-start.14 = (bf16[3,8,640]{2,1,0:T(8,128)(2,1)S(1)}, bf16[3,8,640]{2,1,0:T(8,128)(2,1)S(1)}, u32[]{:S(2)}, u32[]{:S(2)}) collective-permute-start(bf16[3,8,640]{2,1,0:T(8,128)(2,1)S(1)} %copy-done.38), channel_id=1, source_target_pairs={{1,0},{2,1},{3,2},{4,3},{5,4},{6,5},{7,6},{8,7},{9,8},{10,9},{11,1... | collective-permute-start | bytes 92168 | tf_op jit(solution)/shard_map/ppermute | solution.py:822
  158.6 11.6 %shard_map.313 = (bf16[2304,640]{1,0:T(8,128)(2,1)}, bf16[2304,640]{1,0:T(8,128)(2,1)}) custom-call(s32[1]{0:T(128)} %bitcast.c_ref, bf16[3,256,640]{2,1,0:T(8,128)(2,1)} %get-tuple-element.144.refs_0_, bf16[3,256,1280]{2,1,0:T(8,128)(2,1)} %get-tuple-element.133.ig_ref.refs_1_.grad, bf16[3,256,3200]{2,1,0:T(8,128)(2,1)} %get-tuple-element.145.refs_2_, ...), custom_call_target="tpu_custom_call" | custom-call | flops 44040192 | bytes 58982 | tf_op jit(solution)/shard_map/pallas_call | solution.py:515
  172.2 8.8 %shard_map.314 = (bf16[3,256,1280]{2,1,0:T(8,128)(2,1)}, f32[2,128]{1,0:T(2,128)}) custom-call(s32[1]{0:T(128)} %bitcast.c_ref, bf16[3,256,1280]{2,1,0:T(8,128)(2,1)} %get-tuple-element.106.src.out0_ref, bf16[3,256,640]{2,1,0:T(8,128)(2,1)} %get-tuple-element.114.refs_0_.oa_ref, s32[6,256]{1,0:T(8,128)} %rt_ref.1, s32[6,256]{1,0:T(8,128)} %lm_ref.1, ...), custom_call_target="tpu_custom_call" | custom-call | flops 15099494 | bytes 80000 | tf_op jit(solution)/shard_map/pallas_call | solution.py:695
  181.1 3.8 %add_convert_fusion = (bf16[1152,640]{1,0:T(8,128)(2,1)S(1)}, bf16[1152,640]{1,0:T(8,128)(2,1)}) fusion(bf16[2304,640]{1,0:T(8,128)(2,1)} %collective-permute-done.17, s32[]{:T(128)S(6)} %select_n.188, bf16[2304,640]{1,0:T(8,128)(2,1)S(1)} %copy-done.16, s32[]{:T(128)S(6)} %select_n.191), kind=kLoop, calls=%fused_computation.2 | loop fusion | flops 5898240 | bytes 8847368 | tf_op jit(solution)/shard_map/convert_element_type | solution.py:571
  186.5 12.1 %shard_map.315 = (bf16[3,256,640]{2,1,0:T(8,128)(2,1)}, f32[3,640]{1,0:T(4,128)}) custom-call(s32[1]{0:T(128)} %bitcast.c_ref, bf16[3,256,640]{2,1,0:T(8,128)(2,1)} %get-tuple-element.146.refs_3_.cg_ref, bf16[3,16,640]{2,1,0:T(8,128)(2,1)} %pad_maximum_fusion.7.refs_0_, f32[3,256,128]{2,1,0:T(8,128)} %get-tuple-element.110.mk.refs_2_.refs_1_, ...), custom_call_target="tpu_custom_call" | custom-call | flops 32715572 | bytes 100000 | tf_op jit(solution)/shard_map/pallas_call | solution.py:695
  198.6 5.6 %collective-permute-done.18 = bf16[288,640]{1,0:T(8,128)(2,1)S(1)} collective-permute-done((bf16[288,640]{1,0:T(8,128)(2,1)S(1)}, bf16[288,640]{1,0:T(8,128)(2,1)S(1)}, u32[]{:S(2)}, u32[]{:S(2)}) %collective-permute-start.18) | collective-permute-done | bytes 368672 | tf_op jit(solution)/shard_map/ppermute | solution.py:652
  205.4 7.9 %shard_map.316 = (bf16[1280,640]{1,0:T(8,128)(2,1)}, bf16[1280,640]{1,0:T(8,128)(2,1)}) custom-call(s32[1]{0:T(128)} %bitcast.c_ref, bf16[3,256,1280]{2,1,0:T(8,128)(2,1)} %get-tuple-element.166.refs_0_, bf16[3,256,640]{2,1,0:T(8,128)(2,1)} %get-tuple-element.129.ng_ref.refs_1_, bf16[3,256,1280]{2,1,0:T(8,128)(2,1)} %get-tuple-element.167.refs_2_, ...), custom_call_target="tpu_custom_call" | custom-call | flops 25165824 | bytes 32768 | tf_op jit(solution)/shard_map/pallas_call | solution.py:515
  215.4 2.9 add_convert_fusion.6
  219.2 2.0 collective-permute-start.21
  223.2 10.0 %shard_map.317 = (bf16[3,256,1280]{2,1,0:T(8,128)(2,1)}, f32[2,1280]{1,0:T(2,128)}) custom-call(s32[1]{0:T(128)} %bitcast.c_ref, bf16[3,256,640]{2,1,0:T(8,128)(2,1)} %get-tuple-element.168.refs_3_.ng_ref, f32[1,7680]{1,0:T(1,128)} %get-tuple-element.232.v0_ref.v_ref.refs_2_, bf16[3,256,1280]{2,1,0:T(8,128)(2,1)} %get-tuple-element.133.ig_ref.refs_1_.grad, ...), custom_call_target="tpu_custom_call" | custom-call | flops 16357785 | bytes 100000 | tf_op jit(solution)/shard_map/pallas_call | solution.py:695
  233.2 5.6 %collective-permute-done.21 = bf16[576,640]{1,0:T(8,128)(2,1)S(1)} collective-permute-done((bf16[576,640]{1,0:T(8,128)(2,1)}, bf16[576,640]{1,0:T(8,128)(2,1)S(1)}, u32[]{:S(2)}, u32[]{:S(2)}) %collective-permute-start.21) | collective-permute-done | bytes 737312 | tf_op jit(solution)/shard_map/ppermute | solution.py:652
  240.1 2.3 add_convert_fusion.5
  244.7 2.1 collective-permute-start.26
  246.8 8.4 %collective-permute-done.33 = bf16[288,640]{1,0:T(8,128)(2,1)S(1)} collective-permute-done((bf16[288,640]{1,0:T(8,128)(2,1)S(1)}, bf16[288,640]{1,0:T(8,128)(2,1)S(1)}, u32[]{:S(2)}, u32[]{:S(2)}) %collective-permute-start.33) | collective-permute-done | bytes 368672 | tf_op jit(solution)/shard_map/ppermute | solution.py:652
  257.7 2.1 collective-permute-start.41
  259.8 2.0 broadcast_select_fusion.5
  261.9 9.9 %collective-permute-done.34 = bf16[288,640]{1,0:T(8,128)(2,1)S(1)} collective-permute-done((bf16[288,640]{1,0:T(8,128)(2,1)S(1)}, bf16[288,640]{1,0:T(8,128)(2,1)S(1)}, u32[]{:S(2)}, u32[]{:S(2)}) %collective-permute-start.34) | collective-permute-done | bytes 368672 | tf_op jit(solution)/shard_map/ppermute | solution.py:652
  276.4 7.0 %collective-permute-done.35 = bf16[288,640]{1,0:T(8,128)(2,1)S(1)} collective-permute-done((bf16[288,640]{1,0:T(8,128)(2,1)S(1)}, bf16[288,640]{1,0:T(8,128)(2,1)S(1)}, u32[]{:S(2)}, u32[]{:S(2)}) %collective-permute-start.35) | collective-permute-done | bytes 368672 | tf_op jit(solution)/shard_map/ppermute | solution.py:652
  283.5 4.2 %collective-permute-done.42 = bf16[160,640]{1,0:T(8,128)(2,1)S(1)} collective-permute-done((bf16[160,640]{1,0:T(8,128)(2,1)S(1)}, bf16[160,640]{1,0:T(8,128)(2,1)S(1)}, u32[]{:S(2)}, u32[]{:S(2)}) %collective-permute-start.42) | collective-permute-done | bytes 204832 | tf_op jit(solution)/shard_map/ppermute | solution.py:652
  288.2 2.2 collective-permute-done.28
  290.4 5.6 %collective-permute-done.43 = bf16[160,640]{1,0:T(8,128)(2,1)S(1)} collective-permute-done((bf16[160,640]{1,0:T(8,128)(2,1)S(1)}, bf16[160,640]{1,0:T(8,128)(2,1)S(1)}, u32[]{:S(2)}, u32[]{:S(2)}) %collective-permute-start.43) | collective-permute-done | bytes 204832 | tf_op jit(solution)/shard_map/ppermute | solution.py:652
  296.1 3.4 collective-permute-start.29
  302.5 2.3 maximum_bitcast_fusion
  304.7 2.9 collective-permute-done.44
  309.1 6.6 %collective-permute-done.45 = bf16[320,640]{1,0:T(8,128)(2,1)S(1)} collective-permute-done((bf16[320,640]{1,0:T(8,128)(2,1)S(1)}, bf16[320,640]{1,0:T(8,128)(2,1)S(1)}, u32[]{:S(2)}, u32[]{:S(2)}) %collective-permute-start.45) | collective-permute-done | bytes 409632 | tf_op jit(solution)/shard_map/ppermute | solution.py:652
  317.7 8.1 %collective-permute-done.37.refs_5_ = bf16[1152,640]{1,0:T(8,128)(2,1)S(1)} collective-permute-done((bf16[1152,640]{1,0:T(8,128)(2,1)S(1)}, bf16[1152,640]{1,0:T(8,128)(2,1)S(1)}, u32[]{:S(2)}, u32[]{:S(2)}) %collective-permute-start.37) | collective-permute-done | bytes 1474592 | tf_op jit(solution)/shard_map/ppermute | solution.py:652
  327.4 7.3 %collective-permute-done.46.refs_1_ = bf16[640,640]{1,0:T(8,128)(2,1)} collective-permute-done((bf16[640,640]{1,0:T(8,128)(2,1)S(1)}, bf16[640,640]{1,0:T(8,128)(2,1)}, u32[]{:S(2)}, u32[]{:S(2)}) %collective-permute-start.46) | collective-permute-done | bytes 819232 | tf_op jit(solution)/shard_map/ppermute | solution.py:652
  335.1 2.3 maximum_bitcast_fusion.1
  338.9 8.9 %shard_map.318 = (f32[640,1280]{1,0:T(8,128)}, f32[5,640,640]{2,1,0:T(8,128)}) custom-call(s32[1]{0:T(128)} %bitcast.c_ref, s32[7]{0:T(128)} %iota_multiply_fusion.row_ref, s32[2]{0:T(128)} %broadcast_select_fusion.19.sig_ref, bf16[1152,640]{1,0:T(8,128)(2,1)} %copy-done.7, bf16[1152,640]{1,0:T(8,128)(2,1)} %copy-done.18, bf16[1152,640]{1,0:T(8,128)(2,1)} %copy-done.19, ...), custom_call_target="tpu_custom_call" | custom-call | bytes 5000000 | tf_op jit(solution)/shard_map/pallas_call | solution.py:905
  347.9 4.5 %shard_map.319 = f32[1280,640]{1,0:T(8,128)} custom-call(s32[1]{0:T(128)} %bitcast.c_ref, s32[2]{0:T(128)} %add_multiply_fusion.row_ref, s32[2]{0:T(128)} %broadcast_select_fusion.19.sig_ref, bf16[640,640]{1,0:T(8,128)(2,1)} %copy-done.11, bf16[640,640]{1,0:T(8,128)(2,1)} %collective-permute-done.46.refs_1_, ...), custom_call_target="tpu_custom_call" | custom-call | bytes 5000000 | tf_op jit(solution)/shard_map/pallas_call | solution.py:905
  (195 shorter events, 44.4 us)
Async XLA Ops:
  0.6 16.0 %collective-permute-start.4 = (bf16[5,640,640]{2,1,0:T(8,128)(2,1)}, bf16[5,640,640]{2,1,0:T(8,128)(2,1)}, u32[]{:S(2)}, u32[]{:S(2)}) collective-permute-start(bf16[5,640,640]{2,1,0:T(8,128)(2,1)} %bitcast.17), channel_id=1, source_target_pairs={{0,16},{16,0},{1,17},{17,1},{2,18},{18,2},{3,19},{19,3},{4,20},{20... | collective-permute-start | bytes 12288008 | tf_op jit(solution)/shard_map/ppermute | solution.py:648
  2.6 8.0 %collective-permute-start.2 = (f32[1,7680]{1,0:T(1,128)}, f32[1,7680]{1,0:T(1,128)S(1)}, u32[]{:S(2)}, u32[]{:S(2)}) collective-permute-start(f32[1,7680]{1,0:T(1,128)} %shard_map.306), channel_id=1, source_target_pairs={{0,16},{16,0},{1,17},{17,1},{2,18},{18,2},{3,19},{19,3},{4,20},{20... | collective-permute-start | bytes 92168 | tf_op jit(solution)/shard_map/ppermute | solution.py:648
  3.5 9.3 %collective-permute-start = (bf16[3,8,1280]{2,1,0:T(8,128)(2,1)S(1)}, bf16[3,8,1280]{2,1,0:T(8,128)(2,1)S(1)}, u32[]{:S(2)}, u32[]{:S(2)}) collective-permute-start(bf16[3,8,1280]{2,1,0:T(8,128)(2,1)S(1)} %get-tuple-element.204), channel_id=1, source_target_pairs={{0,1},{1,2},{2,3},{3,4},{4,5},{5,6},{6,7},{7,8},{8,9},{9,10},{10,1... | collective-permute-start | bytes 184328 | tf_op jit(solution)/shard_map/ppermute | solution.py:682
  6.5 6.3 %collective-permute-start.1 = (bf16[3,8,1280]{2,1,0:T(8,128)(2,1)S(1)}, bf16[3,8,1280]{2,1,0:T(8,128)(2,1)S(1)}, u32[]{:S(2)}, u32[]{:S(2)}) collective-permute-start(bf16[3,8,1280]{2,1,0:T(8,128)(2,1)S(1)} %get-tuple-element.205), channel_id=1, source_target_pairs={{1,0},{2,1},{3,2},{4,3},{5,4},{6,5},{7,6},{8,7},{9,8},{10,9},{11,1... | collective-permute-start | bytes 184328 | tf_op jit(solution)/shard_map/ppermute | solution.py:682
  10.6 6.1 %collective-permute-start.3 = (bf16[1280,640]{1,0:T(8,128)(2,1)}, bf16[1280,640]{1,0:T(8,128)(2,1)S(1)}, u32[]{:S(2)}, u32[]{:S(2)}) collective-permute-start(bf16[1280,640]{1,0:T(8,128)(2,1)} %bitcast.27), channel_id=1, source_target_pairs={{0,16},{16,0},{1,17},{17,1},{2,18},{18,2},{3,19},{19,3},{4,20},{20... | collective-permute-start | bytes 4915208 | tf_op jit(solution)/shard_map/ppermute | solution.py:648
  47.5 22.0 %collective-permute-start.6 = (bf16[3,128,640]{2,1,0:T(8,128)(2,1)}, bf16[3,128,640]{2,1,0:T(8,128)(2,1)S(1)}, u32[]{:S(2)}, u32[]{:S(2)}) collective-permute-start(bf16[3,128,640]{2,1,0:T(8,128)(2,1)} %get-tuple-element.108), channel_id=1, source_target_pairs={{0,1},{1,2},{2,3},{3,4},{4,5},{5,6},{6,7},{7,8},{8,9},{9,10},{10,1... | collective-permute-start | bytes 1474568 | tf_op jit(solution)/shard_map/ppermute | solution.py:747
  47.5 22.4 %collective-permute-start.7 = (bf16[3,128,640]{2,1,0:T(8,128)(2,1)}, bf16[3,128,640]{2,1,0:T(8,128)(2,1)S(1)}, u32[]{:S(2)}, u32[]{:S(2)}) collective-permute-start(bf16[3,128,640]{2,1,0:T(8,128)(2,1)} %get-tuple-element.109), channel_id=1, source_target_pairs={{1,0},{2,1},{3,2},{4,3},{5,4},{6,5},{7,6},{8,7},{9,8},{10,9},{11,1... | collective-permute-start | bytes 1474568 | tf_op jit(solution)/shard_map/ppermute | solution.py:748
  87.7 23.2 %collective-permute-start.8 = (bf16[3,128,640]{2,1,0:T(8,128)(2,1)}, bf16[3,128,640]{2,1,0:T(8,128)(2,1)S(1)}, u32[]{:S(2)}, u32[]{:S(2)}) collective-permute-start(bf16[3,128,640]{2,1,0:T(8,128)(2,1)} %get-tuple-element.111), channel_id=1, source_target_pairs={{0,1},{1,2},{2,3},{3,4},{4,5},{5,6},{6,7},{7,8},{8,9},{9,10},{10,1... | collective-permute-start | bytes 1474568 | tf_op jit(solution)/shard_map/ppermute | solution.py:766
  89.8 22.9 %collective-permute-start.9 = (bf16[3,128,640]{2,1,0:T(8,128)(2,1)}, bf16[3,128,640]{2,1,0:T(8,128)(2,1)S(1)}, u32[]{:S(2)}, u32[]{:S(2)}) collective-permute-start(bf16[3,128,640]{2,1,0:T(8,128)(2,1)} %get-tuple-element.112), channel_id=1, source_target_pairs={{1,0},{2,1},{3,2},{4,3},{5,4},{6,5},{7,6},{8,7},{9,8},{10,9},{11,1... | collective-permute-start | bytes 1474568 | tf_op jit(solution)/shard_map/ppermute | solution.py:767
  113.5 11.8 %collective-permute-start.10 = (bf16[2304,640]{1,0:T(8,128)(2,1)}, bf16[2304,640]{1,0:T(8,128)(2,1)S(1)}, u32[]{:S(2)}, u32[]{:S(2)}) collective-permute-start(bf16[2304,640]{1,0:T(8,128)(2,1)} %get-tuple-element.120), channel_id=1, source_target_pairs={{0,16},{16,0},{1,17},{17,1},{2,18},{18,2},{3,19},{19,3},{4,20},{20... | collective-permute-start | bytes 8847368 | tf_op jit(solution)/shard_map/ppermute | solution.py:648
  129.5 19.5 %collective-permute-start.11 = (bf16[1152,640]{1,0:T(8,128)(2,1)S(1)}, bf16[1152,640]{1,0:T(8,128)(2,1)}, u32[]{:S(2)}, u32[]{:S(2)}) collective-permute-start(bf16[1152,640]{1,0:T(8,128)(2,1)S(1)} %get-tuple-element.203), channel_id=1, source_target_pairs={{0,1},{1,0},{2,3},{3,2},{4,5},{5,4},{6,7},{7,6},{8,9},{9,8},{10,11... | collective-permute-start | bytes 4423688 | tf_op jit(solution)/shard_map/ppermute | solution.py:652
  150.7 19.5 %collective-permute-start.12 = (bf16[576,640]{1,0:T(8,128)(2,1)S(1)}, bf16[576,640]{1,0:T(8,128)(2,1)S(1)}, u32[]{:S(2)}, u32[]{:S(2)}) collective-permute-start(bf16[576,640]{1,0:T(8,128)(2,1)S(1)} %get-tuple-element.211), channel_id=1, source_target_pairs={{0,4},{1,5},{2,6},{3,7},{4,0},{5,1},{6,2},{7,3},{8,12},{9,13},{10,... | collective-permute-start | bytes 2211848 | tf_op jit(solution)/shard_map/ppermute | solution.py:652
  153.0 17.2 %collective-permute-start.13 = (bf16[3,8,640]{2,1,0:T(8,128)(2,1)S(1)}, bf16[3,8,640]{2,1,0:T(8,128)(2,1)S(1)}, u32[]{:S(2)}, u32[]{:S(2)}) collective-permute-start(bf16[3,8,640]{2,1,0:T(8,128)(2,1)S(1)} %copy-done.39), channel_id=1, source_target_pairs={{0,1},{1,2},{2,3},{3,4},{4,5},{5,6},{6,7},{7,8},{8,9},{9,10},{10,1... | collective-permute-start | bytes 92168 | tf_op jit(solution)/shard_map/ppermute | solution.py:822
  153.5 16.7 %collective-permute-start.14 = (bf16[3,8,640]{2,1,0:T(8,128)(2,1)S(1)}, bf16[3,8,640]{2,1,0:T(8,128)(2,1)S(1)}, u32[]{:S(2)}, u32[]{:S(2)}) collective-permute-start(bf16[3,8,640]{2,1,0:T(8,128)(2,1)S(1)} %copy-done.38), channel_id=1, source_target_pairs={{1,0},{2,1},{3,2},{4,3},{5,4},{6,5},{7,6},{8,7},{9,8},{10,9},{11,1... | collective-permute-start | bytes 92168 | tf_op jit(solution)/shard_map/ppermute | solution.py:822
  170.2 10.8 %collective-permute-start.17 = (bf16[2304,640]{1,0:T(8,128)(2,1)}, bf16[2304,640]{1,0:T(8,128)(2,1)}, u32[]{:S(2)}, u32[]{:S(2)}) collective-permute-start(bf16[2304,640]{1,0:T(8,128)(2,1)} %get-tuple-element.153), channel_id=1, source_target_pairs={{0,16},{16,0},{1,17},{17,1},{2,18},{18,2},{3,19},{19,3},{4,20},{20... | collective-permute-start | bytes 8847368 | tf_op jit(solution)/shard_map/ppermute | solution.py:648
  171.1 9.9 %collective-permute-start.16 = (bf16[288,640]{1,0:T(8,128)(2,1)S(1)}, bf16[288,640]{1,0:T(8,128)(2,1)S(1)}, u32[]{:S(2)}, u32[]{:S(2)}) collective-permute-start(bf16[288,640]{1,0:T(8,128)(2,1)S(1)} %add_convert_fusion.19), channel_id=1, source_target_pairs={{0,2},{1,3},{2,0},{3,1},{4,6},{5,7},{6,4},{7,5},{8,10},{9,11},{10,... | collective-permute-start | bytes 1105928 | tf_op jit(solution)/shard_map/ppermute | solution.py:652
  184.8 28.5 %collective-permute-start.20 = (bf16[1152,640]{1,0:T(8,128)(2,1)}, bf16[1152,640]{1,0:T(8,128)(2,1)}, u32[]{:S(2)}, u32[]{:S(2)}) collective-permute-start(bf16[1152,640]{1,0:T(8,128)(2,1)} %get-tuple-element.199), channel_id=1, source_target_pairs={{0,1},{1,0},{2,3},{3,2},{4,5},{5,4},{6,7},{7,6},{8,9},{9,8},{10,11... | collective-permute-start | bytes 4423688 | tf_op jit(solution)/shard_map/ppermute | solution.py:652
  185.0 19.2 %collective-permute-start.18 = (bf16[288,640]{1,0:T(8,128)(2,1)S(1)}, bf16[288,640]{1,0:T(8,128)(2,1)S(1)}, u32[]{:S(2)}, u32[]{:S(2)}) collective-permute-start(bf16[288,640]{1,0:T(8,128)(2,1)S(1)} %add_convert_fusion.17), channel_id=1, source_target_pairs={{0,8},{1,9},{2,10},{3,11},{4,12},{5,13},{6,14},{7,15},{8,0},{9,1},... | collective-permute-start | bytes 1105928 | tf_op jit(solution)/shard_map/ppermute | solution.py:652
  204.3 9.0 %collective-permute-start.19 = (bf16[288,640]{1,0:T(8,128)(2,1)S(1)}, bf16[288,640]{1,0:T(8,128)(2,1)S(1)}, u32[]{:S(2)}, u32[]{:S(2)}) collective-permute-start(bf16[288,640]{1,0:T(8,128)(2,1)S(1)} %add_convert_fusion.16), channel_id=1, source_target_pairs={{0,2},{1,3},{2,0},{3,1},{4,6},{5,7},{6,4},{7,5},{8,10},{9,11},{10,... | collective-permute-start | bytes 1105928 | tf_op jit(solution)/shard_map/ppermute | solution.py:652
  213.4 25.4 %collective-permute-start.23 = (bf16[1280,640]{1,0:T(8,128)(2,1)}, bf16[1280,640]{1,0:T(8,128)(2,1)}, u32[]{:S(2)}, u32[]{:S(2)}) collective-permute-start(bf16[1280,640]{1,0:T(8,128)(2,1)} %get-tuple-element.173), channel_id=1, source_target_pairs={{0,16},{16,0},{1,17},{17,1},{2,18},{18,2},{3,19},{19,3},{4,20},{20... | collective-permute-start | bytes 4915208 | tf_op jit(solution)/shard_map/ppermute | solution.py:648
  214.9 44.9 %collective-permute-start.15 = (bf16[3,256,1280]{2,1,0:T(8,128)(2,1)}, bf16[3,256,1280]{2,1,0:T(8,128)(2,1)}, u32[]{:S(2)}, u32[]{:S(2)}) collective-permute-start(bf16[3,256,1280]{2,1,0:T(8,128)(2,1)} %broadcast_select_fusion.6), channel_id=1, source_target_pairs={{0,16},{16,0},{1,17},{17,1},{2,18},{18,2},{3,19},{19,3},{4,20},{20... | collective-permute-start | bytes 5898248 | tf_op jit(solution)/shard_map/ppermute | solution.py:648
  219.2 13.9 %collective-permute-start.22 = (bf16[576,640]{1,0:T(8,128)(2,1)}, bf16[576,640]{1,0:T(8,128)(2,1)}, u32[]{:S(2)}, u32[]{:S(2)}) collective-permute-start(bf16[576,640]{1,0:T(8,128)(2,1)} %get-tuple-element.209), channel_id=1, source_target_pairs={{0,4},{1,5},{2,6},{3,7},{4,0},{5,1},{6,2},{7,3},{8,12},{9,13},{10,... | collective-permute-start | bytes 2211848 | tf_op jit(solution)/shard_map/ppermute | solution.py:652
  219.2 19.6 %collective-permute-start.21 = (bf16[576,640]{1,0:T(8,128)(2,1)}, bf16[576,640]{1,0:T(8,128)(2,1)S(1)}, u32[]{:S(2)}, u32[]{:S(2)}) collective-permute-start(bf16[576,640]{1,0:T(8,128)(2,1)} %pad_maximum_fusion.3), channel_id=1, source_target_pairs={{0,4},{1,5},{2,6},{3,7},{4,0},{5,1},{6,2},{7,3},{8,12},{9,13},{10,... | collective-permute-start | bytes 2211848 | tf_op jit(solution)/shard_map/ppermute | solution.py:652
  240.0 4.7 %collective-permute-start.25 = (f32[24,1280]{1,0:T(8,128)S(1)}, f32[24,1280]{1,0:T(8,128)S(1)}, u32[]{:S(2)}, u32[]{:S(2)}) collective-permute-start(f32[24,1280]{1,0:T(8,128)S(1)} %pad.23), channel_id=1, source_target_pairs={{0,16},{16,0},{1,17},{17,1},{2,18},{18,2},{3,19},{19,3},{4,20},{20... | collective-permute-start | bytes 368648 | tf_op jit(solution)/shard_map/ppermute | solution.py:648
  242.4 15.1 %collective-permute-start.40 = (bf16[640,640]{1,0:T(8,128)(2,1)S(1)}, bf16[640,640]{1,0:T(8,128)(2,1)S(1)}, u32[]{:S(2)}, u32[]{:S(2)}) collective-permute-start(bf16[640,640]{1,0:T(8,128)(2,1)S(1)} %get-tuple-element.207), channel_id=1, source_target_pairs={{0,1},{1,0},{2,3},{3,2},{4,5},{5,4},{6,7},{7,6},{8,9},{9,8},{10,11... | collective-permute-start | bytes 2457608 | tf_op jit(solution)/shard_map/ppermute | solution.py:652
  243.6 11.6 %collective-permute-start.33 = (bf16[288,640]{1,0:T(8,128)(2,1)S(1)}, bf16[288,640]{1,0:T(8,128)(2,1)S(1)}, u32[]{:S(2)}, u32[]{:S(2)}) collective-permute-start(bf16[288,640]{1,0:T(8,128)(2,1)S(1)} %add_convert_fusion.14), channel_id=1, source_target_pairs={{0,2},{1,3},{2,0},{3,1},{4,6},{5,7},{6,4},{7,5},{8,10},{9,11},{10,... | collective-permute-start | bytes 1105928 | tf_op jit(solution)/shard_map/ppermute | solution.py:652
  244.7 17.1 %collective-permute-start.26 = (f32[24,1280]{1,0:T(8,128)S(1)}, f32[24,1280]{1,0:T(8,128)S(1)}, u32[]{:S(2)}, u32[]{:S(2)}) collective-permute-start(f32[24,1280]{1,0:T(8,128)S(1)} %pad_add_fusion), channel_id=1, source_target_pairs={{0,1},{1,0},{2,3},{3,2},{4,5},{5,4},{6,7},{7,6},{8,9},{9,8},{10,11... | collective-permute-start | bytes 368648 | tf_op jit(solution)/shard_map/ppermute | solution.py:652
  256.4 15.5 %collective-permute-start.34 = (bf16[288,640]{1,0:T(8,128)(2,1)S(1)}, bf16[288,640]{1,0:T(8,128)(2,1)S(1)}, u32[]{:S(2)}, u32[]{:S(2)}) collective-permute-start(bf16[288,640]{1,0:T(8,128)(2,1)S(1)} %add_convert_fusion.13), channel_id=1, source_target_pairs={{0,8},{1,9},{2,10},{3,11},{4,12},{5,13},{6,14},{7,15},{8,0},{9,1},... | collective-permute-start | bytes 1105928 | tf_op jit(solution)/shard_map/ppermute | solution.py:652
  257.7 15.5 %collective-permute-start.41 = (bf16[320,640]{1,0:T(8,128)(2,1)S(1)}, bf16[320,640]{1,0:T(8,128)(2,1)S(1)}, u32[]{:S(2)}, u32[]{:S(2)}) collective-permute-start(bf16[320,640]{1,0:T(8,128)(2,1)S(1)} %get-tuple-element.213), channel_id=1, source_target_pairs={{0,4},{1,5},{2,6},{3,7},{4,0},{5,1},{6,2},{7,3},{8,12},{9,13},{10,... | collective-permute-start | bytes 1228808 | tf_op jit(solution)/shard_map/ppermute | solution.py:652
  261.9 13.2 %collective-permute-start.27 = (f32[24,1280]{1,0:T(8,128)S(1)}, f32[24,1280]{1,0:T(8,128)S(1)}, u32[]{:S(2)}, u32[]{:S(2)}) collective-permute-start(f32[24,1280]{1,0:T(8,128)S(1)} %add.197), channel_id=1, source_target_pairs={{0,4},{1,5},{2,6},{3,7},{4,0},{5,1},{6,2},{7,3},{8,12},{9,13},{10,... | collective-permute-start | bytes 368648 | tf_op jit(solution)/shard_map/ppermute | solution.py:652
  271.9 11.4 %collective-permute-start.35 = (bf16[288,640]{1,0:T(8,128)(2,1)S(1)}, bf16[288,640]{1,0:T(8,128)(2,1)S(1)}, u32[]{:S(2)}, u32[]{:S(2)}) collective-permute-start(bf16[288,640]{1,0:T(8,128)(2,1)S(1)} %add_convert_fusion.12), channel_id=1, source_target_pairs={{0,2},{1,3},{2,0},{3,1},{4,6},{5,7},{6,4},{7,5},{8,10},{9,11},{10,... | collective-permute-start | bytes 1105928 | tf_op jit(solution)/shard_map/ppermute | solution.py:652
  273.3 14.5 %collective-permute-start.42 = (bf16[160,640]{1,0:T(8,128)(2,1)S(1)}, bf16[160,640]{1,0:T(8,128)(2,1)S(1)}, u32[]{:S(2)}, u32[]{:S(2)}) collective-permute-start(bf16[160,640]{1,0:T(8,128)(2,1)S(1)} %add_convert_fusion.22), channel_id=1, source_target_pairs={{0,2},{1,3},{2,0},{3,1},{4,6},{5,7},{6,4},{7,5},{8,10},{9,11},{10,... | collective-permute-start | bytes 614408 | tf_op jit(solution)/shard_map/ppermute | solution.py:652
  274.8 42.4 %collective-permute-start.30 = (bf16[1152,640]{1,0:T(8,128)(2,1)S(1)}, bf16[1152,640]{1,0:T(8,128)(2,1)S(1)}, u32[]{:S(2)}, u32[]{:S(2)}) collective-permute-start(bf16[1152,640]{1,0:T(8,128)(2,1)S(1)} %pad_maximum_fusion.refs_0_), channel_id=1, source_target_pairs={{0,1},{1,0},{2,3},{3,2},{4,5},{5,4},{6,7},{7,6},{8,9},{9,8},{10,11... | collective-permute-start | bytes 4423688 | tf_op jit(solution)/shard_map/ppermute | solution.py:652
  275.1 42.3 %collective-permute-start.31 = (bf16[1152,640]{1,0:T(8,128)(2,1)S(1)}, bf16[1152,640]{1,0:T(8,128)(2,1)S(1)}, u32[]{:S(2)}, u32[]{:S(2)}) collective-permute-start(bf16[1152,640]{1,0:T(8,128)(2,1)S(1)} %pad_maximum_fusion.refs_0_), channel_id=1, source_target_pairs={{0,16},{16,0},{1,17},{17,1},{2,18},{18,2},{3,19},{19,3},{4,20},{20... | collective-permute-start | bytes 4423688 | tf_op jit(solution)/shard_map/ppermute | solution.py:648
  275.1 15.3 %collective-permute-start.28 = (f32[24,1280]{1,0:T(8,128)S(1)}, f32[24,1280]{1,0:T(8,128)S(1)}, u32[]{:S(2)}, u32[]{:S(2)}) collective-permute-start(f32[24,1280]{1,0:T(8,128)S(1)} %add.198), channel_id=1, source_target_pairs={{0,2},{1,3},{2,0},{3,1},{4,6},{5,7},{6,4},{7,5},{8,10},{9,11},{10,... | collective-permute-start | bytes 368648 | tf_op jit(solution)/shard_map/ppermute | solution.py:652
  283.4 16.1 %collective-permute-start.36 = (bf16[576,640]{1,0:T(8,128)(2,1)S(1)}, bf16[576,640]{1,0:T(8,128)(2,1)S(1)}, u32[]{:S(2)}, u32[]{:S(2)}) collective-permute-start(bf16[576,640]{1,0:T(8,128)(2,1)S(1)} %pad_maximum_fusion.4), channel_id=1, source_target_pairs={{0,4},{1,5},{2,6},{3,7},{4,0},{5,1},{6,2},{7,3},{8,12},{9,13},{10,... | collective-permute-start | bytes 2211848 | tf_op jit(solution)/shard_map/ppermute | solution.py:652
  287.9 8.2 %collective-permute-start.43 = (bf16[160,640]{1,0:T(8,128)(2,1)S(1)}, bf16[160,640]{1,0:T(8,128)(2,1)S(1)}, u32[]{:S(2)}, u32[]{:S(2)}) collective-permute-start(bf16[160,640]{1,0:T(8,128)(2,1)S(1)} %add_convert_fusion.21), channel_id=1, source_target_pairs={{0,8},{1,9},{2,10},{3,11},{4,12},{5,13},{6,14},{7,15},{8,0},{9,1},... | collective-permute-start | bytes 614408 | tf_op jit(solution)/shard_map/ppermute | solution.py:652
  290.4 36.6 %collective-permute-start.24 = (bf16[3,256,1280]{2,1,0:T(8,128)(2,1)S(1)}, bf16[3,256,1280]{2,1,0:T(8,128)(2,1)S(1)}, u32[]{:S(2)}, u32[]{:S(2)}) collective-permute-start(bf16[3,256,1280]{2,1,0:T(8,128)(2,1)S(1)} %broadcast_select_fusion.2), channel_id=1, source_target_pairs={{0,16},{16,0},{1,17},{17,1},{2,18},{18,2},{3,19},{19,3},{4,20},{20... | collective-permute-start | bytes 5898248 | tf_op jit(solution)/shard_map/ppermute | solution.py:648
  296.1 6.4 %collective-permute-start.29 = (f32[24,1280]{1,0:T(8,128)S(1)}, f32[24,1280]{1,0:T(8,128)S(1)}, u32[]{:S(2)}, u32[]{:S(2)}) collective-permute-start(f32[24,1280]{1,0:T(8,128)S(1)} %add.199), channel_id=1, source_target_pairs={{0,8},{1,9},{2,10},{3,11},{4,12},{5,13},{6,14},{7,15},{8,0},{9,1},... | collective-permute-start | bytes 368648 | tf_op jit(solution)/shard_map/ppermute | solution.py:652
  299.6 8.1 %collective-permute-start.44 = (bf16[160,640]{1,0:T(8,128)(2,1)S(1)}, bf16[160,640]{1,0:T(8,128)(2,1)S(1)}, u32[]{:S(2)}, u32[]{:S(2)}) collective-permute-start(bf16[160,640]{1,0:T(8,128)(2,1)S(1)} %add_convert_fusion.20), channel_id=1, source_target_pairs={{0,2},{1,3},{2,0},{3,1},{4,6},{5,7},{6,4},{7,5},{8,10},{9,11},{10,... | collective-permute-start | bytes 614408 | tf_op jit(solution)/shard_map/ppermute | solution.py:652
  302.5 23.3 %collective-permute-start.37 = (bf16[1152,640]{1,0:T(8,128)(2,1)S(1)}, bf16[1152,640]{1,0:T(8,128)(2,1)S(1)}, u32[]{:S(2)}, u32[]{:S(2)}) collective-permute-start(bf16[1152,640]{1,0:T(8,128)(2,1)S(1)} %pad_maximum_fusion.1.refs_4_), channel_id=1, source_target_pairs={{0,1},{1,0},{2,3},{3,2},{4,5},{5,4},{6,7},{7,6},{8,9},{9,8},{10,11... | collective-permute-start | bytes 4423688 | tf_op jit(solution)/shard_map/ppermute | solution.py:652
  307.7 8.0 %collective-permute-start.45 = (bf16[320,640]{1,0:T(8,128)(2,1)S(1)}, bf16[320,640]{1,0:T(8,128)(2,1)S(1)}, u32[]{:S(2)}, u32[]{:S(2)}) collective-permute-start(bf16[320,640]{1,0:T(8,128)(2,1)S(1)} %pad_maximum_fusion.5), channel_id=1, source_target_pairs={{0,4},{1,5},{2,6},{3,7},{4,0},{5,1},{6,2},{7,3},{8,12},{9,13},{10,... | collective-permute-start | bytes 1228808 | tf_op jit(solution)/shard_map/ppermute | solution.py:652
  315.8 18.9 %collective-permute-start.46 = (bf16[640,640]{1,0:T(8,128)(2,1)S(1)}, bf16[640,640]{1,0:T(8,128)(2,1)}, u32[]{:S(2)}, u32[]{:S(2)}) collective-permute-start(bf16[640,640]{1,0:T(8,128)(2,1)S(1)} %pad_maximum_fusion.2.refs_0_), channel_id=1, source_target_pairs={{0,1},{1,0},{2,3},{3,2},{4,5},{5,4},{6,7},{7,6},{8,9},{9,8},{10,11... | collective-permute-start | bytes 2457608 | tf_op jit(solution)/shard_map/ppermute | solution.py:652
  317.1 20.2 %collective-permute-start.32 = (bf16[1152,640]{1,0:T(8,128)(2,1)S(1)}, bf16[1152,640]{1,0:T(8,128)(2,1)S(1)}, u32[]{:S(2)}, u32[]{:S(2)}) collective-permute-start(bf16[1152,640]{1,0:T(8,128)(2,1)S(1)} %collective-permute-done.30.refs_1_), channel_id=1, source_target_pairs={{0,16},{16,0},{1,17},{17,1},{2,18},{18,2},{3,19},{19,3},{4,20},{20... | collective-permute-start | bytes 4423688 | tf_op jit(solution)/shard_map/ppermute | solution.py:648
  317.4 20.0 %collective-permute-start.38 = (bf16[1152,640]{1,0:T(8,128)(2,1)S(1)}, bf16[1152,640]{1,0:T(8,128)(2,1)S(1)}, u32[]{:S(2)}, u32[]{:S(2)}) collective-permute-start(bf16[1152,640]{1,0:T(8,128)(2,1)S(1)} %pad_maximum_fusion.1.refs_4_), channel_id=1, source_target_pairs={{0,16},{16,0},{1,17},{17,1},{2,18},{18,2},{3,19},{19,3},{4,20},{20... | collective-permute-start | bytes 4423688 | tf_op jit(solution)/shard_map/ppermute | solution.py:648
  325.8 11.6 %collective-permute-start.39 = (bf16[1152,640]{1,0:T(8,128)(2,1)S(1)}, bf16[1152,640]{1,0:T(8,128)(2,1)}, u32[]{:S(2)}, u32[]{:S(2)}) collective-permute-start(bf16[1152,640]{1,0:T(8,128)(2,1)S(1)} %collective-permute-done.37.refs_5_), channel_id=1, source_target_pairs={{0,16},{16,0},{1,17},{17,1},{2,18},{18,2},{3,19},{19,3},{4,20},{20... | collective-permute-start | bytes 4423688 | tf_op jit(solution)/shard_map/ppermute | solution.py:648
  327.0 20.9 %collective-permute-start.47 = (bf16[640,640]{1,0:T(8,128)(2,1)S(1)}, bf16[640,640]{1,0:T(8,128)(2,1)}, u32[]{:S(2)}, u32[]{:S(2)}) collective-permute-start(bf16[640,640]{1,0:T(8,128)(2,1)S(1)} %pad_maximum_fusion.2.refs_0_), channel_id=1, source_target_pairs={{0,16},{16,0},{1,17},{17,1},{2,18},{18,2},{3,19},{19,3},{4,20},{20... | collective-permute-start | bytes 2457608 | tf_op jit(solution)/shard_map/ppermute | solution.py:648
  334.7 13.2 %collective-permute-start.48 = (bf16[640,640]{1,0:T(8,128)(2,1)}, bf16[640,640]{1,0:T(8,128)(2,1)}, u32[]{:S(2)}, u32[]{:S(2)}) collective-permute-start(bf16[640,640]{1,0:T(8,128)(2,1)} %collective-permute-done.46.refs_1_), channel_id=1, source_target_pairs={{0,16},{16,0},{1,17},{17,1},{2,18},{18,2},{3,19},{19,3},{4,20},{20... | collective-permute-start | bytes 2457608 | tf_op jit(solution)/shard_map/ppermute | solution.py:648
  (41 other events, 356.5 us)

commit v4 on v3

--- a/solution.py
+++ b/solution.py
@@ -109,6 +109,14 @@
             at += inner
 
 
+def stack_kernel(*refs):
+    at = 0
+    refs[-1][...] = jnp.zeros_like(refs[-1])
+    for ref in refs[:-1]:
+        refs[-1][at : at + ref.shape[0], : ref.shape[1]] = ref[...]
+        at += ref.shape[0]
+
+
 def pack_kernel(*refs):
     at = 0
     for ref in refs[:-1]:
@@ -254,6 +262,9 @@
     for k in range(pieces):
         for j in range(TAPS):
             at = k + j - MID
+            if up_ref is None and (k < MID and j < MID or k >= pieces - MID and j > MID):
+                dst[k * DIL1 : (k + 1) * DIL1, j * inner : (j + 1) * inner] = jnp.zeros((DIL1, inner), BF16)
+                continue
             live = mk[0, k * DIL1 : (k + 1) * DIL1, LIVE1 + j : LIVE1 + j + 1]
             if at < 0:
                 part = up_ref[0, (at + MID) * DIL1 : (at + MID + 1) * DIL1, :]
@@ -264,13 +275,11 @@
             dst[k * DIL1 : (k + 1) * DIL1, j * inner : (j + 1) * inner] = (part.astype(F32) * live).astype(BF16)
 
 
-def f1_kernel(c_ref, mid_ref, up_ref, dn_ref, mk, v1_ref, cot_ref, cwo, cwx, wwo, wwx,
-              st1, oa1, cg1, head, tail, vec, cw1, ww1, c32, e32, acc, sems):
+def e1_kernel(c_ref, mid_ref, mk, cot_ref, cwo, cwx, wwo, wwx, cpart, epart, vec, cw1, ww1, st, acc, sems):
     low = c_ref[0] == 0
     step = pl.program_id(0)
     rows, width = cot_ref.shape[1:]
-    inner = c32.shape[1]
-    v1 = Vectors(v1_ref, width, inner)
+    inner = mid_ref.shape[2]
 
     @pl.when(step == 0)
     def _():
@@ -278,35 +287,65 @@
         pick_copy(low, cwx, cwo, cw1, sems.at[0])
         acc[...] = jnp.zeros_like(acc)
 
+    far_taps(rows, inner, mid_ref, None, None, mk, st)
+    (cot_sum,) = summed_chunks(rows, 16, width, 1, lambda r: (cot_ref[0, pl.ds(r, 16), :].astype(F32),))
+    acc[...] += cot_sum
+
+    @pl.when(step == 0)
+    def _():
+        pick_wait(wwx, ww1, sems.at[1])
+
+    epart[0] = dot_nt(cot_ref[0], ww1[...])
+
+    @pl.when(step == 0)
+    def _():
+        pick_wait(cwx, cw1, sems.at[0])
+
+    cpart[0] = dot_nn(st[...], cw1[...].reshape(TAPS * inner, inner))
+
+    @pl.when(step == pl.num_programs(0) - 1)
+    def _():
+        vec[...] = jnp.sum(acc[...], axis=0, keepdims=True)
+
+
+def f1_kernel(c_ref, mid_ref, up_ref, dn_ref, mk, v1_ref, cpart, epart, cwo, cwx,
+              st1, oa1, cg1, head, tail, vec, cw1, c32, acc, sems):
+    low = c_ref[0] == 0
+    step = pl.program_id(0)
+    rows, inner = mid_ref.shape[1:]
+    width = (v1_ref.shape[1] - 6 * inner) // 3
+    v1 = Vectors(v1_ref, width, inner)
+
+    @pl.when(step == 0)
+    def _():
+        pick_copy(low, cwx, cwo, cw1, sems.at[0])
+        acc[...] = jnp.zeros_like(acc)
+
     far_taps(rows, inner, mid_ref, up_ref, dn_ref, mk, st1.at[0])
-    (cot_sum,) = summed_chunks(rows, 16, width, 1, lambda r: (cot_ref[0, pl.ds(r, 16), :].astype(F32),))
-    acc[3] += cot_sum
 
     @pl.when(step == 0)
     def _():
-        pick_wait(wwx, ww1, sems.at[1])
-
-    e32[...] = dot_nt(cot_ref[0], ww1[...])
-
-    @pl.when(step == 0)
-    def _():
         pick_wait(cwx, cw1, sems.at[0])
 
-    c32[...] = dot_nn(st1[0], cw1[...].reshape(TAPS * inner, inner))
+    side = MID * inner
+    first, last = cw1[:MID].reshape(side, inner), cw1[MID + 1 :].reshape(side, inner)
+    c32[...] = cpart[0]
+    c32[:RIM1, :] += dot_nn(st1[0, :RIM1, :side], first)
+    c32[rows - RIM1 :, :] += dot_nn(st1[0, rows - RIM1 :, side + inner :], last)
 
     def stage(r):
         s = pl.ds(r, 16)
         normed, _, scale = normed_of(c32[s, :] + v1.cb)
         act, slope = gelu_parts(normed * v1.lg + v1.ls)
         oa1[0, s, :] = act.astype(BF16)
-        du, dgain, dshift = norm_back(e32[s, :], slope, normed, scale, v1.lg)
+        du, dgain, dshift = norm_back(epart[0, s, :], slope, normed, scale, v1.lg)
         du = du.astype(BF16)
         cg1[0, s, :] = du
         return dgain, dshift, du.astype(F32)
 
     sums = summed_chunks(rows, 16, inner, 3, stage)
     for k in range(3):
-        acc[k, :, :inner] += sums[k]
+        acc[k] += sums[k]
     head[...] = cg1[:, :RIM1]
     tail[...] = cg1[:, rows - RIM1 :]
 
@@ -437,43 +476,63 @@
         vec[...] = jnp.sum(acc[...], axis=1)
 
 
-def last_kernel(c_ref, ig_ref, v_ref, slc, nc, rsc, wwo, wwx, cg, head, tail, vec, ww, e32, acc, sems):
+def joint_kernel(c_ref, ng_ref, v1_ref, grad, slx, src, mux, rsx, v0_ref, slc, nc, rsc, nwo, nwx, wwo, wwx,
+                 ig, cg, head, tail, vecf, vecl, nw, ww, a32, e32, accf, accl, sems):
     low = c_ref[0] == 0
     step = pl.program_id(0)
-    rows, width = ig_ref.shape[1:]
+    rows, width = grad.shape[1:]
     inner = e32.shape[1]
-    gain = Vectors(v_ref, width, inner).lg
+    first_gain, last_gain = v1_ref[:, :width], Vectors(v0_ref, width, inner).lg
 
     @pl.when(step == 0)
     def _():
-        pick_copy(low, wwo, wwx, ww, sems.at[0])
-        acc[...] = jnp.zeros_like(acc)
-
-    (ig_sum,) = summed_chunks(rows, 16, width, 1, lambda r: (ig_ref[0, pl.ds(r, 16), :].astype(F32),))
-    acc[3] += ig_sum
-
-    @pl.when(step == 0)
-    def _():
-        pick_wait(wwo, ww, sems.at[0])
-
-    e32[...] = dot_nt(ig_ref[0], ww[...])
+        pick_copy(low, nwx, nwo, nw, sems.at[0])
+        pick_copy(low, wwo, wwx, ww, sems.at[1])
+        accf[...] = jnp.zeros_like(accf)
+        accl[...] = jnp.zeros_like(accl)
+        pick_wait(nwx, nw, sems.at[0])
+
+    a32[...] = dot_nt(ng_ref[0], nw[...])
 
     def stage(r):
         s = pl.ds(r, 16)
-        du, dgain, dshift = norm_back(e32[s, :], slc[0, s, :].astype(F32), nc[0, s, :].astype(F32), rsc[0, s, :], gain)
+        scale = rsx[0, s, :]
+        normed = (src[0, s, :].astype(F32) - mux[0, s, :]) * scale
+        du, dgain, dshift = norm_back(a32[s, :], slx[0, s, :].astype(F32), normed, scale, first_gain)
+        out = (grad[0, s, :].astype(F32) + du).astype(BF16)
+        ig[0, s, :] = out
+        return dgain, dshift, out.astype(F32)
+
+    sums = summed_chunks(rows, 16, width, 3, stage)
+    accf[0] += sums[0]
+    accf[1] += sums[1]
+    accl[3] += sums[2]
+
+    @pl.when(step == 0)
+    def _():
+        pick_wait(wwo, ww, sems.at[1])
+
+    e32[...] = dot_nt(ig[0], ww[...])
+
+    def stage2(r):
+        s = pl.ds(r, 16)
+        du, dgain, dshift = norm_back(
+            e32[s, :], slc[0, s, :].astype(F32), nc[0, s, :].astype(F32), rsc[0, s, :], last_gain
+        )
         du = du.astype(BF16)
         cg[0, s, :] = du
         return dgain, dshift, du.astype(F32)
 
-    sums = summed_chunks(rows, 16, inner, 3, stage)
+    sums = summed_chunks(rows, 16, inner, 3, stage2)
     for k in range(3):
-        acc[k, :, :inner] += sums[k]
+        accl[k, :, :inner] += sums[k]
     head[0] = cg[0, : 2 * RIM0, :].astype(F32)[:RIM0].astype(BF16)
     tail[0] = cg[0, rows - 2 * RIM0 :, :].astype(F32)[RIM0:].astype(BF16)
 
     @pl.when(step == pl.num_programs(0) - 1)
     def _():
-        vec[...] = jnp.sum(acc[...], axis=1)
+        vecf[...] = jnp.sum(accf[...], axis=1)
+        vecl[...] = jnp.sum(accl[...], axis=1)
 
 
 def weight_terms(c_arr, pairs, own, tile, unit):
@@ -529,32 +588,40 @@
     )(c_arr, *args)
 
 
-def unpack_kernel(c_ref, row_ref, sig_ref, *refs, sets, count, outs):
+def unpack_kernel(c_ref, row_ref, sig_ref, *refs, sets, shards, outs):
     n = sum(len(g[1]) for g in sets)
-    ins, grads, (held, sem) = refs[:n], refs[n:-2], refs[-2:]
+    ins, grads, (held, sems) = refs[:n], refs[n:-2], refs[-2:]
     s = pl.program_id(0)
-    half = held.shape[2] // 2
-
-    def fetch(numbers):
+    half = grads[0].shape[0] // 2
+
+    def fetch(numbers, base, sem):
+        sign = 2 * sem
         arrays = [ins[i] for i in numbers]
-        shard = held.shape[1] // count
+        shard = sum(a.shape[0] for a in arrays) // (2 * shards)
         first = 0
         for a in arrays:
-            mine = 0 if first < count else 1
+            mine = 0 if first < shards else 1
             for p in range(a.shape[0] // shard):
                 h = c_ref[0] if mine == 0 else 1 - c_ref[0]
-                to = pl.multiple_of(((first + p) % count ^ sig_ref[mine]) * shard, 16)
-                pltpu.make_async_copy(a.at[pl.ds(p * shard, shard)], held.at[h, pl.ds(to, shard)], sem).start()
+                to = pl.multiple_of(((first + p) % shards ^ sig_ref[sign + mine]) * shard + base, 16)
+                pltpu.make_async_copy(a.at[pl.ds(p * shard, shard)], held.at[h, pl.ds(to, shard)], sems.at[sem]).start()
             first += a.shape[0] // shard
 
+    def landed(numbers, base, sem):
+        part = held.at[:, base : base + sum(ins[i].shape[0] for i in numbers) // 2]
+        pltpu.make_async_copy(part, part, sems.at[sem]).wait()
+
     @pl.when(s == 0)
     def _():
-        for core, numbers in sets:
+        for core, numbers, base, sem, _ in sets:
             if core is None:
-                fetch(numbers)
+                fetch(numbers, base, sem)
             else:
-                pl.when(c_ref[0] == core)(functools.partial(fetch, numbers))
-        pltpu.make_async_copy(held, held, sem).wait()
+                pl.when(c_ref[0] == core)(functools.partial(fetch, numbers, base, sem))
+
+    for core, numbers, base, sem, step in sets:
+        if core != 0:
+            pl.when(s == step)(functools.partial(landed, numbers, base, sem))
 
     at = pl.multiple_of(row_ref[s], half)
     for k, grad in enumerate(grads):
@@ -746,28 +813,44 @@
 
     up1 = lax.ppermute(tail1, "dp", ahead)
     dn1 = lax.ppermute(head1, "dp", behind)
-    st1, oa1, cg1, rim_dn, rim_up, vec1 = call(
-        f1_kernel,
+    f_thin = o_each(inner, F32)
+    cpart, epart, vece1 = call(
+        e1_kernel,
         c_arr,
-        (mid1, up1, dn1, mk, v1, output_cotangent, cwo, cwx, wwo, wwx),
-        [e_thin, each(RIM1, inner), each(RIM1, inner), e_masks, vspec, mine(rows, width)] + [ANY] * 4,
-        [taps, thin, thin, o_rim(RIM1), o_rim(RIM1), o_vec(4, width)],
+        (mid1, mk, output_cotangent, cwo, cwx, wwo, wwx),
+        [e_thin, e_masks, mine(rows, width)] + [ANY] * 4,
+        [f_thin, f_thin, o_vec(1, width)],
         [
             pltpu.VMEM((TAPS, inner, inner), BF16),
             pltpu.VMEM((inner, width), BF16),
-            pltpu.VMEM((rows, inner), F32),
-            pltpu.VMEM((rows, inner), F32),
-            pltpu.VMEM((4, 8, width), F32),
+            pltpu.VMEM((rows, TAPS * inner), BF16),
+            pltpu.VMEM((8, width), F32),
             dma((2,)),
         ],
         3.5 * mm, 20_000_000,
     )
+    up1, dn1, cpart, epart = meet([], up1, dn1, cpart, epart)
+    st1, oa1, cg1, rim_dn, rim_up, vec1 = call(
+        f1_kernel,
+        c_arr,
+        (mid1, up1, dn1, mk, v1, cpart, epart, cwo, cwx),
+        [e_thin, each(RIM1, inner), each(RIM1, inner), e_masks, vspec, f_thin[1], f_thin[1], ANY, ANY],
+        [taps, thin, thin, o_rim(RIM1), o_rim(RIM1), o_vec(3, inner)],
+        [
+            pltpu.VMEM((TAPS, inner, inner), BF16),
+            pltpu.VMEM((rows, inner), F32),
+            pltpu.VMEM((3, 8, inner), F32),
+            dma((1,)),
+        ],
+        2 * mm, 20_000_000,
+    )
 
     upg = lax.ppermute(rim_up, "dp", ahead)
     dng = lax.ppermute(rim_dn, "dp", behind)
 
     rest = list(range(2, count.bit_length() - 1))
     big = Route([[0, *rest[:1], 1, *rest[1:]], [1, 0, *rest]], 1, sec, at, count)
+    small_way = Route([[0, 1, *rest], [1, *rest[:1], 0, *rest[1:]]], 1, sec, at, count)
     unit = 16 * count
     terms = functools.partial(weight_terms, own=own, tile=inner, unit=unit)
 
@@ -808,15 +891,22 @@
     ng1 = meet([g1], ng1)
     c_n1 = tie(c_arr, *g1.ready())
     g1.go()
-    ig1, vecf1 = first(c_n1, 1, ng1, v1, output_cotangent, mine(rows, width), slx1, out0, e_wide, mux1, rsx1)
-    cg0, rim_dn0, rim_up0, vecl0 = call(
-        last_kernel,
-        c_arr,
-        (ig1, v0, slc0, nc0, rsc0, wwo, wwx),
-        [e_wide, vspec, e_thin, e_thin, e_one, ANY, ANY],
-        [thin, o_rim(RIM0), o_rim(RIM0), o_vec(4, width)],
-        [pltpu.VMEM((inner, width), BF16), pltpu.VMEM((rows, inner), F32), pltpu.VMEM((4, 8, width), F32), dma((1,))],
-        1.3 * mm, 8_000_000,
+    ig1, cg0, rim_dn0, rim_up0, vecf1, vecl0 = call(
+        joint_kernel,
+        c_n1,
+        (ng1, v1, output_cotangent, slx1, out0, mux1, rsx1, v0, slc0, nc0, rsc0, nwo, nwx, wwo, wwx),
+        [e_thin, vspec, mine(rows, width), e_wide, e_wide, e_one, e_one, vspec, e_thin, e_thin, e_one] + [ANY] * 4,
+        [wide, thin, o_rim(RIM0), o_rim(RIM0), o_vec(2, width), o_vec(4, width)],
+        [
+            pltpu.VMEM((width, inner), BF16),
+            pltpu.VMEM((inner, width), BF16),
+            pltpu.VMEM((rows, width), F32),
+            pltpu.VMEM((rows, inner), F32),
+            pltpu.VMEM((2, 8, width), F32),
+            pltpu.VMEM((4, 8, width), F32),
+            dma((2,)),
+        ],
+        2.6 * mm, 18_000_000,
     )
     cg0, rim_dn0, rim_up0 = meet([g1], cg0, rim_dn0, rim_up0)
     up0, dn0 = lax.ppermute(rim_up0, "dp", ahead), lax.ppermute(rim_dn0, "dp", behind)
@@ -870,7 +960,7 @@
     g4_terms = terms(tie(c_arr, *g1.ready()), [(act1, ng1), (act0, ng0)])
     g1.go()
     g4_terms = meet([g1, g3], *g4_terms)
-    g4 = Chain(*g4_terms, big)
+    g4 = Chain(*g4_terms, small_way)
     g4.go()
     ig0, vecf0 = first(
         tie(c_arr, *g1.ready(), *g3.ready()), 0, ng0, v0, ig1, e_wide, slx0, block_input, mine(rows, width), mux0, rsx0
@@ -879,13 +969,12 @@
     g3.go()
     ig0, vecf0 = meet([g1, g3, g4], ig0, vecf0)
 
-    def padded(v):
-        return jnp.pad(v, ((0, 0), (0, width - v.shape[1])))
-
-    terms_small = [vec1, padded(vecm1), vecf1, vecl0, padded(vecm0), vecf0, padded(tot)]
-    small = jnp.concatenate(terms_small, axis=0)
-    small = jnp.pad(small, ((0, -small.shape[0] % 8), (0, 0)))
-    small = small + swapped(small)
+    smalls = (vec1, vece1, vecm1, vecf1, vecl0, vecm0, vecf0, tot)
+    height = -(-sum(v.shape[0] for v in smalls) // 8) * 8
+    small = pl.pallas_call(stack_kernel, out_shape=jax.ShapeDtypeStruct((height, width), F32))(*smalls)
+    come = swapped(small)
+    block_outputs, input_grads = gathered(*held_out), gathered(*handed(ig0, ig1))
+    small = small + come
     for pairs, _ in big.steps:
         small = small + hop(small, pairs)
     s1, sm1, sf1, sl0, sm0, sf0, st = jnp.split(small, [4, 7, 9, 13, 16, 18], axis=0)
@@ -893,48 +982,36 @@
 
     half = inner // 2
     cols = width // inner
-
-    block_outputs, input_grads = gathered(*held_out), gathered(*handed(ig0, ig1))
-
-    def unpacked(c, chains, row_arr, out_specs, out_shape, firsts):
-        parts, sets = [], []
-        for core, chain in chains:
-            pieces = chain.finish()
-            sets.append((core, list(range(len(parts), len(parts) + len(pieces)))))
-            parts += pieces
-        return pl.pallas_call(
-            functools.partial(unpack_kernel, sets=sets, count=chain.route.shards, outs=firsts),
-            grid_spec=pltpu.PrefetchScalarGridSpec(
-                num_scalar_prefetch=3,
-                grid=(row_arr.shape[0],),
-                in_specs=[ANY] * len(parts),
-                out_specs=out_specs,
-                scratch_shapes=[pltpu.VMEM((2, sum(p.shape[0] for p in pieces) // 2, inner), BF16), dma(())],
-            ),
-            out_shape=out_shape,
-            compiler_params=pltpu.CompilerParams(vmem_limit_bytes=VMEM_LIMIT),
-            cost_estimate=pl.CostEstimate(flops=0, bytes_accessed=5_000_000, transcendentals=0),
-        )(c, row_arr, chain.route.signs, *parts)
-
-    widen_grad, conv_grad = unpacked(
-        tie(c_arr, block_outputs, input_grads),
-        [(1, g1), (0, g3)],
-        jnp.arange(cols + TAPS, dtype=jnp.int32) * half,
-        [
-            pl.BlockSpec((inner, inner), lambda s, *_: (0, jnp.minimum(s, cols - 1))),
-            pl.BlockSpec((1, inner, inner), lambda s, *_: (jnp.maximum(s - cols, 0), 0, 0)),
+    parts, sets, base = [], [], 0
+    for core, chain, sem, step in ((1, g1, 0, 0), (0, g3, 0, 0), (None, g4, 1, TAPS + cols)):
+        pieces = chain.finish()
+        sets.append((core, list(range(len(parts), len(parts) + len(pieces))), sem * base, sem, step))
+        base = (base if sem else 0) + sum(p.shape[0] for p in pieces) // 2
+        parts += pieces
+    top = sets[2][2]
+    wide_rows = jnp.arange(cols + TAPS, dtype=jnp.int32) * half
+    narrow_rows = (jnp.arange(cols, dtype=jnp.int32) + jnp.where(low, cols, 0).astype(jnp.int32)) * half + top
+    widen_grad, conv_grad, narrow_grad = pl.pallas_call(
+        functools.partial(unpack_kernel, sets=sets, shards=big.shards, outs=[0, cols, cols + TAPS]),
+        grid_spec=pltpu.PrefetchScalarGridSpec(
+            num_scalar_prefetch=3,
+            grid=(2 * cols + TAPS,),
+            in_specs=[ANY] * len(parts),
+            out_specs=[
+                pl.BlockSpec((inner, inner), lambda s, *_: (0, jnp.minimum(s, cols - 1))),
+                pl.BlockSpec((1, inner, inner), lambda s, *_: (jnp.clip(s - cols, 0, TAPS - 1), 0, 0)),
+                pl.BlockSpec((inner, inner), lambda s, *_: (jnp.maximum(s - cols - TAPS, 0), 0)),
+            ],
+            scratch_shapes=[pltpu.VMEM((2, base, inner), BF16), dma((2,))],
+        ),
+        out_shape=[
+            jax.ShapeDtypeStruct((inner, width), F32),
+            jax.ShapeDtypeStruct((TAPS, inner, inner), F32),
+            jax.ShapeDtypeStruct((width, inner), F32),
         ],
-        [jax.ShapeDtypeStruct((inner, width), F32), jax.ShapeDtypeStruct((TAPS, inner, inner), F32)],
-        [0, cols],
-    )
-    (narrow_grad,) = unpacked(
-        tie(c_arr, conv_grad),
-        [(None, g4)],
-        (jnp.arange(cols, dtype=jnp.int32) + jnp.where(low, cols, 0).astype(jnp.int32)) * half,
-        [pl.BlockSpec((inner, inner), lambda s, *_: (s, 0))],
-        [jax.ShapeDtypeStruct((width, inner), F32)],
-        [0],
-    )
+        compiler_params=pltpu.CompilerParams(vmem_limit_bytes=VMEM_LIMIT),
+        cost_estimate=pl.CostEstimate(flops=0, bytes_accessed=500_000, transcendentals=0),
+    )(tie(c_arr, block_outputs, input_grads), jnp.concatenate([wide_rows, narrow_rows]), jnp.concatenate([big.signs, small_way.signs]), *parts)
 
     def sel(in0, in1, n=width):
         return jnp.where(low, in0, in1)[None, :n]

time: 354 us -> 342 us (0.966)
  waiting for transfers between devices: 104 us -> 82.1 us
  Pallas kernels: 153 us -> 157 us
    ppermute x1, waiting for transfers between devices: 16.3 us -> 3.65 us  [body(): up1 = lax.ppermute(tail1, 'dp', ahead)]
    ppermute x25, waiting for transfers between devices: 75.6 us -> 66.3 us  [hop(): return lax.ppermute(v, ('section', 'dp'), pairs)]
    pallas_call x8, Pallas kernels: 107 us -> 113 us  [call(): pl.pallas_call(kernel, grid_spec=pltpu.PrefetchScalarGridSpec(num_scalar_...]
  transfers between devices with their start and end apart: 49 -> 49, of which waited for: 21 -> 20; matrix products, arithmetic and copies ran while one was open for 8% -> 9% of each run, Pallas kernels for 29% -> 31%
where the time goes in v4:
time: 342 us; the launch traced here: 340 us
  Pallas kernels  157 us (46%)
  waiting for transfers between devices  82.1 us (24%)
  starting transfers between devices  53 us (15%)
  other arithmetic  35.7 us (10%)
  local copies, waits for them, and re-layouts  10.5 us (3%)
    pallas_call x8, Pallas kernels, call(): pl.pallas_call(kernel, grid_spec=pltpu.PrefetchScalarGridSpec(num_scalar_...  113 us
    ppermute x25, waiting for transfers between devices, hop(): return lax.ppermute(v, ('section', 'dp'), pairs)  66.3 us
    pallas_call x3, Pallas kernels, weight_terms(): pl.pallas_call(kernel, grid_spec=pltpu.PrefetchScalarGridSpec(num_scalar_...  31.1 us
    ppermute x25, starting transfers between devices, hop(): return lax.ppermute(v, ('section', 'dp'), pairs)  25.6 us
    convert_element_type x15, other arithmetic, add_low(): return (one.astype(F32) + other.astype(F32)).astype(BF16)  18.6 us
    pallas_call x1, Pallas kernels, body(): pl.pallas_call(functools.partial(unpack_kernel, sets=sets, shards=big.sha...  10.7 us
    unnamed x81, local copies, waits for them, and re-layouts  8.84 us
  transfers between devices with their start and end apart: 49, of which 20 were waited for; matrix products, arithmetic and copies ran while one was open for 9% of the time, Pallas kernels for 31%

profile of v4, /device:TPU:0, one launch (start us, length us, event | category | flops | bytes accessed | tf_op | source)
XLA Modules:
  0.0 340.2 jit_solution(15493506643049498362)
XLA Ops:
  3.5 3.0 collective-permute-start
  6.5 4.1 %collective-permute-start.1 = (bf16[3,8,1280]{2,1,0:T(8,128)(2,1)S(1)}, bf16[3,8,1280]{2,1,0:T(8,128)(2,1)S(1)}, u32[]{:S(2)}, u32[]{:S(2)}) collective-permute-start(bf16[3,8,1280]{2,1,0:T(8,128)(2,1)S(1)} %get-tuple-element.219), channel_id=1, source_target_pairs={{1,0},{2,1},{3,2},{4,3},{5,4},{6,5},{7,6},{8,7},{9,8},{10,9},{11,1... | collective-permute-start | bytes 184328 | tf_op jit(solution)/shard_map/ppermute | solution.py:749
  14.3 2.3 collective-permute-done.3.nwx
  17.8 29.7 %shard_map.307 = (f32[3,256,128]{2,1,0:T(8,128)}, bf16[3,256,1280]{2,1,0:T(8,128)(2,1)}, bf16[3,256,1280]{2,1,0:T(8,128)(2,1)}, f32[3,256,1]{2,1,0:T(8,128)}, f3...) custom-call(s32[1]{0:T(128)} %bitcast.c_ref, ...), custom_call_target="tpu_custom_call" | custom-call | flops 69206016 | bytes 400000 | tf_op jit(solution)/shard_map/pallas_call | solution.py:762
  47.5 5.6 %collective-permute-start.7 = (bf16[3,128,640]{2,1,0:T(8,128)(2,1)}, bf16[3,128,640]{2,1,0:T(8,128)(2,1)S(1)}, u32[]{:S(2)}, u32[]{:S(2)}) collective-permute-start(bf16[3,128,640]{2,1,0:T(8,128)(2,1)} %get-tuple-element.116), channel_id=1, source_target_pairs={{1,0},{2,1},{3,2},{4,3},{5,4},{6,5},{7,6},{8,7},{9,8},{10,9},{11,1... | collective-permute-start | bytes 1474568 | tf_op jit(solution)/shard_map/ppermute | solution.py:815
  53.2 12.6 %shard_map.308 = (f32[3,256,640]{2,1,0:T(8,128)}, f32[3,256,640]{2,1,0:T(8,128)}, f32[1,1280]{1,0:T(1,128)}) custom-call(s32[1]{0:T(128)} %bitcast.c_ref, bf16[3,256,640]{2,1,0:T(8,128)(2,1)} %get-tuple-element.114.mid_ref, f32[3,256,128]{2,1,0:T(8,128)} %get-tuple-element.117.mk.refs_2_.refs_1_, bf16[6,256,1280]{2,1,0:T(8,128)(2,1)} %grad.1, ...), custom_call_target="tpu_custom_call" | custom-call | flops 44040192 | bytes 200000 | tf_op jit(solution)/shard_map/pallas_call | solution.py:762
  65.8 3.6 %collective-permute-done.6.up_ref = bf16[3,128,640]{2,1,0:T(8,128)(2,1)S(1)} collective-permute-done((bf16[3,128,640]{2,1,0:T(8,128)(2,1)}, bf16[3,128,640]{2,1,0:T(8,128)(2,1)S(1)}, u32[]{:S(2)}, u32[]{:S(2)}) %collective-permute-start.6) | collective-permute-done | bytes 491552 | tf_op jit(solution)/shard_map/ppermute | solution.py:814
  70.8 12.1 %shard_map.309 = (bf16[3,256,3200]{2,1,0:T(8,128)(2,1)}, bf16[3,256,640]{2,1,0:T(8,128)(2,1)}, bf16[3,256,640]{2,1,0:T(8,128)(2,1)}, bf16[3,128,640]{2,1,0:T(8,1...) custom-call(s32[1]{0:T(128)} %bitcast.c_ref, bf16[3,256,640]{2,1,0:T(8,128)(2,1)} %get-tuple-element.114.mid_ref, ...), custom_call_target="tpu_custom_call" | custom-call | flops 25165824 | bytes 200000 | tf_op jit(solution)/shard_map/pallas_call | solution.py:762
  82.9 2.1 collective-permute-start.8
  84.9 3.6 %collective-permute-start.9 = (bf16[3,128,640]{2,1,0:T(8,128)(2,1)}, bf16[3,128,640]{2,1,0:T(8,128)(2,1)S(1)}, u32[]{:S(2)}, u32[]{:S(2)}) collective-permute-start(bf16[3,128,640]{2,1,0:T(8,128)(2,1)} %get-tuple-element.125), channel_id=1, source_target_pairs={{1,0},{2,1},{3,2},{4,3},{5,4},{6,5},{7,6},{8,7},{9,8},{10,9},{11,1... | collective-permute-start | bytes 1474568 | tf_op jit(solution)/shard_map/ppermute | solution.py:849
  88.5 11.6 %shard_map.310 = (bf16[2304,640]{1,0:T(8,128)(2,1)}, bf16[2304,640]{1,0:T(8,128)(2,1)}) custom-call(s32[1]{0:T(128)} %bitcast.c_ref, bf16[3,256,640]{2,1,0:T(8,128)(2,1)} %get-tuple-element.127.refs_0_.oa_ref, bf16[6,256,1280]{2,1,0:T(8,128)(2,1)} %grad.1, bf16[3,256,3200]{2,1,0:T(8,128)(2,1)} %get-tuple-element.128.refs_2_, ...), custom_call_target="tpu_custom_call" | custom-call | flops 44040192 | bytes 58982 | tf_op jit(solution)/shard_map/pallas_call | solution.py:574
  100.1 5.9 %collective-permute-done.8.refs_0_ = bf16[3,128,640]{2,1,0:T(8,128)(2,1)S(1)} collective-permute-done((bf16[3,128,640]{2,1,0:T(8,128)(2,1)}, bf16[3,128,640]{2,1,0:T(8,128)(2,1)S(1)}, u32[]{:S(2)}, u32[]{:S(2)}) %collective-permute-start.8) | collective-permute-done | bytes 491552 | tf_op jit(solution)/shard_map/ppermute | solution.py:848
  106.1 1.8 collective-permute-done.9.refs_1_
  108.7 11.8 %shard_map.311 = (bf16[3,256,640]{2,1,0:T(8,128)(2,1)}, f32[3,640]{1,0:T(4,128)}) custom-call(s32[1]{0:T(128)} %bitcast.c_ref, bf16[3,256,640]{2,1,0:T(8,128)(2,1)} %get-tuple-element.129.refs_3_.cg_ref, bf16[3,128,640]{2,1,0:T(8,128)(2,1)} %copy-done.33, bf16[3,128,640]{2,1,0:T(8,128)(2,1)} %copy-done.34, ...), custom_call_target="tpu_custom_call" | custom-call | flops 32715572 | bytes 100000 | tf_op jit(solution)/shard_map/pallas_call | solution.py:762
  120.5 1.6 copy-done.17
  122.1 2.5 add_convert_fusion.3
  125.5 15.4 %shard_map.312 = (bf16[3,256,1280]{2,1,0:T(8,128)(2,1)}, bf16[3,256,640]{2,1,0:T(8,128)(2,1)}, bf16[3,8,640]{2,1,0:T(8,128)(2,1)}, bf16[3,8,640]{2,1,0:T(8,128)(...) custom-call(s32[1]{0:T(128)} %bitcast.c_ref, bf16[3,256,640]{2,1,0:T(8,128)(2,1)} %get-tuple-element.142.ng_ref.refs_1_, ...), custom_call_target="tpu_custom_call" | custom-call | flops 32715572 | bytes 180000 | tf_op jit(solution)/shard_map/pallas_call | solution.py:762
  140.9 3.3 collective-permute-done.11
  144.2 1.7 add_convert_fusion.8
  145.9 2.2 collective-permute-start.12
  148.4 5.3 %collective-permute-start.14 = (bf16[3,8,640]{2,1,0:T(8,128)(2,1)S(1)}, bf16[3,8,640]{2,1,0:T(8,128)(2,1)S(1)}, u32[]{:S(2)}, u32[]{:S(2)}) collective-permute-start(bf16[3,8,640]{2,1,0:T(8,128)(2,1)S(1)} %copy-done.38), channel_id=1, source_target_pairs={{1,0},{2,1},{3,2},{4,3},{5,4},{6,5},{7,6},{8,7},{9,8},{10,9},{11,1... | collective-permute-start | bytes 92168 | tf_op jit(solution)/shard_map/ppermute | solution.py:912
  153.8 11.6 %shard_map.313 = (bf16[2304,640]{1,0:T(8,128)(2,1)}, bf16[2304,640]{1,0:T(8,128)(2,1)}) custom-call(s32[1]{0:T(128)} %bitcast.c_ref, bf16[3,256,640]{2,1,0:T(8,128)(2,1)} %get-tuple-element.156.refs_0_, bf16[3,256,1280]{2,1,0:T(8,128)(2,1)} %get-tuple-element.157.refs_1_.grad, bf16[3,256,3200]{2,1,0:T(8,128)(2,1)} %get-tuple-element.158.refs_2_, ...), custom_call_target="tpu_custom_call" | custom-call | flops 44040192 | bytes 58982 | tf_op jit(solution)/shard_map/pallas_call | solution.py:574
  167.3 8.8 %shard_map.314 = (bf16[3,256,1280]{2,1,0:T(8,128)(2,1)}, f32[2,128]{1,0:T(2,128)}) custom-call(s32[1]{0:T(128)} %bitcast.c_ref, bf16[3,256,1280]{2,1,0:T(8,128)(2,1)} %get-tuple-element.113.src.out0_ref, bf16[3,256,640]{2,1,0:T(8,128)(2,1)} %get-tuple-element.127.refs_0_.oa_ref, s32[6,256]{1,0:T(8,128)} %rt_ref.1, s32[6,256]{1,0:T(8,128)} %lm_ref.1, ...), custom_call_target="tpu_custom_call" | custom-call | flops 15099494 | bytes 80000 | tf_op jit(solution)/shard_map/pallas_call | solution.py:762
  176.2 3.8 %add_convert_fusion = (bf16[1152,640]{1,0:T(8,128)(2,1)S(1)}, bf16[1152,640]{1,0:T(8,128)(2,1)}) fusion(bf16[2304,640]{1,0:T(8,128)(2,1)} %collective-permute-done.17, s32[]{:T(128)S(6)} %select_n.195, bf16[2304,640]{1,0:T(8,128)(2,1)S(1)} %copy-done.16, s32[]{:T(128)S(6)} %select_n.198), kind=kLoop, calls=%fused_computation.2 | loop fusion | flops 5898240 | bytes 8847368 | tf_op jit(solution)/shard_map/convert_element_type | solution.py:638
  181.6 12.1 %shard_map.315 = (bf16[3,256,640]{2,1,0:T(8,128)(2,1)}, f32[3,640]{1,0:T(4,128)}) custom-call(s32[1]{0:T(128)} %bitcast.c_ref, bf16[3,256,640]{2,1,0:T(8,128)(2,1)} %get-tuple-element.159.refs_3_.cg_ref, bf16[3,16,640]{2,1,0:T(8,128)(2,1)} %pad_maximum_fusion.7.refs_0_, f32[3,256,128]{2,1,0:T(8,128)} %get-tuple-element.117.mk.refs_2_.refs_1_, ...), custom_call_target="tpu_custom_call" | custom-call | flops 32715572 | bytes 100000 | tf_op jit(solution)/shard_map/pallas_call | solution.py:762
  193.8 5.7 %collective-permute-done.18 = bf16[288,640]{1,0:T(8,128)(2,1)S(1)} collective-permute-done((bf16[288,640]{1,0:T(8,128)(2,1)S(1)}, bf16[288,640]{1,0:T(8,128)(2,1)S(1)}, u32[]{:S(2)}, u32[]{:S(2)}) %collective-permute-start.18) | collective-permute-done | bytes 368672 | tf_op jit(solution)/shard_map/ppermute | solution.py:719
  200.6 7.9 %shard_map.316 = (bf16[1280,640]{1,0:T(8,128)(2,1)}, bf16[1280,640]{1,0:T(8,128)(2,1)}) custom-call(s32[1]{0:T(128)} %bitcast.c_ref, bf16[3,256,1280]{2,1,0:T(8,128)(2,1)} %get-tuple-element.179.refs_0_, bf16[3,256,640]{2,1,0:T(8,128)(2,1)} %get-tuple-element.142.ng_ref.refs_1_, bf16[3,256,1280]{2,1,0:T(8,128)(2,1)} %get-tuple-element.180.refs_2_, ...), custom_call_target="tpu_custom_call" | custom-call | flops 25165824 | bytes 32768 | tf_op jit(solution)/shard_map/pallas_call | solution.py:574
  210.6 2.8 add_convert_fusion.6
  213.5 2.0 collective-permute-start.21
  215.5 10.1 %shard_map.317 = (bf16[3,256,1280]{2,1,0:T(8,128)(2,1)}, f32[2,1280]{1,0:T(2,128)}) custom-call(s32[1]{0:T(128)} %bitcast.c_ref, bf16[3,256,640]{2,1,0:T(8,128)(2,1)} %get-tuple-element.181.refs_3_.ng_ref, f32[1,7680]{1,0:T(1,128)} %get-tuple-element.246.v0_ref.refs_2_.v_ref, bf16[3,256,1280]{2,1,0:T(8,128)(2,1)} %get-tuple-element.157.refs_1_.grad, ...), custom_call_target="tpu_custom_call" | custom-call | flops 16357785 | bytes 100000 | tf_op jit(solution)/shard_map/pallas_call | solution.py:762
  225.6 7.5 %collective-permute-done.21 = bf16[576,640]{1,0:T(8,128)(2,1)S(1)} collective-permute-done((bf16[576,640]{1,0:T(8,128)(2,1)S(1)}, bf16[576,640]{1,0:T(8,128)(2,1)S(1)}, u32[]{:S(2)}, u32[]{:S(2)}) %collective-permute-start.21) | collective-permute-done | bytes 737312 | tf_op jit(solution)/shard_map/ppermute | solution.py:719
  233.9 2.7 add_convert_fusion.5
  236.7 1.8 add_convert_fusion.14
  239.7 1.5 shard_map.318
  243.8 2.1 collective-permute-start.26
  245.9 4.5 %collective-permute-done.33 = bf16[288,640]{1,0:T(8,128)(2,1)} collective-permute-done((bf16[288,640]{1,0:T(8,128)(2,1)}, bf16[288,640]{1,0:T(8,128)(2,1)}, u32[]{:S(2)}, u32[]{:S(2)}) %collective-permute-start.33) | collective-permute-done | bytes 368672 | tf_op jit(solution)/shard_map/ppermute | solution.py:719
  255.6 2.0 broadcast_select_fusion.5
  258.7 7.4 %collective-permute-done.34 = bf16[288,640]{1,0:T(8,128)(2,1)S(1)} collective-permute-done((bf16[288,640]{1,0:T(8,128)(2,1)S(1)}, bf16[288,640]{1,0:T(8,128)(2,1)S(1)}, u32[]{:S(2)}, u32[]{:S(2)}) %collective-permute-start.34) | collective-permute-done | bytes 368672 | tf_op jit(solution)/shard_map/ppermute | solution.py:719
  270.2 6.6 %collective-permute-done.35 = bf16[288,640]{1,0:T(8,128)(2,1)S(1)} collective-permute-done((bf16[288,640]{1,0:T(8,128)(2,1)S(1)}, bf16[288,640]{1,0:T(8,128)(2,1)S(1)}, u32[]{:S(2)}, u32[]{:S(2)}) %collective-permute-start.35) | collective-permute-done | bytes 368672 | tf_op jit(solution)/shard_map/ppermute | solution.py:719
  277.1 1.8 collective-permute-start.43
  279.5 10.0 %collective-permute-done.43 = bf16[160,640]{1,0:T(8,128)(2,1)S(1)} collective-permute-done((bf16[160,640]{1,0:T(8,128)(2,1)S(1)}, bf16[160,640]{1,0:T(8,128)(2,1)S(1)}, u32[]{:S(2)}, u32[]{:S(2)}) %collective-permute-start.43) | collective-permute-done | bytes 204832 | tf_op jit(solution)/shard_map/ppermute | solution.py:719
  289.4 3.4 collective-permute-start.29
  293.1 2.6 collective-permute-done.29
  296.7 2.3 maximum_bitcast_fusion
  300.9 10.6 %collective-permute-done.45 = bf16[320,640]{1,0:T(8,128)(2,1)S(1)} collective-permute-done((bf16[320,640]{1,0:T(8,128)(2,1)S(1)}, bf16[320,640]{1,0:T(8,128)(2,1)S(1)}, u32[]{:S(2)}, u32[]{:S(2)}) %collective-permute-start.45) | collective-permute-done | bytes 409632 | tf_op jit(solution)/shard_map/ppermute | solution.py:719
  316.7 7.3 %collective-permute-done.46.refs_9_ = bf16[640,640]{1,0:T(8,128)(2,1)S(1)} collective-permute-done((bf16[640,640]{1,0:T(8,128)(2,1)S(1)}, bf16[640,640]{1,0:T(8,128)(2,1)S(1)}, u32[]{:S(2)}, u32[]{:S(2)}) %collective-permute-start.46) | collective-permute-done | bytes 819232 | tf_op jit(solution)/shard_map/ppermute | solution.py:719
  324.9 2.3 maximum_bitcast_fusion.1
  329.3 10.7 %shard_map.319 = (f32[640,1280]{1,0:T(8,128)}, f32[5,640,640]{2,1,0:T(8,128)}, f32[1280,640]{1,0:T(8,128)}) custom-call(s32[1]{0:T(128)} %bitcast.c_ref, s32[9]{0:T(128)} %pad_add_fusion.row_ref, s32[4]{0:T(128)} %pad_add_fusion.1.sig_ref, bf16[1152,640]{1,0:T(8,128)(2,1)} %copy-done.7, bf16[1152,640]{1,0:T(8,128)(2,1)} %copy-done.19, ...), custom_call_target="tpu_custom_call" | custom-call | bytes 500000 | tf_op jit(solution)/shard_map/pallas_call | solution.py:994
  (192 shorter events, 45.0 us)
Async XLA Ops:
  0.7 16.0 %collective-permute-start.4 = (bf16[5,640,640]{2,1,0:T(8,128)(2,1)}, bf16[5,640,640]{2,1,0:T(8,128)(2,1)}, u32[]{:S(2)}, u32[]{:S(2)}) collective-permute-start(bf16[5,640,640]{2,1,0:T(8,128)(2,1)} %bitcast.19), channel_id=1, source_target_pairs={{0,16},{16,0},{1,17},{17,1},{2,18},{18,2},{3,19},{19,3},{4,20},{20... | collective-permute-start | bytes 12288008 | tf_op jit(solution)/shard_map/ppermute | solution.py:715
  2.6 8.0 %collective-permute-start.2 = (f32[1,7680]{1,0:T(1,128)}, f32[1,7680]{1,0:T(1,128)S(1)}, u32[]{:S(2)}, u32[]{:S(2)}) collective-permute-start(f32[1,7680]{1,0:T(1,128)} %shard_map.306), channel_id=1, source_target_pairs={{0,16},{16,0},{1,17},{17,1},{2,18},{18,2},{3,19},{19,3},{4,20},{20... | collective-permute-start | bytes 92168 | tf_op jit(solution)/shard_map/ppermute | solution.py:715
  3.5 9.3 %collective-permute-start = (bf16[3,8,1280]{2,1,0:T(8,128)(2,1)S(1)}, bf16[3,8,1280]{2,1,0:T(8,128)(2,1)S(1)}, u32[]{:S(2)}, u32[]{:S(2)}) collective-permute-start(bf16[3,8,1280]{2,1,0:T(8,128)(2,1)S(1)} %get-tuple-element.218), channel_id=1, source_target_pairs={{0,1},{1,2},{2,3},{3,4},{4,5},{5,6},{6,7},{7,8},{8,9},{9,10},{10,1... | collective-permute-start | bytes 184328 | tf_op jit(solution)/shard_map/ppermute | solution.py:749
  6.5 6.3 %collective-permute-start.1 = (bf16[3,8,1280]{2,1,0:T(8,128)(2,1)S(1)}, bf16[3,8,1280]{2,1,0:T(8,128)(2,1)S(1)}, u32[]{:S(2)}, u32[]{:S(2)}) collective-permute-start(bf16[3,8,1280]{2,1,0:T(8,128)(2,1)S(1)} %get-tuple-element.219), channel_id=1, source_target_pairs={{1,0},{2,1},{3,2},{4,3},{5,4},{6,5},{7,6},{8,7},{9,8},{10,9},{11,1... | collective-permute-start | bytes 184328 | tf_op jit(solution)/shard_map/ppermute | solution.py:749
  10.6 3.7 %collective-permute-start.5 = (bf16[640,1280]{1,0:T(8,128)(2,1)}, bf16[640,1280]{1,0:T(8,128)(2,1)S(1)}, u32[]{:S(2)}, u32[]{:S(2)}) collective-permute-start(bf16[640,1280]{1,0:T(8,128)(2,1)} %bitcast.25), channel_id=1, source_target_pairs={{0,16},{16,0},{1,17},{17,1},{2,18},{18,2},{3,19},{19,3},{4,20},{20... | collective-permute-start | bytes 4915208 | tf_op jit(solution)/shard_map/ppermute | solution.py:715
  10.6 6.1 %collective-permute-start.3 = (bf16[1280,640]{1,0:T(8,128)(2,1)}, bf16[1280,640]{1,0:T(8,128)(2,1)S(1)}, u32[]{:S(2)}, u32[]{:S(2)}) collective-permute-start(bf16[1280,640]{1,0:T(8,128)(2,1)} %bitcast.30), channel_id=1, source_target_pairs={{0,16},{16,0},{1,17},{17,1},{2,18},{18,2},{3,19},{19,3},{4,20},{20... | collective-permute-start | bytes 4915208 | tf_op jit(solution)/shard_map/ppermute | solution.py:715
  47.5 22.0 %collective-permute-start.6 = (bf16[3,128,640]{2,1,0:T(8,128)(2,1)}, bf16[3,128,640]{2,1,0:T(8,128)(2,1)S(1)}, u32[]{:S(2)}, u32[]{:S(2)}) collective-permute-start(bf16[3,128,640]{2,1,0:T(8,128)(2,1)} %get-tuple-element.115), channel_id=1, source_target_pairs={{0,1},{1,2},{2,3},{3,4},{4,5},{5,6},{6,7},{7,8},{8,9},{9,10},{10,1... | collective-permute-start | bytes 1474568 | tf_op jit(solution)/shard_map/ppermute | solution.py:814
  47.5 22.4 %collective-permute-start.7 = (bf16[3,128,640]{2,1,0:T(8,128)(2,1)}, bf16[3,128,640]{2,1,0:T(8,128)(2,1)S(1)}, u32[]{:S(2)}, u32[]{:S(2)}) collective-permute-start(bf16[3,128,640]{2,1,0:T(8,128)(2,1)} %get-tuple-element.116), channel_id=1, source_target_pairs={{1,0},{2,1},{3,2},{4,3},{5,4},{6,5},{7,6},{8,7},{9,8},{10,9},{11,1... | collective-permute-start | bytes 1474568 | tf_op jit(solution)/shard_map/ppermute | solution.py:815
  82.9 23.2 %collective-permute-start.8 = (bf16[3,128,640]{2,1,0:T(8,128)(2,1)}, bf16[3,128,640]{2,1,0:T(8,128)(2,1)S(1)}, u32[]{:S(2)}, u32[]{:S(2)}) collective-permute-start(bf16[3,128,640]{2,1,0:T(8,128)(2,1)} %get-tuple-element.124), channel_id=1, source_target_pairs={{0,1},{1,2},{2,3},{3,4},{4,5},{5,6},{6,7},{7,8},{8,9},{9,10},{10,1... | collective-permute-start | bytes 1474568 | tf_op jit(solution)/shard_map/ppermute | solution.py:848
  84.9 22.9 %collective-permute-start.9 = (bf16[3,128,640]{2,1,0:T(8,128)(2,1)}, bf16[3,128,640]{2,1,0:T(8,128)(2,1)S(1)}, u32[]{:S(2)}, u32[]{:S(2)}) collective-permute-start(bf16[3,128,640]{2,1,0:T(8,128)(2,1)} %get-tuple-element.125), channel_id=1, source_target_pairs={{1,0},{2,1},{3,2},{4,3},{5,4},{6,5},{7,6},{8,7},{9,8},{10,9},{11,1... | collective-permute-start | bytes 1474568 | tf_op jit(solution)/shard_map/ppermute | solution.py:849
  108.7 11.8 %collective-permute-start.10 = (bf16[2304,640]{1,0:T(8,128)(2,1)}, bf16[2304,640]{1,0:T(8,128)(2,1)S(1)}, u32[]{:S(2)}, u32[]{:S(2)}) collective-permute-start(bf16[2304,640]{1,0:T(8,128)(2,1)} %get-tuple-element.133), channel_id=1, source_target_pairs={{0,16},{16,0},{1,17},{17,1},{2,18},{18,2},{3,19},{19,3},{4,20},{20... | collective-permute-start | bytes 8847368 | tf_op jit(solution)/shard_map/ppermute | solution.py:715
  124.6 19.5 %collective-permute-start.11 = (bf16[1152,640]{1,0:T(8,128)(2,1)S(1)}, bf16[1152,640]{1,0:T(8,128)(2,1)}, u32[]{:S(2)}, u32[]{:S(2)}) collective-permute-start(bf16[1152,640]{1,0:T(8,128)(2,1)S(1)} %get-tuple-element.217), channel_id=1, source_target_pairs={{0,1},{1,0},{2,3},{3,2},{4,5},{5,4},{6,7},{7,6},{8,9},{9,8},{10,11... | collective-permute-start | bytes 4423688 | tf_op jit(solution)/shard_map/ppermute | solution.py:719
  145.9 19.5 %collective-permute-start.12 = (bf16[576,640]{1,0:T(8,128)(2,1)S(1)}, bf16[576,640]{1,0:T(8,128)(2,1)S(1)}, u32[]{:S(2)}, u32[]{:S(2)}) collective-permute-start(bf16[576,640]{1,0:T(8,128)(2,1)S(1)} %get-tuple-element.225), channel_id=1, source_target_pairs={{0,4},{1,5},{2,6},{3,7},{4,0},{5,1},{6,2},{7,3},{8,12},{9,13},{10,... | collective-permute-start | bytes 2211848 | tf_op jit(solution)/shard_map/ppermute | solution.py:719
  148.2 17.2 %collective-permute-start.13 = (bf16[3,8,640]{2,1,0:T(8,128)(2,1)S(1)}, bf16[3,8,640]{2,1,0:T(8,128)(2,1)S(1)}, u32[]{:S(2)}, u32[]{:S(2)}) collective-permute-start(bf16[3,8,640]{2,1,0:T(8,128)(2,1)S(1)} %copy-done.39), channel_id=1, source_target_pairs={{0,1},{1,2},{2,3},{3,4},{4,5},{5,6},{6,7},{7,8},{8,9},{9,10},{10,1... | collective-permute-start | bytes 92168 | tf_op jit(solution)/shard_map/ppermute | solution.py:912
  148.4 17.0 %collective-permute-start.14 = (bf16[3,8,640]{2,1,0:T(8,128)(2,1)S(1)}, bf16[3,8,640]{2,1,0:T(8,128)(2,1)S(1)}, u32[]{:S(2)}, u32[]{:S(2)}) collective-permute-start(bf16[3,8,640]{2,1,0:T(8,128)(2,1)S(1)} %copy-done.38), channel_id=1, source_target_pairs={{1,0},{2,1},{3,2},{4,3},{5,4},{6,5},{7,6},{8,7},{9,8},{10,9},{11,1... | collective-permute-start | bytes 92168 | tf_op jit(solution)/shard_map/ppermute | solution.py:912
  165.4 10.8 %collective-permute-start.17 = (bf16[2304,640]{1,0:T(8,128)(2,1)}, bf16[2304,640]{1,0:T(8,128)(2,1)}, u32[]{:S(2)}, u32[]{:S(2)}) collective-permute-start(bf16[2304,640]{1,0:T(8,128)(2,1)} %get-tuple-element.166), channel_id=1, source_target_pairs={{0,16},{16,0},{1,17},{17,1},{2,18},{18,2},{3,19},{19,3},{4,20},{20... | collective-permute-start | bytes 8847368 | tf_op jit(solution)/shard_map/ppermute | solution.py:715
  166.3 9.9 %collective-permute-start.16 = (bf16[288,640]{1,0:T(8,128)(2,1)S(1)}, bf16[288,640]{1,0:T(8,128)(2,1)S(1)}, u32[]{:S(2)}, u32[]{:S(2)}) collective-permute-start(bf16[288,640]{1,0:T(8,128)(2,1)S(1)} %add_convert_fusion.19), channel_id=1, source_target_pairs={{0,2},{1,3},{2,0},{3,1},{4,6},{5,7},{6,4},{7,5},{8,10},{9,11},{10,... | collective-permute-start | bytes 1105928 | tf_op jit(solution)/shard_map/ppermute | solution.py:719
  180.0 28.5 %collective-permute-start.20 = (bf16[1152,640]{1,0:T(8,128)(2,1)}, bf16[1152,640]{1,0:T(8,128)(2,1)}, u32[]{:S(2)}, u32[]{:S(2)}) collective-permute-start(bf16[1152,640]{1,0:T(8,128)(2,1)} %get-tuple-element.213), channel_id=1, source_target_pairs={{0,1},{1,0},{2,3},{3,2},{4,5},{5,4},{6,7},{7,6},{8,9},{9,8},{10,11... | collective-permute-start | bytes 4423688 | tf_op jit(solution)/shard_map/ppermute | solution.py:719
  180.1 19.3 %collective-permute-start.18 = (bf16[288,640]{1,0:T(8,128)(2,1)S(1)}, bf16[288,640]{1,0:T(8,128)(2,1)S(1)}, u32[]{:S(2)}, u32[]{:S(2)}) collective-permute-start(bf16[288,640]{1,0:T(8,128)(2,1)S(1)} %add_convert_fusion.17), channel_id=1, source_target_pairs={{0,8},{1,9},{2,10},{3,11},{4,12},{5,13},{6,14},{7,15},{8,0},{9,1},... | collective-permute-start | bytes 1105928 | tf_op jit(solution)/shard_map/ppermute | solution.py:719
  199.5 9.0 %collective-permute-start.19 = (bf16[288,640]{1,0:T(8,128)(2,1)S(1)}, bf16[288,640]{1,0:T(8,128)(2,1)S(1)}, u32[]{:S(2)}, u32[]{:S(2)}) collective-permute-start(bf16[288,640]{1,0:T(8,128)(2,1)S(1)} %add_convert_fusion.16), channel_id=1, source_target_pairs={{0,2},{1,3},{2,0},{3,1},{4,6},{5,7},{6,4},{7,5},{8,10},{9,11},{10,... | collective-permute-start | bytes 1105928 | tf_op jit(solution)/shard_map/ppermute | solution.py:719
  208.5 24.6 %collective-permute-start.23 = (bf16[1280,640]{1,0:T(8,128)(2,1)}, bf16[1280,640]{1,0:T(8,128)(2,1)}, u32[]{:S(2)}, u32[]{:S(2)}) collective-permute-start(bf16[1280,640]{1,0:T(8,128)(2,1)} %get-tuple-element.186), channel_id=1, source_target_pairs={{0,16},{16,0},{1,17},{17,1},{2,18},{18,2},{3,19},{19,3},{4,20},{20... | collective-permute-start | bytes 4915208 | tf_op jit(solution)/shard_map/ppermute | solution.py:715
  210.1 45.5 %collective-permute-start.15 = (bf16[3,256,1280]{2,1,0:T(8,128)(2,1)}, bf16[3,256,1280]{2,1,0:T(8,128)(2,1)}, u32[]{:S(2)}, u32[]{:S(2)}) collective-permute-start(bf16[3,256,1280]{2,1,0:T(8,128)(2,1)} %broadcast_select_fusion.6), channel_id=1, source_target_pairs={{0,16},{16,0},{1,17},{17,1},{2,18},{18,2},{3,19},{19,3},{4,20},{20... | collective-permute-start | bytes 5898248 | tf_op jit(solution)/shard_map/ppermute | solution.py:715
  213.4 12.2 %collective-permute-start.22 = (bf16[576,640]{1,0:T(8,128)(2,1)}, bf16[576,640]{1,0:T(8,128)(2,1)}, u32[]{:S(2)}, u32[]{:S(2)}) collective-permute-start(bf16[576,640]{1,0:T(8,128)(2,1)} %get-tuple-element.223), channel_id=1, source_target_pairs={{0,4},{1,5},{2,6},{3,7},{4,0},{5,1},{6,2},{7,3},{8,12},{9,13},{10,... | collective-permute-start | bytes 2211848 | tf_op jit(solution)/shard_map/ppermute | solution.py:719
  213.5 19.6 %collective-permute-start.21 = (bf16[576,640]{1,0:T(8,128)(2,1)S(1)}, bf16[576,640]{1,0:T(8,128)(2,1)S(1)}, u32[]{:S(2)}, u32[]{:S(2)}) collective-permute-start(bf16[576,640]{1,0:T(8,128)(2,1)S(1)} %pad_maximum_fusion.3), channel_id=1, source_target_pairs={{0,4},{1,5},{2,6},{3,7},{4,0},{5,1},{6,2},{7,3},{8,12},{9,13},{10,... | collective-permute-start | bytes 2211848 | tf_op jit(solution)/shard_map/ppermute | solution.py:719
  236.7 16.2 %collective-permute-start.40 = (bf16[640,640]{1,0:T(8,128)(2,1)}, bf16[640,640]{1,0:T(8,128)(2,1)}, u32[]{:S(2)}, u32[]{:S(2)}) collective-permute-start(bf16[640,640]{1,0:T(8,128)(2,1)} %get-tuple-element.221), channel_id=1, source_target_pairs={{0,1},{1,0},{2,3},{3,2},{4,5},{5,4},{6,7},{7,6},{8,9},{9,8},{10,11... | collective-permute-start | bytes 2457608 | tf_op jit(solution)/shard_map/ppermute | solution.py:719
  238.5 11.8 %collective-permute-start.33 = (bf16[288,640]{1,0:T(8,128)(2,1)}, bf16[288,640]{1,0:T(8,128)(2,1)}, u32[]{:S(2)}, u32[]{:S(2)}) collective-permute-start(bf16[288,640]{1,0:T(8,128)(2,1)} %add_convert_fusion.14), channel_id=1, source_target_pairs={{0,2},{1,3},{2,0},{3,1},{4,6},{5,7},{6,4},{7,5},{8,10},{9,11},{10,... | collective-permute-start | bytes 1105928 | tf_op jit(solution)/shard_map/ppermute | solution.py:719
  243.8 13.8 %collective-permute-start.26 = (f32[24,1280]{1,0:T(8,128)S(1)}, f32[24,1280]{1,0:T(8,128)S(1)}, u32[]{:S(2)}, u32[]{:S(2)}) collective-permute-start(f32[24,1280]{1,0:T(8,128)S(1)} %add.203), channel_id=1, source_target_pairs={{0,1},{1,0},{2,3},{3,2},{4,5},{5,4},{6,7},{7,6},{8,9},{9,8},{10,11... | collective-permute-start | bytes 368648 | tf_op jit(solution)/shard_map/ppermute | solution.py:719
  251.6 14.5 %collective-permute-start.34 = (bf16[288,640]{1,0:T(8,128)(2,1)S(1)}, bf16[288,640]{1,0:T(8,128)(2,1)S(1)}, u32[]{:S(2)}, u32[]{:S(2)}) collective-permute-start(bf16[288,640]{1,0:T(8,128)(2,1)S(1)} %add_convert_fusion.13), channel_id=1, source_target_pairs={{0,8},{1,9},{2,10},{3,11},{4,12},{5,13},{6,14},{7,15},{8,0},{9,1},... | collective-permute-start | bytes 1105928 | tf_op jit(solution)/shard_map/ppermute | solution.py:719
  254.2 13.1 %collective-permute-start.41 = (bf16[320,640]{1,0:T(8,128)(2,1)S(1)}, bf16[320,640]{1,0:T(8,128)(2,1)S(1)}, u32[]{:S(2)}, u32[]{:S(2)}) collective-permute-start(bf16[320,640]{1,0:T(8,128)(2,1)S(1)} %get-tuple-element.227), channel_id=1, source_target_pairs={{0,2},{1,3},{2,0},{3,1},{4,6},{5,7},{6,4},{7,5},{8,10},{9,11},{10,... | collective-permute-start | bytes 1228808 | tf_op jit(solution)/shard_map/ppermute | solution.py:719
  257.7 11.8 %collective-permute-start.27 = (f32[24,1280]{1,0:T(8,128)S(1)}, f32[24,1280]{1,0:T(8,128)S(1)}, u32[]{:S(2)}, u32[]{:S(2)}) collective-permute-start(f32[24,1280]{1,0:T(8,128)S(1)} %add.204), channel_id=1, source_target_pairs={{0,4},{1,5},{2,6},{3,7},{4,0},{5,1},{6,2},{7,3},{8,12},{9,13},{10,... | collective-permute-start | bytes 368648 | tf_op jit(solution)/shard_map/ppermute | solution.py:719
  266.2 10.6 %collective-permute-start.35 = (bf16[288,640]{1,0:T(8,128)(2,1)S(1)}, bf16[288,640]{1,0:T(8,128)(2,1)S(1)}, u32[]{:S(2)}, u32[]{:S(2)}) collective-permute-start(bf16[288,640]{1,0:T(8,128)(2,1)S(1)} %add_convert_fusion.12), channel_id=1, source_target_pairs={{0,2},{1,3},{2,0},{3,1},{4,6},{5,7},{6,4},{7,5},{8,10},{9,11},{10,... | collective-permute-start | bytes 1105928 | tf_op jit(solution)/shard_map/ppermute | solution.py:719
  267.3 9.6 %collective-permute-start.42 = (bf16[160,640]{1,0:T(8,128)(2,1)S(1)}, bf16[160,640]{1,0:T(8,128)(2,1)S(1)}, u32[]{:S(2)}, u32[]{:S(2)}) collective-permute-start(bf16[160,640]{1,0:T(8,128)(2,1)S(1)} %add_convert_fusion.22), channel_id=1, source_target_pairs={{0,4},{1,5},{2,6},{3,7},{4,0},{5,1},{6,2},{7,3},{8,12},{9,13},{10,... | collective-permute-start | bytes 614408 | tf_op jit(solution)/shard_map/ppermute | solution.py:719
  267.6 46.2 %collective-permute-start.30 = (bf16[1152,640]{1,0:T(8,128)(2,1)S(1)}, bf16[1152,640]{1,0:T(8,128)(2,1)S(1)}, u32[]{:S(2)}, u32[]{:S(2)}) collective-permute-start(bf16[1152,640]{1,0:T(8,128)(2,1)S(1)} %pad_maximum_fusion.refs_0_), channel_id=1, source_target_pairs={{0,1},{1,0},{2,3},{3,2},{4,5},{5,4},{6,7},{7,6},{8,9},{9,8},{10,11... | collective-permute-start | bytes 4423688 | tf_op jit(solution)/shard_map/ppermute | solution.py:719
  268.8 45.1 %collective-permute-start.31 = (bf16[1152,640]{1,0:T(8,128)(2,1)S(1)}, bf16[1152,640]{1,0:T(8,128)(2,1)S(1)}, u32[]{:S(2)}, u32[]{:S(2)}) collective-permute-start(bf16[1152,640]{1,0:T(8,128)(2,1)S(1)} %pad_maximum_fusion.refs_0_), channel_id=1, source_target_pairs={{0,16},{16,0},{1,17},{17,1},{2,18},{18,2},{3,19},{19,3},{4,20},{20... | collective-permute-start | bytes 4423688 | tf_op jit(solution)/shard_map/ppermute | solution.py:715
  269.5 10.0 %collective-permute-start.28 = (f32[24,1280]{1,0:T(8,128)S(1)}, f32[24,1280]{1,0:T(8,128)S(1)}, u32[]{:S(2)}, u32[]{:S(2)}) collective-permute-start(f32[24,1280]{1,0:T(8,128)S(1)} %add.205), channel_id=1, source_target_pairs={{0,2},{1,3},{2,0},{3,1},{4,6},{5,7},{6,4},{7,5},{8,10},{9,11},{10,... | collective-permute-start | bytes 368648 | tf_op jit(solution)/shard_map/ppermute | solution.py:719
  276.9 16.0 %collective-permute-start.36 = (bf16[576,640]{1,0:T(8,128)(2,1)S(1)}, bf16[576,640]{1,0:T(8,128)(2,1)S(1)}, u32[]{:S(2)}, u32[]{:S(2)}) collective-permute-start(bf16[576,640]{1,0:T(8,128)(2,1)S(1)} %pad_maximum_fusion.4), channel_id=1, source_target_pairs={{0,4},{1,5},{2,6},{3,7},{4,0},{5,1},{6,2},{7,3},{8,12},{9,13},{10,... | collective-permute-start | bytes 2211848 | tf_op jit(solution)/shard_map/ppermute | solution.py:719
  277.1 12.4 %collective-permute-start.43 = (bf16[160,640]{1,0:T(8,128)(2,1)S(1)}, bf16[160,640]{1,0:T(8,128)(2,1)S(1)}, u32[]{:S(2)}, u32[]{:S(2)}) collective-permute-start(bf16[160,640]{1,0:T(8,128)(2,1)S(1)} %add_convert_fusion.21), channel_id=1, source_target_pairs={{0,8},{1,9},{2,10},{3,11},{4,12},{5,13},{6,14},{7,15},{8,0},{9,1},... | collective-permute-start | bytes 614408 | tf_op jit(solution)/shard_map/ppermute | solution.py:719
  279.4 36.8 %collective-permute-start.24 = (bf16[3,256,1280]{2,1,0:T(8,128)(2,1)S(1)}, bf16[3,256,1280]{2,1,0:T(8,128)(2,1)S(1)}, u32[]{:S(2)}, u32[]{:S(2)}) collective-permute-start(bf16[3,256,1280]{2,1,0:T(8,128)(2,1)S(1)} %broadcast_select_fusion.2), channel_id=1, source_target_pairs={{0,16},{16,0},{1,17},{17,1},{2,18},{18,2},{3,19},{19,3},{4,20},{20... | collective-permute-start | bytes 5898248 | tf_op jit(solution)/shard_map/ppermute | solution.py:715
  289.4 6.2 %collective-permute-start.29 = (f32[24,1280]{1,0:T(8,128)S(1)}, f32[24,1280]{1,0:T(8,128)S(1)}, u32[]{:S(2)}, u32[]{:S(2)}) collective-permute-start(f32[24,1280]{1,0:T(8,128)S(1)} %add.206), channel_id=1, source_target_pairs={{0,8},{1,9},{2,10},{3,11},{4,12},{5,13},{6,14},{7,15},{8,0},{9,1},... | collective-permute-start | bytes 368648 | tf_op jit(solution)/shard_map/ppermute | solution.py:719
  292.9 6.1 %collective-permute-start.44 = (bf16[160,640]{1,0:T(8,128)(2,1)S(1)}, bf16[160,640]{1,0:T(8,128)(2,1)S(1)}, u32[]{:S(2)}, u32[]{:S(2)}) collective-permute-start(bf16[160,640]{1,0:T(8,128)(2,1)S(1)} %add_convert_fusion.20), channel_id=1, source_target_pairs={{0,4},{1,5},{2,6},{3,7},{4,0},{5,1},{6,2},{7,3},{8,12},{9,13},{10,... | collective-permute-start | bytes 614408 | tf_op jit(solution)/shard_map/ppermute | solution.py:719
  295.7 19.4 %collective-permute-start.37 = (bf16[1152,640]{1,0:T(8,128)(2,1)S(1)}, bf16[1152,640]{1,0:T(8,128)(2,1)S(1)}, u32[]{:S(2)}, u32[]{:S(2)}) collective-permute-start(bf16[1152,640]{1,0:T(8,128)(2,1)S(1)} %pad_maximum_fusion.1.refs_4_), channel_id=1, source_target_pairs={{0,1},{1,0},{2,3},{3,2},{4,5},{5,4},{6,7},{7,6},{8,9},{9,8},{10,11... | collective-permute-start | bytes 4423688 | tf_op jit(solution)/shard_map/ppermute | solution.py:719
  299.0 12.5 %collective-permute-start.45 = (bf16[320,640]{1,0:T(8,128)(2,1)S(1)}, bf16[320,640]{1,0:T(8,128)(2,1)S(1)}, u32[]{:S(2)}, u32[]{:S(2)}) collective-permute-start(bf16[320,640]{1,0:T(8,128)(2,1)S(1)} %pad_maximum_fusion.5), channel_id=1, source_target_pairs={{0,2},{1,3},{2,0},{3,1},{4,6},{5,7},{6,4},{7,5},{8,10},{9,11},{10,... | collective-permute-start | bytes 1228808 | tf_op jit(solution)/shard_map/ppermute | solution.py:719
  311.6 12.4 %collective-permute-start.46 = (bf16[640,640]{1,0:T(8,128)(2,1)S(1)}, bf16[640,640]{1,0:T(8,128)(2,1)S(1)}, u32[]{:S(2)}, u32[]{:S(2)}) collective-permute-start(bf16[640,640]{1,0:T(8,128)(2,1)S(1)} %pad_maximum_fusion.2.refs_8_), channel_id=1, source_target_pairs={{0,1},{1,0},{2,3},{3,2},{4,5},{5,4},{6,7},{7,6},{8,9},{9,8},{10,11... | collective-permute-start | bytes 2457608 | tf_op jit(solution)/shard_map/ppermute | solution.py:719
  313.8 13.3 %collective-permute-start.32 = (bf16[1152,640]{1,0:T(8,128)(2,1)S(1)}, bf16[1152,640]{1,0:T(8,128)(2,1)S(1)}, u32[]{:S(2)}, u32[]{:S(2)}) collective-permute-start(bf16[1152,640]{1,0:T(8,128)(2,1)S(1)} %collective-permute-done.30.refs_1_), channel_id=1, source_target_pairs={{0,16},{16,0},{1,17},{17,1},{2,18},{18,2},{3,19},{19,3},{4,20},{20... | collective-permute-start | bytes 4423688 | tf_op jit(solution)/shard_map/ppermute | solution.py:715
  313.9 13.3 %collective-permute-start.38 = (bf16[1152,640]{1,0:T(8,128)(2,1)S(1)}, bf16[1152,640]{1,0:T(8,128)(2,1)S(1)}, u32[]{:S(2)}, u32[]{:S(2)}) collective-permute-start(bf16[1152,640]{1,0:T(8,128)(2,1)S(1)} %pad_maximum_fusion.1.refs_4_), channel_id=1, source_target_pairs={{0,16},{16,0},{1,17},{17,1},{2,18},{18,2},{3,19},{19,3},{4,20},{20... | collective-permute-start | bytes 4423688 | tf_op jit(solution)/shard_map/ppermute | solution.py:715
  315.0 14.2 %collective-permute-start.39 = (bf16[1152,640]{1,0:T(8,128)(2,1)S(1)}, bf16[1152,640]{1,0:T(8,128)(2,1)}, u32[]{:S(2)}, u32[]{:S(2)}) collective-permute-start(bf16[1152,640]{1,0:T(8,128)(2,1)S(1)} %collective-permute-done.37.refs_5_), channel_id=1, source_target_pairs={{0,16},{16,0},{1,17},{17,1},{2,18},{18,2},{3,19},{19,3},{4,20},{20... | collective-permute-start | bytes 4423688 | tf_op jit(solution)/shard_map/ppermute | solution.py:715
  316.2 10.9 %collective-permute-start.47 = (bf16[640,640]{1,0:T(8,128)(2,1)S(1)}, bf16[640,640]{1,0:T(8,128)(2,1)S(1)}, u32[]{:S(2)}, u32[]{:S(2)}) collective-permute-start(bf16[640,640]{1,0:T(8,128)(2,1)S(1)} %pad_maximum_fusion.2.refs_8_), channel_id=1, source_target_pairs={{0,16},{16,0},{1,17},{17,1},{2,18},{18,2},{3,19},{19,3},{4,20},{20... | collective-permute-start | bytes 2457608 | tf_op jit(solution)/shard_map/ppermute | solution.py:715
  324.0 3.2 collective-permute-start.48
  (41 other events, 286.4 us)

commit v5 on v4

--- a/solution.py
+++ b/solution.py
@@ -63,7 +63,7 @@
 
 def chunks(rows, size, body):
     steps = rows // size
-    lax.fori_loop(0, steps, lambda i, c: (body(pl.multiple_of(i * size, size)), c)[1], 0, unroll=min(8, steps))
+    lax.fori_loop(0, steps, lambda i, c: (body(pl.multiple_of(i * size, size)), c)[1], 0, unroll=min(16, steps))
 
 
 def summed_chunks(rows, size, width, terms, body):
@@ -72,7 +72,7 @@
     def one(i, held):
         return tuple(h + fold8(v) for h, v in zip(held, body(pl.multiple_of(i * size, size))))
 
-    return lax.fori_loop(0, steps, one, (jnp.zeros((8, width), F32),) * terms, unroll=min(8, steps))
+    return lax.fori_loop(0, steps, one, (jnp.zeros((8, width), F32),) * terms, unroll=min(16, steps))
 
 
 def pick_copy(cond, one, other, dst, sem):

time: 342 us -> 344 us (level); the launches traced: 340 us -> 338 us
  Pallas kernels: 157 us -> 147 us
  waiting for transfers between devices: 82.1 us -> 91.3 us
    pallas_call x8, Pallas kernels: 113 us -> 102 us  [call(): pl.pallas_call(kernel, grid_spec=pltpu.PrefetchScalarGridSpec(num_scalar_...]
    ppermute x25, waiting for transfers between devices: 66.3 us -> 74.3 us  [hop(): return lax.ppermute(v, ('section', 'dp'), pairs)]
  transfers between devices with their start and end apart: 49 -> 49, of which waited for: 20 -> 21; matrix products, arithmetic and copies ran while one was open for 9% -> 9% of each run, Pallas kernels for 31% -> 29%
where the time goes in v5:
time: 344 us; the launch traced here: 338 us
  Pallas kernels  147 us (43%)
  waiting for transfers between devices  91.3 us (27%)
  starting transfers between devices  51.3 us (15%)
  other arithmetic  35.7 us (10%)
  local copies, waits for them, and re-layouts  10.5 us (3%)
    pallas_call x8, Pallas kernels, call(): pl.pallas_call(kernel, grid_spec=pltpu.PrefetchScalarGridSpec(num_scalar_...  102 us
    ppermute x25, waiting for transfers between devices, hop(): return lax.ppermute(v, ('section', 'dp'), pairs)  74.3 us
    pallas_call x3, Pallas kernels, weight_terms(): pl.pallas_call(kernel, grid_spec=pltpu.PrefetchScalarGridSpec(num_scalar_...  31.1 us
    ppermute x25, starting transfers between devices, hop(): return lax.ppermute(v, ('section', 'dp'), pairs)  23.8 us
    convert_element_type x15, other arithmetic, add_low(): return (one.astype(F32) + other.astype(F32)).astype(BF16)  18.6 us
    pallas_call x1, Pallas kernels, body(): pl.pallas_call(functools.partial(unpack_kernel, sets=sets, shards=big.sha...  10.7 us
    unnamed x81, local copies, waits for them, and re-layouts  8.84 us
  transfers between devices with their start and end apart: 49, of which 21 were waited for; matrix products, arithmetic and copies ran while one was open for 9% of the time, Pallas kernels for 29%

profile of v5, /device:TPU:0, one launch (start us, length us, event | category | flops | bytes accessed | tf_op | source)
XLA Modules:
  0.0 337.6 jit_solution(6187552868857390233)
XLA Ops:
  3.5 3.0 collective-permute-start
  6.5 4.1 %collective-permute-start.1 = (bf16[3,8,1280]{2,1,0:T(8,128)(2,1)S(1)}, bf16[3,8,1280]{2,1,0:T(8,128)(2,1)S(1)}, u32[]{:S(2)}, u32[]{:S(2)}) collective-permute-start(bf16[3,8,1280]{2,1,0:T(8,128)(2,1)S(1)} %get-tuple-element.219), channel_id=1, source_target_pairs={{1,0},{2,1},{3,2},{4,3},{5,4},{6,5},{7,6},{8,7},{9,8},{10,9},{11,1... | collective-permute-start | bytes 184328 | tf_op jit(solution)/shard_map/ppermute | solution.py:749
  14.3 2.3 collective-permute-done.3.nwx
  17.8 27.5 %shard_map.307 = (f32[3,256,128]{2,1,0:T(8,128)}, bf16[3,256,1280]{2,1,0:T(8,128)(2,1)}, bf16[3,256,1280]{2,1,0:T(8,128)(2,1)}, f32[3,256,1]{2,1,0:T(8,128)}, f3...) custom-call(s32[1]{0:T(128)} %bitcast.c_ref, ...), custom_call_target="tpu_custom_call" | custom-call | flops 69206016 | bytes 400000 | tf_op jit(solution)/shard_map/pallas_call | solution.py:762
  45.4 5.8 %collective-permute-start.7 = (bf16[3,128,640]{2,1,0:T(8,128)(2,1)}, bf16[3,128,640]{2,1,0:T(8,128)(2,1)S(1)}, u32[]{:S(2)}, u32[]{:S(2)}) collective-permute-start(bf16[3,128,640]{2,1,0:T(8,128)(2,1)} %get-tuple-element.116), channel_id=1, source_target_pairs={{1,0},{2,1},{3,2},{4,3},{5,4},{6,5},{7,6},{8,7},{9,8},{10,9},{11,1... | collective-permute-start | bytes 1474568 | tf_op jit(solution)/shard_map/ppermute | solution.py:815
  51.1 12.6 %shard_map.308 = (f32[3,256,640]{2,1,0:T(8,128)}, f32[3,256,640]{2,1,0:T(8,128)}, f32[1,1280]{1,0:T(1,128)}) custom-call(s32[1]{0:T(128)} %bitcast.c_ref, bf16[3,256,640]{2,1,0:T(8,128)(2,1)} %get-tuple-element.114.mid_ref, f32[3,256,128]{2,1,0:T(8,128)} %get-tuple-element.117.mk.refs_2_.refs_1_, bf16[6,256,1280]{2,1,0:T(8,128)(2,1)} %grad.1, ...), custom_call_target="tpu_custom_call" | custom-call | flops 44040192 | bytes 200000 | tf_op jit(solution)/shard_map/pallas_call | solution.py:762
  63.7 4.0 %collective-permute-done.6.up_ref = bf16[3,128,640]{2,1,0:T(8,128)(2,1)S(1)} collective-permute-done((bf16[3,128,640]{2,1,0:T(8,128)(2,1)}, bf16[3,128,640]{2,1,0:T(8,128)(2,1)S(1)}, u32[]{:S(2)}, u32[]{:S(2)}) %collective-permute-start.6) | collective-permute-done | bytes 491552 | tf_op jit(solution)/shard_map/ppermute | solution.py:814
  69.2 11.4 %shard_map.309 = (bf16[3,256,3200]{2,1,0:T(8,128)(2,1)}, bf16[3,256,640]{2,1,0:T(8,128)(2,1)}, bf16[3,256,640]{2,1,0:T(8,128)(2,1)}, bf16[3,128,640]{2,1,0:T(8,1...) custom-call(s32[1]{0:T(128)} %bitcast.c_ref, bf16[3,256,640]{2,1,0:T(8,128)(2,1)} %get-tuple-element.114.mid_ref, ...), custom_call_target="tpu_custom_call" | custom-call | flops 25165824 | bytes 200000 | tf_op jit(solution)/shard_map/pallas_call | solution.py:762
  80.6 1.9 collective-permute-start.8
  82.6 3.7 %collective-permute-start.9 = (bf16[3,128,640]{2,1,0:T(8,128)(2,1)}, bf16[3,128,640]{2,1,0:T(8,128)(2,1)S(1)}, u32[]{:S(2)}, u32[]{:S(2)}) collective-permute-start(bf16[3,128,640]{2,1,0:T(8,128)(2,1)} %get-tuple-element.125), channel_id=1, source_target_pairs={{1,0},{2,1},{3,2},{4,3},{5,4},{6,5},{7,6},{8,7},{9,8},{10,9},{11,1... | collective-permute-start | bytes 1474568 | tf_op jit(solution)/shard_map/ppermute | solution.py:849
  86.3 11.6 %shard_map.310 = (bf16[2304,640]{1,0:T(8,128)(2,1)}, bf16[2304,640]{1,0:T(8,128)(2,1)}) custom-call(s32[1]{0:T(128)} %bitcast.c_ref, bf16[3,256,640]{2,1,0:T(8,128)(2,1)} %get-tuple-element.127.refs_0_.oa_ref, bf16[6,256,1280]{2,1,0:T(8,128)(2,1)} %grad.1, bf16[3,256,3200]{2,1,0:T(8,128)(2,1)} %get-tuple-element.128.refs_2_, ...), custom_call_target="tpu_custom_call" | custom-call | flops 44040192 | bytes 58982 | tf_op jit(solution)/shard_map/pallas_call | solution.py:574
  97.9 6.3 %collective-permute-done.8.refs_0_ = bf16[3,128,640]{2,1,0:T(8,128)(2,1)S(1)} collective-permute-done((bf16[3,128,640]{2,1,0:T(8,128)(2,1)}, bf16[3,128,640]{2,1,0:T(8,128)(2,1)S(1)}, u32[]{:S(2)}, u32[]{:S(2)}) %collective-permute-start.8) | collective-permute-done | bytes 491552 | tf_op jit(solution)/shard_map/ppermute | solution.py:848
  104.2 2.2 collective-permute-done.9.refs_1_
  107.2 10.9 %shard_map.311 = (bf16[3,256,640]{2,1,0:T(8,128)(2,1)}, f32[3,640]{1,0:T(4,128)}) custom-call(s32[1]{0:T(128)} %bitcast.c_ref, bf16[3,256,640]{2,1,0:T(8,128)(2,1)} %get-tuple-element.129.refs_3_.cg_ref, bf16[3,128,640]{2,1,0:T(8,128)(2,1)} %copy-done.33, bf16[3,128,640]{2,1,0:T(8,128)(2,1)} %copy-done.34, ...), custom_call_target="tpu_custom_call" | custom-call | flops 32715572 | bytes 100000 | tf_op jit(solution)/shard_map/pallas_call | solution.py:762
  118.1 1.6 copy-done.17
  119.7 2.5 add_convert_fusion.3
  122.7 12.5 %shard_map.312 = (bf16[3,256,1280]{2,1,0:T(8,128)(2,1)}, bf16[3,256,640]{2,1,0:T(8,128)(2,1)}, bf16[3,8,640]{2,1,0:T(8,128)(2,1)}, bf16[3,8,640]{2,1,0:T(8,128)(...) custom-call(s32[1]{0:T(128)} %bitcast.c_ref, bf16[3,256,640]{2,1,0:T(8,128)(2,1)} %get-tuple-element.142.ng_ref.refs_1_, ...), custom_call_target="tpu_custom_call" | custom-call | flops 32715572 | bytes 180000 | tf_op jit(solution)/shard_map/pallas_call | solution.py:762
  135.2 6.6 %collective-permute-done.11 = bf16[1152,640]{1,0:T(8,128)(2,1)} collective-permute-done((bf16[1152,640]{1,0:T(8,128)(2,1)S(1)}, bf16[1152,640]{1,0:T(8,128)(2,1)}, u32[]{:S(2)}, u32[]{:S(2)}) %collective-permute-start.11) | collective-permute-done | bytes 1474592 | tf_op jit(solution)/shard_map/ppermute | solution.py:719
  141.8 1.7 add_convert_fusion.8
  143.5 1.6 collective-permute-start.12
  145.3 5.5 %collective-permute-start.14 = (bf16[3,8,640]{2,1,0:T(8,128)(2,1)S(1)}, bf16[3,8,640]{2,1,0:T(8,128)(2,1)S(1)}, u32[]{:S(2)}, u32[]{:S(2)}) collective-permute-start(bf16[3,8,640]{2,1,0:T(8,128)(2,1)S(1)} %copy-done.38), channel_id=1, source_target_pairs={{1,0},{2,1},{3,2},{4,3},{5,4},{6,5},{7,6},{8,7},{9,8},{10,9},{11,1... | collective-permute-start | bytes 92168 | tf_op jit(solution)/shard_map/ppermute | solution.py:912
  150.9 11.6 %shard_map.313 = (bf16[2304,640]{1,0:T(8,128)(2,1)}, bf16[2304,640]{1,0:T(8,128)(2,1)}) custom-call(s32[1]{0:T(128)} %bitcast.c_ref, bf16[3,256,640]{2,1,0:T(8,128)(2,1)} %get-tuple-element.156.refs_0_, bf16[3,256,1280]{2,1,0:T(8,128)(2,1)} %get-tuple-element.157.refs_1_.grad, bf16[3,256,3200]{2,1,0:T(8,128)(2,1)} %get-tuple-element.158.refs_2_, ...), custom_call_target="tpu_custom_call" | custom-call | flops 44040192 | bytes 58982 | tf_op jit(solution)/shard_map/pallas_call | solution.py:574
  164.4 7.6 %shard_map.314 = (bf16[3,256,1280]{2,1,0:T(8,128)(2,1)}, f32[2,128]{1,0:T(2,128)}) custom-call(s32[1]{0:T(128)} %bitcast.c_ref, bf16[3,256,1280]{2,1,0:T(8,128)(2,1)} %get-tuple-element.113.src.out0_ref, bf16[3,256,640]{2,1,0:T(8,128)(2,1)} %get-tuple-element.127.refs_0_.oa_ref, s32[6,256]{1,0:T(8,128)} %rt_ref.1, s32[6,256]{1,0:T(8,128)} %lm_ref.1, ...), custom_call_target="tpu_custom_call" | custom-call | flops 15099494 | bytes 80000 | tf_op jit(solution)/shard_map/pallas_call | solution.py:762
  172.1 3.8 %add_convert_fusion = (bf16[1152,640]{1,0:T(8,128)(2,1)S(1)}, bf16[1152,640]{1,0:T(8,128)(2,1)}) fusion(bf16[2304,640]{1,0:T(8,128)(2,1)} %collective-permute-done.17, s32[]{:T(128)S(6)} %select_n.195, bf16[2304,640]{1,0:T(8,128)(2,1)S(1)} %copy-done.16, s32[]{:T(128)S(6)} %select_n.198), kind=kLoop, calls=%fused_computation.2 | loop fusion | flops 5898240 | bytes 8847368 | tf_op jit(solution)/shard_map/convert_element_type | solution.py:638
  177.5 10.9 %shard_map.315 = (bf16[3,256,640]{2,1,0:T(8,128)(2,1)}, f32[3,640]{1,0:T(4,128)}) custom-call(s32[1]{0:T(128)} %bitcast.c_ref, bf16[3,256,640]{2,1,0:T(8,128)(2,1)} %get-tuple-element.159.refs_3_.cg_ref, bf16[3,16,640]{2,1,0:T(8,128)(2,1)} %pad_maximum_fusion.7.refs_0_, f32[3,256,128]{2,1,0:T(8,128)} %get-tuple-element.117.mk.refs_2_.refs_1_, ...), custom_call_target="tpu_custom_call" | custom-call | flops 32715572 | bytes 100000 | tf_op jit(solution)/shard_map/pallas_call | solution.py:762
  188.4 6.9 %collective-permute-done.18 = bf16[288,640]{1,0:T(8,128)(2,1)S(1)} collective-permute-done((bf16[288,640]{1,0:T(8,128)(2,1)S(1)}, bf16[288,640]{1,0:T(8,128)(2,1)S(1)}, u32[]{:S(2)}, u32[]{:S(2)}) %collective-permute-start.18) | collective-permute-done | bytes 368672 | tf_op jit(solution)/shard_map/ppermute | solution.py:719
  196.7 7.9 %shard_map.316 = (bf16[1280,640]{1,0:T(8,128)(2,1)}, bf16[1280,640]{1,0:T(8,128)(2,1)}) custom-call(s32[1]{0:T(128)} %bitcast.c_ref, bf16[3,256,1280]{2,1,0:T(8,128)(2,1)} %get-tuple-element.179.refs_0_, bf16[3,256,640]{2,1,0:T(8,128)(2,1)} %get-tuple-element.142.ng_ref.refs_1_, bf16[3,256,1280]{2,1,0:T(8,128)(2,1)} %get-tuple-element.180.refs_2_, ...), custom_call_target="tpu_custom_call" | custom-call | flops 25165824 | bytes 32768 | tf_op jit(solution)/shard_map/pallas_call | solution.py:574
  206.7 2.8 add_convert_fusion.6
  209.7 2.0 collective-permute-start.21
  211.7 8.9 %shard_map.317 = (bf16[3,256,1280]{2,1,0:T(8,128)(2,1)}, f32[2,1280]{1,0:T(2,128)}) custom-call(s32[1]{0:T(128)} %bitcast.c_ref, bf16[3,256,640]{2,1,0:T(8,128)(2,1)} %get-tuple-element.181.refs_3_.ng_ref, f32[1,7680]{1,0:T(1,128)} %get-tuple-element.246.v0_ref.refs_2_.v_ref, bf16[3,256,1280]{2,1,0:T(8,128)(2,1)} %get-tuple-element.157.refs_1_.grad, ...), custom_call_target="tpu_custom_call" | custom-call | flops 16357785 | bytes 100000 | tf_op jit(solution)/shard_map/pallas_call | solution.py:762
  221.4 7.8 %collective-permute-done.21 = bf16[576,640]{1,0:T(8,128)(2,1)S(1)} collective-permute-done((bf16[576,640]{1,0:T(8,128)(2,1)S(1)}, bf16[576,640]{1,0:T(8,128)(2,1)S(1)}, u32[]{:S(2)}, u32[]{:S(2)}) %collective-permute-start.21) | collective-permute-done | bytes 737312 | tf_op jit(solution)/shard_map/ppermute | solution.py:719
  230.1 2.7 add_convert_fusion.5
  232.8 1.8 add_convert_fusion.14
  239.7 2.1 collective-permute-start.26
  241.8 4.8 %collective-permute-done.33 = bf16[288,640]{1,0:T(8,128)(2,1)} collective-permute-done((bf16[288,640]{1,0:T(8,128)(2,1)}, bf16[288,640]{1,0:T(8,128)(2,1)}, u32[]{:S(2)}, u32[]{:S(2)}) %collective-permute-start.33) | collective-permute-done | bytes 368672 | tf_op jit(solution)/shard_map/ppermute | solution.py:719
  251.5 2.0 broadcast_select_fusion.5
  254.5 7.4 %collective-permute-done.34 = bf16[288,640]{1,0:T(8,128)(2,1)S(1)} collective-permute-done((bf16[288,640]{1,0:T(8,128)(2,1)S(1)}, bf16[288,640]{1,0:T(8,128)(2,1)S(1)}, u32[]{:S(2)}, u32[]{:S(2)}) %collective-permute-start.34) | collective-permute-done | bytes 368672 | tf_op jit(solution)/shard_map/ppermute | solution.py:719
  266.0 6.6 %collective-permute-done.35 = bf16[288,640]{1,0:T(8,128)(2,1)S(1)} collective-permute-done((bf16[288,640]{1,0:T(8,128)(2,1)S(1)}, bf16[288,640]{1,0:T(8,128)(2,1)S(1)}, u32[]{:S(2)}, u32[]{:S(2)}) %collective-permute-start.35) | collective-permute-done | bytes 368672 | tf_op jit(solution)/shard_map/ppermute | solution.py:719
  272.9 1.5 collective-permute-start.43
  275.3 10.0 %collective-permute-done.43 = bf16[160,640]{1,0:T(8,128)(2,1)S(1)} collective-permute-done((bf16[160,640]{1,0:T(8,128)(2,1)S(1)}, bf16[160,640]{1,0:T(8,128)(2,1)S(1)}, u32[]{:S(2)}, u32[]{:S(2)}) %collective-permute-start.43) | collective-permute-done | bytes 204832 | tf_op jit(solution)/shard_map/ppermute | solution.py:719
  285.3 3.4 %collective-permute-start.29 = (f32[24,1280]{1,0:T(8,128)S(1)}, f32[24,1280]{1,0:T(8,128)S(1)}, u32[]{:S(2)}, u32[]{:S(2)}) collective-permute-start(f32[24,1280]{1,0:T(8,128)S(1)} %add.206), channel_id=1, source_target_pairs={{0,8},{1,9},{2,10},{3,11},{4,12},{5,13},{6,14},{7,15},{8,0},{9,1},... | collective-permute-start | bytes 368648 | tf_op jit(solution)/shard_map/ppermute | solution.py:719
  289.0 4.0 %collective-permute-done.29 = f32[24,1280]{1,0:T(8,128)S(1)} collective-permute-done((f32[24,1280]{1,0:T(8,128)S(1)}, f32[24,1280]{1,0:T(8,128)S(1)}, u32[]{:S(2)}, u32[]{:S(2)}) %collective-permute-start.29) | collective-permute-done | bytes 122912 | tf_op jit(solution)/shard_map/ppermute | solution.py:719
  293.0 2.3 maximum_bitcast_fusion
  296.8 11.0 %collective-permute-done.45 = bf16[320,640]{1,0:T(8,128)(2,1)S(1)} collective-permute-done((bf16[320,640]{1,0:T(8,128)(2,1)S(1)}, bf16[320,640]{1,0:T(8,128)(2,1)S(1)}, u32[]{:S(2)}, u32[]{:S(2)}) %collective-permute-start.45) | collective-permute-done | bytes 409632 | tf_op jit(solution)/shard_map/ppermute | solution.py:719
  307.9 2.1 collective-permute-start.46
  314.0 7.2 %collective-permute-done.46.refs_9_ = bf16[640,640]{1,0:T(8,128)(2,1)S(1)} collective-permute-done((bf16[640,640]{1,0:T(8,128)(2,1)S(1)}, bf16[640,640]{1,0:T(8,128)(2,1)S(1)}, u32[]{:S(2)}, u32[]{:S(2)}) %collective-permute-start.46) | collective-permute-done | bytes 819232 | tf_op jit(solution)/shard_map/ppermute | solution.py:719
  322.0 2.3 maximum_bitcast_fusion.1
  326.5 10.7 %shard_map.319 = (f32[640,1280]{1,0:T(8,128)}, f32[5,640,640]{2,1,0:T(8,128)}, f32[1280,640]{1,0:T(8,128)}) custom-call(s32[1]{0:T(128)} %bitcast.c_ref, s32[9]{0:T(128)} %pad_add_fusion.row_ref, s32[4]{0:T(128)} %pad_add_fusion.1.sig_ref, bf16[1152,640]{1,0:T(8,128)(2,1)} %copy-done.7, bf16[1152,640]{1,0:T(8,128)(2,1)} %copy-done.19, ...), custom_call_target="tpu_custom_call" | custom-call | bytes 500000 | tf_op jit(solution)/shard_map/pallas_call | solution.py:994
  (192 shorter events, 44.6 us)
Async XLA Ops:
  0.7 16.0 %collective-permute-start.4 = (bf16[5,640,640]{2,1,0:T(8,128)(2,1)}, bf16[5,640,640]{2,1,0:T(8,128)(2,1)}, u32[]{:S(2)}, u32[]{:S(2)}) collective-permute-start(bf16[5,640,640]{2,1,0:T(8,128)(2,1)} %bitcast.19), channel_id=1, source_target_pairs={{0,16},{16,0},{1,17},{17,1},{2,18},{18,2},{3,19},{19,3},{4,20},{20... | collective-permute-start | bytes 12288008 | tf_op jit(solution)/shard_map/ppermute | solution.py:715
  2.6 8.0 %collective-permute-start.2 = (f32[1,7680]{1,0:T(1,128)}, f32[1,7680]{1,0:T(1,128)S(1)}, u32[]{:S(2)}, u32[]{:S(2)}) collective-permute-start(f32[1,7680]{1,0:T(1,128)} %shard_map.306), channel_id=1, source_target_pairs={{0,16},{16,0},{1,17},{17,1},{2,18},{18,2},{3,19},{19,3},{4,20},{20... | collective-permute-start | bytes 92168 | tf_op jit(solution)/shard_map/ppermute | solution.py:715
  3.5 9.3 %collective-permute-start = (bf16[3,8,1280]{2,1,0:T(8,128)(2,1)S(1)}, bf16[3,8,1280]{2,1,0:T(8,128)(2,1)S(1)}, u32[]{:S(2)}, u32[]{:S(2)}) collective-permute-start(bf16[3,8,1280]{2,1,0:T(8,128)(2,1)S(1)} %get-tuple-element.218), channel_id=1, source_target_pairs={{0,1},{1,2},{2,3},{3,4},{4,5},{5,6},{6,7},{7,8},{8,9},{9,10},{10,1... | collective-permute-start | bytes 184328 | tf_op jit(solution)/shard_map/ppermute | solution.py:749
  6.5 6.3 %collective-permute-start.1 = (bf16[3,8,1280]{2,1,0:T(8,128)(2,1)S(1)}, bf16[3,8,1280]{2,1,0:T(8,128)(2,1)S(1)}, u32[]{:S(2)}, u32[]{:S(2)}) collective-permute-start(bf16[3,8,1280]{2,1,0:T(8,128)(2,1)S(1)} %get-tuple-element.219), channel_id=1, source_target_pairs={{1,0},{2,1},{3,2},{4,3},{5,4},{6,5},{7,6},{8,7},{9,8},{10,9},{11,1... | collective-permute-start | bytes 184328 | tf_op jit(solution)/shard_map/ppermute | solution.py:749
  10.6 3.7 %collective-permute-start.5 = (bf16[640,1280]{1,0:T(8,128)(2,1)}, bf16[640,1280]{1,0:T(8,128)(2,1)S(1)}, u32[]{:S(2)}, u32[]{:S(2)}) collective-permute-start(bf16[640,1280]{1,0:T(8,128)(2,1)} %bitcast.25), channel_id=1, source_target_pairs={{0,16},{16,0},{1,17},{17,1},{2,18},{18,2},{3,19},{19,3},{4,20},{20... | collective-permute-start | bytes 4915208 | tf_op jit(solution)/shard_map/ppermute | solution.py:715
  10.6 6.1 %collective-permute-start.3 = (bf16[1280,640]{1,0:T(8,128)(2,1)}, bf16[1280,640]{1,0:T(8,128)(2,1)S(1)}, u32[]{:S(2)}, u32[]{:S(2)}) collective-permute-start(bf16[1280,640]{1,0:T(8,128)(2,1)} %bitcast.30), channel_id=1, source_target_pairs={{0,16},{16,0},{1,17},{17,1},{2,18},{18,2},{3,19},{19,3},{4,20},{20... | collective-permute-start | bytes 4915208 | tf_op jit(solution)/shard_map/ppermute | solution.py:715
  45.3 22.5 %collective-permute-start.6 = (bf16[3,128,640]{2,1,0:T(8,128)(2,1)}, bf16[3,128,640]{2,1,0:T(8,128)(2,1)S(1)}, u32[]{:S(2)}, u32[]{:S(2)}) collective-permute-start(bf16[3,128,640]{2,1,0:T(8,128)(2,1)} %get-tuple-element.115), channel_id=1, source_target_pairs={{0,1},{1,2},{2,3},{3,4},{4,5},{5,6},{6,7},{7,8},{8,9},{9,10},{10,1... | collective-permute-start | bytes 1474568 | tf_op jit(solution)/shard_map/ppermute | solution.py:814
  45.4 23.1 %collective-permute-start.7 = (bf16[3,128,640]{2,1,0:T(8,128)(2,1)}, bf16[3,128,640]{2,1,0:T(8,128)(2,1)S(1)}, u32[]{:S(2)}, u32[]{:S(2)}) collective-permute-start(bf16[3,128,640]{2,1,0:T(8,128)(2,1)} %get-tuple-element.116), channel_id=1, source_target_pairs={{1,0},{2,1},{3,2},{4,3},{5,4},{6,5},{7,6},{8,7},{9,8},{10,9},{11,1... | collective-permute-start | bytes 1474568 | tf_op jit(solution)/shard_map/ppermute | solution.py:815
  80.6 23.5 %collective-permute-start.8 = (bf16[3,128,640]{2,1,0:T(8,128)(2,1)}, bf16[3,128,640]{2,1,0:T(8,128)(2,1)S(1)}, u32[]{:S(2)}, u32[]{:S(2)}) collective-permute-start(bf16[3,128,640]{2,1,0:T(8,128)(2,1)} %get-tuple-element.124), channel_id=1, source_target_pairs={{0,1},{1,2},{2,3},{3,4},{4,5},{5,6},{6,7},{7,8},{8,9},{9,10},{10,1... | collective-permute-start | bytes 1474568 | tf_op jit(solution)/shard_map/ppermute | solution.py:848
  82.6 23.8 %collective-permute-start.9 = (bf16[3,128,640]{2,1,0:T(8,128)(2,1)}, bf16[3,128,640]{2,1,0:T(8,128)(2,1)S(1)}, u32[]{:S(2)}, u32[]{:S(2)}) collective-permute-start(bf16[3,128,640]{2,1,0:T(8,128)(2,1)} %get-tuple-element.125), channel_id=1, source_target_pairs={{1,0},{2,1},{3,2},{4,3},{5,4},{6,5},{7,6},{8,7},{9,8},{10,9},{11,1... | collective-permute-start | bytes 1474568 | tf_op jit(solution)/shard_map/ppermute | solution.py:849
  107.1 10.9 %collective-permute-start.10 = (bf16[2304,640]{1,0:T(8,128)(2,1)}, bf16[2304,640]{1,0:T(8,128)(2,1)S(1)}, u32[]{:S(2)}, u32[]{:S(2)}) collective-permute-start(bf16[2304,640]{1,0:T(8,128)(2,1)} %get-tuple-element.133), channel_id=1, source_target_pairs={{0,16},{16,0},{1,17},{17,1},{2,18},{18,2},{3,19},{19,3},{4,20},{20... | collective-permute-start | bytes 8847368 | tf_op jit(solution)/shard_map/ppermute | solution.py:715
  122.2 19.5 %collective-permute-start.11 = (bf16[1152,640]{1,0:T(8,128)(2,1)S(1)}, bf16[1152,640]{1,0:T(8,128)(2,1)}, u32[]{:S(2)}, u32[]{:S(2)}) collective-permute-start(bf16[1152,640]{1,0:T(8,128)(2,1)S(1)} %get-tuple-element.217), channel_id=1, source_target_pairs={{0,1},{1,0},{2,3},{3,2},{4,5},{5,4},{6,7},{7,6},{8,9},{9,8},{10,11... | collective-permute-start | bytes 4423688 | tf_op jit(solution)/shard_map/ppermute | solution.py:719
  143.5 19.0 %collective-permute-start.12 = (bf16[576,640]{1,0:T(8,128)(2,1)S(1)}, bf16[576,640]{1,0:T(8,128)(2,1)S(1)}, u32[]{:S(2)}, u32[]{:S(2)}) collective-permute-start(bf16[576,640]{1,0:T(8,128)(2,1)S(1)} %get-tuple-element.225), channel_id=1, source_target_pairs={{0,4},{1,5},{2,6},{3,7},{4,0},{5,1},{6,2},{7,3},{8,12},{9,13},{10,... | collective-permute-start | bytes 2211848 | tf_op jit(solution)/shard_map/ppermute | solution.py:719
  145.0 17.4 %collective-permute-start.13 = (bf16[3,8,640]{2,1,0:T(8,128)(2,1)S(1)}, bf16[3,8,640]{2,1,0:T(8,128)(2,1)S(1)}, u32[]{:S(2)}, u32[]{:S(2)}) collective-permute-start(bf16[3,8,640]{2,1,0:T(8,128)(2,1)S(1)} %copy-done.39), channel_id=1, source_target_pairs={{0,1},{1,2},{2,3},{3,4},{4,5},{5,6},{6,7},{7,8},{8,9},{9,10},{10,1... | collective-permute-start | bytes 92168 | tf_op jit(solution)/shard_map/ppermute | solution.py:912
  145.3 17.2 %collective-permute-start.14 = (bf16[3,8,640]{2,1,0:T(8,128)(2,1)S(1)}, bf16[3,8,640]{2,1,0:T(8,128)(2,1)S(1)}, u32[]{:S(2)}, u32[]{:S(2)}) collective-permute-start(bf16[3,8,640]{2,1,0:T(8,128)(2,1)S(1)} %copy-done.38), channel_id=1, source_target_pairs={{1,0},{2,1},{3,2},{4,3},{5,4},{6,5},{7,6},{8,7},{9,8},{10,9},{11,1... | collective-permute-start | bytes 92168 | tf_op jit(solution)/shard_map/ppermute | solution.py:912
  162.5 9.6 %collective-permute-start.17 = (bf16[2304,640]{1,0:T(8,128)(2,1)}, bf16[2304,640]{1,0:T(8,128)(2,1)}, u32[]{:S(2)}, u32[]{:S(2)}) collective-permute-start(bf16[2304,640]{1,0:T(8,128)(2,1)} %get-tuple-element.166), channel_id=1, source_target_pairs={{0,16},{16,0},{1,17},{17,1},{2,18},{18,2},{3,19},{19,3},{4,20},{20... | collective-permute-start | bytes 8847368 | tf_op jit(solution)/shard_map/ppermute | solution.py:715
  163.3 8.7 %collective-permute-start.16 = (bf16[288,640]{1,0:T(8,128)(2,1)S(1)}, bf16[288,640]{1,0:T(8,128)(2,1)S(1)}, u32[]{:S(2)}, u32[]{:S(2)}) collective-permute-start(bf16[288,640]{1,0:T(8,128)(2,1)S(1)} %add_convert_fusion.19), channel_id=1, source_target_pairs={{0,2},{1,3},{2,0},{3,1},{4,6},{5,7},{6,4},{7,5},{8,10},{9,11},{10,... | collective-permute-start | bytes 1105928 | tf_op jit(solution)/shard_map/ppermute | solution.py:719
  175.8 28.8 %collective-permute-start.20 = (bf16[1152,640]{1,0:T(8,128)(2,1)}, bf16[1152,640]{1,0:T(8,128)(2,1)}, u32[]{:S(2)}, u32[]{:S(2)}) collective-permute-start(bf16[1152,640]{1,0:T(8,128)(2,1)} %get-tuple-element.213), channel_id=1, source_target_pairs={{0,1},{1,0},{2,3},{3,2},{4,5},{5,4},{6,7},{7,6},{8,9},{9,8},{10,11... | collective-permute-start | bytes 4423688 | tf_op jit(solution)/shard_map/ppermute | solution.py:719
  176.0 19.3 %collective-permute-start.18 = (bf16[288,640]{1,0:T(8,128)(2,1)S(1)}, bf16[288,640]{1,0:T(8,128)(2,1)S(1)}, u32[]{:S(2)}, u32[]{:S(2)}) collective-permute-start(bf16[288,640]{1,0:T(8,128)(2,1)S(1)} %add_convert_fusion.17), channel_id=1, source_target_pairs={{0,8},{1,9},{2,10},{3,11},{4,12},{5,13},{6,14},{7,15},{8,0},{9,1},... | collective-permute-start | bytes 1105928 | tf_op jit(solution)/shard_map/ppermute | solution.py:719
  195.4 9.2 %collective-permute-start.19 = (bf16[288,640]{1,0:T(8,128)(2,1)S(1)}, bf16[288,640]{1,0:T(8,128)(2,1)S(1)}, u32[]{:S(2)}, u32[]{:S(2)}) collective-permute-start(bf16[288,640]{1,0:T(8,128)(2,1)S(1)} %add_convert_fusion.16), channel_id=1, source_target_pairs={{0,2},{1,3},{2,0},{3,1},{4,6},{5,7},{6,4},{7,5},{8,10},{9,11},{10,... | collective-permute-start | bytes 1105928 | tf_op jit(solution)/shard_map/ppermute | solution.py:719
  204.7 24.6 %collective-permute-start.23 = (bf16[1280,640]{1,0:T(8,128)(2,1)}, bf16[1280,640]{1,0:T(8,128)(2,1)}, u32[]{:S(2)}, u32[]{:S(2)}) collective-permute-start(bf16[1280,640]{1,0:T(8,128)(2,1)} %get-tuple-element.186), channel_id=1, source_target_pairs={{0,16},{16,0},{1,17},{17,1},{2,18},{18,2},{3,19},{19,3},{4,20},{20... | collective-permute-start | bytes 4915208 | tf_op jit(solution)/shard_map/ppermute | solution.py:715
  206.2 45.3 %collective-permute-start.15 = (bf16[3,256,1280]{2,1,0:T(8,128)(2,1)}, bf16[3,256,1280]{2,1,0:T(8,128)(2,1)}, u32[]{:S(2)}, u32[]{:S(2)}) collective-permute-start(bf16[3,256,1280]{2,1,0:T(8,128)(2,1)} %broadcast_select_fusion.6), channel_id=1, source_target_pairs={{0,16},{16,0},{1,17},{17,1},{2,18},{18,2},{3,19},{19,3},{4,20},{20... | collective-permute-start | bytes 5898248 | tf_op jit(solution)/shard_map/ppermute | solution.py:715
  209.6 11.8 %collective-permute-start.22 = (bf16[576,640]{1,0:T(8,128)(2,1)}, bf16[576,640]{1,0:T(8,128)(2,1)}, u32[]{:S(2)}, u32[]{:S(2)}) collective-permute-start(bf16[576,640]{1,0:T(8,128)(2,1)} %get-tuple-element.223), channel_id=1, source_target_pairs={{0,4},{1,5},{2,6},{3,7},{4,0},{5,1},{6,2},{7,3},{8,12},{9,13},{10,... | collective-permute-start | bytes 2211848 | tf_op jit(solution)/shard_map/ppermute | solution.py:719
  209.7 19.6 %collective-permute-start.21 = (bf16[576,640]{1,0:T(8,128)(2,1)S(1)}, bf16[576,640]{1,0:T(8,128)(2,1)S(1)}, u32[]{:S(2)}, u32[]{:S(2)}) collective-permute-start(bf16[576,640]{1,0:T(8,128)(2,1)S(1)} %pad_maximum_fusion.3), channel_id=1, source_target_pairs={{0,4},{1,5},{2,6},{3,7},{4,0},{5,1},{6,2},{7,3},{8,12},{9,13},{10,... | collective-permute-start | bytes 2211848 | tf_op jit(solution)/shard_map/ppermute | solution.py:719
  232.8 15.9 %collective-permute-start.40 = (bf16[640,640]{1,0:T(8,128)(2,1)}, bf16[640,640]{1,0:T(8,128)(2,1)}, u32[]{:S(2)}, u32[]{:S(2)}) collective-permute-start(bf16[640,640]{1,0:T(8,128)(2,1)} %get-tuple-element.221), channel_id=1, source_target_pairs={{0,1},{1,0},{2,3},{3,2},{4,5},{5,4},{6,7},{7,6},{8,9},{9,8},{10,11... | collective-permute-start | bytes 2457608 | tf_op jit(solution)/shard_map/ppermute | solution.py:719
  234.7 11.8 %collective-permute-start.33 = (bf16[288,640]{1,0:T(8,128)(2,1)}, bf16[288,640]{1,0:T(8,128)(2,1)}, u32[]{:S(2)}, u32[]{:S(2)}) collective-permute-start(bf16[288,640]{1,0:T(8,128)(2,1)} %add_convert_fusion.14), channel_id=1, source_target_pairs={{0,2},{1,3},{2,0},{3,1},{4,6},{5,7},{6,4},{7,5},{8,10},{9,11},{10,... | collective-permute-start | bytes 1105928 | tf_op jit(solution)/shard_map/ppermute | solution.py:719
  239.7 13.8 %collective-permute-start.26 = (f32[24,1280]{1,0:T(8,128)S(1)}, f32[24,1280]{1,0:T(8,128)S(1)}, u32[]{:S(2)}, u32[]{:S(2)}) collective-permute-start(f32[24,1280]{1,0:T(8,128)S(1)} %add.203), channel_id=1, source_target_pairs={{0,1},{1,0},{2,3},{3,2},{4,5},{5,4},{6,7},{7,6},{8,9},{9,8},{10,11... | collective-permute-start | bytes 368648 | tf_op jit(solution)/shard_map/ppermute | solution.py:719
  247.8 14.2 %collective-permute-start.34 = (bf16[288,640]{1,0:T(8,128)(2,1)S(1)}, bf16[288,640]{1,0:T(8,128)(2,1)S(1)}, u32[]{:S(2)}, u32[]{:S(2)}) collective-permute-start(bf16[288,640]{1,0:T(8,128)(2,1)S(1)} %add_convert_fusion.13), channel_id=1, source_target_pairs={{0,8},{1,9},{2,10},{3,11},{4,12},{5,13},{6,14},{7,15},{8,0},{9,1},... | collective-permute-start | bytes 1105928 | tf_op jit(solution)/shard_map/ppermute | solution.py:719
  250.1 13.1 %collective-permute-start.41 = (bf16[320,640]{1,0:T(8,128)(2,1)S(1)}, bf16[320,640]{1,0:T(8,128)(2,1)S(1)}, u32[]{:S(2)}, u32[]{:S(2)}) collective-permute-start(bf16[320,640]{1,0:T(8,128)(2,1)S(1)} %get-tuple-element.227), channel_id=1, source_target_pairs={{0,2},{1,3},{2,0},{3,1},{4,6},{5,7},{6,4},{7,5},{8,10},{9,11},{10,... | collective-permute-start | bytes 1228808 | tf_op jit(solution)/shard_map/ppermute | solution.py:719
  253.5 11.8 %collective-permute-start.27 = (f32[24,1280]{1,0:T(8,128)S(1)}, f32[24,1280]{1,0:T(8,128)S(1)}, u32[]{:S(2)}, u32[]{:S(2)}) collective-permute-start(f32[24,1280]{1,0:T(8,128)S(1)} %add.204), channel_id=1, source_target_pairs={{0,4},{1,5},{2,6},{3,7},{4,0},{5,1},{6,2},{7,3},{8,12},{9,13},{10,... | collective-permute-start | bytes 368648 | tf_op jit(solution)/shard_map/ppermute | solution.py:719
  262.1 10.6 %collective-permute-start.35 = (bf16[288,640]{1,0:T(8,128)(2,1)S(1)}, bf16[288,640]{1,0:T(8,128)(2,1)S(1)}, u32[]{:S(2)}, u32[]{:S(2)}) collective-permute-start(bf16[288,640]{1,0:T(8,128)(2,1)S(1)} %add_convert_fusion.12), channel_id=1, source_target_pairs={{0,2},{1,3},{2,0},{3,1},{4,6},{5,7},{6,4},{7,5},{8,10},{9,11},{10,... | collective-permute-start | bytes 1105928 | tf_op jit(solution)/shard_map/ppermute | solution.py:719
  263.2 9.6 %collective-permute-start.42 = (bf16[160,640]{1,0:T(8,128)(2,1)S(1)}, bf16[160,640]{1,0:T(8,128)(2,1)S(1)}, u32[]{:S(2)}, u32[]{:S(2)}) collective-permute-start(bf16[160,640]{1,0:T(8,128)(2,1)S(1)} %add_convert_fusion.22), channel_id=1, source_target_pairs={{0,4},{1,5},{2,6},{3,7},{4,0},{5,1},{6,2},{7,3},{8,12},{9,13},{10,... | collective-permute-start | bytes 614408 | tf_op jit(solution)/shard_map/ppermute | solution.py:719
  263.5 47.6 %collective-permute-start.30 = (bf16[1152,640]{1,0:T(8,128)(2,1)S(1)}, bf16[1152,640]{1,0:T(8,128)(2,1)S(1)}, u32[]{:S(2)}, u32[]{:S(2)}) collective-permute-start(bf16[1152,640]{1,0:T(8,128)(2,1)S(1)} %pad_maximum_fusion.refs_0_), channel_id=1, source_target_pairs={{0,1},{1,0},{2,3},{3,2},{4,5},{5,4},{6,7},{7,6},{8,9},{9,8},{10,11... | collective-permute-start | bytes 4423688 | tf_op jit(solution)/shard_map/ppermute | solution.py:719
  264.9 46.2 %collective-permute-start.31 = (bf16[1152,640]{1,0:T(8,128)(2,1)S(1)}, bf16[1152,640]{1,0:T(8,128)(2,1)S(1)}, u32[]{:S(2)}, u32[]{:S(2)}) collective-permute-start(bf16[1152,640]{1,0:T(8,128)(2,1)S(1)} %pad_maximum_fusion.refs_0_), channel_id=1, source_target_pairs={{0,16},{16,0},{1,17},{17,1},{2,18},{18,2},{3,19},{19,3},{4,20},{20... | collective-permute-start | bytes 4423688 | tf_op jit(solution)/shard_map/ppermute | solution.py:715
  265.4 10.0 %collective-permute-start.28 = (f32[24,1280]{1,0:T(8,128)S(1)}, f32[24,1280]{1,0:T(8,128)S(1)}, u32[]{:S(2)}, u32[]{:S(2)}) collective-permute-start(f32[24,1280]{1,0:T(8,128)S(1)} %add.205), channel_id=1, source_target_pairs={{0,2},{1,3},{2,0},{3,1},{4,6},{5,7},{6,4},{7,5},{8,10},{9,11},{10,... | collective-permute-start | bytes 368648 | tf_op jit(solution)/shard_map/ppermute | solution.py:719
  272.8 16.0 %collective-permute-start.36 = (bf16[576,640]{1,0:T(8,128)(2,1)S(1)}, bf16[576,640]{1,0:T(8,128)(2,1)S(1)}, u32[]{:S(2)}, u32[]{:S(2)}) collective-permute-start(bf16[576,640]{1,0:T(8,128)(2,1)S(1)} %pad_maximum_fusion.4), channel_id=1, source_target_pairs={{0,4},{1,5},{2,6},{3,7},{4,0},{5,1},{6,2},{7,3},{8,12},{9,13},{10,... | collective-permute-start | bytes 2211848 | tf_op jit(solution)/shard_map/ppermute | solution.py:719
  272.9 12.4 %collective-permute-start.43 = (bf16[160,640]{1,0:T(8,128)(2,1)S(1)}, bf16[160,640]{1,0:T(8,128)(2,1)S(1)}, u32[]{:S(2)}, u32[]{:S(2)}) collective-permute-start(bf16[160,640]{1,0:T(8,128)(2,1)S(1)} %add_convert_fusion.21), channel_id=1, source_target_pairs={{0,8},{1,9},{2,10},{3,11},{4,12},{5,13},{6,14},{7,15},{8,0},{9,1},... | collective-permute-start | bytes 614408 | tf_op jit(solution)/shard_map/ppermute | solution.py:719
  275.3 38.2 %collective-permute-start.24 = (bf16[3,256,1280]{2,1,0:T(8,128)(2,1)S(1)}, bf16[3,256,1280]{2,1,0:T(8,128)(2,1)S(1)}, u32[]{:S(2)}, u32[]{:S(2)}) collective-permute-start(bf16[3,256,1280]{2,1,0:T(8,128)(2,1)S(1)} %broadcast_select_fusion.2), channel_id=1, source_target_pairs={{0,16},{16,0},{1,17},{17,1},{2,18},{18,2},{3,19},{19,3},{4,20},{20... | collective-permute-start | bytes 5898248 | tf_op jit(solution)/shard_map/ppermute | solution.py:715
  285.3 7.7 %collective-permute-start.29 = (f32[24,1280]{1,0:T(8,128)S(1)}, f32[24,1280]{1,0:T(8,128)S(1)}, u32[]{:S(2)}, u32[]{:S(2)}) collective-permute-start(f32[24,1280]{1,0:T(8,128)S(1)} %add.206), channel_id=1, source_target_pairs={{0,8},{1,9},{2,10},{3,11},{4,12},{5,13},{6,14},{7,15},{8,0},{9,1},... | collective-permute-start | bytes 368648 | tf_op jit(solution)/shard_map/ppermute | solution.py:719
  288.8 6.5 %collective-permute-start.44 = (bf16[160,640]{1,0:T(8,128)(2,1)S(1)}, bf16[160,640]{1,0:T(8,128)(2,1)S(1)}, u32[]{:S(2)}, u32[]{:S(2)}) collective-permute-start(bf16[160,640]{1,0:T(8,128)(2,1)S(1)} %add_convert_fusion.20), channel_id=1, source_target_pairs={{0,4},{1,5},{2,6},{3,7},{4,0},{5,1},{6,2},{7,3},{8,12},{9,13},{10,... | collective-permute-start | bytes 614408 | tf_op jit(solution)/shard_map/ppermute | solution.py:719
  293.0 19.4 %collective-permute-start.37 = (bf16[1152,640]{1,0:T(8,128)(2,1)S(1)}, bf16[1152,640]{1,0:T(8,128)(2,1)S(1)}, u32[]{:S(2)}, u32[]{:S(2)}) collective-permute-start(bf16[1152,640]{1,0:T(8,128)(2,1)S(1)} %pad_maximum_fusion.1.refs_4_), channel_id=1, source_target_pairs={{0,1},{1,0},{2,3},{3,2},{4,5},{5,4},{6,7},{7,6},{8,9},{9,8},{10,11... | collective-permute-start | bytes 4423688 | tf_op jit(solution)/shard_map/ppermute | solution.py:719
  295.3 12.5 %collective-permute-start.45 = (bf16[320,640]{1,0:T(8,128)(2,1)S(1)}, bf16[320,640]{1,0:T(8,128)(2,1)S(1)}, u32[]{:S(2)}, u32[]{:S(2)}) collective-permute-start(bf16[320,640]{1,0:T(8,128)(2,1)S(1)} %pad_maximum_fusion.5), channel_id=1, source_target_pairs={{0,2},{1,3},{2,0},{3,1},{4,6},{5,7},{6,4},{7,5},{8,10},{9,11},{10,... | collective-permute-start | bytes 1228808 | tf_op jit(solution)/shard_map/ppermute | solution.py:719
  307.9 13.2 %collective-permute-start.46 = (bf16[640,640]{1,0:T(8,128)(2,1)S(1)}, bf16[640,640]{1,0:T(8,128)(2,1)S(1)}, u32[]{:S(2)}, u32[]{:S(2)}) collective-permute-start(bf16[640,640]{1,0:T(8,128)(2,1)S(1)} %pad_maximum_fusion.2.refs_8_), channel_id=1, source_target_pairs={{0,1},{1,0},{2,3},{3,2},{4,5},{5,4},{6,7},{7,6},{8,9},{9,8},{10,11... | collective-permute-start | bytes 2457608 | tf_op jit(solution)/shard_map/ppermute | solution.py:719
  311.1 13.2 %collective-permute-start.32 = (bf16[1152,640]{1,0:T(8,128)(2,1)S(1)}, bf16[1152,640]{1,0:T(8,128)(2,1)S(1)}, u32[]{:S(2)}, u32[]{:S(2)}) collective-permute-start(bf16[1152,640]{1,0:T(8,128)(2,1)S(1)} %collective-permute-done.30.refs_1_), channel_id=1, source_target_pairs={{0,16},{16,0},{1,17},{17,1},{2,18},{18,2},{3,19},{19,3},{4,20},{20... | collective-permute-start | bytes 4423688 | tf_op jit(solution)/shard_map/ppermute | solution.py:715
  311.2 13.1 %collective-permute-start.38 = (bf16[1152,640]{1,0:T(8,128)(2,1)S(1)}, bf16[1152,640]{1,0:T(8,128)(2,1)S(1)}, u32[]{:S(2)}, u32[]{:S(2)}) collective-permute-start(bf16[1152,640]{1,0:T(8,128)(2,1)S(1)} %pad_maximum_fusion.1.refs_4_), channel_id=1, source_target_pairs={{0,16},{16,0},{1,17},{17,1},{2,18},{18,2},{3,19},{19,3},{4,20},{20... | collective-permute-start | bytes 4423688 | tf_op jit(solution)/shard_map/ppermute | solution.py:715
  312.4 14.1 %collective-permute-start.39 = (bf16[1152,640]{1,0:T(8,128)(2,1)S(1)}, bf16[1152,640]{1,0:T(8,128)(2,1)}, u32[]{:S(2)}, u32[]{:S(2)}) collective-permute-start(bf16[1152,640]{1,0:T(8,128)(2,1)S(1)} %collective-permute-done.37.refs_5_), channel_id=1, source_target_pairs={{0,16},{16,0},{1,17},{17,1},{2,18},{18,2},{3,19},{19,3},{4,20},{20... | collective-permute-start | bytes 4423688 | tf_op jit(solution)/shard_map/ppermute | solution.py:715
  313.5 10.8 %collective-permute-start.47 = (bf16[640,640]{1,0:T(8,128)(2,1)S(1)}, bf16[640,640]{1,0:T(8,128)(2,1)S(1)}, u32[]{:S(2)}, u32[]{:S(2)}) collective-permute-start(bf16[640,640]{1,0:T(8,128)(2,1)S(1)} %pad_maximum_fusion.2.refs_8_), channel_id=1, source_target_pairs={{0,16},{16,0},{1,17},{17,1},{2,18},{18,2},{3,19},{19,3},{4,20},{20... | collective-permute-start | bytes 2457608 | tf_op jit(solution)/shard_map/ppermute | solution.py:715
  321.1 3.2 collective-permute-start.48
  (41 other events, 284.0 us)
